TPU v7x, 32 devices: a whole 2x2x4 slice. The times are simulated.
32 devices in a mesh: dp: 2 (over core), expert: 16 (over z, y, x).
Axes of the slice: x: 2, y: 2, z: 4, core: 2. Of those that a mesh axis runs over, the one named last changes fastest.
Arguments:
- tokens: bfloat16 [4096, 2048], P(('dp', 'expert')), may hold values from -6 to 6
- out_grad: bfloat16 [4096, 2048], P(('dp', 'expert')), may hold values from -6 to 6
- routes: int32 [4096, 8], P(('dp', 'expert')), may hold values from 0 to 15, all different within a row; in each aligned block of 128 rows (0 to 127, 128 to 255, ...) at most 128 rows name the same one
- probs: bfloat16 [4096, 8], P(('dp', 'expert')), may hold values from 0.019897461 to 1
- w_gate_up: bfloat16 [16, 2048, 768], P('expert'), may hold values from -0.125 to 0.125
- w_down: bfloat16 [16, 384, 2048], P('expert'), may hold values from -0.3125 to 0.3125
- moment_one: float32 [2, 16, 384, 2048], P('dp', 'expert'), may hold values from -12 to 12
- moment_two: float32 [2, 16, 384, 2048], P('dp', 'expert'), may hold values from 1 to 64
- replicas: int32 [16, 2], P('expert'), may hold values from 0 to 1, as said below
- leader: int32 [16], P('expert'), may hold values from 0 to 1
Outputs:
- token_grad: bfloat16 [4096, 2048], P(('dp', 'expert'))
- prob_grad: bfloat16 [4096, 8], P(('dp', 'expert'))
- new_down: bfloat16 [2, 16, 384, 2048], P('dp', 'expert')
- new_moment_one: float32 [2, 16, 384, 2048], P('dp', 'expert')
- new_moment_two: float32 [2, 16, 384, 2048], P('dp', 'expert')
Inputs may be any that keep to these rules, and one draw needn't show every extreme that they name: `routes`: in the 128 rows of one device no expert is named by more than 128 rows. Each expert has one to 2 live replicas, its lead among them.
All inputs are finite; a program needn't handle non-finite values.
Results may differ from a plain program's by a relative error of at most 0.0064.
Values may be sent and summed in bfloat16 or wider, within the bound.
No kernel may reach another device: no remote copies, remote signals or barrier semaphores. Data moves between devices by JAX's collectives and lax.ppermute only.
A program may use at most 128 MiB of HBM per device.

v0:
```python
import functools
import jax
import jax.numpy as jnp
from jax import lax
from jax.experimental import pallas as pl
from jax.experimental.pallas import tpu as pltpu
from jax.sharding import PartitionSpec as P

learn_rate = 0.01
beta_one = 0.9
beta_two = 0.95
adam_eps = 1e-08
weight_decay = 0.1
adam_step = 100

f32 = jnp.float32
bf16 = jnp.bfloat16
plane = 4
lanes = 128
tile = 256


def adam_update(grad, m_old, v_old, w_old):
    m_new = beta_one * m_old + (1.0 - beta_one) * grad
    v_new = beta_two * v_old + (1.0 - beta_two) * grad * grad
    m_hat = m_new / (1.0 - beta_one**adam_step)
    v_hat = v_new / (1.0 - beta_two**adam_step)
    w_wide = w_old.astype(f32)
    w_new = (
        w_wide - learn_rate * (m_hat / (jnp.sqrt(v_hat) + adam_eps) + weight_decay * w_wide)
    ).astype(bf16)
    return (m_new, v_new, w_new)


def hop(value, flip):
    n = lax.axis_size("expert")
    return lax.ppermute(value, "expert", [(i, i ^ flip) for i in range(n)])


def climb(value, way, low, high):
    pairs = [(i, i + way * plane) for i in range(low * plane, high * plane)]
    return lax.ppermute(value, "expert", pairs)


def turn(value, step):
    n = lax.axis_size("dp")
    return lax.ppermute(value, "dp", [((r + step) % n, r) for r in range(n)])


def after(value, *earlier):
    return lax.optimization_barrier((value, *earlier))[0]


def nt(a, b):
    return lax.dot_general(a, b, (((1,), (1,)), ((), ())), preferred_element_type=f32)


def tn(a, b):
    return lax.dot_general(a, b, (((0,), (0,)), ((), ())), preferred_element_type=f32)


def source(layer, k):
    far = layer ^ k
    return ("down", far - layer) if far > layer else ("up", layer - far)


class Pass:
    def __init__(self, tok, model, half, n_ex, n_dp, slots, blocks, last):
        self.tok, self.model, self.half, self.n_ex, self.n_dp = tok, model, half, n_ex, n_dp
        self.slots, self.blocks, self.last = slots, blocks, last
        self.layers = n_ex // plane
        self.rows = tok * len(blocks)
        self.width = model // n_dp
        self.tail = -(-n_ex // 16) * 16

    def kernel(self, n_in, *refs):
        tok, model, half, rows, width = self.tok, self.model, self.half, self.rows, self.width
        n_dp, layers, slots, blocks = self.n_dp, self.layers, self.slots, self.blocks
        ins = dict(zip(self.names, refs[:n_in]))
        n_out = len(self.outs)
        outs = dict(zip(self.outs, refs[n_in : n_in + n_out]))
        scratch = list(refs[n_in + n_out :])
        xs, ys, ps, ws, gu, back, pre, sc, pcol, dx, pr, keep, send = scratch[:13]
        sem_t, sem_w, sem_i, sem_o = scratch[13:17]
        me_dp = lax.axis_index("dp")
        me = lax.axis_index("expert")
        here, layer = lax.rem(me, plane), lax.div(me, plane)

        def row_copies(ref, b):
            at = pl.ds(b * tok, tok)
            return (
                pltpu.make_async_copy(ref.at[pl.ds(0, tok)], xs.at[at], sem_t.at[b, 0]),
                pltpu.make_async_copy(ref.at[pl.ds(tok, tok)], ys.at[at], sem_t.at[b, 1]),
                pltpu.make_async_copy(
                    ref.at[pl.ds(2 * tok, self.tail), pl.ds(0, lanes)],
                    ps.at[b, pl.ds(0, self.tail)],
                    sem_t.at[b, 2],
                ),
            )

        ps[...] = jnp.zeros_like(ps)
        for b, k in enumerate(blocks):
            if k == 0:
                for copy in row_copies(ins["own"], b):
                    copy.start()
                continue
            for z in range(layers):

                @pl.when(layer == z)
                def _(b=b, k=k, z=z):
                    for copy in row_copies(ins[source(z, k)], b):
                        copy.start()

        def weight_copies(i):
            s = slots[i]
            if s == 0:
                return [pltpu.make_async_copy(ins["w0"], ws.at[i % 2], sem_w.at[i, 0])]
            out = []
            for k in range(n_dp):
                for h in range(2):
                    at = lax.rem(me_dp + k, n_dp) * width + h * (width // 2)
                    at = pl.multiple_of(at, width // 2)
                    out.append(
                        pltpu.make_async_copy(
                            ins["w%d_%d_%d" % (s, k, h)],
                            ws.at[i % 2, pl.ds(at, width // 2)],
                            sem_w.at[i, 2 * k + h],
                        )
                    )
            return out

        for copy in weight_copies(0):
            copy.start()
        extra = []
        held = {"dx": 0, "pr": 0, "keep": 0, "send": 0}
        for name, ref in ins.items():
            kind = name[0][:-1] if isinstance(name, tuple) and name[0][:-1] in held else None
            if kind is None:
                continue
            n = ref.shape[0]
            to = {"dx": dx, "pr": pr, "keep": keep, "send": send}[kind].at[pl.ds(held[kind], n)]
            extra.append(pltpu.make_async_copy(ref, to, sem_i.at[len(extra)]))
            held[kind] += n
        if not held["pr"]:
            pr[...] = jnp.zeros_like(pr)
        for copy in extra:
            copy.start()

        for b in range(len(blocks)):
            for copy in row_copies(ins["own"], b):
                copy.wait()
            pcol[pl.ds(b * tok, tok), :] = jnp.transpose(ps[b].astype(f32))
        chunk = min(128, tok)
        lane = lax.broadcasted_iota(jnp.int32, (chunk, lanes), 1)
        pending = []

        for i, s in enumerate(slots):
            for copy in weight_copies(i):
                copy.wait()
            if i + 1 < len(slots):
                for copy in weight_copies(i + 1):
                    copy.start()
            w = ws.at[i % 2]
            for n in range(0, 2 * half, tile):
                gu[:, n : n + tile] = jnp.dot(
                    xs[...], w[:, n : n + tile], preferred_element_type=f32
                )
            back[...] = jnp.dot(ys[...], w[:, 2 * half :], preferred_element_type=f32)
            if i == 0:
                for copy in extra:
                    copy.wait()
            expert = layer * plane + lax.bitwise_xor(here, jnp.int32(s))

            @pl.loop(0, rows // chunk)
            def _(r):
                at = pl.ds(pl.multiple_of(r * chunk, chunk), chunk)
                gate, upper, h = gu[at, :half], gu[at, half:], back[at, :]
                hit = lane == expert
                p = jnp.sum(jnp.where(hit, pcol[at, :], 0.0), axis=1, keepdims=True)
                sigma = jax.nn.sigmoid(gate)
                silu = gate * sigma
                hidden = (silu * upper).astype(bf16).astype(f32)
                pair = jnp.sum(hidden * h, axis=1, keepdims=True)
                pr[at, :] += jnp.where(hit, pair, 0.0)
                grad = p * h
                pre[at, :half] = (grad * upper * (sigma * (1.0 + gate * (1.0 - sigma)))).astype(bf16)
                pre[at, half:] = (grad * silu).astype(bf16)
                sc[at, :] = (p * hidden).astype(bf16)

            add_dx = held["dx"] or i > 0
            for d in range(0, model, 2 * tile):
                at = slice(d, d + 2 * tile)
                part = nt(pre[...], w[at, : 2 * half])
                dx[:, at] = dx[:, at] + part if add_dx else part
            for d in range(0, width, 2 * tile):
                at = slice(d, d + 2 * tile)
                col = pl.ds(pl.multiple_of(me_dp * width + d, tile), 2 * tile)
                part = tn(sc[...], ys[:, col])
                keep[i, :, at] = keep[i, :, at] + part if held["keep"] else part
                for k in range(1, n_dp):
                    col = lax.rem(me_dp + n_dp - k, n_dp) * width + d
                    part = tn(sc[...], ys[:, pl.ds(pl.multiple_of(col, tile), 2 * tile)])
                    if held["send"]:
                        part = send[i, k - 1, :, at].astype(f32) + part
                    send[i, k - 1, :, at] = part.astype(bf16)

            pending.append(
                pltpu.make_async_copy(keep.at[i], outs["keep"].at[i], sem_o.at[2 * i])
            )
            pending.append(
                pltpu.make_async_copy(send.at[i], outs["send"].at[i], sem_o.at[2 * i + 1])
            )
            pending[-2].start()
            pending[-1].start()
        n = 2 * len(slots)
        if not self.last:
            pending.append(pltpu.make_async_copy(dx, outs["dx"], sem_o.at[n]))
            pending.append(pltpu.make_async_copy(pr, outs["pr"], sem_o.at[n + 1]))
            pending[-2].start()
            pending[-1].start()
        else:
            rows_out = scratch[17]
            for b, k in enumerate(blocks):
                at = pl.ds(b * tok, tok)
                rows_out[b, pl.ds(0, tok), :] = dx[at, :].astype(bf16)
                rows_out[b, pl.ds(tok, self.tail), :] = jnp.zeros((self.tail, model), bf16)
                turned = jnp.transpose(pr[at, :])[: self.tail]
                rows_out[b, pl.ds(tok, self.tail), pl.ds(0, lanes)] = turned.astype(bf16)
                dest = lax.bitwise_xor(layer, jnp.int32(k))
                copy = pltpu.make_async_copy(rows_out.at[b], outs["back"].at[dest], sem_o.at[n + b])
                copy.start()
                pending.append(copy)
        for copy in pending:
            copy.wait()

    def call(self, ins):
        tok, model, half, rows, width = self.tok, self.model, self.half, self.rows, self.width
        n_dp, n = self.n_dp, len(self.slots)
        shape = {"keep": ((n, half, width), f32)}
        shape["send"] = ((n, max(n_dp - 1, 1), half, width), bf16)
        if self.last:
            shape["back"] = ((self.layers, tok + self.tail, model), bf16)
        else:
            shape["dx"] = ((rows, model), f32)
            shape["pr"] = ((rows, lanes), f32)
        self.names, self.outs = list(ins), list(shape)
        scratch = [
            pltpu.VMEM((rows, model), bf16),
            pltpu.VMEM((rows, model), bf16),
            pltpu.VMEM((len(self.blocks), tok, lanes), bf16),
            pltpu.VMEM((min(n, 2), model, 3 * half), bf16),
            pltpu.VMEM((rows, 2 * half), f32),
            pltpu.VMEM((rows, half), f32),
            pltpu.VMEM((rows, 2 * half), bf16),
            pltpu.VMEM((rows, half), bf16),
            pltpu.VMEM((rows, lanes), f32),
            pltpu.VMEM((rows, model), f32),
            pltpu.VMEM((rows, lanes), f32),
            pltpu.VMEM((n, half, width), f32),
            pltpu.VMEM((n, max(n_dp - 1, 1), half, width), bf16),
            pltpu.SemaphoreType.DMA((len(self.blocks), 3)),
            pltpu.SemaphoreType.DMA((n, 2 * n_dp)),
            pltpu.SemaphoreType.DMA((8,)),
            pltpu.SemaphoreType.DMA((2 * n + len(self.blocks) + 2,)),
        ]
        if self.last:
            scratch.append(pltpu.VMEM((self.layers, tok + self.tail, model), bf16))
        out = pl.pallas_call(
            functools.partial(self.kernel, len(ins)),
            out_shape=[jax.ShapeDtypeStruct(*v) for v in shape.values()],
            in_specs=[pl.BlockSpec(memory_space=pl.ANY)] * len(ins),
            out_specs=[pl.BlockSpec(memory_space=pl.ANY)] * len(shape),
            scratch_shapes=scratch,
            compiler_params=pltpu.CompilerParams(vmem_limit_bytes=56 * 2**20),
            cost_estimate=pl.CostEstimate(flops=1000, bytes_accessed=1000, transcendentals=0),
        )(*ins.values())
        return dict(zip(shape, out))


def adam_kernel(n_dp, lead_ref, *refs):
    grads = refs[:n_dp]
    m_ref, v_ref, w_ref, m_out, v_out, w_out = refs[n_dp:]
    me_dp = lax.axis_index("dp")
    width = grads[0].shape[1]
    is_lead = lead_ref[0] == me_dp
    for k, ref in enumerate(grads):
        at = lax.rem(me_dp + k, n_dp) * width
        at = pl.ds(pl.multiple_of(at, width), width)
        m_old, v_old = m_ref[0, 0, :, at], v_ref[0, 0, :, at]
        m_new, v_new, w_new = adam_update(ref[...].astype(f32), m_old, v_old, w_ref[0, :, at])
        m_out[0, 0, :, at] = jnp.where(is_lead, m_new, m_old)
        v_out[0, 0, :, at] = jnp.where(is_lead, v_new, v_old)
        w_out[:, at] = w_new


def adam_call(parts, leader, moment_one, moment_two, w_down):
    half, model = w_down.shape[1:]
    step = 48 if half % 48 == 0 else half
    n_dp = len(parts)
    width = model // n_dp
    wide = pl.BlockSpec((1, 1, step, model), lambda i: (0, 0, i, 0))
    return pl.pallas_call(
        functools.partial(adam_kernel, n_dp),
        grid=(half // step,),
        out_shape=[
            jax.ShapeDtypeStruct(moment_one.shape, f32),
            jax.ShapeDtypeStruct(moment_two.shape, f32),
            jax.ShapeDtypeStruct((half, model), bf16),
        ],
        in_specs=[pl.BlockSpec(memory_space=pltpu.SMEM)]
        + [pl.BlockSpec((step, width), lambda i: (i, 0))] * n_dp
        + [wide, wide, pl.BlockSpec((1, step, model), lambda i: (0, i, 0))],
        out_specs=[wide, wide, pl.BlockSpec((step, model), lambda i: (i, 0))],
        compiler_params=pltpu.CompilerParams(vmem_limit_bytes=32 * 2**20),
        cost_estimate=pl.CostEstimate(
            flops=20 * half * model, bytes_accessed=20 * half * model, transcendentals=0
        ),
    )(leader, *parts, moment_one, moment_two, w_down)


def body(
    tokens, out_grad, routes, probs, w_gate_up, w_down, moment_one, moment_two, replicas, leader
):
    tok_dev, model = tokens.shape
    half = w_down.shape[1]
    n_dp = lax.axis_size("dp")
    n_ex = lax.axis_size("expert")
    layers = n_ex // plane
    width = model // n_dp
    me_dp = lax.axis_index("dp")
    me = lax.axis_index("expert")
    layer = me // plane
    tail = -(-n_ex // 16) * 16

    def others(value):
        return [turn(value, k) for k in range(1, n_dp)]

    wide = probs.astype(f32)
    ids = jnp.arange(tail, dtype=jnp.int32)
    chosen = routes.T[None] == ids[:, None, None]
    p_all = jnp.sum(jnp.where(chosen, wide.T[None], 0.0), axis=1).astype(bf16)
    p_all = jnp.pad(p_all, ((0, 0), (0, model - tok_dev)))
    own = jnp.concatenate([tokens, out_grad, p_all], 0)
    w_gu, w_dn = w_gate_up[0], w_down[0]
    w_own = jnp.concatenate([w_gu, w_dn.T], 1)
    p1 = lax.dynamic_slice_in_dim(w_own, me_dp * width, width // 2, 0)
    p2 = lax.dynamic_slice_in_dim(w_own, me_dp * width + width // 2, width // 2, 0)
    up, down = {}, {}
    up[1], down[1] = climb(own, 1, 0, layers - 1), climb(own, -1, 1, layers)
    x_p1, y_p2 = hop(p1, 1), hop(p2, 2)

    p1, p2, up[1], down[1], x_p1, y_p2 = lax.optimization_barrier(
        (p1, p2, up[1], down[1], x_p1, y_p2)
    )
    x_p2, y_p1 = hop(p2, 1), hop(p1, 2)
    if layers > 2:
        up[2], down[2] = climb(up[1], 1, 1, layers - 1), climb(down[1], -1, 1, layers - 1)
    x_o1 = others(x_p1)
    y_o2 = others(after(y_p2, *x_o1))

    (x_p1, y_p2, x_p2, y_p1, x_o1, y_o2, up, down) = lax.optimization_barrier(
        (x_p1, y_p2, x_p2, y_p1, x_o1, y_o2, up, down)
    )
    d_p2, d_p1 = hop(y_p2, 1), hop(x_p1, 2)
    for k in range(3, layers):
        up[k] = climb(up[k - 1], 1, k - 1, layers - 1)
        down[k] = climb(down[k - 1], -1, 1, layers - k + 1)
    x_o2 = others(x_p2)
    y_o1 = others(after(y_p1, *x_o2))
    weights = {"w0": w_own}

    def name_parts(s, firsts, seconds):
        for k in range(n_dp):
            weights["w%d_%d_0" % (s, k)] = firsts[k]
            weights["w%d_%d_1" % (s, k)] = seconds[k]

    name_parts(1, [x_p1] + x_o1, [x_p2] + x_o2)
    name_parts(2, [y_p1] + y_o1, [y_p2] + y_o2)

    def pick(slots, blocks):
        got = {"own": own}
        for k in blocks:
            for z in range(layers):
                if k:
                    way, steps = source(z, k)
                    got[(way, steps)] = (up if way == "up" else down)[steps]
        for name, value in weights.items():
            if int(name[1]) in slots:
                got[name] = value
        return got

    near, far = list(range(layers - 1)), [layers - 1]
    make = functools.partial(Pass, tok_dev, model, half, n_ex, n_dp)

    def carry(*passes):
        return {(k + str(i), i): p[k] for i, (p, keys) in enumerate(passes) for k in keys}

    zero = make([0], near, False).call(pick([0], near))
    one = make([1, 2], near, False).call(pick([1, 2], near) | carry((zero, ("dx", "pr"))))

    zero, one, d_p1, d_p2, up, down = lax.optimization_barrier((zero, one, d_p1, d_p2, up, down))
    d_o1 = others(d_p1)
    d_o2 = others(after(d_p2, *d_o1))
    name_parts(3, [d_p1] + d_o1, [d_p2] + d_o2)
    grads = ("keep", "send")
    two = make([0, 1, 2], far, False).call(pick([0, 1, 2], far) | carry((zero, grads), (one, grads)))
    last = make([3], near + far, True).call(
        pick([3], near + far) | carry((one, ("dx", "pr")), (two, ("dx", "pr")))
    )

    swapped = [turn(two["send"][:, k - 1], k) for k in range(1, n_dp)]
    sent = [
        hop((two["keep"][s] + sum(v[s].astype(f32) for v in swapped)).astype(bf16), s)
        for s in (1, 2)
    ]
    swapped_across = [turn(last["send"][0, k - 1], k) for k in range(1, n_dp)]
    across = last["keep"][0] + sum(v.astype(f32) for v in swapped_across)
    sent.append(hop(across.astype(bf16), 3))
    back = last["back"]

    def term(dest):
        return lax.dynamic_index_in_dim(back, dest, 0, False).astype(f32)

    from_below = from_above = 0.0
    for k in range(layers - 1, 0, -1):
        send_up = (term(jnp.minimum(layer + k, layers - 1)) + from_below).astype(bf16)
        send_down = (term(jnp.maximum(layer - k, 0)) + from_above).astype(bf16)
        send_up, send_down = lax.optimization_barrier((send_up, send_down))
        from_below = climb(send_up, 1, 0, layers - k)
        from_above = climb(send_down, -1, k, layers)
        if k > 1:
            from_below, from_above = from_below.astype(f32), from_above.astype(f32)

    sent = lax.optimization_barrier((sent, send_up, send_down))[0]
    grad = two["keep"][0] + sum(v[0].astype(f32) for v in swapped)
    grad = (grad + sum(v.astype(f32) for v in sent)).astype(bf16)
    parts = [grad] + others(grad)
    new_one, new_two, w_new = adam_call(parts, leader, moment_one, moment_two, w_down)
    lead = leader[0]
    fresh = w_new
    for k in range(1, n_dp):
        fresh = jnp.where((me_dp + k) % n_dp == lead, turn(w_new, k), fresh)

    from_below, from_above = lax.optimization_barrier((from_below, from_above, w_new))[:2]
    total = term(layer) + from_below.astype(f32) + from_above.astype(f32)
    token_grad = total[:tok_dev].astype(bf16)
    pair = total[tok_dev:, :tok_dev]
    prob_grad = jnp.sum(jnp.where(chosen, pair[:, None, :], 0.0), axis=0).T.astype(bf16)
    is_live = replicas[0][me_dp] == 1
    new_down = jnp.where(is_live, fresh, w_dn)[None, None]
    return (token_grad, prob_grad, new_down, new_one, new_two)


def solution(mesh):
    in_specs = (
        P(("dp", "expert"), None),
        P(("dp", "expert"), None),
        P(("dp", "expert"), None),
        P(("dp", "expert"), None),
        P("expert", None, None),
        P("expert", None, None),
        P("dp", "expert", None, None),
        P("dp", "expert", None, None),
        P("expert", None),
        P("expert"),
    )
    out_specs = (
        P(("dp", "expert"), None),
        P(("dp", "expert"), None),
        P("dp", "expert", None, None),
        P("dp", "expert", None, None),
        P("dp", "expert", None, None),
    )
    return jax.shard_map(body, mesh=mesh, in_specs=in_specs, out_specs=out_specs, check_vma=False)
```

profile of v0, /device:TPU:1, one launch (start us, length us, event | category | flops | bytes accessed | tf_op | source)
XLA Modules:
  0.0 257.4 jit_solution(3170355354672205523)
XLA Ops:
  0.6 1.9 copy.16
  2.6 2.2 fusion.5
  4.8 2.1 collective-permute-start.2
  6.9 1.2 collective-permute-start.3
  8.3 3.3 %collective-permute-start = (bf16[272,2048]{1,0:T(8,128)(2,1)S(1)}, bf16[272,2048]{1,0:T(8,128)(2,1)S(1)}, u32[]{:S(2)}, u32[]{:S(2)}) collective-permute-start(bf16[272,2048]{1,0:T(8,128)(2,1)S(1)} %fusion.11.refs_0_), channel_id=1, source_target_pairs={{0,4},{1,5},{2,6},{3,7},{4,8},{5,9},{6,10},{7,11},{8,12},{9,13},{1... | collective-permute-start | bytes 3342344 | tf_op jit(solution)/shard_map/ppermute | solution.py:42
  11.6 1.3 collective-permute-start.1
  12.9 21.2 %collective-permute-done.refs_2_.refs_3_ = bf16[272,2048]{1,0:T(8,128)(2,1)S(1)} collective-permute-done((bf16[272,2048]{1,0:T(8,128)(2,1)S(1)}, bf16[272,2048]{1,0:T(8,128)(2,1)S(1)}, u32[]{:S(2)}, u32[]{:S(2)}) %collective-permute-start) | collective-permute-done | bytes 1114144 | tf_op jit(solution)/shard_map/ppermute | solution.py:42
  34.1 3.9 %collective-permute-done.1.refs_1_.refs_2_ = bf16[272,2048]{1,0:T(8,128)(2,1)S(1)} collective-permute-done((bf16[272,2048]{1,0:T(8,128)(2,1)S(1)}, bf16[272,2048]{1,0:T(8,128)(2,1)S(1)}, u32[]{:S(2)}, u32[]{:S(2)}) %collective-permute-start.1) | collective-permute-done | bytes 1114144 | tf_op jit(solution)/shard_map/ppermute | solution.py:42
  38.0 2.5 collective-permute-start.6
  41.0 2.0 collective-permute-done.6.refs_7_.refs_8_
  43.0 1.0 copy-done.14
  45.1 1.3 collective-permute-start.9
  46.4 28.9 %collective-permute-done.9.refs_3_ = bf16[272,2048]{1,0:T(8,128)(2,1)S(1)} collective-permute-done((bf16[272,2048]{1,0:T(8,128)(2,1)S(1)}, bf16[272,2048]{1,0:T(8,128)(2,1)S(1)}, u32[]{:S(2)}, u32[]{:S(2)}) %collective-permute-start.9) | collective-permute-done | bytes 1114144 | tf_op jit(solution)/shard_map/ppermute | solution.py:42
  75.4 1.0 collective-permute-start.10
  76.4 2.5 collective-permute-done.10.refs_8_.refs_9_
  80.0 1.7 collective-permute-start.14
  81.7 1.5 collective-permute-start.15
  83.2 2.5 pad_maximum_fusion.refs_5_
  85.7 11.4 %shard_map.137 = (f32[1,384,1024]{2,1,0:T(8,128)}, bf16[1,1,384,1024]{3,2,1,0:T(8,128)(2,1)}, f32[384,2048]{1,0:T(8,128)}, f32[384,128]{1,0:T(8,128)}) custom-call(bf16[272,2048]{1,0:T(8,128)(2,1)} %copy-done.3, bf16[272,2048]{1,0:T(8,128)(2,1)} %copy-done.5, bf16[272,2048]{1,0:T(8,128)(2,1)} %copy-done.4, bf16[272,2048]{1,0:T(8,128)(2,1)} %copy-done.10, ...), custom_call_target="tpu_custom_call" | custom-call | flops 1000 | bytes 1000 | tf_op jit(solution)/shard_map/pallas_call | solution.py:268
  97.2 18.3 %shard_map.138 = (f32[2,384,1024]{2,1,0:T(8,128)}, bf16[2,1,384,1024]{3,2,1,0:T(8,128)(2,1)}, f32[384,2048]{1,0:T(8,128)}, f32[384,128]{1,0:T(8,128)}) custom-call(bf16[272,2048]{1,0:T(8,128)(2,1)} %copy-done.3, bf16[272,2048]{1,0:T(8,128)(2,1)} %copy-done.5, bf16[272,2048]{1,0:T(8,128)(2,1)} %copy-done.4, bf16[272,2048]{1,0:T(8,128)(2,1)} %copy-done.10, ...), custom_call_target="tpu_custom_call" | custom-call | flops 1000 | bytes 1000 | tf_op jit(solution)/shard_map/pallas_call | solution.py:268
  116.3 2.7 %collective-permute-done.16.refs_9_ = bf16[512,1152]{1,0:T(8,128)(2,1)S(1)} collective-permute-done((bf16[512,1152]{1,0:T(8,128)(2,1)}, bf16[512,1152]{1,0:T(8,128)(2,1)S(1)}, u32[]{:S(2)}, u32[]{:S(2)}) %collective-permute-start.16) | collective-permute-done | bytes 1179680 | tf_op jit(solution)/shard_map/ppermute | solution.py:47
  119.3 14.1 %shard_map.139 = (f32[3,384,1024]{2,1,0:T(8,128)}, bf16[3,1,384,1024]{3,2,1,0:T(8,128)(2,1)}, f32[128,2048]{1,0:T(8,128)}, f32[128,128]{1,0:T(8,128)}) custom-call(bf16[272,2048]{1,0:T(8,128)(2,1)} %copy-done.3, bf16[272,2048]{1,0:T(8,128)(2,1)} %collective-permute-done.15.refs_1_.refs_5_, bf16[272,2048]{1,0:T(8,128)(2,1)} %copy-done.5, ...), custom_call_target="tpu_custom_call" | custom-call | flops 1000 | bytes 1000 | tf_op jit(solution)/shard_map/pallas_call | solution.py:268
  133.9 1.0 copy-done.20
  135.0 14.9 %shard_map.140 = (f32[1,384,1024]{2,1,0:T(8,128)}, bf16[1,1,384,1024]{3,2,1,0:T(8,128)(2,1)}, bf16[4,144,2048]{2,1,0:T(8,128)(2,1)}) custom-call(bf16[272,2048]{1,0:T(8,128)(2,1)} %copy-done.3, bf16[272,2048]{1,0:T(8,128)(2,1)} %copy-done.5, bf16[272,2048]{1,0:T(8,128)(2,1)} %copy-done.4, bf16[272,2048]{1,0:T(8,128)(2,1)} %copy-done.10, ...), custom_call_target="tpu_custom_call" | custom-call | flops 1000 | bytes 1000 | tf_op jit(solution)/shard_map/pallas_call | solution.py:268
  149.9 2.3 dynamic-slice_bitcast_fusion
  152.2 5.1 %collective-permute-start.18 = (bf16[144,2048]{1,0:T(8,128)(2,1)}, bf16[144,2048]{1,0:T(8,128)(2,1)S(1)}, u32[]{:S(2)}, u32[]{:S(2)}) collective-permute-start(bf16[144,2048]{1,0:T(8,128)(2,1)} %get-tuple-element.111), channel_id=1, source_target_pairs={{0,4},{1,5},{2,6},{3,7},{16,20},{17,21},{18,22},{19,23}} | collective-permute-start | bytes 1769480 | tf_op jit(solution)/shard_map/ppermute | solution.py:42
  157.3 1.5 collective-permute-start.19
  159.3 10.9 %collective-permute-done.18 = bf16[144,2048]{1,0:T(8,128)(2,1)S(1)} collective-permute-done((bf16[144,2048]{1,0:T(8,128)(2,1)}, bf16[144,2048]{1,0:T(8,128)(2,1)S(1)}, u32[]{:S(2)}, u32[]{:S(2)}) %collective-permute-start.18) | collective-permute-done | bytes 589856 | tf_op jit(solution)/shard_map/ppermute | solution.py:42
  170.2 2.5 fusion.7
  172.7 4.8 %collective-permute-start.20 = (bf16[144,2048]{1,0:T(8,128)(2,1)}, bf16[144,2048]{1,0:T(8,128)(2,1)}, u32[]{:S(2)}, u32[]{:S(2)}) collective-permute-start(bf16[144,2048]{1,0:T(8,128)(2,1)} %get-tuple-element.113), channel_id=1, source_target_pairs={{0,4},{1,5},{2,6},{3,7},{4,8},{5,9},{6,10},{7,11},{16,20},{17,21},... | collective-permute-start | bytes 1769480 | tf_op jit(solution)/shard_map/ppermute | solution.py:42
  177.5 1.5 collective-permute-start.21
  179.0 3.9 %fusion.13 = (bf16[384,1024]{1,0:T(8,128)(2,1)S(1)}, bf16[384,1024]{1,0:T(8,128)(2,1)}) fusion(f32[3,384,1024]{2,1,0:T(8,128)} %get-tuple-element.117, bf16[3,384,1024]{2,1,0:T(8,128)(2,1)} %collective-permute-done.24), kind=kLoop, calls=%fused_computation.30 | loop fusion | flops 2359296 | bytes 6291456 | tf_op jit(solution)/shard_map/convert_element_type | solution.py:413
  183.9 1.2 collective-permute-start.26
  185.1 1.1 fusion.1
  186.7 2.0 collective-permute-done.20
  188.7 2.9 %fusion.6 = (bf16[144,2048]{1,0:T(8,128)(2,1)}, bf16[144,2048]{1,0:T(8,128)(2,1)}) fusion(bf16[144,2048]{1,0:T(8,128)(2,1)} %collective-permute-done.21, bf16[4,144,2048]{2,1,0:T(8,128)(2,1)S(1)} %copy-done.11, s32[]{:T(128)S(6)} %max.11, bf16[144,2048]{1,0:T(8,128)(2,1)} %collective-permute-done.20, s32[]{:T(128)S(6)} %select_n.63), kind=kLoop, calls=%fused_computation.18 | loop fusion | flops 2359296 | bytes 3538952 | tf_op jit(solution)/shard_map/convert_element_type | solution.py:427
  191.6 9.4 %collective-permute-done.25 = bf16[384,1024]{1,0:T(8,128)(2,1)} collective-permute-done((bf16[384,1024]{1,0:T(8,128)(2,1)}, bf16[384,1024]{1,0:T(8,128)(2,1)}, u32[]{:S(2)}, u32[]{:S(2)}) %collective-permute-start.25) | collective-permute-done | bytes 786464 | tf_op jit(solution)/shard_map/ppermute | solution.py:37
  201.5 17.1 %collective-permute-done.28 = bf16[384,1024]{1,0:T(8,128)(2,1)} collective-permute-done((bf16[384,1024]{1,0:T(8,128)(2,1)}, bf16[384,1024]{1,0:T(8,128)(2,1)}, u32[]{:S(2)}, u32[]{:S(2)}) %collective-permute-start.28) | collective-permute-done | bytes 786464 | tf_op jit(solution)/shard_map/ppermute | solution.py:37
  218.6 3.0 %fusion.2.refs_0_ = bf16[384,1024]{1,0:T(8,128)(2,1)S(1)} fusion(bf16[384,1024]{1,0:T(8,128)(2,1)} %collective-permute-done.28, bf16[384,1024]{1,0:T(8,128)(2,1)} %collective-permute-done.26, bf16[384,1024]{1,0:T(8,128)(2,1)} %collective-permute-done.25, f32[3,384,1024]{2,1,0:T(8,128)} %get-tuple-element.117, bf16[3,384,1024]{2,1,0:T(8,128)(2,1)} %collective-permute-done.24), kind=kLoop, calls=%fused_computation.10 | loop fusion | flops 3538944 | bytes 5505024 | tf_op jit(solution)/shard_map/convert_element_type | solution.py:436
  221.6 2.3 collective-permute-start.29
  224.5 1.2 collective-permute-done.29.refs_1_
  225.8 5.5 %shard_map.141 = (f32[1,1,384,2048]{3,2,1,0:T(8,128)}, f32[1,1,384,2048]{3,2,1,0:T(8,128)}, bf16[384,2048]{1,0:T(8,128)(2,1)S(1)}) custom-call(s32[1]{0:T(128)} %copy.17.lead_ref, bf16[384,1024]{1,0:T(8,128)(2,1)S(1)} %fusion.2.refs_0_, bf16[384,1024]{1,0:T(8,128)(2,1)S(1)} %collective-permute-done.29.refs_1_, f32[1,1,384,2048]{3,2,1,0:T(8,128)S(1)} %copy-done.1, ...), custom_call_target="tpu_custom_call" | custom-call | flops 15728640 | bytes 15728640 | tf_op jit(solution)/shard_map/pallas_call | solution.py:302
  231.7 2.1 collective-permute-start.22
  233.8 1.3 collective-permute-start.23
  235.6 10.4 %collective-permute-done.22 = bf16[144,2048]{1,0:T(8,128)(2,1)} collective-permute-done((bf16[144,2048]{1,0:T(8,128)(2,1)}, bf16[144,2048]{1,0:T(8,128)(2,1)}, u32[]{:S(2)}, u32[]{:S(2)}) %collective-permute-start.22) | collective-permute-done | bytes 589856 | tf_op jit(solution)/shard_map/ppermute | solution.py:42
  246.1 4.7 %collective-permute-done.23 = bf16[144,2048]{1,0:T(8,128)(2,1)} collective-permute-done((bf16[144,2048]{1,0:T(8,128)(2,1)}, bf16[144,2048]{1,0:T(8,128)(2,1)}, u32[]{:S(2)}, u32[]{:S(2)}) %collective-permute-start.23) | collective-permute-done | bytes 589856 | tf_op jit(solution)/shard_map/ppermute | solution.py:42
  250.8 1.7 fusion.10
  253.9 3.5 %fusion.3 = bf16[1,1,384,2048]{3,2,1,0:T(8,128)(2,1)} fusion(bf16[1,384,2048]{2,1,0:T(8,128)(2,1)S(1)} %copy-done, bf16[384,2048]{1,0:T(8,128)(2,1)} %collective-permute-done.30, bf16[384,2048]{1,0:T(8,128)(2,1)S(1)} %get-tuple-element.124, pred[]{:T(512)S(6)} %eq.29, pred[]{:T(512)} %bitcast.19), kind=kLoop, calls=%fused_computation.12 | loop fusion | flops 1572864 | bytes 6291458 | tf_op jit(solution)/shard_map/broadcast_in_dim | solution.py:450
  (89 shorter events, 9.3 us)
Async XLA Ops:
  2.6 80.6 %copy-start.8 = (bf16[1,2048,768]{2,1,0:T(8,128)(2,1)S(1)}, bf16[1,2048,768]{2,1,0:T(8,128)(2,1)}, u32[]{:S(2)}) copy-start(bf16[1,2048,768]{2,1,0:T(8,128)(2,1)} %param.14) | copy-start | bytes 9437188
  4.8 78.4 %copy-start.7 = (bf16[2048,384]{1,0:T(8,128)(2,1)S(1)}, bf16[2048,384]{1,0:T(8,128)(2,1)}, u32[]{:S(2)}) copy-start(bf16[2048,384]{1,0:T(8,128)(2,1)} %copy-done.6) | copy-start | bytes 4718596
  4.8 33.2 %collective-permute-start.2 = (bf16[512,1152]{1,0:T(8,128)(2,1)S(1)}, bf16[512,1152]{1,0:T(8,128)(2,1)S(1)}, u32[]{:S(2)}, u32[]{:S(2)}) collective-permute-start(bf16[512,1152]{1,0:T(8,128)(2,1)S(1)} %get-tuple-element.70), channel_id=1, source_target_pairs={{0,1},{1,0},{2,3},{3,2},{4,5},{5,4},{6,7},{7,6},{8,9},{9,8},{10,11... | collective-permute-start | bytes 3538952 | tf_op jit(solution)/shard_map/ppermute | solution.py:37
  6.9 31.1 %collective-permute-start.3 = (bf16[512,1152]{1,0:T(8,128)(2,1)S(1)}, bf16[512,1152]{1,0:T(8,128)(2,1)S(1)}, u32[]{:S(2)}, u32[]{:S(2)}) collective-permute-start(bf16[512,1152]{1,0:T(8,128)(2,1)S(1)} %get-tuple-element.69), channel_id=1, source_target_pairs={{0,2},{1,3},{2,0},{3,1},{4,6},{5,7},{6,4},{7,5},{8,10},{9,11},{10,... | collective-permute-start | bytes 3538952 | tf_op jit(solution)/shard_map/ppermute | solution.py:37
  8.3 77.4 %copy-start.3 = (bf16[272,2048]{1,0:T(8,128)(2,1)}, bf16[272,2048]{1,0:T(8,128)(2,1)S(1)}, u32[]{:S(2)}) copy-start(bf16[272,2048]{1,0:T(8,128)(2,1)S(1)} %fusion.11.refs_0_) | copy-start | bytes 3342340
  8.3 25.8 %collective-permute-start = (bf16[272,2048]{1,0:T(8,128)(2,1)S(1)}, bf16[272,2048]{1,0:T(8,128)(2,1)S(1)}, u32[]{:S(2)}, u32[]{:S(2)}) collective-permute-start(bf16[272,2048]{1,0:T(8,128)(2,1)S(1)} %fusion.11.refs_0_), channel_id=1, source_target_pairs={{0,4},{1,5},{2,6},{3,7},{4,8},{5,9},{6,10},{7,11},{8,12},{9,13},{1... | collective-permute-start | bytes 3342344 | tf_op jit(solution)/shard_map/ppermute | solution.py:42
  11.6 26.4 %collective-permute-start.1 = (bf16[272,2048]{1,0:T(8,128)(2,1)S(1)}, bf16[272,2048]{1,0:T(8,128)(2,1)S(1)}, u32[]{:S(2)}, u32[]{:S(2)}) collective-permute-start(bf16[272,2048]{1,0:T(8,128)(2,1)S(1)} %fusion.11.refs_0_), channel_id=1, source_target_pairs={{4,0},{5,1},{6,2},{7,3},{8,4},{9,5},{10,6},{11,7},{12,8},{13,9},{1... | collective-permute-start | bytes 3342344 | tf_op jit(solution)/shard_map/ppermute | solution.py:42
  34.1 51.6 %copy-start.4 = (bf16[272,2048]{1,0:T(8,128)(2,1)}, bf16[272,2048]{1,0:T(8,128)(2,1)S(1)}, u32[]{:S(2)}) copy-start(bf16[272,2048]{1,0:T(8,128)(2,1)S(1)} %collective-permute-done.refs_2_.refs_3_) | copy-start | bytes 3342340
  38.0 47.7 %copy-start.5 = (bf16[272,2048]{1,0:T(8,128)(2,1)}, bf16[272,2048]{1,0:T(8,128)(2,1)S(1)}, u32[]{:S(2)}) copy-start(bf16[272,2048]{1,0:T(8,128)(2,1)S(1)} %collective-permute-done.1.refs_1_.refs_2_) | copy-start | bytes 3342340
  38.0 47.7 %copy-start.12 = (bf16[512,1152]{1,0:T(8,128)(2,1)}, bf16[512,1152]{1,0:T(8,128)(2,1)S(1)}, u32[]{:S(2)}) copy-start(bf16[512,1152]{1,0:T(8,128)(2,1)S(1)} %collective-permute-done.2.refs_5_.refs_6_) | copy-start | bytes 3538948
  38.0 47.7 %copy-start.13 = (bf16[512,1152]{1,0:T(8,128)(2,1)}, bf16[512,1152]{1,0:T(8,128)(2,1)S(1)}, u32[]{:S(2)}) copy-start(bf16[512,1152]{1,0:T(8,128)(2,1)S(1)} %collective-permute-done.3.refs_10_.refs_11_) | copy-start | bytes 3538948
  38.0 5.0 %collective-permute-start.6 = (bf16[512,1152]{1,0:T(8,128)(2,1)S(1)}, bf16[512,1152]{1,0:T(8,128)(2,1)S(1)}, u32[]{:S(2)}, u32[]{:S(2)}) collective-permute-start(bf16[512,1152]{1,0:T(8,128)(2,1)S(1)} %collective-permute-done.2.refs_5_.refs_6_), channel_id=1, source_target_pairs={{16,0},{0,16},{17,1},{1,17},{18,2},{2,18},{19,3},{3,19},{20,4},{4,... | collective-permute-start | bytes 3538952 | tf_op jit(solution)/shard_map/ppermute | solution.py:47
  40.5 34.8 %collective-permute-start.4 = (bf16[512,1152]{1,0:T(8,128)(2,1)S(1)}, bf16[512,1152]{1,0:T(8,128)(2,1)S(1)}, u32[]{:S(2)}, u32[]{:S(2)}) collective-permute-start(bf16[512,1152]{1,0:T(8,128)(2,1)S(1)} %get-tuple-element.69), channel_id=1, source_target_pairs={{0,1},{1,0},{2,3},{3,2},{4,5},{5,4},{6,7},{7,6},{8,9},{9,8},{10,11... | collective-permute-start | bytes 3538952 | tf_op jit(solution)/shard_map/ppermute | solution.py:37
  40.8 34.6 %collective-permute-start.5 = (bf16[512,1152]{1,0:T(8,128)(2,1)S(1)}, bf16[512,1152]{1,0:T(8,128)(2,1)}, u32[]{:S(2)}, u32[]{:S(2)}) collective-permute-start(bf16[512,1152]{1,0:T(8,128)(2,1)S(1)} %get-tuple-element.70), channel_id=1, source_target_pairs={{0,2},{1,3},{2,0},{3,1},{4,6},{5,7},{6,4},{7,5},{8,10},{9,11},{10,... | collective-permute-start | bytes 3538952 | tf_op jit(solution)/shard_map/ppermute | solution.py:37
  44.0 31.4 %collective-permute-start.7 = (bf16[512,1152]{1,0:T(8,128)(2,1)S(1)}, bf16[512,1152]{1,0:T(8,128)(2,1)S(1)}, u32[]{:S(2)}, u32[]{:S(2)}) collective-permute-start(bf16[512,1152]{1,0:T(8,128)(2,1)S(1)} %collective-permute-done.3.refs_10_.refs_11_), channel_id=1, source_target_pairs={{16,0},{0,16},{17,1},{1,17},{18,2},{2,18},{19,3},{3,19},{20,4},{4,... | collective-permute-start | bytes 3538952 | tf_op jit(solution)/shard_map/ppermute | solution.py:47
  44.4 2.0 collective-permute-start.8
  45.1 30.2 %collective-permute-start.9 = (bf16[272,2048]{1,0:T(8,128)(2,1)S(1)}, bf16[272,2048]{1,0:T(8,128)(2,1)S(1)}, u32[]{:S(2)}, u32[]{:S(2)}) collective-permute-start(bf16[272,2048]{1,0:T(8,128)(2,1)S(1)} %collective-permute-done.1.refs_1_.refs_2_), channel_id=1, source_target_pairs={{4,0},{5,1},{6,2},{7,3},{8,4},{9,5},{10,6},{11,7},{20,16},{21,17},... | collective-permute-start | bytes 3342344 | tf_op jit(solution)/shard_map/ppermute | solution.py:42
  46.4 39.3 %copy-start.9 = (bf16[272,2048]{1,0:T(8,128)(2,1)}, bf16[272,2048]{1,0:T(8,128)(2,1)S(1)}, u32[]{:S(2)}) copy-start(bf16[272,2048]{1,0:T(8,128)(2,1)S(1)} %collective-permute-done.8.refs_4_) | copy-start | bytes 3342340
  75.4 10.4 %copy-start.10 = (bf16[272,2048]{1,0:T(8,128)(2,1)}, bf16[272,2048]{1,0:T(8,128)(2,1)S(1)}, u32[]{:S(2)}) copy-start(bf16[272,2048]{1,0:T(8,128)(2,1)S(1)} %collective-permute-done.9.refs_3_) | copy-start | bytes 3342340
  75.4 6.3 %copy-start.16 = (bf16[512,1152]{1,0:T(8,128)(2,1)}, bf16[512,1152]{1,0:T(8,128)(2,1)S(1)}, u32[]{:S(2)}) copy-start(bf16[512,1152]{1,0:T(8,128)(2,1)S(1)} %collective-permute-done.7.refs_12_.refs_13_) | copy-start | bytes 3538948
  75.4 3.5 %collective-permute-start.10 = (bf16[512,1152]{1,0:T(8,128)(2,1)S(1)}, bf16[512,1152]{1,0:T(8,128)(2,1)S(1)}, u32[]{:S(2)}, u32[]{:S(2)}) collective-permute-start(bf16[512,1152]{1,0:T(8,128)(2,1)S(1)} %collective-permute-done.4.refs_6_.refs_7_), channel_id=1, source_target_pairs={{16,0},{0,16},{17,1},{1,17},{18,2},{2,18},{19,3},{3,19},{20,4},{4,... | collective-permute-start | bytes 3538952 | tf_op jit(solution)/shard_map/ppermute | solution.py:47
  78.9 18.3 %collective-permute-start.11 = (bf16[512,1152]{1,0:T(8,128)(2,1)}, bf16[512,1152]{1,0:T(8,128)(2,1)}, u32[]{:S(2)}, u32[]{:S(2)}) collective-permute-start(bf16[512,1152]{1,0:T(8,128)(2,1)} %collective-permute-done.5.refs_9_.refs_10_), channel_id=1, source_target_pairs={{16,0},{0,16},{17,1},{1,17},{18,2},{2,18},{19,3},{3,19},{20,4},{4,... | collective-permute-start | bytes 3538952 | tf_op jit(solution)/shard_map/ppermute | solution.py:47
  79.3 36.2 %collective-permute-start.12 = (bf16[512,1152]{1,0:T(8,128)(2,1)S(1)}, bf16[512,1152]{1,0:T(8,128)(2,1)}, u32[]{:S(2)}, u32[]{:S(2)}) collective-permute-start(bf16[512,1152]{1,0:T(8,128)(2,1)S(1)} %collective-permute-done.2.refs_5_.refs_6_), channel_id=1, source_target_pairs={{0,2},{1,3},{2,0},{3,1},{4,6},{5,7},{6,4},{7,5},{8,10},{9,11},{10,... | collective-permute-start | bytes 3538952 | tf_op jit(solution)/shard_map/ppermute | solution.py:37
  79.5 36.0 %collective-permute-start.13 = (bf16[512,1152]{1,0:T(8,128)(2,1)S(1)}, bf16[512,1152]{1,0:T(8,128)(2,1)}, u32[]{:S(2)}, u32[]{:S(2)}) collective-permute-start(bf16[512,1152]{1,0:T(8,128)(2,1)S(1)} %collective-permute-done.3.refs_10_.refs_11_), channel_id=1, source_target_pairs={{0,1},{1,0},{2,3},{3,2},{4,5},{5,4},{6,7},{7,6},{8,9},{9,8},{10,11... | collective-permute-start | bytes 3538952 | tf_op jit(solution)/shard_map/ppermute | solution.py:37
  80.0 35.5 %collective-permute-start.14 = (bf16[272,2048]{1,0:T(8,128)(2,1)S(1)}, bf16[272,2048]{1,0:T(8,128)(2,1)}, u32[]{:S(2)}, u32[]{:S(2)}) collective-permute-start(bf16[272,2048]{1,0:T(8,128)(2,1)S(1)} %collective-permute-done.8.refs_4_), channel_id=1, source_target_pairs={{8,12},{9,13},{10,14},{11,15},{24,28},{25,29},{26,30},{27,31}} | collective-permute-start | bytes 3342344 | tf_op jit(solution)/shard_map/ppermute | solution.py:42
  81.7 33.8 %collective-permute-start.15 = (bf16[272,2048]{1,0:T(8,128)(2,1)S(1)}, bf16[272,2048]{1,0:T(8,128)(2,1)}, u32[]{:S(2)}, u32[]{:S(2)}) collective-permute-start(bf16[272,2048]{1,0:T(8,128)(2,1)S(1)} %collective-permute-done.9.refs_3_), channel_id=1, source_target_pairs={{4,0},{5,1},{6,2},{7,3},{20,16},{21,17},{22,18},{23,19}} | collective-permute-start | bytes 3342344 | tf_op jit(solution)/shard_map/ppermute | solution.py:42
  115.5 3.5 %collective-permute-start.16 = (bf16[512,1152]{1,0:T(8,128)(2,1)}, bf16[512,1152]{1,0:T(8,128)(2,1)S(1)}, u32[]{:S(2)}, u32[]{:S(2)}) collective-permute-start(bf16[512,1152]{1,0:T(8,128)(2,1)} %collective-permute-done.12.refs_7_), channel_id=1, source_target_pairs={{16,0},{0,16},{17,1},{1,17},{18,2},{2,18},{19,3},{3,19},{20,4},{4,... | collective-permute-start | bytes 3538952 | tf_op jit(solution)/shard_map/ppermute | solution.py:47
  119.0 14.5 %copy-start.19 = (bf16[512,1152]{1,0:T(8,128)(2,1)}, bf16[512,1152]{1,0:T(8,128)(2,1)S(1)}, u32[]{:S(2)}) copy-start(bf16[512,1152]{1,0:T(8,128)(2,1)S(1)} %collective-permute-done.16.refs_9_) | copy-start | bytes 3538948
  119.0 15.0 %collective-permute-start.17 = (bf16[512,1152]{1,0:T(8,128)(2,1)}, bf16[512,1152]{1,0:T(8,128)(2,1)S(1)}, u32[]{:S(2)}, u32[]{:S(2)}) collective-permute-start(bf16[512,1152]{1,0:T(8,128)(2,1)} %collective-permute-done.13.refs_8_), channel_id=1, source_target_pairs={{16,0},{0,16},{17,1},{1,17},{18,2},{2,18},{19,3},{3,19},{20,4},{4,... | collective-permute-start | bytes 3538952 | tf_op jit(solution)/shard_map/ppermute | solution.py:47
  133.5 45.5 %collective-permute-start.24 = (bf16[3,384,1024]{2,1,0:T(8,128)(2,1)}, bf16[3,384,1024]{2,1,0:T(8,128)(2,1)}, u32[]{:S(2)}, u32[]{:S(2)}) collective-permute-start(bf16[3,384,1024]{2,1,0:T(8,128)(2,1)} %bitcast.57), channel_id=1, source_target_pairs={{16,0},{0,16},{17,1},{1,17},{18,2},{2,18},{19,3},{3,19},{20,4},{4,... | collective-permute-start | bytes 7077896 | tf_op jit(solution)/shard_map/ppermute | solution.py:47
  149.9 20.3 %copy-start.11 = (bf16[4,144,2048]{2,1,0:T(8,128)(2,1)S(1)}, bf16[4,144,2048]{2,1,0:T(8,128)(2,1)}, u32[]{:S(2)}) copy-start(bf16[4,144,2048]{2,1,0:T(8,128)(2,1)} %get-tuple-element.110) | copy-start | bytes 7077892
  152.2 18.0 %collective-permute-start.18 = (bf16[144,2048]{1,0:T(8,128)(2,1)}, bf16[144,2048]{1,0:T(8,128)(2,1)S(1)}, u32[]{:S(2)}, u32[]{:S(2)}) collective-permute-start(bf16[144,2048]{1,0:T(8,128)(2,1)} %get-tuple-element.111), channel_id=1, source_target_pairs={{0,4},{1,5},{2,6},{3,7},{16,20},{17,21},{18,22},{19,23}} | collective-permute-start | bytes 1769480 | tf_op jit(solution)/shard_map/ppermute | solution.py:42
  157.3 12.9 %collective-permute-start.19 = (bf16[144,2048]{1,0:T(8,128)(2,1)S(1)}, bf16[144,2048]{1,0:T(8,128)(2,1)}, u32[]{:S(2)}, u32[]{:S(2)}) collective-permute-start(bf16[144,2048]{1,0:T(8,128)(2,1)S(1)} %get-tuple-element.112), channel_id=1, source_target_pairs={{12,8},{13,9},{14,10},{15,11},{28,24},{29,25},{30,26},{31,27}} | collective-permute-start | bytes 1769480 | tf_op jit(solution)/shard_map/ppermute | solution.py:42
  158.8 26.2 %collective-permute-start.27 = (bf16[384,1024]{1,0:T(8,128)(2,1)}, bf16[384,1024]{1,0:T(8,128)(2,1)S(1)}, u32[]{:S(2)}, u32[]{:S(2)}) collective-permute-start(bf16[384,1024]{1,0:T(8,128)(2,1)} %bitcast.58), channel_id=1, source_target_pairs={{16,0},{0,16},{17,1},{1,17},{18,2},{2,18},{19,3},{3,19},{20,4},{4,... | collective-permute-start | bytes 2359304 | tf_op jit(solution)/shard_map/ppermute | solution.py:47
  172.7 16.0 %collective-permute-start.20 = (bf16[144,2048]{1,0:T(8,128)(2,1)}, bf16[144,2048]{1,0:T(8,128)(2,1)}, u32[]{:S(2)}, u32[]{:S(2)}) collective-permute-start(bf16[144,2048]{1,0:T(8,128)(2,1)} %get-tuple-element.113), channel_id=1, source_target_pairs={{0,4},{1,5},{2,6},{3,7},{4,8},{5,9},{6,10},{7,11},{16,20},{17,21},... | collective-permute-start | bytes 1769480 | tf_op jit(solution)/shard_map/ppermute | solution.py:42
  177.5 11.2 %collective-permute-start.21 = (bf16[144,2048]{1,0:T(8,128)(2,1)}, bf16[144,2048]{1,0:T(8,128)(2,1)}, u32[]{:S(2)}, u32[]{:S(2)}) collective-permute-start(bf16[144,2048]{1,0:T(8,128)(2,1)} %get-tuple-element.114), channel_id=1, source_target_pairs={{8,4},{9,5},{10,6},{11,7},{12,8},{13,9},{14,10},{15,11},{24,20},{2... | collective-permute-start | bytes 1769480 | tf_op jit(solution)/shard_map/ppermute | solution.py:42
  179.0 6.1 %copy-start.18 = (f32[1,384,1024]{2,1,0:T(8,128)S(1)}, f32[1,384,1024]{2,1,0:T(8,128)}, u32[]{:S(2)}) copy-start(f32[1,384,1024]{2,1,0:T(8,128)} %get-tuple-element.119) | copy-start | bytes 4718596
  182.9 18.1 %collective-permute-start.25 = (bf16[384,1024]{1,0:T(8,128)(2,1)}, bf16[384,1024]{1,0:T(8,128)(2,1)}, u32[]{:S(2)}, u32[]{:S(2)}) collective-permute-start(bf16[384,1024]{1,0:T(8,128)(2,1)} %get-tuple-element.130), channel_id=1, source_target_pairs={{0,1},{1,0},{2,3},{3,2},{4,5},{5,4},{6,7},{7,6},{8,9},{9,8},{10,11... | collective-permute-start | bytes 2359304 | tf_op jit(solution)/shard_map/ppermute | solution.py:37
  183.9 17.6 %collective-permute-start.26 = (bf16[384,1024]{1,0:T(8,128)(2,1)S(1)}, bf16[384,1024]{1,0:T(8,128)(2,1)}, u32[]{:S(2)}, u32[]{:S(2)}) collective-permute-start(bf16[384,1024]{1,0:T(8,128)(2,1)S(1)} %get-tuple-element.129), channel_id=1, source_target_pairs={{0,2},{1,3},{2,0},{3,1},{4,6},{5,7},{6,4},{7,5},{8,10},{9,11},{10,... | collective-permute-start | bytes 2359304 | tf_op jit(solution)/shard_map/ppermute | solution.py:37
  186.2 32.3 %collective-permute-start.28 = (bf16[384,1024]{1,0:T(8,128)(2,1)}, bf16[384,1024]{1,0:T(8,128)(2,1)}, u32[]{:S(2)}, u32[]{:S(2)}) collective-permute-start(bf16[384,1024]{1,0:T(8,128)(2,1)} %fusion.1), channel_id=1, source_target_pairs={{0,3},{1,2},{2,1},{3,0},{4,7},{5,6},{6,5},{7,4},{8,11},{9,10},{10,... | collective-permute-start | bytes 2359304 | tf_op jit(solution)/shard_map/ppermute | solution.py:37
  188.7 37.1 %copy-start.2 = (f32[1,1,384,2048]{3,2,1,0:T(8,128)S(1)}, f32[1,1,384,2048]{3,2,1,0:T(8,128)}, u32[]{:S(2)}) copy-start(f32[1,1,384,2048]{3,2,1,0:T(8,128)} %refs_3_.1) | copy-start | bytes 9437188
  191.6 34.2 %copy-start = (bf16[1,384,2048]{2,1,0:T(8,128)(2,1)S(1)}, bf16[1,384,2048]{2,1,0:T(8,128)(2,1)}, u32[]{:S(2)}) copy-start(bf16[1,384,2048]{2,1,0:T(8,128)(2,1)} %refs_4_.1) | copy-start | bytes 4718596
  191.6 34.2 %copy-start.1 = (f32[1,1,384,2048]{3,2,1,0:T(8,128)S(1)}, f32[1,1,384,2048]{3,2,1,0:T(8,128)}, u32[]{:S(2)}) copy-start(f32[1,1,384,2048]{3,2,1,0:T(8,128)} %refs_2_.1) | copy-start | bytes 9437188
  221.6 4.2 %collective-permute-start.29 = (bf16[384,1024]{1,0:T(8,128)(2,1)S(1)}, bf16[384,1024]{1,0:T(8,128)(2,1)S(1)}, u32[]{:S(2)}, u32[]{:S(2)}) collective-permute-start(bf16[384,1024]{1,0:T(8,128)(2,1)S(1)} %fusion.2.refs_0_), channel_id=1, source_target_pairs={{16,0},{0,16},{17,1},{1,17},{18,2},{2,18},{19,3},{3,19},{20,4},{4,... | collective-permute-start | bytes 2359304 | tf_op jit(solution)/shard_map/ppermute | solution.py:47
  224.5 10.6 %copy-start.25 = (s32[1,2]{1,0:T(1,128)S(1)}, s32[1,2]{1,0:T(1,128)}, u32[]{:S(2)}) copy-start(s32[1,2]{1,0:T(1,128)} %param.18) | copy-start | bytes 28
  231.3 22.6 %collective-permute-start.30 = (bf16[384,2048]{1,0:T(8,128)(2,1)S(1)}, bf16[384,2048]{1,0:T(8,128)(2,1)}, u32[]{:S(2)}, u32[]{:S(2)}) collective-permute-start(bf16[384,2048]{1,0:T(8,128)(2,1)S(1)} %get-tuple-element.124), channel_id=1, source_target_pairs={{16,0},{0,16},{17,1},{1,17},{18,2},{2,18},{19,3},{3,19},{20,4},{4,... | collective-permute-start | bytes 4718600 | tf_op jit(solution)/shard_map/ppermute | solution.py:47
  231.7 14.4 %collective-permute-start.22 = (bf16[144,2048]{1,0:T(8,128)(2,1)}, bf16[144,2048]{1,0:T(8,128)(2,1)}, u32[]{:S(2)}, u32[]{:S(2)}) collective-permute-start(bf16[144,2048]{1,0:T(8,128)(2,1)} %get-tuple-element.115), channel_id=1, source_target_pairs={{0,4},{1,5},{2,6},{3,7},{4,8},{5,9},{6,10},{7,11},{8,12},{9,13},{1... | collective-permute-start | bytes 1769480 | tf_op jit(solution)/shard_map/ppermute | solution.py:42
  233.8 17.0 %collective-permute-start.23 = (bf16[144,2048]{1,0:T(8,128)(2,1)}, bf16[144,2048]{1,0:T(8,128)(2,1)}, u32[]{:S(2)}, u32[]{:S(2)}) collective-permute-start(bf16[144,2048]{1,0:T(8,128)(2,1)} %get-tuple-element.116), channel_id=1, source_target_pairs={{4,0},{5,1},{6,2},{7,3},{8,4},{9,5},{10,6},{11,7},{12,8},{13,9},{1... | collective-permute-start | bytes 1769480 | tf_op jit(solution)/shard_map/ppermute | solution.py:42
  (9 other events, 35.5 us)
where the time goes:
time: 258 us; the launch traced here: 257 us
  waiting for transfers between devices  117 us (45%)
  Pallas kernels  64.3 us (25%)
  starting transfers between devices  42.2 us (16%)
  other arithmetic  24.6 us (10%)
  local copies, waits for them, and re-layouts  7.19 us (3%)
    ppermute x12, waiting for transfers between devices, climb(): return lax.ppermute(value, 'expert', pairs)  82.1 us
    pallas_call x4, Pallas kernels, call(): pl.pallas_call(functools.partial(self.kernel, len(ins)), out_shape=[jax.S...  58.8 us
    ppermute x9, waiting for transfers between devices, hop(): return lax.ppermute(value, 'expert', [(i, i ^ flip) for i in range(n)])  27 us
    ppermute x12, starting transfers between devices, climb(): return lax.ppermute(value, 'expert', pairs)  26 us
    ppermute x10, starting transfers between devices, turn(): return lax.ppermute(value, 'dp', [((r + step) % n, r) for r in range(n)])  8.94 us
    ppermute x10, waiting for transfers between devices, turn(): return lax.ppermute(value, 'dp', [((r + step) % n, r) for r in range(n)])  8.4 us
    ppermute x9, starting transfers between devices, hop(): return lax.ppermute(value, 'expert', [(i, i ^ flip) for i in range(n)])  7.22 us
    pallas_call x1, Pallas kernels, adam_call(): pl.pallas_call(functools.partial(adam_kernel, n_dp), grid=(half // step,)...  5.5 us
  transfers between devices with their start and end apart: 31, of which 14 were waited for; matrix products, arithmetic and copies ran while one was open for 7% of the time, Pallas kernels for 23%

commit v1 on v0

--- a/solution.py
+++ b/solution.py
@@ -37,8 +37,20 @@
     return lax.ppermute(value, "expert", [(i, i ^ flip) for i in range(n)])
 
 
-def climb(value, way, low, high):
-    pairs = [(i, i + way * plane) for i in range(low * plane, high * plane)]
+def ring(layers):
+    return [z for z in range(layers) if z == 0 or z % 2] + [
+        z for z in range(layers - 1, 0, -1) if z % 2 == 0
+    ]
+
+
+def along(value):
+    n = lax.axis_size("expert")
+    order = ring(n // plane)
+    pairs = [
+        (z * plane + j, order[(r + 1) % len(order)] * plane + j)
+        for r, z in enumerate(order)
+        for j in range(plane)
+    ]
     return lax.ppermute(value, "expert", pairs)
 
 
@@ -57,11 +69,6 @@
 
 def tn(a, b):
     return lax.dot_general(a, b, (((0,), (0,)), ((), ())), preferred_element_type=f32)
-
-
-def source(layer, k):
-    far = layer ^ k
-    return ("down", far - layer) if far > layer else ("up", layer - far)
 
 
 class Pass:
@@ -71,45 +78,34 @@
         self.layers = n_ex // plane
         self.rows = tok * len(blocks)
         self.width = model // n_dp
-        self.tail = -(-n_ex // 16) * 16
 
     def kernel(self, n_in, *refs):
         tok, model, half, rows, width = self.tok, self.model, self.half, self.rows, self.width
-        n_dp, layers, slots, blocks = self.n_dp, self.layers, self.slots, self.blocks
+        n_dp, slots, blocks = self.n_dp, self.slots, self.blocks
         ins = dict(zip(self.names, refs[:n_in]))
         n_out = len(self.outs)
         outs = dict(zip(self.outs, refs[n_in : n_in + n_out]))
         scratch = list(refs[n_in + n_out :])
-        xs, ys, ps, ws, gu, back, pre, sc, pcol, dx, pr, keep, send = scratch[:13]
-        sem_t, sem_w, sem_i, sem_o = scratch[13:17]
+        xs, ys, ps, ws, gu, back, pre, sc, dx, pr, keep, send = scratch[:12]
+        sem_t, sem_w, sem_i, sem_o = scratch[12:16]
         me_dp = lax.axis_index("dp")
         me = lax.axis_index("expert")
         here, layer = lax.rem(me, plane), lax.div(me, plane)
 
-        def row_copies(ref, b):
-            at = pl.ds(b * tok, tok)
+        def row_copies(b):
+            ref, at = ins["t%d" % blocks[b]], pl.ds(b * tok, tok)
+            cols = pl.ds(0, model)
             return (
-                pltpu.make_async_copy(ref.at[pl.ds(0, tok)], xs.at[at], sem_t.at[b, 0]),
-                pltpu.make_async_copy(ref.at[pl.ds(tok, tok)], ys.at[at], sem_t.at[b, 1]),
+                pltpu.make_async_copy(ref.at[pl.ds(0, tok), cols], xs.at[at], sem_t.at[b, 0]),
+                pltpu.make_async_copy(ref.at[pl.ds(tok, tok), cols], ys.at[at], sem_t.at[b, 1]),
                 pltpu.make_async_copy(
-                    ref.at[pl.ds(2 * tok, self.tail), pl.ds(0, lanes)],
-                    ps.at[b, pl.ds(0, self.tail)],
-                    sem_t.at[b, 2],
+                    ref.at[pl.ds(0, tok), pl.ds(model, lanes)], ps.at[at], sem_t.at[b, 2]
                 ),
             )
 
-        ps[...] = jnp.zeros_like(ps)
-        for b, k in enumerate(blocks):
-            if k == 0:
-                for copy in row_copies(ins["own"], b):
-                    copy.start()
-                continue
-            for z in range(layers):
-
-                @pl.when(layer == z)
-                def _(b=b, k=k, z=z):
-                    for copy in row_copies(ins[source(z, k)], b):
-                        copy.start()
+        for b in range(len(blocks)):
+            for copy in row_copies(b):
+                copy.start()
 
         def weight_copies(i):
             s = slots[i]
@@ -147,9 +143,8 @@
             copy.start()
 
         for b in range(len(blocks)):
-            for copy in row_copies(ins["own"], b):
+            for copy in row_copies(b):
                 copy.wait()
-            pcol[pl.ds(b * tok, tok), :] = jnp.transpose(ps[b].astype(f32))
         chunk = min(128, tok)
         lane = lax.broadcasted_iota(jnp.int32, (chunk, lanes), 1)
         pending = []
@@ -176,7 +171,7 @@
                 at = pl.ds(pl.multiple_of(r * chunk, chunk), chunk)
                 gate, upper, h = gu[at, :half], gu[at, half:], back[at, :]
                 hit = lane == expert
-                p = jnp.sum(jnp.where(hit, pcol[at, :], 0.0), axis=1, keepdims=True)
+                p = jnp.sum(jnp.where(hit, ps[at, :].astype(f32), 0.0), axis=1, keepdims=True)
                 sigma = jax.nn.sigmoid(gate)
                 silu = gate * sigma
                 hidden = (silu * upper).astype(bf16).astype(f32)
@@ -219,15 +214,12 @@
             pending[-2].start()
             pending[-1].start()
         else:
-            rows_out = scratch[17]
+            rows_out = scratch[16]
             for b, k in enumerate(blocks):
                 at = pl.ds(b * tok, tok)
-                rows_out[b, pl.ds(0, tok), :] = dx[at, :].astype(bf16)
-                rows_out[b, pl.ds(tok, self.tail), :] = jnp.zeros((self.tail, model), bf16)
-                turned = jnp.transpose(pr[at, :])[: self.tail]
-                rows_out[b, pl.ds(tok, self.tail), pl.ds(0, lanes)] = turned.astype(bf16)
-                dest = lax.bitwise_xor(layer, jnp.int32(k))
-                copy = pltpu.make_async_copy(rows_out.at[b], outs["back"].at[dest], sem_o.at[n + b])
+                rows_out[b, :, pl.ds(0, model)] = dx[at, :].astype(bf16)
+                rows_out[b, :, pl.ds(model, lanes)] = pr[at, :].astype(bf16)
+                copy = pltpu.make_async_copy(rows_out.at[b], outs["back"].at[k], sem_o.at[n + b])
                 copy.start()
                 pending.append(copy)
         for copy in pending:
@@ -239,7 +231,7 @@
         shape = {"keep": ((n, half, width), f32)}
         shape["send"] = ((n, max(n_dp - 1, 1), half, width), bf16)
         if self.last:
-            shape["back"] = ((self.layers, tok + self.tail, model), bf16)
+            shape["back"] = ((self.layers, tok, model + lanes), bf16)
         else:
             shape["dx"] = ((rows, model), f32)
             shape["pr"] = ((rows, lanes), f32)
@@ -247,13 +239,12 @@
         scratch = [
             pltpu.VMEM((rows, model), bf16),
             pltpu.VMEM((rows, model), bf16),
-            pltpu.VMEM((len(self.blocks), tok, lanes), bf16),
+            pltpu.VMEM((rows, lanes), bf16),
             pltpu.VMEM((min(n, 2), model, 3 * half), bf16),
             pltpu.VMEM((rows, 2 * half), f32),
             pltpu.VMEM((rows, half), f32),
             pltpu.VMEM((rows, 2 * half), bf16),
             pltpu.VMEM((rows, half), bf16),
-            pltpu.VMEM((rows, lanes), f32),
             pltpu.VMEM((rows, model), f32),
             pltpu.VMEM((rows, lanes), f32),
             pltpu.VMEM((n, half, width), f32),
@@ -264,7 +255,7 @@
             pltpu.SemaphoreType.DMA((2 * n + len(self.blocks) + 2,)),
         ]
         if self.last:
-            scratch.append(pltpu.VMEM((self.layers, tok + self.tail, model), bf16))
+            scratch.append(pltpu.VMEM((self.layers, tok, model + lanes), bf16))
         out = pl.pallas_call(
             functools.partial(self.kernel, len(ins)),
             out_shape=[jax.ShapeDtypeStruct(*v) for v in shape.values()],
@@ -313,7 +304,7 @@
         out_specs=[wide, wide, pl.BlockSpec((step, model), lambda i: (i, 0))],
         compiler_params=pltpu.CompilerParams(vmem_limit_bytes=32 * 2**20),
         cost_estimate=pl.CostEstimate(
-            flops=20 * half * model, bytes_accessed=20 * half * model, transcendentals=0
+            flops=1000, bytes_accessed=1000, transcendentals=0
         ),
     )(leader, *parts, moment_one, moment_two, w_down)
 
@@ -328,45 +319,39 @@
     layers = n_ex // plane
     width = model // n_dp
     me_dp = lax.axis_index("dp")
-    me = lax.axis_index("expert")
-    layer = me // plane
-    tail = -(-n_ex // 16) * 16
-
     def others(value):
         return [turn(value, k) for k in range(1, n_dp)]
 
     wide = probs.astype(f32)
-    ids = jnp.arange(tail, dtype=jnp.int32)
-    chosen = routes.T[None] == ids[:, None, None]
-    p_all = jnp.sum(jnp.where(chosen, wide.T[None], 0.0), axis=1).astype(bf16)
-    p_all = jnp.pad(p_all, ((0, 0), (0, model - tok_dev)))
-    own = jnp.concatenate([tokens, out_grad, p_all], 0)
+    ids = jnp.arange(lanes, dtype=jnp.int32)
+    chosen = routes[:, :, None] == ids[None, None, :]
+    p_all = jnp.sum(jnp.where(chosen, wide[:, :, None], 0.0), axis=1).astype(bf16)
+    own = jnp.concatenate(
+        [
+            jnp.concatenate([tokens, p_all], 1),
+            jnp.concatenate([out_grad, jnp.zeros_like(p_all)], 1),
+        ],
+        0,
+    )
     w_gu, w_dn = w_gate_up[0], w_down[0]
     w_own = jnp.concatenate([w_gu, w_dn.T], 1)
     p1 = lax.dynamic_slice_in_dim(w_own, me_dp * width, width // 2, 0)
     p2 = lax.dynamic_slice_in_dim(w_own, me_dp * width + width // 2, width // 2, 0)
-    up, down = {}, {}
-    up[1], down[1] = climb(own, 1, 0, layers - 1), climb(own, -1, 1, layers)
+    held = [own, along(own)]
     x_p1, y_p2 = hop(p1, 1), hop(p2, 2)
 
-    p1, p2, up[1], down[1], x_p1, y_p2 = lax.optimization_barrier(
-        (p1, p2, up[1], down[1], x_p1, y_p2)
-    )
+    p1, p2, held, x_p1, y_p2 = lax.optimization_barrier((p1, p2, held, x_p1, y_p2))
     x_p2, y_p1 = hop(p2, 1), hop(p1, 2)
-    if layers > 2:
-        up[2], down[2] = climb(up[1], 1, 1, layers - 1), climb(down[1], -1, 1, layers - 1)
-    x_o1 = others(x_p1)
-    y_o2 = others(after(y_p2, *x_o1))
-
-    (x_p1, y_p2, x_p2, y_p1, x_o1, y_o2, up, down) = lax.optimization_barrier(
-        (x_p1, y_p2, x_p2, y_p1, x_o1, y_o2, up, down)
+    while len(held) < layers - 1:
+        held.append(along(held[-1]))
+    x_o1, y_o2 = others(x_p1), others(y_p2)
+
+    (x_p1, y_p2, x_p2, y_p1, x_o1, y_o2, held) = lax.optimization_barrier(
+        (x_p1, y_p2, x_p2, y_p1, x_o1, y_o2, held)
     )
     d_p2, d_p1 = hop(y_p2, 1), hop(x_p1, 2)
-    for k in range(3, layers):
-        up[k] = climb(up[k - 1], 1, k - 1, layers - 1)
-        down[k] = climb(down[k - 1], -1, 1, layers - k + 1)
-    x_o2 = others(x_p2)
-    y_o1 = others(after(y_p1, *x_o2))
+    final = along(held[-1])
+    x_o2, y_o1 = others(x_p2), others(y_p1)
     weights = {"w0": w_own}
 
     def name_parts(s, firsts, seconds):
@@ -378,12 +363,7 @@
     name_parts(2, [y_p1] + y_o1, [y_p2] + y_o2)
 
     def pick(slots, blocks):
-        got = {"own": own}
-        for k in blocks:
-            for z in range(layers):
-                if k:
-                    way, steps = source(z, k)
-                    got[(way, steps)] = (up if way == "up" else down)[steps]
+        got = {"t%d" % k: held[k] for k in blocks}
         for name, value in weights.items():
             if int(name[1]) in slots:
                 got[name] = value
@@ -398,9 +378,12 @@
     zero = make([0], near, False).call(pick([0], near))
     one = make([1, 2], near, False).call(pick([1, 2], near) | carry((zero, ("dx", "pr"))))
 
-    zero, one, d_p1, d_p2, up, down = lax.optimization_barrier((zero, one, d_p1, d_p2, up, down))
+    zero, one, d_p1, d_p2, held, final = lax.optimization_barrier(
+        (zero, one, d_p1, d_p2, held, final)
+    )
+    held.append(final)
     d_o1 = others(d_p1)
-    d_o2 = others(after(d_p2, *d_o1))
+    d_o2 = others(d_p2)
     name_parts(3, [d_p1] + d_o1, [d_p2] + d_o2)
     grads = ("keep", "send")
     two = make([0, 1, 2], far, False).call(pick([0, 1, 2], far) | carry((zero, grads), (one, grads)))
@@ -409,30 +392,22 @@
     )
 
     swapped = [turn(two["send"][:, k - 1], k) for k in range(1, n_dp)]
-    sent = [
-        hop((two["keep"][s] + sum(v[s].astype(f32) for v in swapped)).astype(bf16), s)
-        for s in (1, 2)
-    ]
+    last, swapped, keep = lax.optimization_barrier((last, swapped, two["keep"]))
+    leaving = [(keep[s] + sum(v[s].astype(f32) for v in swapped)).astype(bf16) for s in (1, 2)]
+    leaving, last = lax.optimization_barrier((leaving, last))
+    sent = [hop(leaving[0], 1), hop(leaving[1], 2)]
     swapped_across = [turn(last["send"][0, k - 1], k) for k in range(1, n_dp)]
     across = last["keep"][0] + sum(v.astype(f32) for v in swapped_across)
-    sent.append(hop(across.astype(bf16), 3))
+    across = across.astype(bf16)
+    sent.append(hop(across, 3))
     back = last["back"]
-
-    def term(dest):
-        return lax.dynamic_index_in_dim(back, dest, 0, False).astype(f32)
-
-    from_below = from_above = 0.0
-    for k in range(layers - 1, 0, -1):
-        send_up = (term(jnp.minimum(layer + k, layers - 1)) + from_below).astype(bf16)
-        send_down = (term(jnp.maximum(layer - k, 0)) + from_above).astype(bf16)
-        send_up, send_down = lax.optimization_barrier((send_up, send_down))
-        from_below = climb(send_up, 1, 0, layers - k)
-        from_above = climb(send_down, -1, k, layers)
-        if k > 1:
-            from_below, from_above = from_below.astype(f32), from_above.astype(f32)
-
-    sent = lax.optimization_barrier((sent, send_up, send_down))[0]
-    grad = two["keep"][0] + sum(v[0].astype(f32) for v in swapped)
+    passing = along(back[1])
+    for k in range(2, layers):
+        passing = (passing.astype(f32) + back[k].astype(f32)).astype(bf16)
+        passing = along(after(passing, across) if k == 2 else passing)
+
+    sent, passing = lax.optimization_barrier((sent, passing))
+    grad = keep[0] + sum(v[0].astype(f32) for v in swapped)
     grad = (grad + sum(v.astype(f32) for v in sent)).astype(bf16)
     parts = [grad] + others(grad)
     new_one, new_two, w_new = adam_call(parts, leader, moment_one, moment_two, w_down)
@@ -441,11 +416,10 @@
     for k in range(1, n_dp):
         fresh = jnp.where((me_dp + k) % n_dp == lead, turn(w_new, k), fresh)
 
-    from_below, from_above = lax.optimization_barrier((from_below, from_above, w_new))[:2]
-    total = term(layer) + from_below.astype(f32) + from_above.astype(f32)
-    token_grad = total[:tok_dev].astype(bf16)
-    pair = total[tok_dev:, :tok_dev]
-    prob_grad = jnp.sum(jnp.where(chosen, pair[:, None, :], 0.0), axis=0).T.astype(bf16)
+    total = back[0].astype(f32) + passing.astype(f32)
+    token_grad = total[:, :model].astype(bf16)
+    pair = total[:, model:]
+    prob_grad = jnp.sum(jnp.where(chosen, pair[:, None, :], 0.0), axis=2).astype(bf16)
     is_live = replicas[0][me_dp] == 1
     new_down = jnp.where(is_live, fresh, w_dn)[None, None]
     return (token_grad, prob_grad, new_down, new_one, new_two)

time: 258 us -> 219 us (0.85)
  waiting for transfers between devices: 117 us -> 100 us
  starting transfers between devices: 42.2 us -> 27.9 us
  other arithmetic: 24.6 us -> 16.5 us
    ppermute x12 -> x6, starting transfers between devices: 26 us -> 9.17 us  [along(): return lax.ppermute(value, 'expert', pairs)]
    ppermute x12 -> x6, waiting for transfers between devices: 82.1 us -> 70.3 us  [along(): return lax.ppermute(value, 'expert', pairs)]
    convert_element_type x4, other arithmetic: 10.5 us -> 1.1 us  [the longest x1 0.57 us: body(): (keep[s] + sum((v[s].astype(f32) for v in swapped))).astype(bf16)]
    ppermute x9, waiting for transfers between devices: 27 us -> 21.3 us  [hop(): return lax.ppermute(value, 'expert', [(i, i ^ flip) for i in range(n)])]
    concatenate x2, other arithmetic: 4.7 us -> 7.45 us  [body(): w_own = jnp.concatenate([w_gu, w_dn.T], 1)]
  transfers between devices with their start and end apart: 31 -> 25, of which waited for: 14 -> 9; matrix products, arithmetic and copies ran while one was open for 7% -> 5% of each run, Pallas kernels for 23% -> 20%
where the time goes in v1:
time: 219 us; the launch traced here: 217 us
  waiting for transfers between devices  100 us (46%)
  Pallas kernels  64 us (29%)
  starting transfers between devices  27.9 us (13%)
  other arithmetic  16.5 us (8%)
  local copies, waits for them, and re-layouts  6.64 us (3%)
    ppermute x6, waiting for transfers between devices, along(): return lax.ppermute(value, 'expert', pairs)  70.3 us
    pallas_call x4, Pallas kernels, call(): pl.pallas_call(functools.partial(self.kernel, len(ins)), out_shape=[jax.S...  58.6 us
    ppermute x9, waiting for transfers between devices, hop(): return lax.ppermute(value, 'expert', [(i, i ^ flip) for i in range(n)])  21.3 us
    ppermute x10, starting transfers between devices, turn(): return lax.ppermute(value, 'dp', [((r + step) % n, r) for r in range(n)])  9.55 us
    ppermute x9, starting transfers between devices, hop(): return lax.ppermute(value, 'expert', [(i, i ^ flip) for i in range(n)])  9.22 us
    ppermute x6, starting transfers between devices, along(): return lax.ppermute(value, 'expert', pairs)  9.17 us
    ppermute x10, waiting for transfers between devices, turn(): return lax.ppermute(value, 'dp', [((r + step) % n, r) for r in range(n)])  8.49 us
    concatenate x2, other arithmetic, body(): w_own = jnp.concatenate([w_gu, w_dn.T], 1)  7.45 us
  transfers between devices with their start and end apart: 25, of which 9 were waited for; matrix products, arithmetic and copies ran while one was open for 5% of the time, Pallas kernels for 20%

profile of v1, /device:TPU:1, one launch (start us, length us, event | category | flops | bytes accessed | tf_op | source)
XLA Modules:
  0.0 216.9 jit_solution(12061877953196952398)
XLA Ops:
  0.6 1.9 copy.18
  2.6 3.0 %fusion.5 = (bf16[512,1152]{1,0:T(8,128)(2,1)}, bf16[512,1152]{1,0:T(8,128)(2,1)}) fusion(s32[]{:T(128)S(6)} %select_n.39, bf16[2048,768]{1,0:T(8,128)(2,1)} %bitcast.38, bf16[2048,384]{1,0:T(8,128)(2,1)S(1)} %copy.18, s32[]{:T(128)S(6)} %select_n.38), kind=kLoop, calls=%fused_computation.16 | loop fusion | flops 4718592 | bytes 7077896 | tf_op jit(solution)/shard_map/concatenate | solution.py:337
  5.6 2.0 collective-permute-start.1
  7.6 1.2 collective-permute-start.2
  9.4 1.1 fusion.6.refs_0_
  10.6 1.3 collective-permute-start
  11.9 24.4 %collective-permute-done.refs_1_ = bf16[256,2176]{1,0:T(8,128)(2,1)S(1)} collective-permute-done((bf16[256,2176]{1,0:T(8,128)(2,1)S(1)}, bf16[256,2176]{1,0:T(8,128)(2,1)S(1)}, u32[]{:S(2)}, u32[]{:S(2)}) %collective-permute-start) | collective-permute-done | bytes 1114144 | tf_op jit(solution)/shard_map/ppermute | solution.py:54
  36.7 0.5 collective-permute-start.4
  37.2 2.4 %collective-permute-start.5 = (bf16[512,1152]{1,0:T(8,128)(2,1)S(1)}, bf16[512,1152]{1,0:T(8,128)(2,1)S(1)}, u32[]{:S(2)}, u32[]{:S(2)}) collective-permute-start(bf16[512,1152]{1,0:T(8,128)(2,1)S(1)} %collective-permute-done.1.refs_3_.refs_2_), channel_id=1, source_target_pairs={{16,0},{0,16},{17,1},{1,17},{18,2},{2,18},{19,3},{3,19},{20,4},{4,... | collective-permute-start | bytes 3538952 | tf_op jit(solution)/shard_map/ppermute | solution.py:59
  39.6 0.6 collective-permute-start.7
  40.1 26.0 %collective-permute-done.7.refs_2_ = bf16[256,2176]{1,0:T(8,128)(2,1)S(1)} collective-permute-done((bf16[256,2176]{1,0:T(8,128)(2,1)S(1)}, bf16[256,2176]{1,0:T(8,128)(2,1)S(1)}, u32[]{:S(2)}, u32[]{:S(2)}) %collective-permute-start.7) | collective-permute-done | bytes 1114144 | tf_op jit(solution)/shard_map/ppermute | solution.py:54
  66.2 1.4 collective-permute-start.8
  67.7 1.3 collective-permute-start.10
  69.0 1.2 collective-permute-start.11
  70.2 0.5 collective-permute-start.12
  70.7 4.4 %pad_maximum_fusion.refs_3_.refs_1_ = bf16[2048,1152]{1,0:T(8,128)(2,1)} fusion(bf16[2048,384]{1,0:T(8,128)(2,1)S(1)} %copy.18, bf16[2048,768]{1,0:T(8,128)(2,1)} %bitcast.39), kind=kLoop, calls=%fused_computation.2 | loop fusion | flops 9437184 | bytes 9437184 | tf_op jit(solution)/shard_map/concatenate | solution.py:337
  75.2 11.4 %shard_map.137 = (f32[1,384,1024]{2,1,0:T(8,128)}, bf16[1,1,384,1024]{3,2,1,0:T(8,128)(2,1)}, f32[384,2048]{1,0:T(8,128)}, f32[384,128]{1,0:T(8,128)}) custom-call(bf16[256,2176]{1,0:T(8,128)(2,1)} %copy-done.3, bf16[256,2176]{1,0:T(8,128)(2,1)} %copy-done.4, bf16[256,2176]{1,0:T(8,128)(2,1)} %copy-done.5, bf16[2048,1152]{1,0:T(8,128)(2,1)} %pad_maximum_fusion.refs_3_.refs_1_), custom_call_target="tpu_custom_call" | custom-call | flops 1000 | bytes 1000 | tf_op jit(solution)/shard_map/pallas_call | solution.py:259
  86.6 18.2 %shard_map.138 = (f32[2,384,1024]{2,1,0:T(8,128)}, bf16[2,1,384,1024]{3,2,1,0:T(8,128)(2,1)}, f32[384,2048]{1,0:T(8,128)}, f32[384,128]{1,0:T(8,128)}) custom-call(bf16[256,2176]{1,0:T(8,128)(2,1)} %copy-done.3, bf16[256,2176]{1,0:T(8,128)(2,1)} %copy-done.4, bf16[256,2176]{1,0:T(8,128)(2,1)} %copy-done.5, bf16[512,1152]{1,0:T(8,128)(2,1)} %copy-done.6, ...), custom_call_target="tpu_custom_call" | custom-call | flops 1000 | bytes 1000 | tf_op jit(solution)/shard_map/pallas_call | solution.py:259
  104.9 14.1 %shard_map.139 = (f32[3,384,1024]{2,1,0:T(8,128)}, bf16[3,1,384,1024]{3,2,1,0:T(8,128)(2,1)}, f32[128,2048]{1,0:T(8,128)}, f32[128,128]{1,0:T(8,128)}) custom-call(bf16[256,2176]{1,0:T(8,128)(2,1)} %collective-permute-done.12.refs_0_.refs_3_, bf16[2048,1152]{1,0:T(8,128)(2,1)} %pad_maximum_fusion.refs_3_.refs_1_, bf16[512,1152]{1,0:T(8,128)(2,1)} %copy-done.6, ...), custom_call_target="tpu_custom_call" | custom-call | flops 1000 | bytes 1000 | tf_op jit(solution)/shard_map/pallas_call | solution.py:259
  119.0 1.3 collective-permute-start.15
  120.4 0.4 collective-permute-start.14
  120.9 5.5 %collective-permute-done.13.refs_6_ = bf16[512,1152]{1,0:T(8,128)(2,1)S(1)} collective-permute-done((bf16[512,1152]{1,0:T(8,128)(2,1)}, bf16[512,1152]{1,0:T(8,128)(2,1)S(1)}, u32[]{:S(2)}, u32[]{:S(2)}) %collective-permute-start.13) | collective-permute-done | bytes 1179680 | tf_op jit(solution)/shard_map/ppermute | solution.py:59
  126.4 1.7 collective-permute-done.14.refs_7_
  128.1 1.0 copy-done.14
  129.1 14.8 %shard_map.140 = (f32[1,384,1024]{2,1,0:T(8,128)}, bf16[1,1,384,1024]{3,2,1,0:T(8,128)(2,1)}, bf16[4,128,2176]{2,1,0:T(8,128)(2,1)}) custom-call(bf16[256,2176]{1,0:T(8,128)(2,1)} %copy-done.3, bf16[256,2176]{1,0:T(8,128)(2,1)} %copy-done.4, bf16[256,2176]{1,0:T(8,128)(2,1)} %copy-done.5, bf16[256,2176]{1,0:T(8,128)(2,1)} %collective-permute-done.12.refs_0_.refs_3_, ...), custom_call_target="tpu_custom_call" | custom-call | flops 1000 | bytes 1000 | tf_op jit(solution)/shard_map/pallas_call | solution.py:259
  144.0 0.6 fusion.10
  144.5 0.8 copy-done.10
  145.3 1.1 copy-done.11
  146.5 3.2 %collective-permute-start.20 = (bf16[128,2176]{1,0:T(8,128)(2,1)S(1)}, bf16[128,2176]{1,0:T(8,128)(2,1)S(1)}, u32[]{:S(2)}, u32[]{:S(2)}) collective-permute-start(bf16[128,2176]{1,0:T(8,128)(2,1)S(1)} %slice_bitcast_fusion), channel_id=1, source_target_pairs={{0,4},{1,5},{2,6},{3,7},{4,12},{5,13},{6,14},{7,15},{12,8},{13,9},... | collective-permute-start | bytes 1671176 | tf_op jit(solution)/shard_map/ppermute | solution.py:54
  149.6 0.7 collective-permute-start.18
  150.3 11.0 %collective-permute-done.20 = bf16[128,2176]{1,0:T(8,128)(2,1)S(1)} collective-permute-done((bf16[128,2176]{1,0:T(8,128)(2,1)S(1)}, bf16[128,2176]{1,0:T(8,128)(2,1)S(1)}, u32[]{:S(2)}, u32[]{:S(2)}) %collective-permute-start.20) | collective-permute-done | bytes 557088 | tf_op jit(solution)/shard_map/ppermute | solution.py:54
  161.7 2.3 %collective-permute-start.21 = (bf16[128,2176]{1,0:T(8,128)(2,1)S(1)}, bf16[128,2176]{1,0:T(8,128)(2,1)S(1)}, u32[]{:S(2)}, u32[]{:S(2)}) collective-permute-start(bf16[128,2176]{1,0:T(8,128)(2,1)S(1)} %fusion.8), channel_id=1, source_target_pairs={{0,4},{1,5},{2,6},{3,7},{4,12},{5,13},{6,14},{7,15},{12,8},{13,9},... | collective-permute-start | bytes 1671176 | tf_op jit(solution)/shard_map/ppermute | solution.py:54
  164.4 2.2 %collective-permute-start.19 = (bf16[384,1024]{1,0:T(8,128)(2,1)S(1)}, bf16[384,1024]{1,0:T(8,128)(2,1)S(1)}, u32[]{:S(2)}, u32[]{:S(2)}) collective-permute-start(bf16[384,1024]{1,0:T(8,128)(2,1)S(1)} %fusion.2), channel_id=1, source_target_pairs={{0,3},{1,2},{2,1},{3,0},{4,7},{5,6},{6,5},{7,4},{8,11},{9,10},{10,... | collective-permute-start | bytes 2359304 | tf_op jit(solution)/shard_map/ppermute | solution.py:37
  166.6 9.0 %collective-permute-done.21 = bf16[128,2176]{1,0:T(8,128)(2,1)S(1)} collective-permute-done((bf16[128,2176]{1,0:T(8,128)(2,1)S(1)}, bf16[128,2176]{1,0:T(8,128)(2,1)S(1)}, u32[]{:S(2)}, u32[]{:S(2)}) %collective-permute-start.21) | collective-permute-done | bytes 557088 | tf_op jit(solution)/shard_map/ppermute | solution.py:54
  175.7 1.4 collective-permute-start.22
  177.1 4.4 %collective-permute-done.16 = bf16[384,1024]{1,0:T(8,128)(2,1)S(1)} collective-permute-done((bf16[384,1024]{1,0:T(8,128)(2,1)S(1)}, bf16[384,1024]{1,0:T(8,128)(2,1)S(1)}, u32[]{:S(2)}, u32[]{:S(2)}) %collective-permute-start.16) | collective-permute-done | bytes 786464 | tf_op jit(solution)/shard_map/ppermute | solution.py:37
  181.5 16.8 %collective-permute-done.19 = bf16[384,1024]{1,0:T(8,128)(2,1)S(1)} collective-permute-done((bf16[384,1024]{1,0:T(8,128)(2,1)S(1)}, bf16[384,1024]{1,0:T(8,128)(2,1)S(1)}, u32[]{:S(2)}, u32[]{:S(2)}) %collective-permute-start.19) | collective-permute-done | bytes 786464 | tf_op jit(solution)/shard_map/ppermute | solution.py:37
  198.3 2.1 fusion.1.refs_0_
  200.4 2.7 %collective-permute-start.23 = (bf16[384,1024]{1,0:T(8,128)(2,1)S(1)}, bf16[384,1024]{1,0:T(8,128)(2,1)S(1)}, u32[]{:S(2)}, u32[]{:S(2)}) collective-permute-start(bf16[384,1024]{1,0:T(8,128)(2,1)S(1)} %fusion.1.refs_0_), channel_id=1, source_target_pairs={{16,0},{0,16},{17,1},{1,17},{18,2},{2,18},{19,3},{3,19},{20,4},{4,... | collective-permute-start | bytes 2359304 | tf_op jit(solution)/shard_map/ppermute | solution.py:59
  203.8 1.2 collective-permute-done.23.refs_1_
  205.1 5.5 %shard_map.141 = (f32[1,1,384,2048]{3,2,1,0:T(8,128)}, f32[1,1,384,2048]{3,2,1,0:T(8,128)}, bf16[384,2048]{1,0:T(8,128)(2,1)S(1)}) custom-call(s32[1]{0:T(128)} %copy.22.lead_ref, bf16[384,1024]{1,0:T(8,128)(2,1)S(1)} %fusion.1.refs_0_, bf16[384,1024]{1,0:T(8,128)(2,1)S(1)} %collective-permute-done.23.refs_1_, f32[1,1,384,2048]{3,2,1,0:T(8,128)S(1)} %copy-done.1, ...), custom_call_target="tpu_custom_call" | custom-call | flops 1000 | bytes 1000 | tf_op jit(solution)/shard_map/pallas_call | solution.py:293
  210.5 0.4 collective-permute-start.24
  210.9 0.7 fusion.11
  211.6 1.3 convert_add_fusion.2
  212.9 0.9 slice.66
  213.8 0.4 select_reduce_fusion
  214.2 0.7 copy.21
  214.9 2.0 fusion.3
  (74 shorter events, 2.2 us)
Async XLA Ops:
  2.5 6.3 %copy-start.17 = (s32[128,8]{0,1:T(8,128)S(1)}, s32[128,8]{0,1:T(8,128)}, u32[]{:S(2)}) copy-start(s32[128,8]{0,1:T(8,128)} %param.12) | copy-start | bytes 12292
  2.5 6.4 %copy-start.18 = (bf16[128,8]{0,1:T(8,128)(2,1)S(1)}, bf16[128,8]{0,1:T(8,128)(2,1)}, u32[]{:S(2)}) copy-start(bf16[128,8]{0,1:T(8,128)(2,1)} %param.13) | copy-start | bytes 6148
  2.5 6.9 %copy-start.16 = (bf16[128,2048]{1,0:T(8,128)(2,1)S(1)}, bf16[128,2048]{1,0:T(8,128)(2,1)}, u32[]{:S(2)}) copy-start(bf16[128,2048]{1,0:T(8,128)(2,1)} %param.11) | copy-start | bytes 1572868
  5.6 30.8 %collective-permute-start.1 = (bf16[512,1152]{1,0:T(8,128)(2,1)}, bf16[512,1152]{1,0:T(8,128)(2,1)S(1)}, u32[]{:S(2)}, u32[]{:S(2)}) collective-permute-start(bf16[512,1152]{1,0:T(8,128)(2,1)} %get-tuple-element.68), channel_id=1, source_target_pairs={{0,1},{1,0},{2,3},{3,2},{4,5},{5,4},{6,7},{7,6},{8,9},{9,8},{10,11... | collective-permute-start | bytes 3538952 | tf_op jit(solution)/shard_map/ppermute | solution.py:37
  7.6 28.8 %collective-permute-start.2 = (bf16[512,1152]{1,0:T(8,128)(2,1)}, bf16[512,1152]{1,0:T(8,128)(2,1)}, u32[]{:S(2)}, u32[]{:S(2)}) collective-permute-start(bf16[512,1152]{1,0:T(8,128)(2,1)} %get-tuple-element.67), channel_id=1, source_target_pairs={{0,2},{1,3},{2,0},{3,1},{4,6},{5,7},{6,4},{7,5},{8,10},{9,11},{10,... | collective-permute-start | bytes 3538952 | tf_op jit(solution)/shard_map/ppermute | solution.py:37
  10.6 64.5 %copy-start.3 = (bf16[256,2176]{1,0:T(8,128)(2,1)}, bf16[256,2176]{1,0:T(8,128)(2,1)S(1)}, u32[]{:S(2)}) copy-start(bf16[256,2176]{1,0:T(8,128)(2,1)S(1)} %fusion.6.refs_0_) | copy-start | bytes 3342340
  10.6 25.8 %collective-permute-start = (bf16[256,2176]{1,0:T(8,128)(2,1)S(1)}, bf16[256,2176]{1,0:T(8,128)(2,1)S(1)}, u32[]{:S(2)}, u32[]{:S(2)}) collective-permute-start(bf16[256,2176]{1,0:T(8,128)(2,1)S(1)} %fusion.6.refs_0_), channel_id=1, source_target_pairs={{0,4},{1,5},{2,6},{3,7},{4,12},{5,13},{6,14},{7,15},{12,8},{13,9},... | collective-permute-start | bytes 3342344 | tf_op jit(solution)/shard_map/ppermute | solution.py:54
  36.4 38.8 %copy-start.4 = (bf16[256,2176]{1,0:T(8,128)(2,1)}, bf16[256,2176]{1,0:T(8,128)(2,1)S(1)}, u32[]{:S(2)}) copy-start(bf16[256,2176]{1,0:T(8,128)(2,1)S(1)} %collective-permute-done.refs_1_) | copy-start | bytes 3342340
  36.4 38.8 %copy-start.6 = (bf16[512,1152]{1,0:T(8,128)(2,1)}, bf16[512,1152]{1,0:T(8,128)(2,1)S(1)}, u32[]{:S(2)}) copy-start(bf16[512,1152]{1,0:T(8,128)(2,1)S(1)} %collective-permute-done.1.refs_3_.refs_2_) | copy-start | bytes 3538948
  36.4 29.7 %collective-permute-start.3 = (bf16[512,1152]{1,0:T(8,128)(2,1)}, bf16[512,1152]{1,0:T(8,128)(2,1)S(1)}, u32[]{:S(2)}, u32[]{:S(2)}) collective-permute-start(bf16[512,1152]{1,0:T(8,128)(2,1)} %get-tuple-element.67), channel_id=1, source_target_pairs={{0,1},{1,0},{2,3},{3,2},{4,5},{5,4},{6,7},{7,6},{8,9},{9,8},{10,11... | collective-permute-start | bytes 3538952 | tf_op jit(solution)/shard_map/ppermute | solution.py:37
  36.7 29.4 %collective-permute-start.4 = (bf16[512,1152]{1,0:T(8,128)(2,1)}, bf16[512,1152]{1,0:T(8,128)(2,1)}, u32[]{:S(2)}, u32[]{:S(2)}) collective-permute-start(bf16[512,1152]{1,0:T(8,128)(2,1)} %get-tuple-element.68), channel_id=1, source_target_pairs={{0,2},{1,3},{2,0},{3,1},{4,6},{5,7},{6,4},{7,5},{8,10},{9,11},{10,... | collective-permute-start | bytes 3538952 | tf_op jit(solution)/shard_map/ppermute | solution.py:37
  37.2 29.0 %collective-permute-start.5 = (bf16[512,1152]{1,0:T(8,128)(2,1)S(1)}, bf16[512,1152]{1,0:T(8,128)(2,1)S(1)}, u32[]{:S(2)}, u32[]{:S(2)}) collective-permute-start(bf16[512,1152]{1,0:T(8,128)(2,1)S(1)} %collective-permute-done.1.refs_3_.refs_2_), channel_id=1, source_target_pairs={{16,0},{0,16},{17,1},{1,17},{18,2},{2,18},{19,3},{3,19},{20,4},{4,... | collective-permute-start | bytes 3538952 | tf_op jit(solution)/shard_map/ppermute | solution.py:59
  39.6 26.6 %collective-permute-start.6 = (bf16[512,1152]{1,0:T(8,128)(2,1)}, bf16[512,1152]{1,0:T(8,128)(2,1)S(1)}, u32[]{:S(2)}, u32[]{:S(2)}) collective-permute-start(bf16[512,1152]{1,0:T(8,128)(2,1)} %collective-permute-done.2.refs_8_.refs_7_), channel_id=1, source_target_pairs={{16,0},{0,16},{17,1},{1,17},{18,2},{2,18},{19,3},{3,19},{20,4},{4,... | collective-permute-start | bytes 3538952 | tf_op jit(solution)/shard_map/ppermute | solution.py:59
  39.6 26.5 %collective-permute-start.7 = (bf16[256,2176]{1,0:T(8,128)(2,1)S(1)}, bf16[256,2176]{1,0:T(8,128)(2,1)S(1)}, u32[]{:S(2)}, u32[]{:S(2)}) collective-permute-start(bf16[256,2176]{1,0:T(8,128)(2,1)S(1)} %collective-permute-done.refs_1_), channel_id=1, source_target_pairs={{0,4},{1,5},{2,6},{3,7},{4,12},{5,13},{6,14},{7,15},{12,8},{13,9},... | collective-permute-start | bytes 3342344 | tf_op jit(solution)/shard_map/ppermute | solution.py:54
  66.1 9.0 %copy-start.5 = (bf16[256,2176]{1,0:T(8,128)(2,1)}, bf16[256,2176]{1,0:T(8,128)(2,1)S(1)}, u32[]{:S(2)}) copy-start(bf16[256,2176]{1,0:T(8,128)(2,1)S(1)} %collective-permute-done.7.refs_2_) | copy-start | bytes 3342340
  66.1 9.0 %copy-start.7 = (bf16[512,1152]{1,0:T(8,128)(2,1)}, bf16[512,1152]{1,0:T(8,128)(2,1)S(1)}, u32[]{:S(2)}) copy-start(bf16[512,1152]{1,0:T(8,128)(2,1)S(1)} %collective-permute-done.3.refs_4_.refs_3_) | copy-start | bytes 3538948
  66.1 2.8 %copy-start.8 = (bf16[512,1152]{1,0:T(8,128)(2,1)}, bf16[512,1152]{1,0:T(8,128)(2,1)S(1)}, u32[]{:S(2)}) copy-start(bf16[512,1152]{1,0:T(8,128)(2,1)S(1)} %collective-permute-done.5.refs_5_.refs_4_) | copy-start | bytes 3538948
  66.2 4.0 %copy-start.9 = (bf16[512,1152]{1,0:T(8,128)(2,1)}, bf16[512,1152]{1,0:T(8,128)(2,1)S(1)}, u32[]{:S(2)}) copy-start(bf16[512,1152]{1,0:T(8,128)(2,1)S(1)} %collective-permute-done.6.refs_10_.refs_9_) | copy-start | bytes 3538948
  66.2 20.4 %collective-permute-start.8 = (bf16[512,1152]{1,0:T(8,128)(2,1)S(1)}, bf16[512,1152]{1,0:T(8,128)(2,1)}, u32[]{:S(2)}, u32[]{:S(2)}) collective-permute-start(bf16[512,1152]{1,0:T(8,128)(2,1)S(1)} %collective-permute-done.3.refs_4_.refs_3_), channel_id=1, source_target_pairs={{16,0},{0,16},{17,1},{1,17},{18,2},{2,18},{19,3},{3,19},{20,4},{4,... | collective-permute-start | bytes 3538952 | tf_op jit(solution)/shard_map/ppermute | solution.py:59
  67.6 19.0 %collective-permute-start.9 = (bf16[512,1152]{1,0:T(8,128)(2,1)}, bf16[512,1152]{1,0:T(8,128)(2,1)}, u32[]{:S(2)}, u32[]{:S(2)}) collective-permute-start(bf16[512,1152]{1,0:T(8,128)(2,1)} %collective-permute-done.4.refs_7_.refs_6_), channel_id=1, source_target_pairs={{16,0},{0,16},{17,1},{1,17},{18,2},{2,18},{19,3},{3,19},{20,4},{4,... | collective-permute-start | bytes 3538952 | tf_op jit(solution)/shard_map/ppermute | solution.py:59
  67.7 37.2 %collective-permute-start.10 = (bf16[512,1152]{1,0:T(8,128)(2,1)S(1)}, bf16[512,1152]{1,0:T(8,128)(2,1)}, u32[]{:S(2)}, u32[]{:S(2)}) collective-permute-start(bf16[512,1152]{1,0:T(8,128)(2,1)S(1)} %collective-permute-done.1.refs_3_.refs_2_), channel_id=1, source_target_pairs={{0,2},{1,3},{2,0},{3,1},{4,6},{5,7},{6,4},{7,5},{8,10},{9,11},{10,... | collective-permute-start | bytes 3538952 | tf_op jit(solution)/shard_map/ppermute | solution.py:37
  69.0 35.9 %collective-permute-start.11 = (bf16[512,1152]{1,0:T(8,128)(2,1)}, bf16[512,1152]{1,0:T(8,128)(2,1)}, u32[]{:S(2)}, u32[]{:S(2)}) collective-permute-start(bf16[512,1152]{1,0:T(8,128)(2,1)} %collective-permute-done.2.refs_8_.refs_7_), channel_id=1, source_target_pairs={{0,1},{1,0},{2,3},{3,2},{4,5},{5,4},{6,7},{7,6},{8,9},{9,8},{10,11... | collective-permute-start | bytes 3538952 | tf_op jit(solution)/shard_map/ppermute | solution.py:37
  70.2 34.7 %collective-permute-start.12 = (bf16[256,2176]{1,0:T(8,128)(2,1)S(1)}, bf16[256,2176]{1,0:T(8,128)(2,1)}, u32[]{:S(2)}, u32[]{:S(2)}) collective-permute-start(bf16[256,2176]{1,0:T(8,128)(2,1)S(1)} %collective-permute-done.7.refs_2_), channel_id=1, source_target_pairs={{0,4},{1,5},{2,6},{3,7},{4,12},{5,13},{6,14},{7,15},{12,8},{13,9},... | collective-permute-start | bytes 3342344 | tf_op jit(solution)/shard_map/ppermute | solution.py:54
  119.0 24.9 %collective-permute-start.15 = (bf16[3,384,1024]{2,1,0:T(8,128)(2,1)}, bf16[3,384,1024]{2,1,0:T(8,128)(2,1)S(1)}, u32[]{:S(2)}, u32[]{:S(2)}) collective-permute-start(bf16[3,384,1024]{2,1,0:T(8,128)(2,1)} %bitcast.42), channel_id=1, source_target_pairs={{16,0},{0,16},{17,1},{1,17},{18,2},{2,18},{19,3},{3,19},{20,4},{4,... | collective-permute-start | bytes 7077896 | tf_op jit(solution)/shard_map/ppermute | solution.py:59
  120.4 6.1 %collective-permute-start.13 = (bf16[512,1152]{1,0:T(8,128)(2,1)}, bf16[512,1152]{1,0:T(8,128)(2,1)S(1)}, u32[]{:S(2)}, u32[]{:S(2)}) collective-permute-start(bf16[512,1152]{1,0:T(8,128)(2,1)} %collective-permute-done.10.refs_4_), channel_id=1, source_target_pairs={{16,0},{0,16},{17,1},{1,17},{18,2},{2,18},{19,3},{3,19},{20,4},{4,... | collective-permute-start | bytes 3538952 | tf_op jit(solution)/shard_map/ppermute | solution.py:59
  120.4 7.7 %collective-permute-start.14 = (bf16[512,1152]{1,0:T(8,128)(2,1)}, bf16[512,1152]{1,0:T(8,128)(2,1)S(1)}, u32[]{:S(2)}, u32[]{:S(2)}) collective-permute-start(bf16[512,1152]{1,0:T(8,128)(2,1)} %collective-permute-done.11.refs_5_), channel_id=1, source_target_pairs={{16,0},{0,16},{17,1},{1,17},{18,2},{2,18},{19,3},{3,19},{20,4},{4,... | collective-permute-start | bytes 3538952 | tf_op jit(solution)/shard_map/ppermute | solution.py:59
  126.4 2.7 %copy-start.13 = (bf16[512,1152]{1,0:T(8,128)(2,1)}, bf16[512,1152]{1,0:T(8,128)(2,1)S(1)}, u32[]{:S(2)}) copy-start(bf16[512,1152]{1,0:T(8,128)(2,1)S(1)} %collective-permute-done.13.refs_6_) | copy-start | bytes 3538948
  128.1 1.0 copy-start.14
  129.1 14.8 %slice-start = ((s8[4718592]{0:T(1024)(128)(4,1)}), s8[4194304]{0:T(1024)(128)(4,1)S(1)}, s32[]{:S(2)}) async-start(s8[4718592]{0:T(1024)(128)(4,1)} %bitcast.40), calls=%async_computation | async-start | bytes 8388608
  129.1 14.8 %slice-start.1 = ((s8[4718592]{0:T(1024)(128)(4,1)}), s8[524288]{0:T(1024)(128)(4,1)S(1)}, s32[]{:S(2)}) async-start(s8[4718592]{0:T(1024)(128)(4,1)} %bitcast.40), calls=%async_computation.1 | async-start | bytes 1048576
  143.9 1.4 copy-start.10
  143.9 2.5 %copy-start.11 = (bf16[4,128,2176]{2,1,0:T(8,128)(2,1)S(1)}, bf16[4,128,2176]{2,1,0:T(8,128)(2,1)}, u32[]{:S(2)}) copy-start(bf16[4,128,2176]{2,1,0:T(8,128)(2,1)} %get-tuple-element.112) | copy-start | bytes 6684676
  144.0 5.7 %copy-start.19 = (bf16[1,1,384,1024]{3,2,1,0:T(8,128)(2,1)S(1)}, bf16[1,1,384,1024]{3,2,1,0:T(8,128)(2,1)}, u32[]{:S(2)}) copy-start(bf16[1,1,384,1024]{3,2,1,0:T(8,128)(2,1)} %get-tuple-element.116) | copy-start | bytes 2359300
  145.3 16.0 %copy-start.12 = (f32[1,384,1024]{2,1,0:T(8,128)S(1)}, f32[1,384,1024]{2,1,0:T(8,128)}, u32[]{:S(2)}) copy-start(f32[1,384,1024]{2,1,0:T(8,128)} %get-tuple-element.115) | copy-start | bytes 4718596
  146.5 14.8 %collective-permute-start.20 = (bf16[128,2176]{1,0:T(8,128)(2,1)S(1)}, bf16[128,2176]{1,0:T(8,128)(2,1)S(1)}, u32[]{:S(2)}, u32[]{:S(2)}) collective-permute-start(bf16[128,2176]{1,0:T(8,128)(2,1)S(1)} %slice_bitcast_fusion), channel_id=1, source_target_pairs={{0,4},{1,5},{2,6},{3,7},{4,12},{5,13},{6,14},{7,15},{12,8},{13,9},... | collective-permute-start | bytes 1671176 | tf_op jit(solution)/shard_map/ppermute | solution.py:54
  149.6 11.8 %collective-permute-start.18 = (bf16[384,1024]{1,0:T(8,128)(2,1)S(1)}, bf16[384,1024]{1,0:T(8,128)(2,1)S(1)}, u32[]{:S(2)}, u32[]{:S(2)}) collective-permute-start(bf16[384,1024]{1,0:T(8,128)(2,1)S(1)} %bitcast.43), channel_id=1, source_target_pairs={{16,0},{0,16},{17,1},{1,17},{18,2},{2,18},{19,3},{3,19},{20,4},{4,... | collective-permute-start | bytes 2359304 | tf_op jit(solution)/shard_map/ppermute | solution.py:59
  161.4 43.7 %copy-start.2 = (f32[1,1,384,2048]{3,2,1,0:T(8,128)S(1)}, f32[1,1,384,2048]{3,2,1,0:T(8,128)}, u32[]{:S(2)}) copy-start(f32[1,1,384,2048]{3,2,1,0:T(8,128)} %refs_3_.1) | copy-start | bytes 9437188
  161.7 13.9 %collective-permute-start.21 = (bf16[128,2176]{1,0:T(8,128)(2,1)S(1)}, bf16[128,2176]{1,0:T(8,128)(2,1)S(1)}, u32[]{:S(2)}, u32[]{:S(2)}) collective-permute-start(bf16[128,2176]{1,0:T(8,128)(2,1)S(1)} %fusion.8), channel_id=1, source_target_pairs={{0,4},{1,5},{2,6},{3,7},{4,12},{5,13},{6,14},{7,15},{12,8},{13,9},... | collective-permute-start | bytes 1671176 | tf_op jit(solution)/shard_map/ppermute | solution.py:54
  163.9 17.5 %collective-permute-start.16 = (bf16[384,1024]{1,0:T(8,128)(2,1)S(1)}, bf16[384,1024]{1,0:T(8,128)(2,1)S(1)}, u32[]{:S(2)}, u32[]{:S(2)}) collective-permute-start(bf16[384,1024]{1,0:T(8,128)(2,1)S(1)} %get-tuple-element.113), channel_id=1, source_target_pairs={{0,1},{1,0},{2,3},{3,2},{4,5},{5,4},{6,7},{7,6},{8,9},{9,8},{10,11... | collective-permute-start | bytes 2359304 | tf_op jit(solution)/shard_map/ppermute | solution.py:37
  164.2 17.3 %collective-permute-start.17 = (bf16[384,1024]{1,0:T(8,128)(2,1)S(1)}, bf16[384,1024]{1,0:T(8,128)(2,1)S(1)}, u32[]{:S(2)}, u32[]{:S(2)}) collective-permute-start(bf16[384,1024]{1,0:T(8,128)(2,1)S(1)} %get-tuple-element.114), channel_id=1, source_target_pairs={{0,2},{1,3},{2,0},{3,1},{4,6},{5,7},{6,4},{7,5},{8,10},{9,11},{10,... | collective-permute-start | bytes 2359304 | tf_op jit(solution)/shard_map/ppermute | solution.py:37
  164.4 33.9 %collective-permute-start.19 = (bf16[384,1024]{1,0:T(8,128)(2,1)S(1)}, bf16[384,1024]{1,0:T(8,128)(2,1)S(1)}, u32[]{:S(2)}, u32[]{:S(2)}) collective-permute-start(bf16[384,1024]{1,0:T(8,128)(2,1)S(1)} %fusion.2), channel_id=1, source_target_pairs={{0,3},{1,2},{2,1},{3,0},{4,7},{5,6},{6,5},{7,4},{8,11},{9,10},{10,... | collective-permute-start | bytes 2359304 | tf_op jit(solution)/shard_map/ppermute | solution.py:37
  175.7 29.4 %copy-start = (bf16[1,384,2048]{2,1,0:T(8,128)(2,1)S(1)}, bf16[1,384,2048]{2,1,0:T(8,128)(2,1)}, u32[]{:S(2)}) copy-start(bf16[1,384,2048]{2,1,0:T(8,128)(2,1)} %refs_4_.1) | copy-start | bytes 4718596
  175.7 29.4 %copy-start.1 = (f32[1,1,384,2048]{3,2,1,0:T(8,128)S(1)}, f32[1,1,384,2048]{3,2,1,0:T(8,128)}, u32[]{:S(2)}) copy-start(f32[1,1,384,2048]{3,2,1,0:T(8,128)} %refs_2_.1) | copy-start | bytes 9437188
  175.7 22.6 %collective-permute-start.22 = (bf16[128,2176]{1,0:T(8,128)(2,1)S(1)}, bf16[128,2176]{1,0:T(8,128)(2,1)S(1)}, u32[]{:S(2)}, u32[]{:S(2)}) collective-permute-start(bf16[128,2176]{1,0:T(8,128)(2,1)S(1)} %fusion.7), channel_id=1, source_target_pairs={{0,4},{1,5},{2,6},{3,7},{4,12},{5,13},{6,14},{7,15},{12,8},{13,9},... | collective-permute-start | bytes 1671176 | tf_op jit(solution)/shard_map/ppermute | solution.py:54
  198.3 5.5 %copy-start.15 = (bf16[128,2176]{1,0:T(8,128)(2,1)}, bf16[128,2176]{1,0:T(8,128)(2,1)S(1)}, u32[]{:S(2)}) copy-start(bf16[128,2176]{1,0:T(8,128)(2,1)S(1)} %collective-permute-done.22) | copy-start | bytes 1671172
  200.4 4.6 %collective-permute-start.23 = (bf16[384,1024]{1,0:T(8,128)(2,1)S(1)}, bf16[384,1024]{1,0:T(8,128)(2,1)S(1)}, u32[]{:S(2)}, u32[]{:S(2)}) collective-permute-start(bf16[384,1024]{1,0:T(8,128)(2,1)S(1)} %fusion.1.refs_0_), channel_id=1, source_target_pairs={{16,0},{0,16},{17,1},{1,17},{18,2},{2,18},{19,3},{3,19},{20,4},{4,... | collective-permute-start | bytes 2359304 | tf_op jit(solution)/shard_map/ppermute | solution.py:59
  203.8 7.1 %copy-start.20 = (s32[1,2]{1,0:T(1,128)S(1)}, s32[1,2]{1,0:T(1,128)}, u32[]{:S(2)}) copy-start(s32[1,2]{1,0:T(1,128)} %param.18) | copy-start | bytes 28
  210.5 4.3 %collective-permute-start.24 = (bf16[384,2048]{1,0:T(8,128)(2,1)S(1)}, bf16[384,2048]{1,0:T(8,128)(2,1)}, u32[]{:S(2)}, u32[]{:S(2)}) collective-permute-start(bf16[384,2048]{1,0:T(8,128)(2,1)S(1)} %get-tuple-element.122), channel_id=1, source_target_pairs={{16,0},{0,16},{17,1},{1,17},{18,2},{2,18},{19,3},{3,19},{20,4},{4,... | collective-permute-start | bytes 4718600 | tf_op jit(solution)/shard_map/ppermute | solution.py:59

commit v2 on v1

--- a/solution.py
+++ b/solution.py
@@ -72,10 +72,9 @@
 
 
 class Pass:
-    def __init__(self, tok, model, half, n_ex, n_dp, slots, blocks, last):
-        self.tok, self.model, self.half, self.n_ex, self.n_dp = tok, model, half, n_ex, n_dp
-        self.slots, self.blocks, self.last = slots, blocks, last
-        self.layers = n_ex // plane
+    def __init__(self, tok, model, half, n_dp, slots, blocks, spans, back=False):
+        self.tok, self.model, self.half, self.n_dp = tok, model, half, n_dp
+        self.slots, self.blocks, self.spans, self.back = slots, blocks, spans, back
         self.rows = tok * len(blocks)
         self.width = model // n_dp
 
@@ -86,8 +85,8 @@
         n_out = len(self.outs)
         outs = dict(zip(self.outs, refs[n_in : n_in + n_out]))
         scratch = list(refs[n_in + n_out :])
-        xs, ys, ps, ws, gu, back, pre, sc, dx, pr, keep, send = scratch[:12]
-        sem_t, sem_w, sem_i, sem_o = scratch[12:16]
+        xs, ys, ps, ws, gu, hs, pre, sc, dx, pr, keep, send = scratch[:12]
+        sem_t, sem_w, sem_i, sem_k, sem_o = scratch[12:17]
         me_dp = lax.axis_index("dp")
         me = lax.axis_index("expert")
         here, layer = lax.rem(me, plane), lax.div(me, plane)
@@ -102,10 +101,6 @@
                     ref.at[pl.ds(0, tok), pl.ds(model, lanes)], ps.at[at], sem_t.at[b, 2]
                 ),
             )
-
-        for b in range(len(blocks)):
-            for copy in row_copies(b):
-                copy.start()
 
         def weight_copies(i):
             s = slots[i]
@@ -125,20 +120,33 @@
                     )
             return out
 
+        for b in range(len(blocks)):
+            for copy in row_copies(b):
+                copy.start()
         for copy in weight_copies(0):
             copy.start()
         extra = []
-        held = {"dx": 0, "pr": 0, "keep": 0, "send": 0}
-        for name, ref in ins.items():
-            kind = name[0][:-1] if isinstance(name, tuple) and name[0][:-1] in held else None
-            if kind is None:
+        for b, place in enumerate(self.sums):
+            at = pl.ds(b * tok, tok)
+            if place is None:
+                dx[at, :] = jnp.zeros((tok, model), f32)
+                pr[at, :] = jnp.zeros((tok, lanes), f32)
                 continue
-            n = ref.shape[0]
-            to = {"dx": dx, "pr": pr, "keep": keep, "send": send}[kind].at[pl.ds(held[kind], n)]
-            extra.append(pltpu.make_async_copy(ref, to, sem_i.at[len(extra)]))
-            held[kind] += n
-        if not held["pr"]:
-            pr[...] = jnp.zeros_like(pr)
+            j, row = place
+            came = pl.ds(row * tok, tok)
+            extra.append(
+                pltpu.make_async_copy(ins["dx%d" % j].at[came], dx.at[at], sem_i.at[b, 0])
+            )
+            extra.append(
+                pltpu.make_async_copy(ins["pr%d" % j].at[came], pr.at[at], sem_i.at[b, 1])
+            )
+        filled = 0
+        for j in range(self.n_grads):
+            n = ins["keep%d" % j].shape[0]
+            at = pl.ds(filled, n)
+            extra.append(pltpu.make_async_copy(ins["keep%d" % j], keep.at[at], sem_k.at[j, 0]))
+            extra.append(pltpu.make_async_copy(ins["send%d" % j], send.at[at], sem_k.at[j, 1]))
+            filled += n
         for copy in extra:
             copy.start()
 
@@ -156,20 +164,22 @@
                 for copy in weight_copies(i + 1):
                     copy.start()
             w = ws.at[i % 2]
+            low, high = (tok * b for b in self.spans[i])
+            mine = slice(low, high)
             for n in range(0, 2 * half, tile):
-                gu[:, n : n + tile] = jnp.dot(
-                    xs[...], w[:, n : n + tile], preferred_element_type=f32
+                gu[mine, n : n + tile] = jnp.dot(
+                    xs[mine, :], w[:, n : n + tile], preferred_element_type=f32
                 )
-            back[...] = jnp.dot(ys[...], w[:, 2 * half :], preferred_element_type=f32)
+            hs[mine, :] = jnp.dot(ys[mine, :], w[:, 2 * half :], preferred_element_type=f32)
             if i == 0:
                 for copy in extra:
                     copy.wait()
             expert = layer * plane + lax.bitwise_xor(here, jnp.int32(s))
 
-            @pl.loop(0, rows // chunk)
+            @pl.loop(low // chunk, high // chunk)
             def _(r):
                 at = pl.ds(pl.multiple_of(r * chunk, chunk), chunk)
-                gate, upper, h = gu[at, :half], gu[at, half:], back[at, :]
+                gate, upper, h = gu[at, :half], gu[at, half:], hs[at, :]
                 hit = lane == expert
                 p = jnp.sum(jnp.where(hit, ps[at, :].astype(f32), 0.0), axis=1, keepdims=True)
                 sigma = jax.nn.sigmoid(gate)
@@ -182,20 +192,19 @@
                 pre[at, half:] = (grad * silu).astype(bf16)
                 sc[at, :] = (p * hidden).astype(bf16)
 
-            add_dx = held["dx"] or i > 0
             for d in range(0, model, 2 * tile):
                 at = slice(d, d + 2 * tile)
-                part = nt(pre[...], w[at, : 2 * half])
-                dx[:, at] = dx[:, at] + part if add_dx else part
+                dx[mine, at] = dx[mine, at] + nt(pre[mine, :], w[at, : 2 * half])
             for d in range(0, width, 2 * tile):
                 at = slice(d, d + 2 * tile)
                 col = pl.ds(pl.multiple_of(me_dp * width + d, tile), 2 * tile)
-                part = tn(sc[...], ys[:, col])
-                keep[i, :, at] = keep[i, :, at] + part if held["keep"] else part
+                part = tn(sc[mine, :], ys[mine, col])
+                keep[i, :, at] = keep[i, :, at] + part if filled else part
                 for k in range(1, n_dp):
                     col = lax.rem(me_dp + n_dp - k, n_dp) * width + d
-                    part = tn(sc[...], ys[:, pl.ds(pl.multiple_of(col, tile), 2 * tile)])
-                    if held["send"]:
+                    col = pl.ds(pl.multiple_of(col, tile), 2 * tile)
+                    part = tn(sc[mine, :], ys[mine, col])
+                    if filled:
                         part = send[i, k - 1, :, at].astype(f32) + part
                     send[i, k - 1, :, at] = part.astype(bf16)
 
@@ -208,30 +217,41 @@
             pending[-2].start()
             pending[-1].start()
         n = 2 * len(slots)
-        if not self.last:
+        if not self.back:
             pending.append(pltpu.make_async_copy(dx, outs["dx"], sem_o.at[n]))
             pending.append(pltpu.make_async_copy(pr, outs["pr"], sem_o.at[n + 1]))
             pending[-2].start()
             pending[-1].start()
         else:
-            rows_out = scratch[16]
-            for b, k in enumerate(blocks):
+            rows_out = scratch[17]
+            for b in range(len(blocks)):
                 at = pl.ds(b * tok, tok)
                 rows_out[b, :, pl.ds(0, model)] = dx[at, :].astype(bf16)
                 rows_out[b, :, pl.ds(model, lanes)] = pr[at, :].astype(bf16)
-                copy = pltpu.make_async_copy(rows_out.at[b], outs["back"].at[k], sem_o.at[n + b])
+                copy = pltpu.make_async_copy(rows_out.at[b], outs["back"].at[b], sem_o.at[n + b])
                 copy.start()
                 pending.append(copy)
         for copy in pending:
             copy.wait()
 
-    def call(self, ins):
+    def call(self, ins, sums=(), grads=()):
         tok, model, half, rows, width = self.tok, self.model, self.half, self.rows, self.width
         n_dp, n = self.n_dp, len(self.slots)
+        ins = dict(ins)
+        self.sums = [None] * len(self.blocks)
+        for j, (earlier, out) in enumerate(sums):
+            for b, block in enumerate(self.blocks):
+                if block in earlier.blocks:
+                    self.sums[b] = (j, earlier.blocks.index(block))
+            ins["dx%d" % j], ins["pr%d" % j] = out["dx"], out["pr"]
+        self.n_grads = len(grads)
+        for j, out in enumerate(grads):
+            ins["keep%d" % j], ins["send%d" % j] = out["keep"], out["send"]
         shape = {"keep": ((n, half, width), f32)}
         shape["send"] = ((n, max(n_dp - 1, 1), half, width), bf16)
-        if self.last:
-            shape["back"] = ((self.layers, tok, model + lanes), bf16)
+        out_rows = (len(self.blocks), tok, model + lanes)
+        if self.back:
+            shape["back"] = (out_rows, bf16)
         else:
             shape["dx"] = ((rows, model), f32)
             shape["pr"] = ((rows, lanes), f32)
@@ -251,11 +271,12 @@
             pltpu.VMEM((n, max(n_dp - 1, 1), half, width), bf16),
             pltpu.SemaphoreType.DMA((len(self.blocks), 3)),
             pltpu.SemaphoreType.DMA((n, 2 * n_dp)),
-            pltpu.SemaphoreType.DMA((8,)),
+            pltpu.SemaphoreType.DMA((len(self.blocks), 2)),
+            pltpu.SemaphoreType.DMA((max(self.n_grads, 1), 2)),
             pltpu.SemaphoreType.DMA((2 * n + len(self.blocks) + 2,)),
         ]
-        if self.last:
-            scratch.append(pltpu.VMEM((self.layers, tok, model + lanes), bf16))
+        if self.back:
+            scratch.append(pltpu.VMEM(out_rows, bf16))
         out = pl.pallas_call(
             functools.partial(self.kernel, len(ins)),
             out_shape=[jax.ShapeDtypeStruct(*v) for v in shape.values()],
@@ -340,71 +361,71 @@
     held = [own, along(own)]
     x_p1, y_p2 = hop(p1, 1), hop(p2, 2)
 
-    p1, p2, held, x_p1, y_p2 = lax.optimization_barrier((p1, p2, held, x_p1, y_p2))
+    weights = {"w0": w_own}
+    make = functools.partial(Pass, tok_dev, model, half, n_dp)
+    last_block = layers - 1
+    near = list(range(last_block))
+
+    def pick(p):
+        got = {"t%d" % k: held[k] for k in p.blocks}
+        return got | {k: v for k, v in weights.items() if int(k[1]) in p.slots}
+
+    def name_parts(s, firsts, seconds):
+        for k in range(n_dp):
+            weights["w%d_%d_0" % (s, k)] = firsts[k]
+            weights["w%d_%d_1" % (s, k)] = seconds[k]
+
+    p1, p2, held, x_p1, y_p2, w_own = lax.optimization_barrier((p1, p2, held, x_p1, y_p2, w_own))
+    weights["w0"] = w_own
     x_p2, y_p1 = hop(p2, 1), hop(p1, 2)
+    zero_pass = make([0], near[:2], [(0, 2)])
+    zero = zero_pass.call(pick(zero_pass))
     while len(held) < layers - 1:
         held.append(along(held[-1]))
     x_o1, y_o2 = others(x_p1), others(y_p2)
 
-    (x_p1, y_p2, x_p2, y_p1, x_o1, y_o2, held) = lax.optimization_barrier(
-        (x_p1, y_p2, x_p2, y_p1, x_o1, y_o2, held)
+    (x_p1, y_p2, x_p2, y_p1, x_o1, y_o2, held, zero) = lax.optimization_barrier(
+        (x_p1, y_p2, x_p2, y_p1, x_o1, y_o2, held, zero)
     )
     d_p2, d_p1 = hop(y_p2, 1), hop(x_p1, 2)
     final = along(held[-1])
     x_o2, y_o1 = others(x_p2), others(y_p1)
-    weights = {"w0": w_own}
-
-    def name_parts(s, firsts, seconds):
-        for k in range(n_dp):
-            weights["w%d_%d_0" % (s, k)] = firsts[k]
-            weights["w%d_%d_1" % (s, k)] = seconds[k]
-
     name_parts(1, [x_p1] + x_o1, [x_p2] + x_o2)
     name_parts(2, [y_p1] + y_o1, [y_p2] + y_o2)
-
-    def pick(slots, blocks):
-        got = {"t%d" % k: held[k] for k in blocks}
-        for name, value in weights.items():
-            if int(name[1]) in slots:
-                got[name] = value
-        return got
-
-    near, far = list(range(layers - 1)), [layers - 1]
-    make = functools.partial(Pass, tok_dev, model, half, n_ex, n_dp)
-
-    def carry(*passes):
-        return {(k + str(i), i): p[k] for i, (p, keys) in enumerate(passes) for k in keys}
-
-    zero = make([0], near, False).call(pick([0], near))
-    one = make([1, 2], near, False).call(pick([1, 2], near) | carry((zero, ("dx", "pr"))))
+    one_pass = make([1, 2], near, [(0, last_block)] * 2)
+    one = one_pass.call(pick(one_pass), sums=[(zero_pass, zero)])
 
     zero, one, d_p1, d_p2, held, final = lax.optimization_barrier(
         (zero, one, d_p1, d_p2, held, final)
     )
     held.append(final)
-    d_o1 = others(d_p1)
-    d_o2 = others(d_p2)
+    d_o1, d_o2 = others(d_p1), others(d_p2)
     name_parts(3, [d_p1] + d_o1, [d_p2] + d_o2)
-    grads = ("keep", "send")
-    two = make([0, 1, 2], far, False).call(pick([0, 1, 2], far) | carry((zero, grads), (one, grads)))
-    last = make([3], near + far, True).call(
-        pick([3], near + far) | carry((one, ("dx", "pr")), (two, ("dx", "pr")))
-    )
-
-    swapped = [turn(two["send"][:, k - 1], k) for k in range(1, n_dp)]
-    last, swapped, keep = lax.optimization_barrier((last, swapped, two["keep"]))
+    rest = list(range(2, layers))
+    two_pass = make([0, 1, 2], rest, [(0, len(rest))] + [(len(rest) - 1, len(rest))] * 2)
+    two = two_pass.call(pick(two_pass), sums=[(one_pass, one)], grads=[zero, one])
+    two_send = after(two["send"], d_o1, d_o2)
+    swapped = [turn(two_send[:, k - 1], k) for k in range(1, n_dp)]
+    keep = two["keep"]
+    sums = [(one_pass, one), (two_pass, two)]
+    first_pass = make([3], [1], [(0, 1)], True)
+    first = first_pass.call(pick(first_pass), sums=sums)
+    first, swapped, keep = lax.optimization_barrier((first, swapped, keep))
+    passing = along(first["back"][0])
     leaving = [(keep[s] + sum(v[s].astype(f32) for v in swapped)).astype(bf16) for s in (1, 2)]
-    leaving, last = lax.optimization_barrier((leaving, last))
     sent = [hop(leaving[0], 1), hop(leaving[1], 2)]
+    others_pass = make([3], [0] + rest, [(0, len(rest) + 1)], True)
+    last = others_pass.call(pick(others_pass), sums=sums, grads=[first])
+    last, passing, sent = lax.optimization_barrier((last, passing, sent))
+
+    back = last["back"]
     swapped_across = [turn(last["send"][0, k - 1], k) for k in range(1, n_dp)]
     across = last["keep"][0] + sum(v.astype(f32) for v in swapped_across)
     across = across.astype(bf16)
     sent.append(hop(across, 3))
-    back = last["back"]
-    passing = along(back[1])
     for k in range(2, layers):
-        passing = (passing.astype(f32) + back[k].astype(f32)).astype(bf16)
-        passing = along(after(passing, across) if k == 2 else passing)
+        passing = (passing.astype(f32) + back[k - 1].astype(f32)).astype(bf16)
+        passing = along(after(passing, across) if k == 3 else passing)
 
     sent, passing = lax.optimization_barrier((sent, passing))
     grad = keep[0] + sum(v[0].astype(f32) for v in swapped)

time: 219 us -> 197 us (0.90)
  waiting for transfers between devices: 100 us -> 77.8 us
  other arithmetic: 16.5 us -> 21.4 us
  starting transfers between devices: 27.9 us -> 23.2 us
  Pallas kernels: 64 us -> 67.9 us
    ppermute x9, waiting for transfers between devices: 21.3 us -> 3.84 us  [hop(): return lax.ppermute(value, 'expert', [(i, i ^ flip) for i in range(n)])]
    ppermute x10, waiting for transfers between devices: 8.49 us -> 1.78 us  [turn(): return lax.ppermute(value, 'dp', [((r + step) % n, r) for r in range(n)])]
    ppermute x6, starting transfers between devices: 9.17 us -> 4.05 us  [along(): return lax.ppermute(value, 'expert', pairs)]
    pallas_call x4 -> x5, Pallas kernels: 58.6 us -> 62.4 us  [call(): pl.pallas_call(functools.partial(self.kernel, len(ins)), out_shape=[jax.S...]
    convert_element_type x2, other arithmetic: 0.26 us -> 2.53 us  [body(): passing = (passing.astype(f32) + back[k - 1].astype(f32)).astype(bf16)]
  transfers between devices with their start and end apart: 25 -> 25, of which waited for: 9 -> 11; matrix products, arithmetic and copies ran while one was open for 5% -> 7% of each run, Pallas kernels for 20% -> 32%
where the time goes in v2:
time: 197 us
  waiting for transfers between devices  77.8 us (39%)
  Pallas kernels  67.9 us (34%)
  starting transfers between devices  23.2 us (12%)
  other arithmetic  21.4 us (11%)
  local copies, waits for them, and re-layouts  5.14 us (3%)
    ppermute x6, waiting for transfers between devices, along(): return lax.ppermute(value, 'expert', pairs)  72.2 us
    pallas_call x5, Pallas kernels, call(): pl.pallas_call(functools.partial(self.kernel, len(ins)), out_shape=[jax.S...  62.4 us
    ppermute x10, starting transfers between devices, turn(): return lax.ppermute(value, 'dp', [((r + step) % n, r) for r in range(n)])  10.9 us
    ppermute x9, starting transfers between devices, hop(): return lax.ppermute(value, 'expert', [(i, i ^ flip) for i in range(n)])  8.31 us
    concatenate x2, other arithmetic, body(): w_own = jnp.concatenate([w_gu, w_dn.T], 1)  7.35 us
    pallas_call x1, Pallas kernels, adam_call(): pl.pallas_call(functools.partial(adam_kernel, n_dp), grid=(half // step,)...  5.48 us
    ppermute x6, starting transfers between devices, along(): return lax.ppermute(value, 'expert', pairs)  4.05 us
  transfers between devices with their start and end apart: 25, of which 11 were waited for; matrix products, arithmetic and copies ran while one was open for 7% of the time, Pallas kernels for 32%

profile of v2, /device:TPU:1, one launch (start us, length us, event | category | flops | bytes accessed | tf_op | source)
XLA Modules:
  0.0 197.0 jit_solution(7849746542262006707)
XLA Ops:
  0.6 1.9 copy.18
  2.5 3.0 %fusion.5 = (bf16[512,1152]{1,0:T(8,128)(2,1)}, bf16[512,1152]{1,0:T(8,128)(2,1)}) fusion(s32[]{:T(128)S(6)} %select_n.39, bf16[2048,768]{1,0:T(8,128)(2,1)} %bitcast.37, bf16[2048,384]{1,0:T(8,128)(2,1)S(1)} %copy.18, s32[]{:T(128)S(6)} %select_n.38), kind=kLoop, calls=%fused_computation.16 | loop fusion | flops 4718592 | bytes 7077896 | tf_op jit(solution)/shard_map/concatenate | solution.py:358
  5.5 2.0 %collective-permute-start.1 = (bf16[512,1152]{1,0:T(8,128)(2,1)}, bf16[512,1152]{1,0:T(8,128)(2,1)S(1)}, u32[]{:S(2)}, u32[]{:S(2)}) collective-permute-start(bf16[512,1152]{1,0:T(8,128)(2,1)} %get-tuple-element.78), channel_id=1, source_target_pairs={{0,1},{1,0},{2,3},{3,2},{4,5},{5,4},{6,7},{7,6},{8,9},{9,8},{10,11... | collective-permute-start | bytes 3538952 | tf_op jit(solution)/shard_map/ppermute | solution.py:37
  7.5 1.2 collective-permute-start.2
  9.4 1.3 fusion.6.refs_0_
  10.7 1.3 collective-permute-start
  12.0 4.4 %pad_maximum_fusion.refs_2_ = bf16[2048,1152]{1,0:T(8,128)(2,1)} fusion(bf16[2048,384]{1,0:T(8,128)(2,1)S(1)} %copy.18, bf16[2048,768]{1,0:T(8,128)(2,1)} %bitcast.38), kind=kLoop, calls=%fused_computation.2 | loop fusion | flops 9437184 | bytes 9437184 | tf_op jit(solution)/shard_map/concatenate | solution.py:358
  16.4 20.0 %collective-permute-done.refs_1_.refs_0_ = bf16[256,2176]{1,0:T(8,128)(2,1)S(1)} collective-permute-done((bf16[256,2176]{1,0:T(8,128)(2,1)S(1)}, bf16[256,2176]{1,0:T(8,128)(2,1)S(1)}, u32[]{:S(2)}, u32[]{:S(2)}) %collective-permute-start) | collective-permute-done | bytes 1114144 | tf_op jit(solution)/shard_map/ppermute | solution.py:54
  36.8 0.5 collective-permute-start.4
  37.2 2.4 %collective-permute-start.5 = (bf16[512,1152]{1,0:T(8,128)(2,1)S(1)}, bf16[512,1152]{1,0:T(8,128)(2,1)S(1)}, u32[]{:S(2)}, u32[]{:S(2)}) collective-permute-start(bf16[512,1152]{1,0:T(8,128)(2,1)S(1)} %collective-permute-done.1.refs_3_), channel_id=1, source_target_pairs={{16,0},{0,16},{17,1},{1,17},{18,2},{2,18},{19,3},{3,19},{20,4},{4,... | collective-permute-start | bytes 3538952 | tf_op jit(solution)/shard_map/ppermute | solution.py:59
  39.7 0.6 collective-permute-start.7
  40.2 8.5 %shard_map.137 = (f32[1,384,1024]{2,1,0:T(8,128)}, bf16[1,1,384,1024]{3,2,1,0:T(8,128)(2,1)}, f32[256,2048]{1,0:T(8,128)}, f32[256,128]{1,0:T(8,128)}) custom-call(bf16[256,2176]{1,0:T(8,128)(2,1)} %copy-done.3, bf16[256,2176]{1,0:T(8,128)(2,1)} %copy-done.4, bf16[2048,1152]{1,0:T(8,128)(2,1)} %pad_maximum_fusion.refs_2_), custom_call_target="tpu_custom_call" | custom-call | flops 1000 | bytes 1000 | tf_op jit(solution)/shard_map/pallas_call | solution.py:280
  48.8 17.4 %collective-permute-done.7.refs_2_.refs_0_.refs_1_ = bf16[256,2176]{1,0:T(8,128)(2,1)S(1)} collective-permute-done((bf16[256,2176]{1,0:T(8,128)(2,1)S(1)}, bf16[256,2176]{1,0:T(8,128)(2,1)S(1)}, u32[]{:S(2)}, u32[]{:S(2)}) %collective-permute-start.7) | collective-permute-done | bytes 1114144 | tf_op jit(solution)/shard_map/ppermute | solution.py:54
  66.3 1.4 collective-permute-start.8
  67.8 1.3 collective-permute-start.10
  69.0 1.2 collective-permute-start.11
  70.3 0.5 collective-permute-start.12
  71.0 1.0 copy-done.10
  72.1 17.9 %shard_map.138 = (f32[2,384,1024]{2,1,0:T(8,128)}, bf16[2,1,384,1024]{3,2,1,0:T(8,128)(2,1)}, f32[384,2048]{1,0:T(8,128)}, f32[384,128]{1,0:T(8,128)}) custom-call(bf16[256,2176]{1,0:T(8,128)(2,1)} %copy-done.3, bf16[256,2176]{1,0:T(8,128)(2,1)} %copy-done.4, bf16[256,2176]{1,0:T(8,128)(2,1)} %copy-done.5, bf16[512,1152]{1,0:T(8,128)(2,1)} %copy-done.6, ...), custom_call_target="tpu_custom_call" | custom-call | flops 1000 | bytes 1000 | tf_op jit(solution)/shard_map/pallas_call | solution.py:280
  90.0 6.3 %collective-permute-done.12.refs_1_.refs_2_ = bf16[256,2176]{1,0:T(8,128)(2,1)S(1)} collective-permute-done((bf16[256,2176]{1,0:T(8,128)(2,1)S(1)}, bf16[256,2176]{1,0:T(8,128)(2,1)S(1)}, u32[]{:S(2)}, u32[]{:S(2)}) %collective-permute-start.12) | collective-permute-done | bytes 1114144 | tf_op jit(solution)/shard_map/ppermute | solution.py:54
  96.2 2.0 %collective-permute-start.13 = (bf16[512,1152]{1,0:T(8,128)(2,1)}, bf16[512,1152]{1,0:T(8,128)(2,1)S(1)}, u32[]{:S(2)}, u32[]{:S(2)}) collective-permute-start(bf16[512,1152]{1,0:T(8,128)(2,1)} %collective-permute-done.10.refs_1_.refs_3_), channel_id=1, source_target_pairs={{16,0},{0,16},{17,1},{1,17},{18,2},{2,18},{19,3},{3,19},{20,4},{4,... | collective-permute-start | bytes 3538952 | tf_op jit(solution)/shard_map/ppermute | solution.py:59
  98.3 16.0 %shard_map.139 = (f32[3,384,1024]{2,1,0:T(8,128)}, bf16[3,1,384,1024]{3,2,1,0:T(8,128)(2,1)}, f32[256,2048]{1,0:T(8,128)}, f32[256,128]{1,0:T(8,128)}) custom-call(bf16[256,2176]{1,0:T(8,128)(2,1)} %copy-done.5, bf16[256,2176]{1,0:T(8,128)(2,1)} %copy-done.13, bf16[2048,1152]{1,0:T(8,128)(2,1)} %pad_maximum_fusion.refs_2_, bf16[512,1152]{1,0:T(8,128)(2,1)} %copy-done.6, ...), custom_call_target="tpu_custom_call" | custom-call | flops 1000 | bytes 1000 | tf_op jit(solution)/shard_map/pallas_call | solution.py:280
  114.3 0.9 collective-permute-start.15
  115.7 7.3 %shard_map.140 = (f32[1,384,1024]{2,1,0:T(8,128)}, bf16[1,1,384,1024]{3,2,1,0:T(8,128)(2,1)}, bf16[1,128,2176]{2,1,0:T(8,128)(2,1)}) custom-call(bf16[256,2176]{1,0:T(8,128)(2,1)} %copy-done.4, bf16[512,1152]{1,0:T(8,128)(2,1)} %collective-permute-done.10.refs_1_.refs_3_, bf16[512,1152]{1,0:T(8,128)(2,1)} %collective-permute-done.11.refs_2_.refs_4_, ...), custom_call_target="tpu_custom_call" | custom-call | flops 1000 | bytes 1000 | tf_op jit(solution)/shard_map/pallas_call | solution.py:280
  123.0 1.9 fusion.10
  125.0 1.1 collective-permute-start.17
  126.3 0.5 collective-permute-start.16
  126.8 12.7 %shard_map.141 = (f32[1,384,1024]{2,1,0:T(8,128)}, bf16[1,1,384,1024]{3,2,1,0:T(8,128)(2,1)}, bf16[3,128,2176]{2,1,0:T(8,128)(2,1)}) custom-call(bf16[256,2176]{1,0:T(8,128)(2,1)} %copy-done.3, bf16[256,2176]{1,0:T(8,128)(2,1)} %copy-done.5, bf16[256,2176]{1,0:T(8,128)(2,1)} %copy-done.13, bf16[512,1152]{1,0:T(8,128)(2,1)} %collective-permute-done.10.refs_1_.refs_3_, ...), custom_call_target="tpu_custom_call" | custom-call | flops 1000 | bytes 1000 | tf_op jit(solution)/shard_map/pallas_call | solution.py:280
  139.5 0.8 collective-permute-done.16
  140.4 2.3 %collective-permute-done.17 = bf16[384,1024]{1,0:T(8,128)(2,1)S(1)} collective-permute-done((bf16[384,1024]{1,0:T(8,128)(2,1)S(1)}, bf16[384,1024]{1,0:T(8,128)(2,1)S(1)}, u32[]{:S(2)}, u32[]{:S(2)}) %collective-permute-start.17) | collective-permute-done | bytes 786464 | tf_op jit(solution)/shard_map/ppermute | solution.py:37
  142.7 1.5 collective-permute-done.18
  144.2 1.8 collective-permute-start.19
  146.0 1.4 fusion.8
  147.4 0.5 collective-permute-start.21
  148.4 0.4 collective-permute-start.20
  148.8 13.8 %collective-permute-done.21 = bf16[128,2176]{1,0:T(8,128)(2,1)S(1)} collective-permute-done((bf16[128,2176]{1,0:T(8,128)(2,1)S(1)}, bf16[128,2176]{1,0:T(8,128)(2,1)S(1)}, u32[]{:S(2)}, u32[]{:S(2)}) %collective-permute-start.21) | collective-permute-done | bytes 557088 | tf_op jit(solution)/shard_map/ppermute | solution.py:54
  162.6 1.2 fusion.7
  163.8 0.6 collective-permute-start.22
  164.4 13.9 %collective-permute-done.22 = bf16[128,2176]{1,0:T(8,128)(2,1)} collective-permute-done((bf16[128,2176]{1,0:T(8,128)(2,1)S(1)}, bf16[128,2176]{1,0:T(8,128)(2,1)}, u32[]{:S(2)}, u32[]{:S(2)}) %collective-permute-start.22) | collective-permute-done | bytes 557088 | tf_op jit(solution)/shard_map/ppermute | solution.py:54
  178.2 1.8 fusion.1.refs_0_
  180.1 1.7 collective-permute-start.23
  182.5 1.2 collective-permute-done.23.refs_1_
  183.7 5.5 %shard_map.142 = (f32[1,1,384,2048]{3,2,1,0:T(8,128)}, f32[1,1,384,2048]{3,2,1,0:T(8,128)}, bf16[384,2048]{1,0:T(8,128)(2,1)S(1)}) custom-call(s32[1]{0:T(128)} %copy.22.lead_ref, bf16[384,1024]{1,0:T(8,128)(2,1)S(1)} %fusion.1.refs_0_, bf16[384,1024]{1,0:T(8,128)(2,1)S(1)} %collective-permute-done.23.refs_1_, f32[1,1,384,2048]{3,2,1,0:T(8,128)S(1)} %copy-done.1, ...), custom_call_target="tpu_custom_call" | custom-call | flops 1000 | bytes 1000 | tf_op jit(solution)/shard_map/pallas_call | solution.py:314
  189.6 0.7 fusion.11
  190.3 1.3 convert_add_fusion.2
  191.6 0.9 slice.61
  192.9 0.7 copy.21
  193.5 3.4 %fusion.3 = bf16[1,1,384,2048]{3,2,1,0:T(8,128)(2,1)} fusion(bf16[1,384,2048]{2,1,0:T(8,128)(2,1)S(1)} %copy-done, bf16[384,2048]{1,0:T(8,128)(2,1)} %collective-permute-done.24, bf16[384,2048]{1,0:T(8,128)(2,1)S(1)} %get-tuple-element.142, pred[]{:T(512)S(6)} %eq.29, pred[]{:T(512)} %bitcast.12), kind=kLoop, calls=%fused_computation.12 | loop fusion | flops 1572864 | bytes 6291458 | tf_op jit(solution)/shard_map/broadcast_in_dim | solution.py:445
  (68 shorter events, 3.4 us)
Async XLA Ops:
  2.5 6.3 %copy-start.15 = (s32[128,8]{0,1:T(8,128)S(1)}, s32[128,8]{0,1:T(8,128)}, u32[]{:S(2)}) copy-start(s32[128,8]{0,1:T(8,128)} %param.12) | copy-start | bytes 12292
  2.5 6.4 %copy-start.16 = (bf16[128,8]{0,1:T(8,128)(2,1)S(1)}, bf16[128,8]{0,1:T(8,128)(2,1)}, u32[]{:S(2)}) copy-start(bf16[128,8]{0,1:T(8,128)(2,1)} %param.13) | copy-start | bytes 6148
  5.5 30.9 %collective-permute-start.1 = (bf16[512,1152]{1,0:T(8,128)(2,1)}, bf16[512,1152]{1,0:T(8,128)(2,1)S(1)}, u32[]{:S(2)}, u32[]{:S(2)}) collective-permute-start(bf16[512,1152]{1,0:T(8,128)(2,1)} %get-tuple-element.78), channel_id=1, source_target_pairs={{0,1},{1,0},{2,3},{3,2},{4,5},{5,4},{6,7},{7,6},{8,9},{9,8},{10,11... | collective-permute-start | bytes 3538952 | tf_op jit(solution)/shard_map/ppermute | solution.py:37
  7.5 28.9 %collective-permute-start.2 = (bf16[512,1152]{1,0:T(8,128)(2,1)}, bf16[512,1152]{1,0:T(8,128)(2,1)}, u32[]{:S(2)}, u32[]{:S(2)}) collective-permute-start(bf16[512,1152]{1,0:T(8,128)(2,1)} %get-tuple-element.77), channel_id=1, source_target_pairs={{0,2},{1,3},{2,0},{3,1},{4,6},{5,7},{6,4},{7,5},{8,10},{9,11},{10,... | collective-permute-start | bytes 3538952 | tf_op jit(solution)/shard_map/ppermute | solution.py:37
  10.7 5.8 %copy-start.3 = (bf16[256,2176]{1,0:T(8,128)(2,1)}, bf16[256,2176]{1,0:T(8,128)(2,1)S(1)}, u32[]{:S(2)}) copy-start(bf16[256,2176]{1,0:T(8,128)(2,1)S(1)} %fusion.6.refs_0_) | copy-start | bytes 3342340
  10.7 25.8 %collective-permute-start = (bf16[256,2176]{1,0:T(8,128)(2,1)S(1)}, bf16[256,2176]{1,0:T(8,128)(2,1)S(1)}, u32[]{:S(2)}, u32[]{:S(2)}) collective-permute-start(bf16[256,2176]{1,0:T(8,128)(2,1)S(1)} %fusion.6.refs_0_), channel_id=1, source_target_pairs={{0,4},{1,5},{2,6},{3,7},{4,12},{5,13},{6,14},{7,15},{12,8},{13,9},... | collective-permute-start | bytes 3342344 | tf_op jit(solution)/shard_map/ppermute | solution.py:54
  36.4 3.8 %copy-start.4 = (bf16[256,2176]{1,0:T(8,128)(2,1)}, bf16[256,2176]{1,0:T(8,128)(2,1)S(1)}, u32[]{:S(2)}) copy-start(bf16[256,2176]{1,0:T(8,128)(2,1)S(1)} %collective-permute-done.refs_1_.refs_0_) | copy-start | bytes 3342340
  36.4 31.3 %copy-start.6 = (bf16[512,1152]{1,0:T(8,128)(2,1)}, bf16[512,1152]{1,0:T(8,128)(2,1)S(1)}, u32[]{:S(2)}) copy-start(bf16[512,1152]{1,0:T(8,128)(2,1)S(1)} %collective-permute-done.1.refs_3_) | copy-start | bytes 3538948
  36.5 29.7 %collective-permute-start.3 = (bf16[512,1152]{1,0:T(8,128)(2,1)}, bf16[512,1152]{1,0:T(8,128)(2,1)S(1)}, u32[]{:S(2)}, u32[]{:S(2)}) collective-permute-start(bf16[512,1152]{1,0:T(8,128)(2,1)} %get-tuple-element.77), channel_id=1, source_target_pairs={{0,1},{1,0},{2,3},{3,2},{4,5},{5,4},{6,7},{7,6},{8,9},{9,8},{10,11... | collective-permute-start | bytes 3538952 | tf_op jit(solution)/shard_map/ppermute | solution.py:37
  36.8 29.4 %collective-permute-start.4 = (bf16[512,1152]{1,0:T(8,128)(2,1)}, bf16[512,1152]{1,0:T(8,128)(2,1)S(1)}, u32[]{:S(2)}, u32[]{:S(2)}) collective-permute-start(bf16[512,1152]{1,0:T(8,128)(2,1)} %get-tuple-element.78), channel_id=1, source_target_pairs={{0,2},{1,3},{2,0},{3,1},{4,6},{5,7},{6,4},{7,5},{8,10},{9,11},{10,... | collective-permute-start | bytes 3538952 | tf_op jit(solution)/shard_map/ppermute | solution.py:37
  37.2 29.0 %collective-permute-start.5 = (bf16[512,1152]{1,0:T(8,128)(2,1)S(1)}, bf16[512,1152]{1,0:T(8,128)(2,1)S(1)}, u32[]{:S(2)}, u32[]{:S(2)}) collective-permute-start(bf16[512,1152]{1,0:T(8,128)(2,1)S(1)} %collective-permute-done.1.refs_3_), channel_id=1, source_target_pairs={{16,0},{0,16},{17,1},{1,17},{18,2},{2,18},{19,3},{3,19},{20,4},{4,... | collective-permute-start | bytes 3538952 | tf_op jit(solution)/shard_map/ppermute | solution.py:59
  39.7 26.6 %collective-permute-start.6 = (bf16[512,1152]{1,0:T(8,128)(2,1)}, bf16[512,1152]{1,0:T(8,128)(2,1)}, u32[]{:S(2)}, u32[]{:S(2)}) collective-permute-start(bf16[512,1152]{1,0:T(8,128)(2,1)} %collective-permute-done.2.refs_8_), channel_id=1, source_target_pairs={{16,0},{0,16},{17,1},{1,17},{18,2},{2,18},{19,3},{3,19},{20,4},{4,... | collective-permute-start | bytes 3538952 | tf_op jit(solution)/shard_map/ppermute | solution.py:59
  39.7 26.5 %collective-permute-start.7 = (bf16[256,2176]{1,0:T(8,128)(2,1)S(1)}, bf16[256,2176]{1,0:T(8,128)(2,1)S(1)}, u32[]{:S(2)}, u32[]{:S(2)}) collective-permute-start(bf16[256,2176]{1,0:T(8,128)(2,1)S(1)} %collective-permute-done.refs_1_.refs_0_), channel_id=1, source_target_pairs={{0,4},{1,5},{2,6},{3,7},{4,12},{5,13},{6,14},{7,15},{12,8},{13,9},... | collective-permute-start | bytes 3342344 | tf_op jit(solution)/shard_map/ppermute | solution.py:54
  66.2 5.9 %copy-start.5 = (bf16[256,2176]{1,0:T(8,128)(2,1)}, bf16[256,2176]{1,0:T(8,128)(2,1)S(1)}, u32[]{:S(2)}) copy-start(bf16[256,2176]{1,0:T(8,128)(2,1)S(1)} %collective-permute-done.7.refs_2_.refs_0_.refs_1_) | copy-start | bytes 3342340
  66.2 5.9 %copy-start.7 = (bf16[512,1152]{1,0:T(8,128)(2,1)}, bf16[512,1152]{1,0:T(8,128)(2,1)S(1)}, u32[]{:S(2)}) copy-start(bf16[512,1152]{1,0:T(8,128)(2,1)S(1)} %collective-permute-done.3.refs_4_) | copy-start | bytes 3538948
  66.2 5.9 %copy-start.8 = (bf16[512,1152]{1,0:T(8,128)(2,1)}, bf16[512,1152]{1,0:T(8,128)(2,1)S(1)}, u32[]{:S(2)}) copy-start(bf16[512,1152]{1,0:T(8,128)(2,1)S(1)} %collective-permute-done.4.refs_7_) | copy-start | bytes 3538948
  66.2 5.8 %copy-start.9 = (bf16[512,1152]{1,0:T(8,128)(2,1)}, bf16[512,1152]{1,0:T(8,128)(2,1)S(1)}, u32[]{:S(2)}) copy-start(bf16[512,1152]{1,0:T(8,128)(2,1)S(1)} %collective-permute-done.5.refs_5_) | copy-start | bytes 3538948
  66.3 4.8 %collective-permute-start.8 = (bf16[512,1152]{1,0:T(8,128)(2,1)S(1)}, bf16[512,1152]{1,0:T(8,128)(2,1)S(1)}, u32[]{:S(2)}, u32[]{:S(2)}) collective-permute-start(bf16[512,1152]{1,0:T(8,128)(2,1)S(1)} %collective-permute-done.3.refs_4_), channel_id=1, source_target_pairs={{16,0},{0,16},{17,1},{1,17},{18,2},{2,18},{19,3},{3,19},{20,4},{4,... | collective-permute-start | bytes 3538952 | tf_op jit(solution)/shard_map/ppermute | solution.py:59
  67.7 4.4 %collective-permute-start.9 = (bf16[512,1152]{1,0:T(8,128)(2,1)S(1)}, bf16[512,1152]{1,0:T(8,128)(2,1)}, u32[]{:S(2)}, u32[]{:S(2)}) collective-permute-start(bf16[512,1152]{1,0:T(8,128)(2,1)S(1)} %collective-permute-done.4.refs_7_), channel_id=1, source_target_pairs={{16,0},{0,16},{17,1},{1,17},{18,2},{2,18},{19,3},{3,19},{20,4},{4,... | collective-permute-start | bytes 3538952 | tf_op jit(solution)/shard_map/ppermute | solution.py:59
  67.8 28.5 %collective-permute-start.10 = (bf16[512,1152]{1,0:T(8,128)(2,1)S(1)}, bf16[512,1152]{1,0:T(8,128)(2,1)}, u32[]{:S(2)}, u32[]{:S(2)}) collective-permute-start(bf16[512,1152]{1,0:T(8,128)(2,1)S(1)} %collective-permute-done.1.refs_3_), channel_id=1, source_target_pairs={{0,2},{1,3},{2,0},{3,1},{4,6},{5,7},{6,4},{7,5},{8,10},{9,11},{10,... | collective-permute-start | bytes 3538952 | tf_op jit(solution)/shard_map/ppermute | solution.py:37
  69.0 27.2 %collective-permute-start.11 = (bf16[512,1152]{1,0:T(8,128)(2,1)}, bf16[512,1152]{1,0:T(8,128)(2,1)}, u32[]{:S(2)}, u32[]{:S(2)}) collective-permute-start(bf16[512,1152]{1,0:T(8,128)(2,1)} %collective-permute-done.2.refs_8_), channel_id=1, source_target_pairs={{0,1},{1,0},{2,3},{3,2},{4,5},{5,4},{6,7},{7,6},{8,9},{9,8},{10,11... | collective-permute-start | bytes 3538952 | tf_op jit(solution)/shard_map/ppermute | solution.py:37
  70.3 26.0 %collective-permute-start.12 = (bf16[256,2176]{1,0:T(8,128)(2,1)S(1)}, bf16[256,2176]{1,0:T(8,128)(2,1)S(1)}, u32[]{:S(2)}, u32[]{:S(2)}) collective-permute-start(bf16[256,2176]{1,0:T(8,128)(2,1)S(1)} %collective-permute-done.7.refs_2_.refs_0_.refs_1_), channel_id=1, source_target_pairs={{0,4},{1,5},{2,6},{3,7},{4,12},{5,13},{6,14},{7,15},{12,8},{13,9},... | collective-permute-start | bytes 3342344 | tf_op jit(solution)/shard_map/ppermute | solution.py:54
  71.0 1.0 copy-start.10
  96.2 2.1 %copy-start.13 = (bf16[256,2176]{1,0:T(8,128)(2,1)}, bf16[256,2176]{1,0:T(8,128)(2,1)S(1)}, u32[]{:S(2)}) copy-start(bf16[256,2176]{1,0:T(8,128)(2,1)S(1)} %collective-permute-done.12.refs_1_.refs_2_) | copy-start | bytes 3342340
  96.2 18.0 %collective-permute-start.13 = (bf16[512,1152]{1,0:T(8,128)(2,1)}, bf16[512,1152]{1,0:T(8,128)(2,1)S(1)}, u32[]{:S(2)}, u32[]{:S(2)}) collective-permute-start(bf16[512,1152]{1,0:T(8,128)(2,1)} %collective-permute-done.10.refs_1_.refs_3_), channel_id=1, source_target_pairs={{16,0},{0,16},{17,1},{1,17},{18,2},{2,18},{19,3},{3,19},{20,4},{4,... | collective-permute-start | bytes 3538952 | tf_op jit(solution)/shard_map/ppermute | solution.py:59
  98.2 16.1 %collective-permute-start.14 = (bf16[512,1152]{1,0:T(8,128)(2,1)}, bf16[512,1152]{1,0:T(8,128)(2,1)S(1)}, u32[]{:S(2)}, u32[]{:S(2)}) collective-permute-start(bf16[512,1152]{1,0:T(8,128)(2,1)} %collective-permute-done.11.refs_2_.refs_4_), channel_id=1, source_target_pairs={{16,0},{0,16},{17,1},{1,17},{18,2},{2,18},{19,3},{3,19},{20,4},{4,... | collective-permute-start | bytes 3538952 | tf_op jit(solution)/shard_map/ppermute | solution.py:59
  114.3 1.0 copy-start.11
  114.3 1.4 copy-start.12
  114.3 8.7 %collective-permute-start.15 = (bf16[3,384,1024]{2,1,0:T(8,128)(2,1)}, bf16[3,384,1024]{2,1,0:T(8,128)(2,1)}, u32[]{:S(2)}, u32[]{:S(2)}) collective-permute-start(bf16[3,384,1024]{2,1,0:T(8,128)(2,1)} %bitcast.41), channel_id=1, source_target_pairs={{16,0},{0,16},{17,1},{1,17},{18,2},{2,18},{19,3},{3,19},{20,4},{4,... | collective-permute-start | bytes 7077896 | tf_op jit(solution)/shard_map/ppermute | solution.py:59
  115.2 7.8 %slice-start = ((s8[4718592]{0:T(1024)(128)(4,1)}), s8[4194304]{0:T(1024)(128)(4,1)S(1)}, s32[]{:S(2)}) async-start(s8[4718592]{0:T(1024)(128)(4,1)} %bitcast.39), calls=%async_computation | async-start | bytes 8388608
  115.7 7.3 %slice-start.1 = ((s8[4718592]{0:T(1024)(128)(4,1)}), s8[524288]{0:T(1024)(128)(4,1)S(1)}, s32[]{:S(2)}) async-start(s8[4718592]{0:T(1024)(128)(4,1)} %bitcast.39), calls=%async_computation.1 | async-start | bytes 1048576
  125.0 17.7 %collective-permute-start.17 = (bf16[384,1024]{1,0:T(8,128)(2,1)S(1)}, bf16[384,1024]{1,0:T(8,128)(2,1)S(1)}, u32[]{:S(2)}, u32[]{:S(2)}) collective-permute-start(bf16[384,1024]{1,0:T(8,128)(2,1)S(1)} %get-tuple-element.151), channel_id=1, source_target_pairs={{0,1},{1,0},{2,3},{3,2},{4,5},{5,4},{6,7},{7,6},{8,9},{9,8},{10,11... | collective-permute-start | bytes 2359304 | tf_op jit(solution)/shard_map/ppermute | solution.py:37
  126.1 18.1 %collective-permute-start.18 = (bf16[384,1024]{1,0:T(8,128)(2,1)S(1)}, bf16[384,1024]{1,0:T(8,128)(2,1)S(1)}, u32[]{:S(2)}, u32[]{:S(2)}) collective-permute-start(bf16[384,1024]{1,0:T(8,128)(2,1)S(1)} %get-tuple-element.150), channel_id=1, source_target_pairs={{0,2},{1,3},{2,0},{3,1},{4,6},{5,7},{6,4},{7,5},{8,10},{9,11},{10,... | collective-permute-start | bytes 2359304 | tf_op jit(solution)/shard_map/ppermute | solution.py:37
  126.3 14.1 %collective-permute-start.16 = (bf16[128,2176]{1,0:T(8,128)(2,1)}, bf16[128,2176]{1,0:T(8,128)(2,1)}, u32[]{:S(2)}, u32[]{:S(2)}) collective-permute-start(bf16[128,2176]{1,0:T(8,128)(2,1)} %bitcast.4), channel_id=1, source_target_pairs={{0,4},{1,5},{2,6},{3,7},{4,12},{5,13},{6,14},{7,15},{12,8},{13,9},... | collective-permute-start | bytes 1671176 | tf_op jit(solution)/shard_map/ppermute | solution.py:54
  139.5 8.6 %copy-start.14 = (f32[1,384,1024]{2,1,0:T(8,128)S(1)}, f32[1,384,1024]{2,1,0:T(8,128)}, u32[]{:S(2)}) copy-start(f32[1,384,1024]{2,1,0:T(8,128)} %get-tuple-element.134) | copy-start | bytes 4718596
  144.2 4.0 %collective-permute-start.19 = (bf16[384,1024]{1,0:T(8,128)(2,1)}, bf16[384,1024]{1,0:T(8,128)(2,1)S(1)}, u32[]{:S(2)}, u32[]{:S(2)}) collective-permute-start(bf16[384,1024]{1,0:T(8,128)(2,1)} %bitcast.42), channel_id=1, source_target_pairs={{16,0},{0,16},{17,1},{1,17},{18,2},{2,18},{19,3},{3,19},{20,4},{4,... | collective-permute-start | bytes 2359304 | tf_op jit(solution)/shard_map/ppermute | solution.py:59
  147.4 15.2 %collective-permute-start.21 = (bf16[128,2176]{1,0:T(8,128)(2,1)S(1)}, bf16[128,2176]{1,0:T(8,128)(2,1)S(1)}, u32[]{:S(2)}, u32[]{:S(2)}) collective-permute-start(bf16[128,2176]{1,0:T(8,128)(2,1)S(1)} %fusion.8), channel_id=1, source_target_pairs={{0,4},{1,5},{2,6},{3,7},{4,12},{5,13},{6,14},{7,15},{12,8},{13,9},... | collective-permute-start | bytes 1671176 | tf_op jit(solution)/shard_map/ppermute | solution.py:54
  148.2 35.6 %copy-start.2 = (f32[1,1,384,2048]{3,2,1,0:T(8,128)S(1)}, f32[1,1,384,2048]{3,2,1,0:T(8,128)}, u32[]{:S(2)}) copy-start(f32[1,1,384,2048]{3,2,1,0:T(8,128)} %refs_3_.1) | copy-start | bytes 9437188
  148.4 29.8 %collective-permute-start.20 = (bf16[384,1024]{1,0:T(8,128)(2,1)S(1)}, bf16[384,1024]{1,0:T(8,128)(2,1)S(1)}, u32[]{:S(2)}, u32[]{:S(2)}) collective-permute-start(bf16[384,1024]{1,0:T(8,128)(2,1)S(1)} %fusion.2), channel_id=1, source_target_pairs={{0,3},{1,2},{2,1},{3,0},{4,7},{5,6},{6,5},{7,4},{8,11},{9,10},{10,... | collective-permute-start | bytes 2359304 | tf_op jit(solution)/shard_map/ppermute | solution.py:37
  163.8 19.9 %copy-start = (bf16[1,384,2048]{2,1,0:T(8,128)(2,1)S(1)}, bf16[1,384,2048]{2,1,0:T(8,128)(2,1)}, u32[]{:S(2)}) copy-start(bf16[1,384,2048]{2,1,0:T(8,128)(2,1)} %refs_4_.1) | copy-start | bytes 4718596
  163.8 19.9 %copy-start.1 = (f32[1,1,384,2048]{3,2,1,0:T(8,128)S(1)}, f32[1,1,384,2048]{3,2,1,0:T(8,128)}, u32[]{:S(2)}) copy-start(f32[1,1,384,2048]{3,2,1,0:T(8,128)} %refs_2_.1) | copy-start | bytes 9437188
  163.8 14.4 %collective-permute-start.22 = (bf16[128,2176]{1,0:T(8,128)(2,1)S(1)}, bf16[128,2176]{1,0:T(8,128)(2,1)}, u32[]{:S(2)}, u32[]{:S(2)}) collective-permute-start(bf16[128,2176]{1,0:T(8,128)(2,1)S(1)} %fusion.7), channel_id=1, source_target_pairs={{0,4},{1,5},{2,6},{3,7},{4,12},{5,13},{6,14},{7,15},{12,8},{13,9},... | collective-permute-start | bytes 1671176 | tf_op jit(solution)/shard_map/ppermute | solution.py:54
  180.1 3.7 %collective-permute-start.23 = (bf16[384,1024]{1,0:T(8,128)(2,1)S(1)}, bf16[384,1024]{1,0:T(8,128)(2,1)S(1)}, u32[]{:S(2)}, u32[]{:S(2)}) collective-permute-start(bf16[384,1024]{1,0:T(8,128)(2,1)S(1)} %fusion.1.refs_0_), channel_id=1, source_target_pairs={{16,0},{0,16},{17,1},{1,17},{18,2},{2,18},{19,3},{3,19},{20,4},{4,... | collective-permute-start | bytes 2359304 | tf_op jit(solution)/shard_map/ppermute | solution.py:59
  182.5 7.1 %copy-start.17 = (s32[1,2]{1,0:T(1,128)S(1)}, s32[1,2]{1,0:T(1,128)}, u32[]{:S(2)}) copy-start(s32[1,2]{1,0:T(1,128)} %param.18) | copy-start | bytes 28
  189.2 4.3 %collective-permute-start.24 = (bf16[384,2048]{1,0:T(8,128)(2,1)S(1)}, bf16[384,2048]{1,0:T(8,128)(2,1)}, u32[]{:S(2)}, u32[]{:S(2)}) collective-permute-start(bf16[384,2048]{1,0:T(8,128)(2,1)S(1)} %get-tuple-element.142), channel_id=1, source_target_pairs={{16,0},{0,16},{17,1},{1,17},{18,2},{2,18},{19,3},{3,19},{20,4},{4,... | collective-permute-start | bytes 4718600 | tf_op jit(solution)/shard_map/ppermute | solution.py:59

commit v3 on v2

--- a/solution.py
+++ b/solution.py
@@ -72,9 +72,10 @@
 
 
 class Pass:
-    def __init__(self, tok, model, half, n_dp, slots, blocks, spans, back=False):
+    def __init__(self, tok, model, half, n_dp, slots, blocks, spans, back=0):
         self.tok, self.model, self.half, self.n_dp = tok, model, half, n_dp
         self.slots, self.blocks, self.spans, self.back = slots, blocks, spans, back
+        self.left = blocks[back:]
         self.rows = tok * len(blocks)
         self.width = model // n_dp
 
@@ -141,11 +142,11 @@
                 pltpu.make_async_copy(ins["pr%d" % j].at[came], pr.at[at], sem_i.at[b, 1])
             )
         filled = 0
-        for j in range(self.n_grads):
-            n = ins["keep%d" % j].shape[0]
-            at = pl.ds(filled, n)
-            extra.append(pltpu.make_async_copy(ins["keep%d" % j], keep.at[at], sem_k.at[j, 0]))
-            extra.append(pltpu.make_async_copy(ins["send%d" % j], send.at[at], sem_k.at[j, 1]))
+        for j, (low, n) in enumerate(self.grads):
+            at, came = pl.ds(filled, n), pl.ds(low, n)
+            for name, ref, sem in (("keep", keep, 0), ("send", send, 1)):
+                ref_in = ins["%s%d" % (name, j)].at[came]
+                extra.append(pltpu.make_async_copy(ref_in, ref.at[at], sem_k.at[j, sem]))
             filled += n
         for copy in extra:
             copy.start()
@@ -199,12 +200,12 @@
                 at = slice(d, d + 2 * tile)
                 col = pl.ds(pl.multiple_of(me_dp * width + d, tile), 2 * tile)
                 part = tn(sc[mine, :], ys[mine, col])
-                keep[i, :, at] = keep[i, :, at] + part if filled else part
+                keep[i, :, at] = keep[i, :, at] + part if i < filled else part
                 for k in range(1, n_dp):
                     col = lax.rem(me_dp + n_dp - k, n_dp) * width + d
                     col = pl.ds(pl.multiple_of(col, tile), 2 * tile)
                     part = tn(sc[mine, :], ys[mine, col])
-                    if filled:
+                    if i < filled:
                         part = send[i, k - 1, :, at].astype(f32) + part
                     send[i, k - 1, :, at] = part.astype(bf16)
 
@@ -217,20 +218,20 @@
             pending[-2].start()
             pending[-1].start()
         n = 2 * len(slots)
-        if not self.back:
-            pending.append(pltpu.make_async_copy(dx, outs["dx"], sem_o.at[n]))
-            pending.append(pltpu.make_async_copy(pr, outs["pr"], sem_o.at[n + 1]))
+        if self.left:
+            at = pl.ds(self.back * tok, len(self.left) * tok)
+            pending.append(pltpu.make_async_copy(dx.at[at], outs["dx"], sem_o.at[n]))
+            pending.append(pltpu.make_async_copy(pr.at[at], outs["pr"], sem_o.at[n + 1]))
             pending[-2].start()
             pending[-1].start()
-        else:
+        for b in range(self.back):
             rows_out = scratch[17]
-            for b in range(len(blocks)):
-                at = pl.ds(b * tok, tok)
-                rows_out[b, :, pl.ds(0, model)] = dx[at, :].astype(bf16)
-                rows_out[b, :, pl.ds(model, lanes)] = pr[at, :].astype(bf16)
-                copy = pltpu.make_async_copy(rows_out.at[b], outs["back"].at[b], sem_o.at[n + b])
-                copy.start()
-                pending.append(copy)
+            at = pl.ds(b * tok, tok)
+            rows_out[b, :, pl.ds(0, model)] = dx[at, :].astype(bf16)
+            rows_out[b, :, pl.ds(model, lanes)] = pr[at, :].astype(bf16)
+            copy = pltpu.make_async_copy(rows_out.at[b], outs["back"].at[b], sem_o.at[n + 2 + b])
+            copy.start()
+            pending.append(copy)
         for copy in pending:
             copy.wait()
 
@@ -241,20 +242,20 @@
         self.sums = [None] * len(self.blocks)
         for j, (earlier, out) in enumerate(sums):
             for b, block in enumerate(self.blocks):
-                if block in earlier.blocks:
-                    self.sums[b] = (j, earlier.blocks.index(block))
+                if block in earlier.left:
+                    self.sums[b] = (j, earlier.left.index(block))
             ins["dx%d" % j], ins["pr%d" % j] = out["dx"], out["pr"]
-        self.n_grads = len(grads)
-        for j, out in enumerate(grads):
+        self.grads = [rows_from for _, rows_from in grads]
+        for j, (out, _) in enumerate(grads):
             ins["keep%d" % j], ins["send%d" % j] = out["keep"], out["send"]
         shape = {"keep": ((n, half, width), f32)}
         shape["send"] = ((n, max(n_dp - 1, 1), half, width), bf16)
-        out_rows = (len(self.blocks), tok, model + lanes)
+        out_rows = (self.back, tok, model + lanes)
         if self.back:
             shape["back"] = (out_rows, bf16)
-        else:
-            shape["dx"] = ((rows, model), f32)
-            shape["pr"] = ((rows, lanes), f32)
+        if self.left:
+            shape["dx"] = ((len(self.left) * tok, model), f32)
+            shape["pr"] = ((len(self.left) * tok, lanes), f32)
         self.names, self.outs = list(ins), list(shape)
         scratch = [
             pltpu.VMEM((rows, model), bf16),
@@ -272,7 +273,7 @@
             pltpu.SemaphoreType.DMA((len(self.blocks), 3)),
             pltpu.SemaphoreType.DMA((n, 2 * n_dp)),
             pltpu.SemaphoreType.DMA((len(self.blocks), 2)),
-            pltpu.SemaphoreType.DMA((max(self.n_grads, 1), 2)),
+            pltpu.SemaphoreType.DMA((max(len(self.grads), 1), 2)),
             pltpu.SemaphoreType.DMA((2 * n + len(self.blocks) + 2,)),
         ]
         if self.back:
@@ -290,16 +291,18 @@
 
 
 def adam_kernel(n_dp, lead_ref, *refs):
-    grads = refs[:n_dp]
-    m_ref, v_ref, w_ref, m_out, v_out, w_out = refs[n_dp:]
+    grads = refs[: 2 * n_dp]
+    m_ref, v_ref, w_ref, m_out, v_out, w_out = refs[2 * n_dp :]
+    upper = pl.program_id(0) < pl.num_programs(0) // 2
     me_dp = lax.axis_index("dp")
     width = grads[0].shape[1]
     is_lead = lead_ref[0] == me_dp
-    for k, ref in enumerate(grads):
+    for k in range(n_dp):
+        grad = jnp.where(upper, grads[2 * k][...].astype(f32), grads[2 * k + 1][...].astype(f32))
         at = lax.rem(me_dp + k, n_dp) * width
         at = pl.ds(pl.multiple_of(at, width), width)
         m_old, v_old = m_ref[0, 0, :, at], v_ref[0, 0, :, at]
-        m_new, v_new, w_new = adam_update(ref[...].astype(f32), m_old, v_old, w_ref[0, :, at])
+        m_new, v_new, w_new = adam_update(grad, m_old, v_old, w_ref[0, :, at])
         m_out[0, 0, :, at] = jnp.where(is_lead, m_new, m_old)
         v_out[0, 0, :, at] = jnp.where(is_lead, v_new, v_old)
         w_out[:, at] = w_new
@@ -307,27 +310,32 @@
 
 def adam_call(parts, leader, moment_one, moment_two, w_down):
     half, model = w_down.shape[1:]
-    step = 48 if half % 48 == 0 else half
+    step = 48 if half % 96 == 0 else half // 2
+    steps = half // step
     n_dp = len(parts)
     width = model // n_dp
     wide = pl.BlockSpec((1, 1, step, model), lambda i: (0, 0, i, 0))
     return pl.pallas_call(
         functools.partial(adam_kernel, n_dp),
-        grid=(half // step,),
+        grid=(steps,),
         out_shape=[
             jax.ShapeDtypeStruct(moment_one.shape, f32),
             jax.ShapeDtypeStruct(moment_two.shape, f32),
             jax.ShapeDtypeStruct((half, model), bf16),
         ],
         in_specs=[pl.BlockSpec(memory_space=pltpu.SMEM)]
-        + [pl.BlockSpec((step, width), lambda i: (i, 0))] * n_dp
+        + [
+            pl.BlockSpec((step, width), lambda i: (jnp.minimum(i, steps // 2 - 1), 0)),
+            pl.BlockSpec((step, width), lambda i: (jnp.maximum(i - steps // 2, 0), 0)),
+        ]
+        * n_dp
         + [wide, wide, pl.BlockSpec((1, step, model), lambda i: (0, i, 0))],
         out_specs=[wide, wide, pl.BlockSpec((step, model), lambda i: (i, 0))],
         compiler_params=pltpu.CompilerParams(vmem_limit_bytes=32 * 2**20),
         cost_estimate=pl.CostEstimate(
             flops=1000, bytes_accessed=1000, transcendentals=0
         ),
-    )(leader, *parts, moment_one, moment_two, w_down)
+    )(leader, *[v for pair in parts for v in pair], moment_one, moment_two, w_down)
 
 
 def body(
@@ -392,52 +400,52 @@
     x_o2, y_o1 = others(x_p2), others(y_p1)
     name_parts(1, [x_p1] + x_o1, [x_p2] + x_o2)
     name_parts(2, [y_p1] + y_o1, [y_p2] + y_o2)
-    one_pass = make([1, 2], near, [(0, last_block)] * 2)
-    one = one_pass.call(pick(one_pass), sums=[(zero_pass, zero)])
-
-    zero, one, d_p1, d_p2, held, final = lax.optimization_barrier(
-        (zero, one, d_p1, d_p2, held, final)
-    )
+    one_pass = make([0, 1, 2], near, [(2, last_block)] + [(0, last_block)] * 2)
+    one = one_pass.call(pick(one_pass), sums=[(zero_pass, zero)], grads=[(zero, (0, 1))])
+
+    one, d_p1, d_p2, held, final = lax.optimization_barrier((one, d_p1, d_p2, held, final))
     held.append(final)
     d_o1, d_o2 = others(d_p1), others(d_p2)
     name_parts(3, [d_p1] + d_o1, [d_p2] + d_o2)
-    rest = list(range(2, layers))
-    two_pass = make([0, 1, 2], rest, [(0, len(rest))] + [(len(rest) - 1, len(rest))] * 2)
-    two = two_pass.call(pick(two_pass), sums=[(one_pass, one)], grads=[zero, one])
+    two_pass = make([0, 1, 2], [last_block], [(0, 1)] * 3)
+    two = two_pass.call(pick(two_pass), grads=[(one, (0, 3))])
     two_send = after(two["send"], d_o1, d_o2)
     swapped = [turn(two_send[:, k - 1], k) for k in range(1, n_dp)]
     keep = two["keep"]
+
     sums = [(one_pass, one), (two_pass, two)]
-    first_pass = make([3], [1], [(0, 1)], True)
+    early = near[1:]
+    first_pass = make([3], early, [(0, len(early))], len(early))
     first = first_pass.call(pick(first_pass), sums=sums)
     first, swapped, keep = lax.optimization_barrier((first, swapped, keep))
     passing = along(first["back"][0])
     leaving = [(keep[s] + sum(v[s].astype(f32) for v in swapped)).astype(bf16) for s in (1, 2)]
     sent = [hop(leaving[0], 1), hop(leaving[1], 2)]
-    others_pass = make([3], [0] + rest, [(0, len(rest) + 1)], True)
-    last = others_pass.call(pick(others_pass), sums=sums, grads=[first])
-    last, passing, sent = lax.optimization_barrier((last, passing, sent))
-
-    back = last["back"]
-    swapped_across = [turn(last["send"][0, k - 1], k) for k in range(1, n_dp)]
-    across = last["keep"][0] + sum(v.astype(f32) for v in swapped_across)
-    across = across.astype(bf16)
-    sent.append(hop(across, 3))
+    rest_pass = make([3], [0, last_block], [(0, 2)], 2)
+    last = rest_pass.call(pick(rest_pass), sums=sums, grads=[(first, (0, 1))])
+    sent, last_keep, last_send = lax.optimization_barrier((sent, last["keep"], last["send"]))
+
+    across = last_keep[0]
+    for k in range(1, n_dp):
+        across = across + turn(last_send[0, k - 1], k).astype(f32)
+    sent.append(hop(across.astype(bf16), 3))
     for k in range(2, layers):
-        passing = (passing.astype(f32) + back[k - 1].astype(f32)).astype(bf16)
-        passing = along(after(passing, across) if k == 3 else passing)
-
-    sent, passing = lax.optimization_barrier((sent, passing))
+        term = first["back"][k - 1] if k < last_block else last["back"][1]
+        passing = along((passing.astype(f32) + term.astype(f32)).astype(bf16))
+
     grad = keep[0] + sum(v[0].astype(f32) for v in swapped)
     grad = (grad + sum(v.astype(f32) for v in sent)).astype(bf16)
-    parts = [grad] + others(grad)
+    cut = half // 2
+    halves = [others(grad[:cut]), others(grad[cut:])]
+    halves, passing = lax.optimization_barrier((halves, passing))
+    parts = [(grad[:cut], grad[cut:])] + list(zip(*halves))
     new_one, new_two, w_new = adam_call(parts, leader, moment_one, moment_two, w_down)
     lead = leader[0]
     fresh = w_new
     for k in range(1, n_dp):
         fresh = jnp.where((me_dp + k) % n_dp == lead, turn(w_new, k), fresh)
 
-    total = back[0].astype(f32) + passing.astype(f32)
+    total = last["back"][0].astype(f32) + passing.astype(f32)
     token_grad = total[:, :model].astype(bf16)
     pair = total[:, model:]
     prob_grad = jnp.sum(jnp.where(chosen, pair[:, None, :], 0.0), axis=2).astype(bf16)

time: 197 us -> 193 us (0.980); the launches traced: 197 us -> 191 us
  waiting for transfers between devices: 77.8 us -> 72.5 us
  other arithmetic: 21.4 us -> 18.9 us
    ppermute x6, waiting for transfers between devices: 72.2 us -> 59.4 us  [along(): return lax.ppermute(value, 'expert', pairs)]
    ppermute x9, waiting for transfers between devices: 3.84 us -> 12.6 us  [hop(): return lax.ppermute(value, 'expert', [(i, i ^ flip) for i in range(n)])]
    ppermute x10 -> x11, starting transfers between devices: 10.9 us -> 12.2 us  [turn(): return lax.ppermute(value, 'dp', [((r + step) % n, r) for r in range(n)])]
  transfers between devices with their start and end apart: 25 -> 26, of which waited for: 11 -> 8; matrix products, arithmetic and copies ran while one was open for 7% -> 8% of each run, Pallas kernels for 32% -> 32%
where the time goes in v3:
time: 193 us; the launch traced here: 191 us
  waiting for transfers between devices  72.5 us (38%)
  Pallas kernels  66.9 us (35%)
  starting transfers between devices  24.4 us (13%)
  other arithmetic  18.9 us (10%)
  local copies, waits for them, and re-layouts  6.33 us (3%)
    pallas_call x5, Pallas kernels, call(): pl.pallas_call(functools.partial(self.kernel, len(ins)), out_shape=[jax.S...  61.2 us
    ppermute x6, waiting for transfers between devices, along(): return lax.ppermute(value, 'expert', pairs)  59.4 us
    ppermute x9, waiting for transfers between devices, hop(): return lax.ppermute(value, 'expert', [(i, i ^ flip) for i in range(n)])  12.6 us
    ppermute x11, starting transfers between devices, turn(): return lax.ppermute(value, 'dp', [((r + step) % n, r) for r in range(n)])  12.2 us
    ppermute x9, starting transfers between devices, hop(): return lax.ppermute(value, 'expert', [(i, i ^ flip) for i in range(n)])  8.26 us
    concatenate x2, other arithmetic, body(): w_own = jnp.concatenate([w_gu, w_dn.T], 1)  7.46 us
    pallas_call x1, Pallas kernels, adam_call(): pl.pallas_call(functools.partial(adam_kernel, n_dp), grid=(steps,), out_s...  5.68 us
    ppermute x6, starting transfers between devices, along(): return lax.ppermute(value, 'expert', pairs)  3.94 us
  transfers between devices with their start and end apart: 26, of which 8 were waited for; matrix products, arithmetic and copies ran while one was open for 8% of the time, Pallas kernels for 32%

profile of v3, /device:TPU:1, one launch (start us, length us, event | category | flops | bytes accessed | tf_op | source)
XLA Modules:
  0.0 190.8 jit_solution(14820644438574225001)
XLA Ops:
  0.6 1.9 copy.18
  2.6 3.0 %fusion.5 = (bf16[512,1152]{1,0:T(8,128)(2,1)}, bf16[512,1152]{1,0:T(8,128)(2,1)}) fusion(s32[]{:T(128)S(6)} %select_n.39, bf16[2048,768]{1,0:T(8,128)(2,1)} %bitcast.38, bf16[2048,384]{1,0:T(8,128)(2,1)S(1)} %copy.18, s32[]{:T(128)S(6)} %select_n.38), kind=kLoop, calls=%fused_computation.16 | loop fusion | flops 4718592 | bytes 7077896 | tf_op jit(solution)/shard_map/concatenate | solution.py:366
  5.6 2.0 %collective-permute-start.1 = (bf16[512,1152]{1,0:T(8,128)(2,1)}, bf16[512,1152]{1,0:T(8,128)(2,1)S(1)}, u32[]{:S(2)}, u32[]{:S(2)}) collective-permute-start(bf16[512,1152]{1,0:T(8,128)(2,1)} %get-tuple-element.72), channel_id=1, source_target_pairs={{0,1},{1,0},{2,3},{3,2},{4,5},{5,4},{6,7},{7,6},{8,9},{9,8},{10,11... | collective-permute-start | bytes 3538952 | tf_op jit(solution)/shard_map/ppermute | solution.py:37
  7.6 1.2 collective-permute-start.2
  9.4 1.1 fusion.6.refs_0_
  10.6 1.3 collective-permute-start
  11.9 4.4 %pad_maximum_fusion.refs_2_.refs_3_.refs_1_ = bf16[2048,1152]{1,0:T(8,128)(2,1)} fusion(bf16[2048,384]{1,0:T(8,128)(2,1)S(1)} %copy.18, bf16[2048,768]{1,0:T(8,128)(2,1)} %bitcast.39), kind=kLoop, calls=%fused_computation.2 | loop fusion | flops 9437184 | bytes 9437184 | tf_op jit(solution)/shard_map/concatenate | solution.py:366
  16.4 20.0 %collective-permute-done.refs_1_.refs_0_ = bf16[256,2176]{1,0:T(8,128)(2,1)S(1)} collective-permute-done((bf16[256,2176]{1,0:T(8,128)(2,1)S(1)}, bf16[256,2176]{1,0:T(8,128)(2,1)S(1)}, u32[]{:S(2)}, u32[]{:S(2)}) %collective-permute-start) | collective-permute-done | bytes 1114144 | tf_op jit(solution)/shard_map/ppermute | solution.py:54
  36.7 0.5 collective-permute-start.4
  37.2 2.4 %collective-permute-start.5 = (bf16[512,1152]{1,0:T(8,128)(2,1)S(1)}, bf16[512,1152]{1,0:T(8,128)(2,1)S(1)}, u32[]{:S(2)}, u32[]{:S(2)}) collective-permute-start(bf16[512,1152]{1,0:T(8,128)(2,1)S(1)} %collective-permute-done.1.refs_4_.refs_2_), channel_id=1, source_target_pairs={{16,0},{0,16},{17,1},{1,17},{18,2},{2,18},{19,3},{3,19},{20,4},{4,... | collective-permute-start | bytes 3538952 | tf_op jit(solution)/shard_map/ppermute | solution.py:59
  39.6 0.6 collective-permute-start.7
  40.2 8.5 %shard_map.137 = (f32[1,384,1024]{2,1,0:T(8,128)}, bf16[1,1,384,1024]{3,2,1,0:T(8,128)(2,1)}, f32[256,2048]{1,0:T(8,128)}, f32[256,128]{1,0:T(8,128)}) custom-call(bf16[256,2176]{1,0:T(8,128)(2,1)} %copy-done.3, bf16[256,2176]{1,0:T(8,128)(2,1)} %copy-done.4, bf16[2048,1152]{1,0:T(8,128)(2,1)} %pad_maximum_fusion.refs_2_.refs_3_.refs_1_), custom_call_target="tpu_custom_call" | custom-call | flops 1000 | bytes 1000 | tf_op jit(solution)/shard_map/pallas_call | solution.py:281
  48.7 17.5 %collective-permute-done.7.refs_2_.refs_1_ = bf16[256,2176]{1,0:T(8,128)(2,1)} collective-permute-done((bf16[256,2176]{1,0:T(8,128)(2,1)S(1)}, bf16[256,2176]{1,0:T(8,128)(2,1)}, u32[]{:S(2)}, u32[]{:S(2)}) %collective-permute-start.7) | collective-permute-done | bytes 1114144 | tf_op jit(solution)/shard_map/ppermute | solution.py:54
  66.3 1.4 collective-permute-start.8
  67.7 1.3 collective-permute-start.9
  69.1 1.3 collective-permute-start.10
  70.3 1.2 collective-permute-start.11
  71.6 0.4 collective-permute-start.12
  72.0 1.0 copy-done.14
  73.0 20.6 %shard_map.138 = (f32[3,384,1024]{2,1,0:T(8,128)}, bf16[3,1,384,1024]{3,2,1,0:T(8,128)(2,1)}, f32[384,2048]{1,0:T(8,128)}, f32[384,128]{1,0:T(8,128)}) custom-call(bf16[256,2176]{1,0:T(8,128)(2,1)} %copy-done.3, bf16[256,2176]{1,0:T(8,128)(2,1)} %copy-done.4, bf16[256,2176]{1,0:T(8,128)(2,1)} %collective-permute-done.7.refs_2_.refs_1_, ...), custom_call_target="tpu_custom_call" | custom-call | flops 1000 | bytes 1000 | tf_op jit(solution)/shard_map/pallas_call | solution.py:281
  93.6 4.7 %collective-permute-done.12.refs_0_.refs_1_ = bf16[256,2176]{1,0:T(8,128)(2,1)} collective-permute-done((bf16[256,2176]{1,0:T(8,128)(2,1)}, bf16[256,2176]{1,0:T(8,128)(2,1)}, u32[]{:S(2)}, u32[]{:S(2)}) %collective-permute-start.12) | collective-permute-done | bytes 1114144 | tf_op jit(solution)/shard_map/ppermute | solution.py:54
  98.4 1.5 collective-permute-start.13
  99.9 13.9 %shard_map.139 = (f32[3,384,1024]{2,1,0:T(8,128)}, bf16[3,1,384,1024]{3,2,1,0:T(8,128)(2,1)}, f32[128,2048]{1,0:T(8,128)}, f32[128,128]{1,0:T(8,128)}) custom-call(bf16[256,2176]{1,0:T(8,128)(2,1)} %collective-permute-done.12.refs_0_.refs_1_, bf16[2048,1152]{1,0:T(8,128)(2,1)} %pad_maximum_fusion.refs_2_.refs_3_.refs_1_, bf16[512,1152]{1,0:T(8,128)(2,1)} %copy-done.9, ...), custom_call_target="tpu_custom_call" | custom-call | flops 1000 | bytes 1000 | tf_op jit(solution)/shard_map/pallas_call | solution.py:281
  113.9 0.7 collective-permute-start.15
  115.3 8.9 %shard_map.140 = (f32[1,384,1024]{2,1,0:T(8,128)}, bf16[1,1,384,1024]{3,2,1,0:T(8,128)(2,1)}, bf16[2,128,2176]{2,1,0:T(8,128)(2,1)}) custom-call(bf16[256,2176]{1,0:T(8,128)(2,1)} %copy-done.4, bf16[256,2176]{1,0:T(8,128)(2,1)} %collective-permute-done.7.refs_2_.refs_1_, bf16[512,1152]{1,0:T(8,128)(2,1)} %copy-done.5, bf16[512,1152]{1,0:T(8,128)(2,1)} %copy-done.6, ...), custom_call_target="tpu_custom_call" | custom-call | flops 1000 | bytes 1000 | tf_op jit(solution)/shard_map/pallas_call | solution.py:281
  124.2 1.8 fusion.10
  126.5 0.8 slice_bitcast_fusion
  127.3 0.5 collective-permute-start.22
  127.8 9.3 %shard_map.141 = (f32[1,384,1024]{2,1,0:T(8,128)}, bf16[1,1,384,1024]{3,2,1,0:T(8,128)(2,1)}, bf16[2,128,2176]{2,1,0:T(8,128)(2,1)}) custom-call(bf16[256,2176]{1,0:T(8,128)(2,1)} %copy-done.3, bf16[256,2176]{1,0:T(8,128)(2,1)} %collective-permute-done.12.refs_0_.refs_1_, bf16[512,1152]{1,0:T(8,128)(2,1)} %copy-done.5, bf16[512,1152]{1,0:T(8,128)(2,1)} %copy-done.6, ...), custom_call_target="tpu_custom_call" | custom-call | flops 1000 | bytes 1000 | tf_op jit(solution)/shard_map/pallas_call | solution.py:281
  137.1 7.6 %collective-permute-done.16 = bf16[384,1024]{1,0:T(8,128)(2,1)} collective-permute-done((bf16[384,1024]{1,0:T(8,128)(2,1)}, bf16[384,1024]{1,0:T(8,128)(2,1)}, u32[]{:S(2)}, u32[]{:S(2)}) %collective-permute-start.16) | collective-permute-done | bytes 786464 | tf_op jit(solution)/shard_map/ppermute | solution.py:37
  144.8 1.7 collective-permute-start.18
  146.5 1.2 fusion.8
  147.7 0.6 collective-permute-start.23
  148.9 1.2 collective-permute-start.19
  150.1 12.8 %collective-permute-done.23 = bf16[128,2176]{1,0:T(8,128)(2,1)S(1)} collective-permute-done((bf16[128,2176]{1,0:T(8,128)(2,1)S(1)}, bf16[128,2176]{1,0:T(8,128)(2,1)S(1)}, u32[]{:S(2)}, u32[]{:S(2)}) %collective-permute-start.23) | collective-permute-done | bytes 557088 | tf_op jit(solution)/shard_map/ppermute | solution.py:54
  163.1 0.6 collective-permute-start.24
  163.6 5.0 %collective-permute-done.19 = bf16[384,1024]{1,0:T(8,128)(2,1)S(1)} collective-permute-done((bf16[384,1024]{1,0:T(8,128)(2,1)S(1)}, bf16[384,1024]{1,0:T(8,128)(2,1)S(1)}, u32[]{:S(2)}, u32[]{:S(2)}) %collective-permute-start.19) | collective-permute-done | bytes 786464 | tf_op jit(solution)/shard_map/ppermute | solution.py:37
  168.6 2.2 %fusion.2 = bf16[384,1024]{1,0:T(8,128)(2,1)S(1)} fusion(bf16[384,1024]{1,0:T(8,128)(2,1)S(1)} %collective-permute-done.19, bf16[384,1024]{1,0:T(8,128)(2,1)} %collective-permute-done.17, bf16[384,1024]{1,0:T(8,128)(2,1)} %collective-permute-done.16, f32[3,384,1024]{2,1,0:T(8,128)S(1)} %bitcast.41, bf16[3,384,1024]{2,1,0:T(8,128)(2,1)S(1)} %collective-permute-done.15), kind=kLoop, calls=%fused_computation.10 | loop fusion | flops 3538944 | bytes 5505024 | tf_op jit(solution)/shard_map/convert_element_type | solution.py:437
  170.9 1.3 collective-permute-start.20
  173.0 4.4 %collective-permute-done.24 = bf16[128,2176]{1,0:T(8,128)(2,1)S(1)} collective-permute-done((bf16[128,2176]{1,0:T(8,128)(2,1)S(1)}, bf16[128,2176]{1,0:T(8,128)(2,1)S(1)}, u32[]{:S(2)}, u32[]{:S(2)}) %collective-permute-start.24) | collective-permute-done | bytes 557088 | tf_op jit(solution)/shard_map/ppermute | solution.py:54
  177.4 5.7 %shard_map.142 = (f32[1,1,384,2048]{3,2,1,0:T(8,128)}, f32[1,1,384,2048]{3,2,1,0:T(8,128)}, bf16[384,2048]{1,0:T(8,128)(2,1)S(1)}) custom-call(s32[1]{0:T(128)} %copy.22.lead_ref, bf16[192,1024]{1,0:T(8,128)(2,1)S(1)} %get-tuple-element.143.refs_0_, bf16[192,1024]{1,0:T(8,128)(2,1)S(1)} %get-tuple-element.142.refs_1_, ...), custom_call_target="tpu_custom_call" | custom-call | flops 1000 | bytes 1000 | tf_op jit(solution)/shard_map/pallas_call | solution.py:318
  183.1 1.7 collective-permute-start.25
  184.8 0.7 fusion.12
  185.4 1.3 convert_add_fusion.2
  186.8 0.9 slice.78
  187.7 0.4 select_reduce_fusion
  188.0 0.7 copy.21
  188.7 2.0 %fusion.3 = bf16[1,1,384,2048]{3,2,1,0:T(8,128)(2,1)} fusion(bf16[1,384,2048]{2,1,0:T(8,128)(2,1)S(1)} %copy-done, bf16[384,2048]{1,0:T(8,128)(2,1)} %collective-permute-done.25, bf16[384,2048]{1,0:T(8,128)(2,1)S(1)} %get-tuple-element.130, pred[]{:T(512)S(6)} %eq.29, pred[]{:T(512)} %bitcast.13), kind=kLoop, calls=%fused_computation.12 | loop fusion | flops 1572864 | bytes 6291458 | tf_op jit(solution)/shard_map/broadcast_in_dim | solution.py:453
  (82 shorter events, 3.3 us)
Async XLA Ops:
  2.5 6.3 %copy-start.20 = (s32[128,8]{0,1:T(8,128)S(1)}, s32[128,8]{0,1:T(8,128)}, u32[]{:S(2)}) copy-start(s32[128,8]{0,1:T(8,128)} %param.12) | copy-start | bytes 12292
  2.5 6.4 %copy-start.21 = (bf16[128,8]{0,1:T(8,128)(2,1)S(1)}, bf16[128,8]{0,1:T(8,128)(2,1)}, u32[]{:S(2)}) copy-start(bf16[128,8]{0,1:T(8,128)(2,1)} %param.13) | copy-start | bytes 6148
  2.5 6.9 %copy-start.19 = (bf16[128,2048]{1,0:T(8,128)(2,1)S(1)}, bf16[128,2048]{1,0:T(8,128)(2,1)}, u32[]{:S(2)}) copy-start(bf16[128,2048]{1,0:T(8,128)(2,1)} %param.11) | copy-start | bytes 1572868
  5.6 30.8 %collective-permute-start.1 = (bf16[512,1152]{1,0:T(8,128)(2,1)}, bf16[512,1152]{1,0:T(8,128)(2,1)S(1)}, u32[]{:S(2)}, u32[]{:S(2)}) collective-permute-start(bf16[512,1152]{1,0:T(8,128)(2,1)} %get-tuple-element.72), channel_id=1, source_target_pairs={{0,1},{1,0},{2,3},{3,2},{4,5},{5,4},{6,7},{7,6},{8,9},{9,8},{10,11... | collective-permute-start | bytes 3538952 | tf_op jit(solution)/shard_map/ppermute | solution.py:37
  7.6 28.8 %collective-permute-start.2 = (bf16[512,1152]{1,0:T(8,128)(2,1)}, bf16[512,1152]{1,0:T(8,128)(2,1)}, u32[]{:S(2)}, u32[]{:S(2)}) collective-permute-start(bf16[512,1152]{1,0:T(8,128)(2,1)} %get-tuple-element.71), channel_id=1, source_target_pairs={{0,2},{1,3},{2,0},{3,1},{4,6},{5,7},{6,4},{7,5},{8,10},{9,11},{10,... | collective-permute-start | bytes 3538952 | tf_op jit(solution)/shard_map/ppermute | solution.py:37
  10.6 5.8 %copy-start.3 = (bf16[256,2176]{1,0:T(8,128)(2,1)}, bf16[256,2176]{1,0:T(8,128)(2,1)S(1)}, u32[]{:S(2)}) copy-start(bf16[256,2176]{1,0:T(8,128)(2,1)S(1)} %fusion.6.refs_0_) | copy-start | bytes 3342340
  10.6 25.8 %collective-permute-start = (bf16[256,2176]{1,0:T(8,128)(2,1)S(1)}, bf16[256,2176]{1,0:T(8,128)(2,1)S(1)}, u32[]{:S(2)}, u32[]{:S(2)}) collective-permute-start(bf16[256,2176]{1,0:T(8,128)(2,1)S(1)} %fusion.6.refs_0_), channel_id=1, source_target_pairs={{0,4},{1,5},{2,6},{3,7},{4,12},{5,13},{6,14},{7,15},{12,8},{13,9},... | collective-permute-start | bytes 3342344 | tf_op jit(solution)/shard_map/ppermute | solution.py:54
  36.4 3.8 %copy-start.4 = (bf16[256,2176]{1,0:T(8,128)(2,1)}, bf16[256,2176]{1,0:T(8,128)(2,1)S(1)}, u32[]{:S(2)}) copy-start(bf16[256,2176]{1,0:T(8,128)(2,1)S(1)} %collective-permute-done.refs_1_.refs_0_) | copy-start | bytes 3342340
  36.4 32.7 %copy-start.9 = (bf16[512,1152]{1,0:T(8,128)(2,1)}, bf16[512,1152]{1,0:T(8,128)(2,1)S(1)}, u32[]{:S(2)}) copy-start(bf16[512,1152]{1,0:T(8,128)(2,1)S(1)} %collective-permute-done.1.refs_4_.refs_2_) | copy-start | bytes 3538948
  36.4 29.8 %collective-permute-start.3 = (bf16[512,1152]{1,0:T(8,128)(2,1)}, bf16[512,1152]{1,0:T(8,128)(2,1)S(1)}, u32[]{:S(2)}, u32[]{:S(2)}) collective-permute-start(bf16[512,1152]{1,0:T(8,128)(2,1)} %get-tuple-element.71), channel_id=1, source_target_pairs={{0,1},{1,0},{2,3},{3,2},{4,5},{5,4},{6,7},{7,6},{8,9},{9,8},{10,11... | collective-permute-start | bytes 3538952 | tf_op jit(solution)/shard_map/ppermute | solution.py:37
  36.7 29.5 %collective-permute-start.4 = (bf16[512,1152]{1,0:T(8,128)(2,1)}, bf16[512,1152]{1,0:T(8,128)(2,1)S(1)}, u32[]{:S(2)}, u32[]{:S(2)}) collective-permute-start(bf16[512,1152]{1,0:T(8,128)(2,1)} %get-tuple-element.72), channel_id=1, source_target_pairs={{0,2},{1,3},{2,0},{3,1},{4,6},{5,7},{6,4},{7,5},{8,10},{9,11},{10,... | collective-permute-start | bytes 3538952 | tf_op jit(solution)/shard_map/ppermute | solution.py:37
  37.2 29.1 %collective-permute-start.5 = (bf16[512,1152]{1,0:T(8,128)(2,1)S(1)}, bf16[512,1152]{1,0:T(8,128)(2,1)S(1)}, u32[]{:S(2)}, u32[]{:S(2)}) collective-permute-start(bf16[512,1152]{1,0:T(8,128)(2,1)S(1)} %collective-permute-done.1.refs_4_.refs_2_), channel_id=1, source_target_pairs={{16,0},{0,16},{17,1},{1,17},{18,2},{2,18},{19,3},{3,19},{20,4},{4,... | collective-permute-start | bytes 3538952 | tf_op jit(solution)/shard_map/ppermute | solution.py:59
  39.6 26.7 %collective-permute-start.6 = (bf16[512,1152]{1,0:T(8,128)(2,1)}, bf16[512,1152]{1,0:T(8,128)(2,1)S(1)}, u32[]{:S(2)}, u32[]{:S(2)}) collective-permute-start(bf16[512,1152]{1,0:T(8,128)(2,1)} %collective-permute-done.2.refs_9_.refs_7_), channel_id=1, source_target_pairs={{16,0},{0,16},{17,1},{1,17},{18,2},{2,18},{19,3},{3,19},{20,4},{4,... | collective-permute-start | bytes 3538952 | tf_op jit(solution)/shard_map/ppermute | solution.py:59
  39.6 26.6 %collective-permute-start.7 = (bf16[256,2176]{1,0:T(8,128)(2,1)S(1)}, bf16[256,2176]{1,0:T(8,128)(2,1)}, u32[]{:S(2)}, u32[]{:S(2)}) collective-permute-start(bf16[256,2176]{1,0:T(8,128)(2,1)S(1)} %collective-permute-done.refs_1_.refs_0_), channel_id=1, source_target_pairs={{0,4},{1,5},{2,6},{3,7},{4,12},{5,13},{6,14},{7,15},{12,8},{13,9},... | collective-permute-start | bytes 3342344 | tf_op jit(solution)/shard_map/ppermute | solution.py:54
  66.2 5.8 %copy-start.10 = (bf16[512,1152]{1,0:T(8,128)(2,1)}, bf16[512,1152]{1,0:T(8,128)(2,1)S(1)}, u32[]{:S(2)}) copy-start(bf16[512,1152]{1,0:T(8,128)(2,1)S(1)} %collective-permute-done.3.refs_5_.refs_3_) | copy-start | bytes 3538948
  66.2 5.8 %copy-start.11 = (bf16[512,1152]{1,0:T(8,128)(2,1)}, bf16[512,1152]{1,0:T(8,128)(2,1)S(1)}, u32[]{:S(2)}) copy-start(bf16[512,1152]{1,0:T(8,128)(2,1)S(1)} %collective-permute-done.4.refs_8_.refs_6_) | copy-start | bytes 3538948
  66.2 1.5 copy-start.12
  66.3 5.7 %collective-permute-start.8 = (bf16[512,1152]{1,0:T(8,128)(2,1)S(1)}, bf16[512,1152]{1,0:T(8,128)(2,1)S(1)}, u32[]{:S(2)}, u32[]{:S(2)}) collective-permute-start(bf16[512,1152]{1,0:T(8,128)(2,1)S(1)} %collective-permute-done.3.refs_5_.refs_3_), channel_id=1, source_target_pairs={{16,0},{0,16},{17,1},{1,17},{18,2},{2,18},{19,3},{3,19},{20,4},{4,... | collective-permute-start | bytes 3538952 | tf_op jit(solution)/shard_map/ppermute | solution.py:59
  67.7 4.3 %collective-permute-start.9 = (bf16[512,1152]{1,0:T(8,128)(2,1)S(1)}, bf16[512,1152]{1,0:T(8,128)(2,1)}, u32[]{:S(2)}, u32[]{:S(2)}) collective-permute-start(bf16[512,1152]{1,0:T(8,128)(2,1)S(1)} %collective-permute-done.4.refs_8_.refs_6_), channel_id=1, source_target_pairs={{16,0},{0,16},{17,1},{1,17},{18,2},{2,18},{19,3},{3,19},{20,4},{4,... | collective-permute-start | bytes 3538952 | tf_op jit(solution)/shard_map/ppermute | solution.py:59
  69.1 29.3 %collective-permute-start.10 = (bf16[512,1152]{1,0:T(8,128)(2,1)S(1)}, bf16[512,1152]{1,0:T(8,128)(2,1)S(1)}, u32[]{:S(2)}, u32[]{:S(2)}) collective-permute-start(bf16[512,1152]{1,0:T(8,128)(2,1)S(1)} %collective-permute-done.1.refs_4_.refs_2_), channel_id=1, source_target_pairs={{0,2},{1,3},{2,0},{3,1},{4,6},{5,7},{6,4},{7,5},{8,10},{9,11},{10,... | collective-permute-start | bytes 3538952 | tf_op jit(solution)/shard_map/ppermute | solution.py:37
  70.3 28.0 %collective-permute-start.11 = (bf16[512,1152]{1,0:T(8,128)(2,1)}, bf16[512,1152]{1,0:T(8,128)(2,1)S(1)}, u32[]{:S(2)}, u32[]{:S(2)}) collective-permute-start(bf16[512,1152]{1,0:T(8,128)(2,1)} %collective-permute-done.2.refs_9_.refs_7_), channel_id=1, source_target_pairs={{0,1},{1,0},{2,3},{3,2},{4,5},{5,4},{6,7},{7,6},{8,9},{9,8},{10,11... | collective-permute-start | bytes 3538952 | tf_op jit(solution)/shard_map/ppermute | solution.py:37
  71.6 26.8 %collective-permute-start.12 = (bf16[256,2176]{1,0:T(8,128)(2,1)}, bf16[256,2176]{1,0:T(8,128)(2,1)}, u32[]{:S(2)}, u32[]{:S(2)}) collective-permute-start(bf16[256,2176]{1,0:T(8,128)(2,1)} %collective-permute-done.7.refs_2_.refs_1_), channel_id=1, source_target_pairs={{0,4},{1,5},{2,6},{3,7},{4,12},{5,13},{6,14},{7,15},{12,8},{13,9},... | collective-permute-start | bytes 3342344 | tf_op jit(solution)/shard_map/ppermute | solution.py:54
  98.3 15.5 %copy-start.5 = (bf16[512,1152]{1,0:T(8,128)(2,1)}, bf16[512,1152]{1,0:T(8,128)(2,1)S(1)}, u32[]{:S(2)}) copy-start(bf16[512,1152]{1,0:T(8,128)(2,1)S(1)} %collective-permute-done.10.refs_2_) | copy-start | bytes 3538948
  98.3 15.5 %copy-start.6 = (bf16[512,1152]{1,0:T(8,128)(2,1)}, bf16[512,1152]{1,0:T(8,128)(2,1)S(1)}, u32[]{:S(2)}) copy-start(bf16[512,1152]{1,0:T(8,128)(2,1)S(1)} %collective-permute-done.11.refs_3_) | copy-start | bytes 3538948
  98.4 15.5 %collective-permute-start.13 = (bf16[512,1152]{1,0:T(8,128)(2,1)S(1)}, bf16[512,1152]{1,0:T(8,128)(2,1)S(1)}, u32[]{:S(2)}, u32[]{:S(2)}) collective-permute-start(bf16[512,1152]{1,0:T(8,128)(2,1)S(1)} %collective-permute-done.10.refs_2_), channel_id=1, source_target_pairs={{16,0},{0,16},{17,1},{1,17},{18,2},{2,18},{19,3},{3,19},{20,4},{4,... | collective-permute-start | bytes 3538952 | tf_op jit(solution)/shard_map/ppermute | solution.py:59
  99.8 14.0 %collective-permute-start.14 = (bf16[512,1152]{1,0:T(8,128)(2,1)S(1)}, bf16[512,1152]{1,0:T(8,128)(2,1)S(1)}, u32[]{:S(2)}, u32[]{:S(2)}) collective-permute-start(bf16[512,1152]{1,0:T(8,128)(2,1)S(1)} %collective-permute-done.11.refs_3_), channel_id=1, source_target_pairs={{16,0},{0,16},{17,1},{1,17},{18,2},{2,18},{19,3},{3,19},{20,4},{4,... | collective-permute-start | bytes 3538952 | tf_op jit(solution)/shard_map/ppermute | solution.py:59
  113.8 1.4 copy-start.7
  113.9 10.3 %collective-permute-start.15 = (bf16[3,384,1024]{2,1,0:T(8,128)(2,1)}, bf16[3,384,1024]{2,1,0:T(8,128)(2,1)S(1)}, u32[]{:S(2)}, u32[]{:S(2)}) collective-permute-start(bf16[3,384,1024]{2,1,0:T(8,128)(2,1)} %bitcast.42), channel_id=1, source_target_pairs={{16,0},{0,16},{17,1},{1,17},{18,2},{2,18},{19,3},{3,19},{20,4},{4,... | collective-permute-start | bytes 7077896 | tf_op jit(solution)/shard_map/ppermute | solution.py:59
  114.9 9.3 %slice-start = ((s8[4718592]{0:T(1024)(128)(4,1)}), s8[4194304]{0:T(1024)(128)(4,1)S(1)}, s32[]{:S(2)}) async-start(s8[4718592]{0:T(1024)(128)(4,1)} %bitcast.40), calls=%async_computation | async-start | bytes 8388608
  115.3 8.9 %slice-start.1 = ((s8[4718592]{0:T(1024)(128)(4,1)}), s8[524288]{0:T(1024)(128)(4,1)S(1)}, s32[]{:S(2)}) async-start(s8[4718592]{0:T(1024)(128)(4,1)} %bitcast.40), calls=%async_computation.1 | async-start | bytes 1048576
  124.2 2.2 %copy-start.17 = (bf16[2,128,2176]{2,1,0:T(8,128)(2,1)S(1)}, bf16[2,128,2176]{2,1,0:T(8,128)(2,1)}, u32[]{:S(2)}) copy-start(bf16[2,128,2176]{2,1,0:T(8,128)(2,1)} %get-tuple-element.126) | copy-start | bytes 3342340
  126.0 18.8 %collective-permute-start.16 = (bf16[384,1024]{1,0:T(8,128)(2,1)}, bf16[384,1024]{1,0:T(8,128)(2,1)}, u32[]{:S(2)}, u32[]{:S(2)}) collective-permute-start(bf16[384,1024]{1,0:T(8,128)(2,1)} %get-tuple-element.139), channel_id=1, source_target_pairs={{0,1},{1,0},{2,3},{3,2},{4,5},{5,4},{6,7},{7,6},{8,9},{9,8},{10,11... | collective-permute-start | bytes 2359304 | tf_op jit(solution)/shard_map/ppermute | solution.py:37
  126.2 18.5 %collective-permute-start.17 = (bf16[384,1024]{1,0:T(8,128)(2,1)}, bf16[384,1024]{1,0:T(8,128)(2,1)}, u32[]{:S(2)}, u32[]{:S(2)}) collective-permute-start(bf16[384,1024]{1,0:T(8,128)(2,1)} %get-tuple-element.138), channel_id=1, source_target_pairs={{0,2},{1,3},{2,0},{3,1},{4,6},{5,7},{6,4},{7,5},{8,10},{9,11},{10,... | collective-permute-start | bytes 2359304 | tf_op jit(solution)/shard_map/ppermute | solution.py:37
  127.3 19.2 %collective-permute-start.22 = (bf16[128,2176]{1,0:T(8,128)(2,1)}, bf16[128,2176]{1,0:T(8,128)(2,1)}, u32[]{:S(2)}, u32[]{:S(2)}) collective-permute-start(bf16[128,2176]{1,0:T(8,128)(2,1)} %slice_bitcast_fusion), channel_id=1, source_target_pairs={{0,4},{1,5},{2,6},{3,7},{4,12},{5,13},{6,14},{7,15},{12,8},{13,9},... | collective-permute-start | bytes 1671176 | tf_op jit(solution)/shard_map/ppermute | solution.py:54
  137.1 11.5 %copy-start.15 = (f32[1,384,1024]{2,1,0:T(8,128)S(1)}, f32[1,384,1024]{2,1,0:T(8,128)}, u32[]{:S(2)}) copy-start(f32[1,384,1024]{2,1,0:T(8,128)} %get-tuple-element.124) | copy-start | bytes 4718596
  144.8 3.9 %collective-permute-start.18 = (bf16[384,1024]{1,0:T(8,128)(2,1)}, bf16[384,1024]{1,0:T(8,128)(2,1)S(1)}, u32[]{:S(2)}, u32[]{:S(2)}) collective-permute-start(bf16[384,1024]{1,0:T(8,128)(2,1)} %bitcast.43), channel_id=1, source_target_pairs={{16,0},{0,16},{17,1},{1,17},{18,2},{2,18},{19,3},{3,19},{20,4},{4,... | collective-permute-start | bytes 2359304 | tf_op jit(solution)/shard_map/ppermute | solution.py:59
  147.7 15.2 %copy-start.16 = (bf16[2,128,2176]{2,1,0:T(8,128)(2,1)S(1)}, bf16[2,128,2176]{2,1,0:T(8,128)(2,1)}, u32[]{:S(2)}) copy-start(bf16[2,128,2176]{2,1,0:T(8,128)(2,1)} %get-tuple-element.117) | copy-start | bytes 3342340
  147.7 15.2 %collective-permute-start.23 = (bf16[128,2176]{1,0:T(8,128)(2,1)S(1)}, bf16[128,2176]{1,0:T(8,128)(2,1)S(1)}, u32[]{:S(2)}, u32[]{:S(2)}) collective-permute-start(bf16[128,2176]{1,0:T(8,128)(2,1)S(1)} %fusion.8), channel_id=1, source_target_pairs={{0,4},{1,5},{2,6},{3,7},{4,12},{5,13},{6,14},{7,15},{12,8},{13,9},... | collective-permute-start | bytes 1671176 | tf_op jit(solution)/shard_map/ppermute | solution.py:54
  148.9 19.7 %collective-permute-start.19 = (bf16[384,1024]{1,0:T(8,128)(2,1)S(1)}, bf16[384,1024]{1,0:T(8,128)(2,1)S(1)}, u32[]{:S(2)}, u32[]{:S(2)}) collective-permute-start(bf16[384,1024]{1,0:T(8,128)(2,1)S(1)} %fusion.1), channel_id=1, source_target_pairs={{0,3},{1,2},{2,1},{3,0},{4,7},{5,6},{6,5},{7,4},{8,11},{9,10},{10,... | collective-permute-start | bytes 2359304 | tf_op jit(solution)/shard_map/ppermute | solution.py:37
  162.9 14.5 %copy-start.2 = (f32[1,1,384,2048]{3,2,1,0:T(8,128)S(1)}, f32[1,1,384,2048]{3,2,1,0:T(8,128)}, u32[]{:S(2)}) copy-start(f32[1,1,384,2048]{3,2,1,0:T(8,128)} %refs_5_.1) | copy-start | bytes 9437188
  163.1 14.3 %collective-permute-start.24 = (bf16[128,2176]{1,0:T(8,128)(2,1)S(1)}, bf16[128,2176]{1,0:T(8,128)(2,1)S(1)}, u32[]{:S(2)}, u32[]{:S(2)}) collective-permute-start(bf16[128,2176]{1,0:T(8,128)(2,1)S(1)} %fusion.7), channel_id=1, source_target_pairs={{0,4},{1,5},{2,6},{3,7},{4,12},{5,13},{6,14},{7,15},{12,8},{13,9},... | collective-permute-start | bytes 1671176 | tf_op jit(solution)/shard_map/ppermute | solution.py:54
  168.6 8.8 %copy-start.1 = (f32[1,1,384,2048]{3,2,1,0:T(8,128)S(1)}, f32[1,1,384,2048]{3,2,1,0:T(8,128)}, u32[]{:S(2)}) copy-start(f32[1,1,384,2048]{3,2,1,0:T(8,128)} %refs_4_.1) | copy-start | bytes 9437188
  170.9 6.5 %copy-start = (bf16[1,384,2048]{2,1,0:T(8,128)(2,1)S(1)}, bf16[1,384,2048]{2,1,0:T(8,128)(2,1)}, u32[]{:S(2)}) copy-start(bf16[1,384,2048]{2,1,0:T(8,128)(2,1)} %refs_6_.1) | copy-start | bytes 4718596
  170.9 6.4 %collective-permute-start.20 = (bf16[192,1024]{1,0:T(8,128)(2,1)S(1)}, bf16[192,1024]{1,0:T(8,128)(2,1)S(1)}, u32[]{:S(2)}, u32[]{:S(2)}) collective-permute-start(bf16[192,1024]{1,0:T(8,128)(2,1)S(1)} %get-tuple-element.143.refs_0_), channel_id=1, source_target_pairs={{16,0},{0,16},{17,1},{1,17},{18,2},{2,18},{19,3},{3,19},{20,4},{4,... | collective-permute-start | bytes 1179656 | tf_op jit(solution)/shard_map/ppermute | solution.py:59
  172.2 5.2 %collective-permute-start.21 = (bf16[192,1024]{1,0:T(8,128)(2,1)S(1)}, bf16[192,1024]{1,0:T(8,128)(2,1)S(1)}, u32[]{:S(2)}, u32[]{:S(2)}) collective-permute-start(bf16[192,1024]{1,0:T(8,128)(2,1)S(1)} %get-tuple-element.142.refs_1_), channel_id=1, source_target_pairs={{16,0},{0,16},{17,1},{1,17},{18,2},{2,18},{19,3},{3,19},{20,4},{4,... | collective-permute-start | bytes 1179656 | tf_op jit(solution)/shard_map/ppermute | solution.py:59
  172.9 11.8 %copy-start.22 = (s32[1,2]{1,0:T(1,128)S(1)}, s32[1,2]{1,0:T(1,128)}, u32[]{:S(2)}) copy-start(s32[1,2]{1,0:T(1,128)} %param.18) | copy-start | bytes 28
  177.4 5.7 %copy-start.18 = (bf16[128,2176]{1,0:T(8,128)(2,1)}, bf16[128,2176]{1,0:T(8,128)(2,1)S(1)}, u32[]{:S(2)}) copy-start(bf16[128,2176]{1,0:T(8,128)(2,1)S(1)} %collective-permute-done.24) | copy-start | bytes 1671172
  183.1 5.6 %collective-permute-start.25 = (bf16[384,2048]{1,0:T(8,128)(2,1)S(1)}, bf16[384,2048]{1,0:T(8,128)(2,1)}, u32[]{:S(2)}, u32[]{:S(2)}) collective-permute-start(bf16[384,2048]{1,0:T(8,128)(2,1)S(1)} %get-tuple-element.130), channel_id=1, source_target_pairs={{16,0},{0,16},{17,1},{1,17},{18,2},{2,18},{19,3},{3,19},{20,4},{4,... | collective-permute-start | bytes 4718600 | tf_op jit(solution)/shard_map/ppermute | solution.py:59
  (3 other events, 3.5 us)

commit v4 on v3

--- a/solution.py
+++ b/solution.py
@@ -229,7 +229,7 @@
             at = pl.ds(b * tok, tok)
             rows_out[b, :, pl.ds(0, model)] = dx[at, :].astype(bf16)
             rows_out[b, :, pl.ds(model, lanes)] = pr[at, :].astype(bf16)
-            copy = pltpu.make_async_copy(rows_out.at[b], outs["back"].at[b], sem_o.at[n + 2 + b])
+            copy = pltpu.make_async_copy(rows_out.at[b], outs["back%d" % b], sem_o.at[n + 2 + b])
             copy.start()
             pending.append(copy)
         for copy in pending:
@@ -252,7 +252,8 @@
         shape["send"] = ((n, max(n_dp - 1, 1), half, width), bf16)
         out_rows = (self.back, tok, model + lanes)
         if self.back:
-            shape["back"] = (out_rows, bf16)
+            for b in range(self.back):
+                shape["back%d" % b] = (out_rows[1:], bf16)
         if self.left:
             shape["dx"] = ((len(self.left) * tok, model), f32)
             shape["pr"] = ((len(self.left) * tok, lanes), f32)
@@ -351,7 +352,11 @@
     def others(value):
         return [turn(value, k) for k in range(1, n_dp)]
 
-    wide = probs.astype(f32)
+    w_gu, w_dn = w_gate_up[0], w_down[0]
+    w_own = jnp.concatenate([w_gu, w_dn.T], 1)
+    p1 = lax.dynamic_slice_in_dim(w_own, me_dp * width, width // 2, 0)
+    p2 = lax.dynamic_slice_in_dim(w_own, me_dp * width + width // 2, width // 2, 0)
+    wide = after(probs, p1, p2).astype(f32)
     ids = jnp.arange(lanes, dtype=jnp.int32)
     chosen = routes[:, :, None] == ids[None, None, :]
     p_all = jnp.sum(jnp.where(chosen, wide[:, :, None], 0.0), axis=1).astype(bf16)
@@ -362,12 +367,8 @@
         ],
         0,
     )
-    w_gu, w_dn = w_gate_up[0], w_down[0]
-    w_own = jnp.concatenate([w_gu, w_dn.T], 1)
-    p1 = lax.dynamic_slice_in_dim(w_own, me_dp * width, width // 2, 0)
-    p2 = lax.dynamic_slice_in_dim(w_own, me_dp * width + width // 2, width // 2, 0)
     held = [own, along(own)]
-    x_p1, y_p2 = hop(p1, 1), hop(p2, 2)
+    x_p1, y_p2, x_p2, y_p1 = hop(p1, 1), hop(p2, 2), hop(p2, 1), hop(p1, 2)
 
     weights = {"w0": w_own}
     make = functools.partial(Pass, tok_dev, model, half, n_dp)
@@ -383,16 +384,15 @@
             weights["w%d_%d_0" % (s, k)] = firsts[k]
             weights["w%d_%d_1" % (s, k)] = seconds[k]
 
-    p1, p2, held, x_p1, y_p2, w_own = lax.optimization_barrier((p1, p2, held, x_p1, y_p2, w_own))
+    held, w_own, x_p1, y_p2 = lax.optimization_barrier((held, w_own, x_p1, y_p2))
+    x_o1, y_o2 = others(x_p1), others(y_p2)
     weights["w0"] = w_own
-    x_p2, y_p1 = hop(p2, 1), hop(p1, 2)
     zero_pass = make([0], near[:2], [(0, 2)])
     zero = zero_pass.call(pick(zero_pass))
     while len(held) < layers - 1:
         held.append(along(held[-1]))
-    x_o1, y_o2 = others(x_p1), others(y_p2)
-
-    (x_p1, y_p2, x_p2, y_p1, x_o1, y_o2, held, zero) = lax.optimization_barrier(
+
+    x_p1, y_p2, x_p2, y_p1, x_o1, y_o2, held, zero = lax.optimization_barrier(
         (x_p1, y_p2, x_p2, y_p1, x_o1, y_o2, held, zero)
     )
     d_p2, d_p1 = hop(y_p2, 1), hop(x_p1, 2)
@@ -418,34 +418,47 @@
     first_pass = make([3], early, [(0, len(early))], len(early))
     first = first_pass.call(pick(first_pass), sums=sums)
     first, swapped, keep = lax.optimization_barrier((first, swapped, keep))
-    passing = along(first["back"][0])
-    leaving = [(keep[s] + sum(v[s].astype(f32) for v in swapped)).astype(bf16) for s in (1, 2)]
-    sent = [hop(leaving[0], 1), hop(leaving[1], 2)]
+    passing = along(first["back0"])
+    cut = half // 2
+    rows_of = [slice(0, cut), slice(cut, half)]
+
+    def leaving(r, keep, swapped):
+        total = [keep[s][r] + sum(v[s][r].astype(f32) for v in swapped) for s in (1, 2)]
+        return [hop(total[0].astype(bf16), 1), hop(total[1].astype(bf16), 2)]
+
+    sent = leaving(rows_of[0], keep, swapped)
     rest_pass = make([3], [0, last_block], [(0, 2)], 2)
     last = rest_pass.call(pick(rest_pass), sums=sums, grads=[(first, (0, 1))])
-    sent, last_keep, last_send = lax.optimization_barrier((sent, last["keep"], last["send"]))
+    sent, last_keep, last_send, keep, swapped = lax.optimization_barrier(
+        (sent, last["keep"], last["send"], keep, swapped)
+    )
 
     across = last_keep[0]
     for k in range(1, n_dp):
         across = across + turn(last_send[0, k - 1], k).astype(f32)
-    sent.append(hop(across.astype(bf16), 3))
+    sent_late = leaving(rows_of[1], keep, swapped)
+    sent_across = hop(across.astype(bf16), 3)
     for k in range(2, layers):
-        term = first["back"][k - 1] if k < last_block else last["back"][1]
+        term = first["back%d" % (k - 1)] if k < last_block else last["back1"]
+        if k == last_block:
+            sent_late[0], passing = lax.optimization_barrier((sent_late[0], passing))
         passing = along((passing.astype(f32) + term.astype(f32)).astype(bf16))
 
-    grad = keep[0] + sum(v[0].astype(f32) for v in swapped)
-    grad = (grad + sum(v.astype(f32) for v in sent)).astype(bf16)
-    cut = half // 2
-    halves = [others(grad[:cut]), others(grad[cut:])]
+    grads = []
+    for r, came in zip(rows_of, (sent, sent_late)):
+        grad = keep[0][r] + sum(v[0][r].astype(f32) for v in swapped)
+        grad = grad + sum(v.astype(f32) for v in came) + sent_across[r].astype(f32)
+        grads.append(grad.astype(bf16))
+    halves = [others(grad) for grad in grads]
     halves, passing = lax.optimization_barrier((halves, passing))
-    parts = [(grad[:cut], grad[cut:])] + list(zip(*halves))
+    parts = [tuple(grads)] + list(zip(*halves))
     new_one, new_two, w_new = adam_call(parts, leader, moment_one, moment_two, w_down)
     lead = leader[0]
     fresh = w_new
     for k in range(1, n_dp):
         fresh = jnp.where((me_dp + k) % n_dp == lead, turn(w_new, k), fresh)
 
-    total = last["back"][0].astype(f32) + passing.astype(f32)
+    total = last["back0"].astype(f32) + passing.astype(f32)
     token_grad = total[:, :model].astype(bf16)
     pair = total[:, model:]
     prob_grad = jnp.sum(jnp.where(chosen, pair[:, None, :], 0.0), axis=2).astype(bf16)

time: 193 us -> 189 us (0.979)
  waiting for transfers between devices: 72.5 us -> 68.5 us
  starting transfers between devices: 24.4 us -> 28.3 us
    ppermute x6, waiting for transfers between devices: 59.4 us -> 30.2 us  [along(): return lax.ppermute(value, 'expert', pairs)]
    ppermute x9 -> x11, waiting for transfers between devices: 12.6 us -> 35.2 us  [hop(): return lax.ppermute(value, 'expert', [(i, i ^ flip) for i in range(n)])]
    ppermute x6, starting transfers between devices: 3.94 us -> 8.44 us  [along(): return lax.ppermute(value, 'expert', pairs)]
    ppermute x11, waiting for transfers between devices: 0.43 us -> 3.13 us  [turn(): return lax.ppermute(value, 'dp', [((r + step) % n, r) for r in range(n)])]
    ppermute x9 -> x11, starting transfers between devices: 8.26 us -> 9.46 us  [hop(): return lax.ppermute(value, 'expert', [(i, i ^ flip) for i in range(n)])]
    convert_element_type x3 -> x4, other arithmetic: 4.25 us -> 3.72 us  [the longest x1 2.07 us: body(): grads.append(grad.astype(bf16))]
  transfers between devices with their start and end apart: 26 -> 28, of which waited for: 8 -> 14; matrix products, arithmetic and copies ran while one was open for 8% -> 7% of each run, Pallas kernels for 32% -> 32%
where the time goes in v4:
time: 189 us; the launch traced here: 188 us
  waiting for transfers between devices  68.5 us (36%)
  Pallas kernels  66.7 us (35%)
  starting transfers between devices  28.3 us (15%)
  other arithmetic  18.7 us (10%)
  local copies, waits for them, and re-layouts  4.48 us (2%)
    pallas_call x5, Pallas kernels, call(): pl.pallas_call(functools.partial(self.kernel, len(ins)), out_shape=[jax.S...  61.1 us
    ppermute x11, waiting for transfers between devices, hop(): return lax.ppermute(value, 'expert', [(i, i ^ flip) for i in range(n)])  35.2 us
    ppermute x6, waiting for transfers between devices, along(): return lax.ppermute(value, 'expert', pairs)  30.2 us
    ppermute x11, starting transfers between devices, turn(): return lax.ppermute(value, 'dp', [((r + step) % n, r) for r in range(n)])  10.4 us
    ppermute x11, starting transfers between devices, hop(): return lax.ppermute(value, 'expert', [(i, i ^ flip) for i in range(n)])  9.46 us
    ppermute x6, starting transfers between devices, along(): return lax.ppermute(value, 'expert', pairs)  8.44 us
    concatenate x2, other arithmetic, body(): w_own = jnp.concatenate([w_gu, w_dn.T], 1)  7.46 us
    pallas_call x1, Pallas kernels, adam_call(): pl.pallas_call(functools.partial(adam_kernel, n_dp), grid=(steps,), out_s...  5.66 us
  transfers between devices with their start and end apart: 28, of which 14 were waited for; matrix products, arithmetic and copies ran while one was open for 7% of the time, Pallas kernels for 32%

profile of v4, /device:TPU:1, one launch (start us, length us, event | category | flops | bytes accessed | tf_op | source)
XLA Modules:
  0.0 188.3 jit_solution(5862591868580783987)
XLA Ops:
  0.6 1.9 copy.19
  2.6 3.0 %fusion.4 = (bf16[512,1152]{1,0:T(8,128)(2,1)}, bf16[512,1152]{1,0:T(8,128)(2,1)}) fusion(s32[]{:T(128)S(6)} %select_n.39, bf16[2048,768]{1,0:T(8,128)(2,1)} %bitcast.39, bf16[2048,384]{1,0:T(8,128)(2,1)S(1)} %copy.19, s32[]{:T(128)S(6)} %select_n.38), kind=kLoop, calls=%fused_computation.12 | loop fusion | flops 4718592 | bytes 7077896 | tf_op jit(solution)/shard_map/concatenate | solution.py:356
  5.6 2.0 %collective-permute-start.1 = (bf16[512,1152]{1,0:T(8,128)(2,1)}, bf16[512,1152]{1,0:T(8,128)(2,1)S(1)}, u32[]{:S(2)}, u32[]{:S(2)}) collective-permute-start(bf16[512,1152]{1,0:T(8,128)(2,1)} %get-tuple-element.157), channel_id=1, source_target_pairs={{0,1},{1,0},{2,3},{3,2},{4,5},{5,4},{6,7},{7,6},{8,9},{9,8},{10,11... | collective-permute-start | bytes 3538952 | tf_op jit(solution)/shard_map/ppermute | solution.py:37
  7.6 1.2 collective-permute-start.2
  9.4 1.1 fusion.5.refs_0_
  10.6 1.3 collective-permute-start
  12.4 4.4 %pad_maximum_fusion.refs_2_.refs_3_.refs_1_ = bf16[2048,1152]{1,0:T(8,128)(2,1)} fusion(bf16[2048,384]{1,0:T(8,128)(2,1)S(1)} %copy.19, bf16[2048,768]{1,0:T(8,128)(2,1)} %bitcast.40), kind=kLoop, calls=%fused_computation.2 | loop fusion | flops 9437184 | bytes 9437184 | tf_op jit(solution)/shard_map/concatenate | solution.py:356
  16.9 19.5 %collective-permute-done.refs_1_.refs_0_ = bf16[256,2176]{1,0:T(8,128)(2,1)S(1)} collective-permute-done((bf16[256,2176]{1,0:T(8,128)(2,1)S(1)}, bf16[256,2176]{1,0:T(8,128)(2,1)S(1)}, u32[]{:S(2)}, u32[]{:S(2)}) %collective-permute-start) | collective-permute-done | bytes 1114144 | tf_op jit(solution)/shard_map/ppermute | solution.py:54
  36.4 2.2 %collective-permute-start.5 = (bf16[512,1152]{1,0:T(8,128)(2,1)S(1)}, bf16[512,1152]{1,0:T(8,128)(2,1)S(1)}, u32[]{:S(2)}, u32[]{:S(2)}) collective-permute-start(bf16[512,1152]{1,0:T(8,128)(2,1)S(1)} %collective-permute-done.1.refs_4_.refs_2_), channel_id=1, source_target_pairs={{16,0},{0,16},{17,1},{1,17},{18,2},{2,18},{19,3},{3,19},{20,4},{4,... | collective-permute-start | bytes 3538952 | tf_op jit(solution)/shard_map/ppermute | solution.py:59
  38.7 0.5 collective-permute-start.7
  39.2 8.5 %shard_map.137 = (f32[1,384,1024]{2,1,0:T(8,128)}, bf16[1,1,384,1024]{3,2,1,0:T(8,128)(2,1)}, f32[256,2048]{1,0:T(8,128)}, f32[256,128]{1,0:T(8,128)}) custom-call(bf16[256,2176]{1,0:T(8,128)(2,1)} %copy-done.3, bf16[256,2176]{1,0:T(8,128)(2,1)} %copy-done.4, bf16[2048,1152]{1,0:T(8,128)(2,1)} %pad_maximum_fusion.refs_2_.refs_3_.refs_1_), custom_call_target="tpu_custom_call" | custom-call | flops 1000 | bytes 1000 | tf_op jit(solution)/shard_map/pallas_call | solution.py:282
  47.7 11.2 %collective-permute-done.3.refs_5_.refs_3_ = bf16[512,1152]{1,0:T(8,128)(2,1)S(1)} collective-permute-done((bf16[512,1152]{1,0:T(8,128)(2,1)}, bf16[512,1152]{1,0:T(8,128)(2,1)S(1)}, u32[]{:S(2)}, u32[]{:S(2)}) %collective-permute-start.3) | collective-permute-done | bytes 1179680 | tf_op jit(solution)/shard_map/ppermute | solution.py:37
  58.9 0.8 collective-permute-done.4.refs_8_.refs_6_
  59.7 5.7 %collective-permute-done.7.refs_2_.refs_1_ = bf16[256,2176]{1,0:T(8,128)(2,1)} collective-permute-done((bf16[256,2176]{1,0:T(8,128)(2,1)S(1)}, bf16[256,2176]{1,0:T(8,128)(2,1)}, u32[]{:S(2)}, u32[]{:S(2)}) %collective-permute-start.7) | collective-permute-done | bytes 1114144 | tf_op jit(solution)/shard_map/ppermute | solution.py:54
  65.4 1.3 collective-permute-start.8
  66.8 1.3 collective-permute-start.9
  68.7 0.4 collective-permute-start.12
  69.2 1.8 collective-permute-done.9.refs_10_.refs_8_
  71.0 20.6 %shard_map.138 = (f32[3,384,1024]{2,1,0:T(8,128)}, bf16[3,1,384,1024]{3,2,1,0:T(8,128)(2,1)}, f32[384,2048]{1,0:T(8,128)}, f32[384,128]{1,0:T(8,128)}) custom-call(bf16[256,2176]{1,0:T(8,128)(2,1)} %copy-done.3, bf16[256,2176]{1,0:T(8,128)(2,1)} %copy-done.4, bf16[256,2176]{1,0:T(8,128)(2,1)} %collective-permute-done.7.refs_2_.refs_1_, ...), custom_call_target="tpu_custom_call" | custom-call | flops 1000 | bytes 1000 | tf_op jit(solution)/shard_map/pallas_call | solution.py:282
  91.7 3.8 %collective-permute-done.12.refs_0_.refs_1_ = bf16[256,2176]{1,0:T(8,128)(2,1)} collective-permute-done((bf16[256,2176]{1,0:T(8,128)(2,1)}, bf16[256,2176]{1,0:T(8,128)(2,1)}, u32[]{:S(2)}, u32[]{:S(2)}) %collective-permute-start.12) | collective-permute-done | bytes 1114144 | tf_op jit(solution)/shard_map/ppermute | solution.py:54
  96.0 1.0 collective-permute-start.13
  97.0 13.9 %shard_map.139 = (f32[3,384,1024]{2,1,0:T(8,128)}, bf16[3,1,384,1024]{3,2,1,0:T(8,128)(2,1)}, f32[128,2048]{1,0:T(8,128)}, f32[128,128]{1,0:T(8,128)}) custom-call(bf16[256,2176]{1,0:T(8,128)(2,1)} %collective-permute-done.12.refs_0_.refs_1_, bf16[2048,1152]{1,0:T(8,128)(2,1)} %pad_maximum_fusion.refs_2_.refs_3_.refs_1_, bf16[512,1152]{1,0:T(8,128)(2,1)} %copy-done.10, ...), custom_call_target="tpu_custom_call" | custom-call | flops 1000 | bytes 1000 | tf_op jit(solution)/shard_map/pallas_call | solution.py:282
  111.0 0.7 collective-permute-start.15
  112.4 8.9 %shard_map.140 = (f32[1,384,1024]{2,1,0:T(8,128)}, bf16[1,1,384,1024]{3,2,1,0:T(8,128)(2,1)}, bf16[128,2176]{1,0:T(8,128)(2,1)}, bf16[128,2176]{1,0:T(8,128)(2,1)}) custom-call(bf16[256,2176]{1,0:T(8,128)(2,1)} %copy-done.4, bf16[256,2176]{1,0:T(8,128)(2,1)} %collective-permute-done.7.refs_2_.refs_1_, bf16[512,1152]{1,0:T(8,128)(2,1)} %copy-done.6, ...), custom_call_target="tpu_custom_call" | custom-call | flops 1000 | bytes 1000 | tf_op jit(solution)/shard_map/pallas_call | solution.py:282
  121.3 0.8 collective-permute-start.22
  122.1 1.2 fusion.11
  123.3 1.2 collective-permute-start.16
  124.5 1.1 collective-permute-start.17
  125.6 9.2 %shard_map.141 = (f32[1,384,1024]{2,1,0:T(8,128)}, bf16[1,1,384,1024]{3,2,1,0:T(8,128)(2,1)}, bf16[128,2176]{1,0:T(8,128)(2,1)}, bf16[128,2176]{1,0:T(8,128)(2,1)}) custom-call(bf16[256,2176]{1,0:T(8,128)(2,1)} %copy-done.3, bf16[256,2176]{1,0:T(8,128)(2,1)} %collective-permute-done.12.refs_0_.refs_1_, bf16[512,1152]{1,0:T(8,128)(2,1)} %copy-done.6, ...), custom_call_target="tpu_custom_call" | custom-call | flops 1000 | bytes 1000 | tf_op jit(solution)/shard_map/pallas_call | solution.py:282
  134.8 1.5 collective-permute-start.18
  136.5 3.1 %collective-permute-start.23 = (bf16[128,2176]{1,0:T(8,128)(2,1)S(1)}, bf16[128,2176]{1,0:T(8,128)(2,1)S(1)}, u32[]{:S(2)}, u32[]{:S(2)}) collective-permute-start(bf16[128,2176]{1,0:T(8,128)(2,1)S(1)} %add_convert_fusion.1), channel_id=1, source_target_pairs={{0,4},{1,5},{2,6},{3,7},{4,12},{5,13},{6,14},{7,15},{12,8},{13,9},... | collective-permute-start | bytes 1671176 | tf_op jit(solution)/shard_map/ppermute | solution.py:54
  140.5 2.1 %collective-permute-start.19 = (bf16[384,1024]{1,0:T(8,128)(2,1)S(1)}, bf16[384,1024]{1,0:T(8,128)(2,1)S(1)}, u32[]{:S(2)}, u32[]{:S(2)}) collective-permute-start(bf16[384,1024]{1,0:T(8,128)(2,1)S(1)} %fusion.1), channel_id=1, source_target_pairs={{0,3},{1,2},{2,1},{3,0},{4,7},{5,6},{6,5},{7,4},{8,11},{9,10},{10,... | collective-permute-start | bytes 2359304 | tf_op jit(solution)/shard_map/ppermute | solution.py:37
  142.9 7.4 %collective-permute-done.21 = bf16[192,1024]{1,0:T(8,128)(2,1)S(1)} collective-permute-done((bf16[192,1024]{1,0:T(8,128)(2,1)S(1)}, bf16[192,1024]{1,0:T(8,128)(2,1)S(1)}, u32[]{:S(2)}, u32[]{:S(2)}) %collective-permute-start.21) | collective-permute-done | bytes 393248 | tf_op jit(solution)/shard_map/ppermute | solution.py:37
  150.3 1.3 collective-permute-done.23
  151.8 2.3 %collective-permute-start.26 = (bf16[128,2176]{1,0:T(8,128)(2,1)S(1)}, bf16[128,2176]{1,0:T(8,128)(2,1)S(1)}, u32[]{:S(2)}, u32[]{:S(2)}) collective-permute-start(bf16[128,2176]{1,0:T(8,128)(2,1)S(1)} %add_convert_fusion), channel_id=1, source_target_pairs={{0,4},{1,5},{2,6},{3,7},{4,12},{5,13},{6,14},{7,15},{12,8},{13,9},... | collective-permute-start | bytes 1671176 | tf_op jit(solution)/shard_map/ppermute | solution.py:54
  154.0 15.2 %collective-permute-done.24 = bf16[192,1024]{1,0:T(8,128)(2,1)S(1)} collective-permute-done((bf16[192,1024]{1,0:T(8,128)(2,1)S(1)}, bf16[192,1024]{1,0:T(8,128)(2,1)S(1)}, u32[]{:S(2)}, u32[]{:S(2)}) %collective-permute-start.24) | collective-permute-done | bytes 393248 | tf_op jit(solution)/shard_map/ppermute | solution.py:37
  169.2 2.1 %fusion.7 = (bf16[192,1024]{1,0:T(8,128)(2,1)S(1)}, bf16[192,1024]{1,0:T(8,128)(2,1)S(1)}) fusion(bf16[192,1024]{1,0:T(8,128)(2,1)S(1)} %collective-permute-done.24, bf16[192,1024]{1,0:T(8,128)(2,1)S(1)} %collective-permute-done.21, f32[3,384,1024]{2,1,0:T(8,128)S(1)} %copy-done.5, bf16[384,1024]{1,0:T(8,128)(2,1)S(1)} %collective-permute-done.19, ...), kind=kLoop, calls=%fused_computation.20 | loop fusion | flops 3538944 | bytes 5505024 | tf_op jit(solution)/shard_map/convert_element_type | solution.py:451
  171.3 1.8 collective-permute-start.20
  173.9 0.6 collective-permute-done.20.refs_2_
  174.4 0.6 collective-permute-done.25.refs_3_
  175.0 5.7 %shard_map.142 = (f32[1,1,384,2048]{3,2,1,0:T(8,128)}, f32[1,1,384,2048]{3,2,1,0:T(8,128)}, bf16[384,2048]{1,0:T(8,128)(2,1)S(1)}) custom-call(s32[1]{0:T(128)} %copy.22.lead_ref, bf16[192,1024]{1,0:T(8,128)(2,1)S(1)} %get-tuple-element.151.refs_0_, bf16[192,1024]{1,0:T(8,128)(2,1)S(1)} %get-tuple-element.150.refs_1_, ...), custom_call_target="tpu_custom_call" | custom-call | flops 1000 | bytes 1000 | tf_op jit(solution)/shard_map/pallas_call | solution.py:319
  180.7 0.4 collective-permute-start.27
  181.1 0.6 fusion.14
  181.7 1.3 convert_add_fusion
  183.0 0.9 slice.128
  183.9 0.4 select_reduce_fusion
  184.3 0.7 copy.21
  184.9 3.4 %fusion.2 = bf16[1,1,384,2048]{3,2,1,0:T(8,128)(2,1)} fusion(bf16[1,384,2048]{2,1,0:T(8,128)(2,1)S(1)} %copy-done, bf16[384,2048]{1,0:T(8,128)(2,1)} %collective-permute-done.27, bf16[384,2048]{1,0:T(8,128)(2,1)S(1)} %get-tuple-element.142, pred[]{:T(512)S(6)} %eq.29, pred[]{:T(512)} %bitcast.12), kind=kLoop, calls=%fused_computation.10 | loop fusion | flops 1572864 | bytes 6291458 | tf_op jit(solution)/shard_map/broadcast_in_dim | solution.py:466
  (84 shorter events, 4.9 us)
Async XLA Ops:
  2.5 6.3 %copy-start.23 = (bf16[128,8]{0,1:T(8,128)(2,1)S(1)}, bf16[128,8]{0,1:T(8,128)(2,1)}, u32[]{:S(2)}) copy-start(bf16[128,8]{0,1:T(8,128)(2,1)} %param.13) | copy-start | bytes 6148
  2.5 6.4 %copy-start.22 = (s32[128,8]{0,1:T(8,128)S(1)}, s32[128,8]{0,1:T(8,128)}, u32[]{:S(2)}) copy-start(s32[128,8]{0,1:T(8,128)} %param.12) | copy-start | bytes 12292
  2.5 6.9 %copy-start.21 = (bf16[128,2048]{1,0:T(8,128)(2,1)S(1)}, bf16[128,2048]{1,0:T(8,128)(2,1)}, u32[]{:S(2)}) copy-start(bf16[128,2048]{1,0:T(8,128)(2,1)} %param.11) | copy-start | bytes 1572868
  5.6 30.8 %collective-permute-start.1 = (bf16[512,1152]{1,0:T(8,128)(2,1)}, bf16[512,1152]{1,0:T(8,128)(2,1)S(1)}, u32[]{:S(2)}, u32[]{:S(2)}) collective-permute-start(bf16[512,1152]{1,0:T(8,128)(2,1)} %get-tuple-element.157), channel_id=1, source_target_pairs={{0,1},{1,0},{2,3},{3,2},{4,5},{5,4},{6,7},{7,6},{8,9},{9,8},{10,11... | collective-permute-start | bytes 3538952 | tf_op jit(solution)/shard_map/ppermute | solution.py:37
  7.6 28.8 %collective-permute-start.2 = (bf16[512,1152]{1,0:T(8,128)(2,1)}, bf16[512,1152]{1,0:T(8,128)(2,1)}, u32[]{:S(2)}, u32[]{:S(2)}) collective-permute-start(bf16[512,1152]{1,0:T(8,128)(2,1)} %get-tuple-element.156), channel_id=1, source_target_pairs={{0,2},{1,3},{2,0},{3,1},{4,6},{5,7},{6,4},{7,5},{8,10},{9,11},{10,... | collective-permute-start | bytes 3538952 | tf_op jit(solution)/shard_map/ppermute | solution.py:37
  10.6 6.3 %copy-start.3 = (bf16[256,2176]{1,0:T(8,128)(2,1)}, bf16[256,2176]{1,0:T(8,128)(2,1)S(1)}, u32[]{:S(2)}) copy-start(bf16[256,2176]{1,0:T(8,128)(2,1)S(1)} %fusion.5.refs_0_) | copy-start | bytes 3342340
  10.6 25.8 %collective-permute-start = (bf16[256,2176]{1,0:T(8,128)(2,1)S(1)}, bf16[256,2176]{1,0:T(8,128)(2,1)S(1)}, u32[]{:S(2)}, u32[]{:S(2)}) collective-permute-start(bf16[256,2176]{1,0:T(8,128)(2,1)S(1)} %fusion.5.refs_0_), channel_id=1, source_target_pairs={{0,4},{1,5},{2,6},{3,7},{4,12},{5,13},{6,14},{7,15},{12,8},{13,9},... | collective-permute-start | bytes 3342344 | tf_op jit(solution)/shard_map/ppermute | solution.py:54
  11.9 47.0 %collective-permute-start.3 = (bf16[512,1152]{1,0:T(8,128)(2,1)}, bf16[512,1152]{1,0:T(8,128)(2,1)S(1)}, u32[]{:S(2)}, u32[]{:S(2)}) collective-permute-start(bf16[512,1152]{1,0:T(8,128)(2,1)} %get-tuple-element.156), channel_id=1, source_target_pairs={{0,1},{1,0},{2,3},{3,2},{4,5},{5,4},{6,7},{7,6},{8,9},{9,8},{10,11... | collective-permute-start | bytes 3538952 | tf_op jit(solution)/shard_map/ppermute | solution.py:37
  12.2 47.5 %collective-permute-start.4 = (bf16[512,1152]{1,0:T(8,128)(2,1)}, bf16[512,1152]{1,0:T(8,128)(2,1)S(1)}, u32[]{:S(2)}, u32[]{:S(2)}) collective-permute-start(bf16[512,1152]{1,0:T(8,128)(2,1)} %get-tuple-element.157), channel_id=1, source_target_pairs={{0,2},{1,3},{2,0},{3,1},{4,6},{5,7},{6,4},{7,5},{8,10},{9,11},{10,... | collective-permute-start | bytes 3538952 | tf_op jit(solution)/shard_map/ppermute | solution.py:37
  36.4 2.8 %copy-start.4 = (bf16[256,2176]{1,0:T(8,128)(2,1)}, bf16[256,2176]{1,0:T(8,128)(2,1)S(1)}, u32[]{:S(2)}) copy-start(bf16[256,2176]{1,0:T(8,128)(2,1)S(1)} %collective-permute-done.refs_1_.refs_0_) | copy-start | bytes 3342340
  36.4 31.7 %copy-start.10 = (bf16[512,1152]{1,0:T(8,128)(2,1)}, bf16[512,1152]{1,0:T(8,128)(2,1)S(1)}, u32[]{:S(2)}) copy-start(bf16[512,1152]{1,0:T(8,128)(2,1)S(1)} %collective-permute-done.1.refs_4_.refs_2_) | copy-start | bytes 3538948
  36.4 29.0 %collective-permute-start.5 = (bf16[512,1152]{1,0:T(8,128)(2,1)S(1)}, bf16[512,1152]{1,0:T(8,128)(2,1)S(1)}, u32[]{:S(2)}, u32[]{:S(2)}) collective-permute-start(bf16[512,1152]{1,0:T(8,128)(2,1)S(1)} %collective-permute-done.1.refs_4_.refs_2_), channel_id=1, source_target_pairs={{16,0},{0,16},{17,1},{1,17},{18,2},{2,18},{19,3},{3,19},{20,4},{4,... | collective-permute-start | bytes 3538952 | tf_op jit(solution)/shard_map/ppermute | solution.py:59
  38.6 26.8 %collective-permute-start.6 = (bf16[512,1152]{1,0:T(8,128)(2,1)}, bf16[512,1152]{1,0:T(8,128)(2,1)S(1)}, u32[]{:S(2)}, u32[]{:S(2)}) collective-permute-start(bf16[512,1152]{1,0:T(8,128)(2,1)} %collective-permute-done.2.refs_9_.refs_7_), channel_id=1, source_target_pairs={{16,0},{0,16},{17,1},{1,17},{18,2},{2,18},{19,3},{3,19},{20,4},{4,... | collective-permute-start | bytes 3538952 | tf_op jit(solution)/shard_map/ppermute | solution.py:59
  38.7 26.7 %collective-permute-start.7 = (bf16[256,2176]{1,0:T(8,128)(2,1)S(1)}, bf16[256,2176]{1,0:T(8,128)(2,1)}, u32[]{:S(2)}, u32[]{:S(2)}) collective-permute-start(bf16[256,2176]{1,0:T(8,128)(2,1)S(1)} %collective-permute-done.refs_1_.refs_0_), channel_id=1, source_target_pairs={{0,4},{1,5},{2,6},{3,7},{4,12},{5,13},{6,14},{7,15},{12,8},{13,9},... | collective-permute-start | bytes 3342344 | tf_op jit(solution)/shard_map/ppermute | solution.py:54
  58.9 12.1 %copy-start.11 = (bf16[512,1152]{1,0:T(8,128)(2,1)}, bf16[512,1152]{1,0:T(8,128)(2,1)S(1)}, u32[]{:S(2)}) copy-start(bf16[512,1152]{1,0:T(8,128)(2,1)S(1)} %collective-permute-done.3.refs_5_.refs_3_) | copy-start | bytes 3538948
  59.7 11.3 %copy-start.12 = (bf16[512,1152]{1,0:T(8,128)(2,1)}, bf16[512,1152]{1,0:T(8,128)(2,1)S(1)}, u32[]{:S(2)}) copy-start(bf16[512,1152]{1,0:T(8,128)(2,1)S(1)} %collective-permute-done.4.refs_8_.refs_6_) | copy-start | bytes 3538948
  65.4 3.8 %collective-permute-start.8 = (bf16[512,1152]{1,0:T(8,128)(2,1)S(1)}, bf16[512,1152]{1,0:T(8,128)(2,1)S(1)}, u32[]{:S(2)}, u32[]{:S(2)}) collective-permute-start(bf16[512,1152]{1,0:T(8,128)(2,1)S(1)} %collective-permute-done.3.refs_5_.refs_3_), channel_id=1, source_target_pairs={{16,0},{0,16},{17,1},{1,17},{18,2},{2,18},{19,3},{3,19},{20,4},{4,... | collective-permute-start | bytes 3538952 | tf_op jit(solution)/shard_map/ppermute | solution.py:59
  66.8 4.2 %collective-permute-start.9 = (bf16[512,1152]{1,0:T(8,128)(2,1)S(1)}, bf16[512,1152]{1,0:T(8,128)(2,1)}, u32[]{:S(2)}, u32[]{:S(2)}) collective-permute-start(bf16[512,1152]{1,0:T(8,128)(2,1)S(1)} %collective-permute-done.4.refs_8_.refs_6_), channel_id=1, source_target_pairs={{16,0},{0,16},{17,1},{1,17},{18,2},{2,18},{19,3},{3,19},{20,4},{4,... | collective-permute-start | bytes 3538952 | tf_op jit(solution)/shard_map/ppermute | solution.py:59
  68.1 27.7 %collective-permute-start.10 = (bf16[512,1152]{1,0:T(8,128)(2,1)S(1)}, bf16[512,1152]{1,0:T(8,128)(2,1)S(1)}, u32[]{:S(2)}, u32[]{:S(2)}) collective-permute-start(bf16[512,1152]{1,0:T(8,128)(2,1)S(1)} %collective-permute-done.1.refs_4_.refs_2_), channel_id=1, source_target_pairs={{0,2},{1,3},{2,0},{3,1},{4,6},{5,7},{6,4},{7,5},{8,10},{9,11},{10,... | collective-permute-start | bytes 3538952 | tf_op jit(solution)/shard_map/ppermute | solution.py:37
  68.4 27.6 %collective-permute-start.11 = (bf16[512,1152]{1,0:T(8,128)(2,1)}, bf16[512,1152]{1,0:T(8,128)(2,1)S(1)}, u32[]{:S(2)}, u32[]{:S(2)}) collective-permute-start(bf16[512,1152]{1,0:T(8,128)(2,1)} %collective-permute-done.2.refs_9_.refs_7_), channel_id=1, source_target_pairs={{0,1},{1,0},{2,3},{3,2},{4,5},{5,4},{6,7},{7,6},{8,9},{9,8},{10,11... | collective-permute-start | bytes 3538952 | tf_op jit(solution)/shard_map/ppermute | solution.py:37
  68.7 26.8 %collective-permute-start.12 = (bf16[256,2176]{1,0:T(8,128)(2,1)}, bf16[256,2176]{1,0:T(8,128)(2,1)}, u32[]{:S(2)}, u32[]{:S(2)}) collective-permute-start(bf16[256,2176]{1,0:T(8,128)(2,1)} %collective-permute-done.7.refs_2_.refs_1_), channel_id=1, source_target_pairs={{0,4},{1,5},{2,6},{3,7},{4,12},{5,13},{6,14},{7,15},{12,8},{13,9},... | collective-permute-start | bytes 3342344 | tf_op jit(solution)/shard_map/ppermute | solution.py:54
  95.8 15.2 %copy-start.6 = (bf16[512,1152]{1,0:T(8,128)(2,1)}, bf16[512,1152]{1,0:T(8,128)(2,1)S(1)}, u32[]{:S(2)}) copy-start(bf16[512,1152]{1,0:T(8,128)(2,1)S(1)} %collective-permute-done.10.refs_2_) | copy-start | bytes 3538948
  96.0 14.9 %copy-start.7 = (bf16[512,1152]{1,0:T(8,128)(2,1)}, bf16[512,1152]{1,0:T(8,128)(2,1)S(1)}, u32[]{:S(2)}) copy-start(bf16[512,1152]{1,0:T(8,128)(2,1)S(1)} %collective-permute-done.11.refs_3_) | copy-start | bytes 3538948
  96.0 14.9 %collective-permute-start.13 = (bf16[512,1152]{1,0:T(8,128)(2,1)S(1)}, bf16[512,1152]{1,0:T(8,128)(2,1)S(1)}, u32[]{:S(2)}, u32[]{:S(2)}) collective-permute-start(bf16[512,1152]{1,0:T(8,128)(2,1)S(1)} %collective-permute-done.10.refs_2_), channel_id=1, source_target_pairs={{16,0},{0,16},{17,1},{1,17},{18,2},{2,18},{19,3},{3,19},{20,4},{4,... | collective-permute-start | bytes 3538952 | tf_op jit(solution)/shard_map/ppermute | solution.py:59
  97.0 14.0 %collective-permute-start.14 = (bf16[512,1152]{1,0:T(8,128)(2,1)S(1)}, bf16[512,1152]{1,0:T(8,128)(2,1)S(1)}, u32[]{:S(2)}, u32[]{:S(2)}) collective-permute-start(bf16[512,1152]{1,0:T(8,128)(2,1)S(1)} %collective-permute-done.11.refs_3_), channel_id=1, source_target_pairs={{16,0},{0,16},{17,1},{1,17},{18,2},{2,18},{19,3},{3,19},{20,4},{4,... | collective-permute-start | bytes 3538952 | tf_op jit(solution)/shard_map/ppermute | solution.py:59
  111.0 10.3 %collective-permute-start.15 = (bf16[3,384,1024]{2,1,0:T(8,128)(2,1)}, bf16[3,384,1024]{2,1,0:T(8,128)(2,1)S(1)}, u32[]{:S(2)}, u32[]{:S(2)}) collective-permute-start(bf16[3,384,1024]{2,1,0:T(8,128)(2,1)} %bitcast.41), channel_id=1, source_target_pairs={{16,0},{0,16},{17,1},{1,17},{18,2},{2,18},{19,3},{3,19},{20,4},{4,... | collective-permute-start | bytes 7077896 | tf_op jit(solution)/shard_map/ppermute | solution.py:59
  112.4 9.7 %copy-start.5 = (f32[3,384,1024]{2,1,0:T(8,128)S(1)}, f32[3,384,1024]{2,1,0:T(8,128)}, u32[]{:S(2)}) copy-start(f32[3,384,1024]{2,1,0:T(8,128)} %get-tuple-element.128) | copy-start | bytes 14155780
  121.3 18.3 %copy-start.16 = (bf16[3,384,1024]{2,1,0:T(8,128)(2,1)}, bf16[3,384,1024]{2,1,0:T(8,128)(2,1)S(1)}, u32[]{:S(2)}) copy-start(bf16[3,384,1024]{2,1,0:T(8,128)(2,1)S(1)} %collective-permute-done.15) | copy-start | bytes 7077892
  121.3 15.0 %collective-permute-start.22 = (bf16[128,2176]{1,0:T(8,128)(2,1)}, bf16[128,2176]{1,0:T(8,128)(2,1)S(1)}, u32[]{:S(2)}, u32[]{:S(2)}) collective-permute-start(bf16[128,2176]{1,0:T(8,128)(2,1)} %get-tuple-element.134), channel_id=1, source_target_pairs={{0,4},{1,5},{2,6},{3,7},{4,12},{5,13},{6,14},{7,15},{12,8},{13,9},... | collective-permute-start | bytes 1671176 | tf_op jit(solution)/shard_map/ppermute | solution.py:54
  123.3 11.5 %collective-permute-start.16 = (bf16[192,1024]{1,0:T(8,128)(2,1)}, bf16[192,1024]{1,0:T(8,128)(2,1)}, u32[]{:S(2)}, u32[]{:S(2)}) collective-permute-start(bf16[192,1024]{1,0:T(8,128)(2,1)} %get-tuple-element.155), channel_id=1, source_target_pairs={{0,1},{1,0},{2,3},{3,2},{4,5},{5,4},{6,7},{7,6},{8,9},{9,8},{10,11... | collective-permute-start | bytes 1179656 | tf_op jit(solution)/shard_map/ppermute | solution.py:37
  124.5 11.9 %copy-start.20 = (bf16[128,2176]{1,0:T(8,128)(2,1)S(1)}, bf16[128,2176]{1,0:T(8,128)(2,1)}, u32[]{:S(2)}) copy-start(bf16[128,2176]{1,0:T(8,128)(2,1)} %get-tuple-element.135) | copy-start | bytes 1671172
  124.5 10.3 %collective-permute-start.17 = (bf16[192,1024]{1,0:T(8,128)(2,1)}, bf16[192,1024]{1,0:T(8,128)(2,1)}, u32[]{:S(2)}, u32[]{:S(2)}) collective-permute-start(bf16[192,1024]{1,0:T(8,128)(2,1)} %get-tuple-element.154), channel_id=1, source_target_pairs={{0,2},{1,3},{2,0},{3,1},{4,6},{5,7},{6,4},{7,5},{8,10},{9,11},{10,... | collective-permute-start | bytes 1179656 | tf_op jit(solution)/shard_map/ppermute | solution.py:37
  134.8 5.4 %collective-permute-start.18 = (bf16[384,1024]{1,0:T(8,128)(2,1)}, bf16[384,1024]{1,0:T(8,128)(2,1)S(1)}, u32[]{:S(2)}, u32[]{:S(2)}) collective-permute-start(bf16[384,1024]{1,0:T(8,128)(2,1)} %bitcast.42), channel_id=1, source_target_pairs={{16,0},{0,16},{17,1},{1,17},{18,2},{2,18},{19,3},{3,19},{20,4},{4,... | collective-permute-start | bytes 2359304 | tf_op jit(solution)/shard_map/ppermute | solution.py:59
  136.5 3.7 %copy-start.17 = (f32[1,384,1024]{2,1,0:T(8,128)S(1)}, f32[1,384,1024]{2,1,0:T(8,128)}, u32[]{:S(2)}) copy-start(f32[1,384,1024]{2,1,0:T(8,128)} %get-tuple-element.132) | copy-start | bytes 4718596
  136.5 15.1 %collective-permute-start.23 = (bf16[128,2176]{1,0:T(8,128)(2,1)S(1)}, bf16[128,2176]{1,0:T(8,128)(2,1)S(1)}, u32[]{:S(2)}, u32[]{:S(2)}) collective-permute-start(bf16[128,2176]{1,0:T(8,128)(2,1)S(1)} %add_convert_fusion.1), channel_id=1, source_target_pairs={{0,4},{1,5},{2,6},{3,7},{4,12},{5,13},{6,14},{7,15},{12,8},{13,9},... | collective-permute-start | bytes 1671176 | tf_op jit(solution)/shard_map/ppermute | solution.py:54
  139.9 11.8 %copy-start.19 = (bf16[128,2176]{1,0:T(8,128)(2,1)S(1)}, bf16[128,2176]{1,0:T(8,128)(2,1)}, u32[]{:S(2)}) copy-start(bf16[128,2176]{1,0:T(8,128)(2,1)} %get-tuple-element.138) | copy-start | bytes 1671172
  139.9 10.5 %collective-permute-start.21 = (bf16[192,1024]{1,0:T(8,128)(2,1)S(1)}, bf16[192,1024]{1,0:T(8,128)(2,1)S(1)}, u32[]{:S(2)}, u32[]{:S(2)}) collective-permute-start(bf16[192,1024]{1,0:T(8,128)(2,1)S(1)} %get-tuple-element.152), channel_id=1, source_target_pairs={{0,1},{1,0},{2,3},{3,2},{4,5},{5,4},{6,7},{7,6},{8,9},{9,8},{10,11... | collective-permute-start | bytes 1179656 | tf_op jit(solution)/shard_map/ppermute | solution.py:37
  140.2 34.8 %copy-start.2 = (f32[1,1,384,2048]{3,2,1,0:T(8,128)S(1)}, f32[1,1,384,2048]{3,2,1,0:T(8,128)}, u32[]{:S(2)}) copy-start(f32[1,1,384,2048]{3,2,1,0:T(8,128)} %refs_5_.1) | copy-start | bytes 9437188
  140.5 28.7 %collective-permute-start.19 = (bf16[384,1024]{1,0:T(8,128)(2,1)S(1)}, bf16[384,1024]{1,0:T(8,128)(2,1)S(1)}, u32[]{:S(2)}, u32[]{:S(2)}) collective-permute-start(bf16[384,1024]{1,0:T(8,128)(2,1)S(1)} %fusion.1), channel_id=1, source_target_pairs={{0,3},{1,2},{2,1},{3,0},{4,7},{5,6},{6,5},{7,4},{8,11},{9,10},{10,... | collective-permute-start | bytes 2359304 | tf_op jit(solution)/shard_map/ppermute | solution.py:37
  142.6 26.6 %collective-permute-start.24 = (bf16[192,1024]{1,0:T(8,128)(2,1)S(1)}, bf16[192,1024]{1,0:T(8,128)(2,1)S(1)}, u32[]{:S(2)}, u32[]{:S(2)}) collective-permute-start(bf16[192,1024]{1,0:T(8,128)(2,1)S(1)} %get-tuple-element.153), channel_id=1, source_target_pairs={{0,2},{1,3},{2,0},{3,1},{4,6},{5,7},{6,4},{7,5},{8,10},{9,11},{10,... | collective-permute-start | bytes 1179656 | tf_op jit(solution)/shard_map/ppermute | solution.py:37
  151.8 23.3 %copy-start = (bf16[1,384,2048]{2,1,0:T(8,128)(2,1)S(1)}, bf16[1,384,2048]{2,1,0:T(8,128)(2,1)}, u32[]{:S(2)}) copy-start(bf16[1,384,2048]{2,1,0:T(8,128)(2,1)} %refs_6_.1) | copy-start | bytes 4718596
  151.8 23.2 %copy-start.1 = (f32[1,1,384,2048]{3,2,1,0:T(8,128)S(1)}, f32[1,1,384,2048]{3,2,1,0:T(8,128)}, u32[]{:S(2)}) copy-start(f32[1,1,384,2048]{3,2,1,0:T(8,128)} %refs_4_.1) | copy-start | bytes 9437188
  151.8 22.1 %collective-permute-start.26 = (bf16[128,2176]{1,0:T(8,128)(2,1)S(1)}, bf16[128,2176]{1,0:T(8,128)(2,1)S(1)}, u32[]{:S(2)}, u32[]{:S(2)}) collective-permute-start(bf16[128,2176]{1,0:T(8,128)(2,1)S(1)} %add_convert_fusion), channel_id=1, source_target_pairs={{0,4},{1,5},{2,6},{3,7},{4,12},{5,13},{6,14},{7,15},{12,8},{13,9},... | collective-permute-start | bytes 1671176 | tf_op jit(solution)/shard_map/ppermute | solution.py:54
  171.3 3.2 %collective-permute-start.20 = (bf16[192,1024]{1,0:T(8,128)(2,1)S(1)}, bf16[192,1024]{1,0:T(8,128)(2,1)S(1)}, u32[]{:S(2)}, u32[]{:S(2)}) collective-permute-start(bf16[192,1024]{1,0:T(8,128)(2,1)S(1)} %get-tuple-element.151.refs_0_), channel_id=1, source_target_pairs={{16,0},{0,16},{17,1},{1,17},{18,2},{2,18},{19,3},{3,19},{20,4},{4,... | collective-permute-start | bytes 1179656 | tf_op jit(solution)/shard_map/ppermute | solution.py:59
  173.1 1.9 %collective-permute-start.25 = (bf16[192,1024]{1,0:T(8,128)(2,1)S(1)}, bf16[192,1024]{1,0:T(8,128)(2,1)S(1)}, u32[]{:S(2)}, u32[]{:S(2)}) collective-permute-start(bf16[192,1024]{1,0:T(8,128)(2,1)S(1)} %get-tuple-element.150.refs_1_), channel_id=1, source_target_pairs={{16,0},{0,16},{17,1},{1,17},{18,2},{2,18},{19,3},{3,19},{20,4},{4,... | collective-permute-start | bytes 1179656 | tf_op jit(solution)/shard_map/ppermute | solution.py:59
  173.8 7.2 %copy-start.24 = (s32[1,2]{1,0:T(1,128)S(1)}, s32[1,2]{1,0:T(1,128)}, u32[]{:S(2)}) copy-start(s32[1,2]{1,0:T(1,128)} %param.18) | copy-start | bytes 28
  173.9 6.8 %copy-start.18 = (bf16[128,2176]{1,0:T(8,128)(2,1)}, bf16[128,2176]{1,0:T(8,128)(2,1)S(1)}, u32[]{:S(2)}) copy-start(bf16[128,2176]{1,0:T(8,128)(2,1)S(1)} %collective-permute-done.26) | copy-start | bytes 1671172
  180.7 4.3 %collective-permute-start.27 = (bf16[384,2048]{1,0:T(8,128)(2,1)S(1)}, bf16[384,2048]{1,0:T(8,128)(2,1)}, u32[]{:S(2)}, u32[]{:S(2)}) collective-permute-start(bf16[384,2048]{1,0:T(8,128)(2,1)S(1)} %get-tuple-element.142), channel_id=1, source_target_pairs={{16,0},{0,16},{17,1},{1,17},{18,2},{2,18},{19,3},{3,19},{20,4},{4,... | collective-permute-start | bytes 4718600 | tf_op jit(solution)/shard_map/ppermute | solution.py:59
  (5 other events, 7.1 us)

commit v5 on v4

--- a/solution.py
+++ b/solution.py
@@ -1,4 +1,5 @@
 import functools
+import math
 import jax
 import jax.numpy as jnp
 from jax import lax
@@ -94,12 +95,12 @@
 
         def row_copies(b):
             ref, at = ins["t%d" % blocks[b]], pl.ds(b * tok, tok)
-            cols = pl.ds(0, model)
+            first, second = pl.ds(0, model), pl.ds(model, model)
             return (
-                pltpu.make_async_copy(ref.at[pl.ds(0, tok), cols], xs.at[at], sem_t.at[b, 0]),
-                pltpu.make_async_copy(ref.at[pl.ds(tok, tok), cols], ys.at[at], sem_t.at[b, 1]),
+                pltpu.make_async_copy(ref.at[:, first], xs.at[at], sem_t.at[b, 0]),
+                pltpu.make_async_copy(ref.at[:, second], ys.at[at], sem_t.at[b, 1]),
                 pltpu.make_async_copy(
-                    ref.at[pl.ds(0, tok), pl.ds(model, lanes)], ps.at[at], sem_t.at[b, 2]
+                    ref.at[:, pl.ds(2 * model, lanes)], ps.at[at], sem_t.at[b, 2]
                 ),
             )
 
@@ -291,10 +292,69 @@
         return dict(zip(shape, out))
 
 
-def adam_kernel(n_dp, lead_ref, *refs):
+def pack_kernel(n_dp, x_ref, y_ref, routes, probs, gu_ref, dn_ref, p1, p2, own, *scratch):
+    wide, turned, rows, sem = scratch
+    tok, model = x_ref.shape
+    part, half = wide.shape[0], turned.shape[0]
+    at = pl.ds(pl.multiple_of(lax.axis_index("dp") * part, part), part)
+    copies = [
+        pltpu.make_async_copy(dn_ref.at[0, :, at], turned, sem.at[0]),
+        pltpu.make_async_copy(gu_ref.at[0, at], wide.at[:, pl.ds(0, 2 * half)], sem.at[1]),
+        pltpu.make_async_copy(x_ref, rows.at[:, pl.ds(0, model)], sem.at[2]),
+        pltpu.make_async_copy(y_ref, rows.at[:, pl.ds(model, model)], sem.at[3]),
+    ]
+    for copy in copies:
+        copy.start()
+    expert = lax.broadcasted_iota(jnp.int32, (lanes, tok), 0)
+    named = jnp.zeros((lanes, tok), f32)
+    p = probs[...].astype(f32)
+    for k in range(routes.shape[0]):
+        named = named + jnp.where(expert == routes[k : k + 1, :], p[k : k + 1, :], 0.0)
+    rows[:, 2 * model :] = jnp.transpose(named).astype(bf16)
+    copies[0].wait()
+    wide[:, 2 * half :] = jnp.transpose(turned[...])
+    copies[1].wait()
+    first, second = pl.ds(0, part // 2), pl.ds(part // 2, part // 2)
+    leaving = [
+        pltpu.make_async_copy(wide.at[first], p1, sem.at[4]),
+        pltpu.make_async_copy(wide.at[second], p2, sem.at[5]),
+        pltpu.make_async_copy(rows, own, sem.at[6]),
+    ]
+    leaving[0].start()
+    leaving[1].start()
+    copies[2].wait()
+    copies[3].wait()
+    leaving[2].start()
+    for copy in leaving:
+        copy.wait()
+
+
+def pack(tokens, out_grad, routes, probs, w_gate_up, w_down, n_dp):
+    tok, model = tokens.shape
+    half = w_down.shape[1]
+    part = model // n_dp
+    piece = jax.ShapeDtypeStruct((part // 2, 3 * half), bf16)
+    anywhere, inside = pl.BlockSpec(memory_space=pl.ANY), pl.BlockSpec(memory_space=pltpu.VMEM)
+    return pl.pallas_call(
+        functools.partial(pack_kernel, n_dp),
+        out_shape=[piece, piece, jax.ShapeDtypeStruct((tok, 2 * model + lanes), bf16)],
+        in_specs=[anywhere, anywhere, inside, inside, anywhere, anywhere],
+        out_specs=[anywhere] * 3,
+        scratch_shapes=[
+            pltpu.VMEM((part, 3 * half), bf16),
+            pltpu.VMEM((half, part), bf16),
+            pltpu.VMEM((tok, 2 * model + lanes), bf16),
+            pltpu.SemaphoreType.DMA((7,)),
+        ],
+        compiler_params=pltpu.CompilerParams(vmem_limit_bytes=56 * 2**20),
+        cost_estimate=pl.CostEstimate(flops=1000, bytes_accessed=1000, transcendentals=0),
+    )(tokens, out_grad, routes.T, probs.T, w_gate_up, w_down)
+
+
+def adam_kernel(n_dp, cut, lead_ref, *refs):
     grads = refs[: 2 * n_dp]
     m_ref, v_ref, w_ref, m_out, v_out, w_out = refs[2 * n_dp :]
-    upper = pl.program_id(0) < pl.num_programs(0) // 2
+    upper = pl.program_id(0) < cut
     me_dp = lax.axis_index("dp")
     width = grads[0].shape[1]
     is_lead = lead_ref[0] == me_dp
@@ -311,13 +371,13 @@
 
 def adam_call(parts, leader, moment_one, moment_two, w_down):
     half, model = w_down.shape[1:]
-    step = 48 if half % 96 == 0 else half // 2
-    steps = half // step
+    step = math.gcd(64, math.gcd(*[part.shape[0] for part in parts[0]]))
+    steps, cut = half // step, parts[0][0].shape[0] // step
     n_dp = len(parts)
     width = model // n_dp
     wide = pl.BlockSpec((1, 1, step, model), lambda i: (0, 0, i, 0))
     return pl.pallas_call(
-        functools.partial(adam_kernel, n_dp),
+        functools.partial(adam_kernel, n_dp, cut),
         grid=(steps,),
         out_shape=[
             jax.ShapeDtypeStruct(moment_one.shape, f32),
@@ -326,8 +386,8 @@
         ],
         in_specs=[pl.BlockSpec(memory_space=pltpu.SMEM)]
         + [
-            pl.BlockSpec((step, width), lambda i: (jnp.minimum(i, steps // 2 - 1), 0)),
-            pl.BlockSpec((step, width), lambda i: (jnp.maximum(i - steps // 2, 0), 0)),
+            pl.BlockSpec((step, width), lambda i: (jnp.minimum(i, cut - 1), 0)),
+            pl.BlockSpec((step, width), lambda i: (jnp.maximum(i - cut, 0), 0)),
         ]
         * n_dp
         + [wide, wide, pl.BlockSpec((1, step, model), lambda i: (0, i, 0))],
@@ -352,21 +412,9 @@
     def others(value):
         return [turn(value, k) for k in range(1, n_dp)]
 
-    w_gu, w_dn = w_gate_up[0], w_down[0]
+    p1, p2, own = pack(tokens, out_grad, routes, probs, w_gate_up, w_down, n_dp)
+    w_gu, w_dn = w_gate_up[0], after(w_down, own)[0]
     w_own = jnp.concatenate([w_gu, w_dn.T], 1)
-    p1 = lax.dynamic_slice_in_dim(w_own, me_dp * width, width // 2, 0)
-    p2 = lax.dynamic_slice_in_dim(w_own, me_dp * width + width // 2, width // 2, 0)
-    wide = after(probs, p1, p2).astype(f32)
-    ids = jnp.arange(lanes, dtype=jnp.int32)
-    chosen = routes[:, :, None] == ids[None, None, :]
-    p_all = jnp.sum(jnp.where(chosen, wide[:, :, None], 0.0), axis=1).astype(bf16)
-    own = jnp.concatenate(
-        [
-            jnp.concatenate([tokens, p_all], 1),
-            jnp.concatenate([out_grad, jnp.zeros_like(p_all)], 1),
-        ],
-        0,
-    )
     held = [own, along(own)]
     x_p1, y_p2, x_p2, y_p1 = hop(p1, 1), hop(p2, 2), hop(p2, 1), hop(p1, 2)
 
@@ -419,7 +467,7 @@
     first = first_pass.call(pick(first_pass), sums=sums)
     first, swapped, keep = lax.optimization_barrier((first, swapped, keep))
     passing = along(first["back0"])
-    cut = half // 2
+    cut = half * 2 // 3
     rows_of = [slice(0, cut), slice(cut, half)]
 
     def leaving(r, keep, swapped):
@@ -461,6 +509,7 @@
     total = last["back0"].astype(f32) + passing.astype(f32)
     token_grad = total[:, :model].astype(bf16)
     pair = total[:, model:]
+    chosen = routes[:, :, None] == jnp.arange(lanes, dtype=jnp.int32)[None, None, :]
     prob_grad = jnp.sum(jnp.where(chosen, pair[:, None, :], 0.0), axis=2).astype(bf16)
     is_live = replicas[0][me_dp] == 1
     new_down = jnp.where(is_live, fresh, w_dn)[None, None]

time: 189 us -> 186 us (0.984)
  waiting for transfers between devices: 68.5 us -> 62.4 us
  Pallas kernels: 66.7 us -> 70.8 us
    pallas_call x1 -> x2, Pallas kernels: 5.66 us -> 9.6 us  [the longest x1 5.22 us: adam_call(): pl.pallas_call(functools.partial(adam_kernel, n_dp, cut), grid=(steps,),...]
    ppermute x6, waiting for transfers between devices: 30.2 us -> 27.4 us  [along(): return lax.ppermute(value, 'expert', pairs)]
    ppermute x11, waiting for transfers between devices: 35.2 us -> 32.6 us  [hop(): return lax.ppermute(value, 'expert', [(i, i ^ flip) for i in range(n)])]
    concatenate x2 -> x1, other arithmetic: 7.46 us -> 4.88 us  [body(): w_own = jnp.concatenate([w_gu, w_dn.T], 1)]
    convert_element_type x2, other arithmetic: 1.4 us -> 3.7 us  [leaving(): return [hop(total[0].astype(bf16), 1), hop(total[1].astype(bf16), 2)]]
  transfers between devices with their start and end apart: 28 -> 28, of which waited for: 14 -> 15; matrix products, arithmetic and copies ran while one was open for 7% -> 9% of each run, Pallas kernels for 32% -> 33%
where the time goes in v5:
time: 186 us
  Pallas kernels  70.8 us (38%)
  waiting for transfers between devices  62.4 us (34%)
  starting transfers between devices  29.4 us (16%)
  other arithmetic  17.8 us (10%)
  local copies, waits for them, and re-layouts  4.12 us (2%)
    pallas_call x5, Pallas kernels, call(): pl.pallas_call(functools.partial(self.kernel, len(ins)), out_shape=[jax.S...  61.2 us
    ppermute x11, waiting for transfers between devices, hop(): return lax.ppermute(value, 'expert', [(i, i ^ flip) for i in range(n)])  32.6 us
    ppermute x6, waiting for transfers between devices, along(): return lax.ppermute(value, 'expert', pairs)  27.4 us
    ppermute x11, starting transfers between devices, turn(): return lax.ppermute(value, 'dp', [((r + step) % n, r) for r in range(n)])  11.3 us
    ppermute x6, starting transfers between devices, along(): return lax.ppermute(value, 'expert', pairs)  9.32 us
    ppermute x11, starting transfers between devices, hop(): return lax.ppermute(value, 'expert', [(i, i ^ flip) for i in range(n)])  8.85 us
    pallas_call x1, Pallas kernels, adam_call(): pl.pallas_call(functools.partial(adam_kernel, n_dp, cut), grid=(steps,),...  5.22 us
    concatenate x1, other arithmetic, body(): w_own = jnp.concatenate([w_gu, w_dn.T], 1)  4.88 us
  transfers between devices with their start and end apart: 28, of which 15 were waited for; matrix products, arithmetic and copies ran while one was open for 9% of the time, Pallas kernels for 33%

profile of v5, /device:TPU:1, one launch (start us, length us, event | category | flops | bytes accessed | tf_op | source)
XLA Modules:
  0.0 186.0 jit_solution(9284089656113968104)
XLA Ops:
  0.6 4.4 %shard_map.137 = (bf16[512,1152]{1,0:T(8,128)(2,1)}, bf16[512,1152]{1,0:T(8,128)(2,1)}, bf16[128,4224]{1,0:T(8,128)(2,1)}) custom-call(bf16[128,2048]{1,0:T(8,128)(2,1)} %x_ref.1, bf16[128,2048]{1,0:T(8,128)(2,1)} %y_ref.1, s32[8,128]{1,0:T(8,128)} %bitcast.42, bf16[8,128]{1,0:T(8,128)(2,1)} %bitcast.43, bf16[1,2048,768]{2,1,0:T(8,128)(2,1)} %gu_ref.1, ...), custom_call_target="tpu_custom_call" | custom-call | flops 1000 | bytes 1000 | tf_op jit(solution)/shard_map/pallas_call | solution.py:338
  5.0 2.1 %collective-permute-start.1 = (bf16[512,1152]{1,0:T(8,128)(2,1)}, bf16[512,1152]{1,0:T(8,128)(2,1)}, u32[]{:S(2)}, u32[]{:S(2)}) collective-permute-start(bf16[512,1152]{1,0:T(8,128)(2,1)} %get-tuple-element.80), channel_id=1, source_target_pairs={{0,1},{1,0},{2,3},{3,2},{4,5},{5,4},{6,7},{7,6},{8,9},{9,8},{10,11... | collective-permute-start | bytes 3538952 | tf_op jit(solution)/shard_map/ppermute | solution.py:38
  7.1 1.2 collective-permute-start.2
  8.4 1.3 collective-permute-start
  10.2 1.6 copy.17
  11.7 4.9 %pad_maximum_fusion.refs_2_.refs_3_.refs_1_ = bf16[2048,1152]{1,0:T(8,128)(2,1)} fusion(bf16[2048,384]{1,0:T(8,128)(2,1)} %copy.17, bf16[2048,768]{1,0:T(8,128)(2,1)} %bitcast.41), kind=kLoop, calls=%fused_computation | loop fusion | flops 9437184 | bytes 9437184 | tf_op jit(solution)/shard_map/concatenate | solution.py:417
  16.6 17.0 %collective-permute-done.refs_1_.refs_0_ = bf16[128,4224]{1,0:T(8,128)(2,1)S(1)} collective-permute-done((bf16[128,4224]{1,0:T(8,128)(2,1)}, bf16[128,4224]{1,0:T(8,128)(2,1)S(1)}, u32[]{:S(2)}, u32[]{:S(2)}) %collective-permute-start) | collective-permute-done | bytes 1081376 | tf_op jit(solution)/shard_map/ppermute | solution.py:55
  34.0 3.3 %collective-permute-start.5 = (bf16[512,1152]{1,0:T(8,128)(2,1)}, bf16[512,1152]{1,0:T(8,128)(2,1)S(1)}, u32[]{:S(2)}, u32[]{:S(2)}) collective-permute-start(bf16[512,1152]{1,0:T(8,128)(2,1)} %collective-permute-done.1.refs_4_.refs_2_), channel_id=1, source_target_pairs={{16,0},{0,16},{17,1},{1,17},{18,2},{2,18},{19,3},{3,19},{20,4},{4,... | collective-permute-start | bytes 3538952 | tf_op jit(solution)/shard_map/ppermute | solution.py:60
  37.3 1.3 collective-permute-start.7
  38.6 8.5 %shard_map.138 = (f32[1,384,1024]{2,1,0:T(8,128)}, bf16[1,1,384,1024]{3,2,1,0:T(8,128)(2,1)}, f32[256,2048]{1,0:T(8,128)}, f32[256,128]{1,0:T(8,128)}) custom-call(bf16[128,4224]{1,0:T(8,128)(2,1)} %get-tuple-element.108.refs_0_, bf16[128,4224]{1,0:T(8,128)(2,1)} %copy-done.3, bf16[2048,1152]{1,0:T(8,128)(2,1)} %pad_maximum_fusion.refs_2_.refs_3_.refs_1_), custom_call_target="tpu_custom_call" | custom-call | flops 1000 | bytes 1000 | tf_op jit(solution)/shard_map/pallas_call | solution.py:283
  47.1 11.3 %collective-permute-done.3.refs_5_.refs_3_ = bf16[512,1152]{1,0:T(8,128)(2,1)} collective-permute-done((bf16[512,1152]{1,0:T(8,128)(2,1)}, bf16[512,1152]{1,0:T(8,128)(2,1)}, u32[]{:S(2)}, u32[]{:S(2)}) %collective-permute-start.3) | collective-permute-done | bytes 1179680 | tf_op jit(solution)/shard_map/ppermute | solution.py:38
  58.4 0.8 collective-permute-done.4.refs_8_.refs_6_
  59.3 3.9 %collective-permute-done.7.refs_2_.refs_1_ = bf16[128,4224]{1,0:T(8,128)(2,1)S(1)} collective-permute-done((bf16[128,4224]{1,0:T(8,128)(2,1)S(1)}, bf16[128,4224]{1,0:T(8,128)(2,1)S(1)}, u32[]{:S(2)}, u32[]{:S(2)}) %collective-permute-start.7) | collective-permute-done | bytes 1081376 | tf_op jit(solution)/shard_map/ppermute | solution.py:55
  63.1 1.4 collective-permute-start.8
  64.6 0.9 collective-permute-start.9
  65.5 1.2 collective-permute-start.10
  67.5 1.6 collective-permute-done.9.refs_10_.refs_8_
  69.1 20.6 %shard_map.139 = (f32[3,384,1024]{2,1,0:T(8,128)}, bf16[3,1,384,1024]{3,2,1,0:T(8,128)(2,1)}, f32[384,2048]{1,0:T(8,128)}, f32[384,128]{1,0:T(8,128)}) custom-call(bf16[128,4224]{1,0:T(8,128)(2,1)} %get-tuple-element.108.refs_0_, bf16[128,4224]{1,0:T(8,128)(2,1)} %copy-done.3, bf16[128,4224]{1,0:T(8,128)(2,1)} %copy-done.12, ...), custom_call_target="tpu_custom_call" | custom-call | flops 1000 | bytes 1000 | tf_op jit(solution)/shard_map/pallas_call | solution.py:283
  89.7 3.4 %collective-permute-done.12.refs_0_.refs_1_ = bf16[128,4224]{1,0:T(8,128)(2,1)} collective-permute-done((bf16[128,4224]{1,0:T(8,128)(2,1)}, bf16[128,4224]{1,0:T(8,128)(2,1)}, u32[]{:S(2)}, u32[]{:S(2)}) %collective-permute-start.12) | collective-permute-done | bytes 1081376 | tf_op jit(solution)/shard_map/ppermute | solution.py:55
  93.4 0.8 collective-permute-done.11.refs_3_
  94.2 1.1 collective-permute-start.13
  95.3 13.9 %shard_map.140 = (f32[3,384,1024]{2,1,0:T(8,128)}, bf16[3,1,384,1024]{3,2,1,0:T(8,128)(2,1)}, f32[128,2048]{1,0:T(8,128)}, f32[128,128]{1,0:T(8,128)}) custom-call(bf16[128,4224]{1,0:T(8,128)(2,1)} %collective-permute-done.12.refs_0_.refs_1_, bf16[2048,1152]{1,0:T(8,128)(2,1)} %pad_maximum_fusion.refs_2_.refs_3_.refs_1_, ...), custom_call_target="tpu_custom_call" | custom-call | flops 1000 | bytes 1000 | tf_op jit(solution)/shard_map/pallas_call | solution.py:283
  109.3 0.6 collective-permute-start.15
  110.7 8.9 %shard_map.141 = (f32[1,384,1024]{2,1,0:T(8,128)}, bf16[1,1,384,1024]{3,2,1,0:T(8,128)(2,1)}, bf16[128,2176]{1,0:T(8,128)(2,1)}, bf16[128,2176]{1,0:T(8,128)(2,1)}) custom-call(bf16[128,4224]{1,0:T(8,128)(2,1)} %copy-done.3, bf16[128,4224]{1,0:T(8,128)(2,1)} %copy-done.12, bf16[512,1152]{1,0:T(8,128)(2,1)} %copy-done.5, bf16[512,1152]{1,0:T(8,128)(2,1)} %copy-done.6, ...), custom_call_target="tpu_custom_call" | custom-call | flops 1000 | bytes 1000 | tf_op jit(solution)/shard_map/pallas_call | solution.py:283
  119.6 0.8 collective-permute-start.22
  120.4 2.5 %fusion.5 = (bf16[256,1024]{1,0:T(8,128)(2,1)}, bf16[256,1024]{1,0:T(8,128)(2,1)}) fusion(f32[3,384,1024]{2,1,0:T(8,128)S(1)} %copy-done.4, bf16[3,384,1024]{2,1,0:T(8,128)(2,1)} %collective-permute-done.15), kind=kLoop, calls=%fused_computation.15 | loop fusion | flops 1572864 | bytes 4194304 | tf_op jit(solution)/shard_map/convert_element_type | solution.py:475
  123.7 9.2 %shard_map.142 = (f32[1,384,1024]{2,1,0:T(8,128)}, bf16[1,1,384,1024]{3,2,1,0:T(8,128)(2,1)}, bf16[128,2176]{1,0:T(8,128)(2,1)}, bf16[128,2176]{1,0:T(8,128)(2,1)}) custom-call(bf16[128,4224]{1,0:T(8,128)(2,1)} %get-tuple-element.108.refs_0_, bf16[128,4224]{1,0:T(8,128)(2,1)} %collective-permute-done.12.refs_0_.refs_1_, bf16[512,1152]{1,0:T(8,128)(2,1)} %copy-done.5, ...), custom_call_target="tpu_custom_call" | custom-call | flops 1000 | bytes 1000 | tf_op jit(solution)/shard_map/pallas_call | solution.py:283
  133.0 3.0 %collective-permute-done.16 = bf16[256,1024]{1,0:T(8,128)(2,1)S(1)} collective-permute-done((bf16[256,1024]{1,0:T(8,128)(2,1)}, bf16[256,1024]{1,0:T(8,128)(2,1)S(1)}, u32[]{:S(2)}, u32[]{:S(2)}) %collective-permute-start.16) | collective-permute-done | bytes 524320 | tf_op jit(solution)/shard_map/ppermute | solution.py:38
  136.0 2.1 %collective-permute-start.18 = (bf16[384,1024]{1,0:T(8,128)(2,1)}, bf16[384,1024]{1,0:T(8,128)(2,1)S(1)}, u32[]{:S(2)}, u32[]{:S(2)}) collective-permute-start(bf16[384,1024]{1,0:T(8,128)(2,1)} %bitcast.45), channel_id=1, source_target_pairs={{16,0},{0,16},{17,1},{1,17},{18,2},{2,18},{19,3},{3,19},{20,4},{4,... | collective-permute-start | bytes 2359304 | tf_op jit(solution)/shard_map/ppermute | solution.py:60
  138.3 3.2 %collective-permute-start.23 = (bf16[128,2176]{1,0:T(8,128)(2,1)S(1)}, bf16[128,2176]{1,0:T(8,128)(2,1)S(1)}, u32[]{:S(2)}, u32[]{:S(2)}) collective-permute-start(bf16[128,2176]{1,0:T(8,128)(2,1)S(1)} %add_convert_fusion.1), channel_id=1, source_target_pairs={{0,4},{1,5},{2,6},{3,7},{4,12},{5,13},{6,14},{7,15},{12,8},{13,9},... | collective-permute-start | bytes 1671176 | tf_op jit(solution)/shard_map/ppermute | solution.py:55
  141.5 1.2 fusion.8
  142.7 1.0 collective-permute-start.21
  143.9 0.5 collective-permute-start.19
  144.5 1.2 collective-permute-start.24
  145.7 4.6 %collective-permute-done.21 = bf16[128,1024]{1,0:T(8,128)(2,1)S(1)} collective-permute-done((bf16[128,1024]{1,0:T(8,128)(2,1)S(1)}, bf16[128,1024]{1,0:T(8,128)(2,1)S(1)}, u32[]{:S(2)}, u32[]{:S(2)}) %collective-permute-start.21) | collective-permute-done | bytes 262176 | tf_op jit(solution)/shard_map/ppermute | solution.py:38
  150.3 3.2 %collective-permute-done.23 = bf16[128,2176]{1,0:T(8,128)(2,1)S(1)} collective-permute-done((bf16[128,2176]{1,0:T(8,128)(2,1)S(1)}, bf16[128,2176]{1,0:T(8,128)(2,1)S(1)}, u32[]{:S(2)}, u32[]{:S(2)}) %collective-permute-start.23) | collective-permute-done | bytes 557088 | tf_op jit(solution)/shard_map/ppermute | solution.py:55
  153.6 2.3 %collective-permute-start.26 = (bf16[128,2176]{1,0:T(8,128)(2,1)S(1)}, bf16[128,2176]{1,0:T(8,128)(2,1)S(1)}, u32[]{:S(2)}, u32[]{:S(2)}) collective-permute-start(bf16[128,2176]{1,0:T(8,128)(2,1)S(1)} %add_convert_fusion), channel_id=1, source_target_pairs={{0,4},{1,5},{2,6},{3,7},{4,12},{5,13},{6,14},{7,15},{12,8},{13,9},... | collective-permute-start | bytes 1671176 | tf_op jit(solution)/shard_map/ppermute | solution.py:55
  155.9 11.3 %collective-permute-done.19 = bf16[384,1024]{1,0:T(8,128)(2,1)S(1)} collective-permute-done((bf16[384,1024]{1,0:T(8,128)(2,1)S(1)}, bf16[384,1024]{1,0:T(8,128)(2,1)S(1)}, u32[]{:S(2)}, u32[]{:S(2)}) %collective-permute-start.19) | collective-permute-done | bytes 786464 | tf_op jit(solution)/shard_map/ppermute | solution.py:38
  167.2 1.8 fusion.3.refs_0_
  168.9 1.2 collective-permute-start.20
  170.2 1.1 fusion.7.refs_1_
  172.1 0.8 collective-permute-done.25.refs_3_
  173.0 5.2 %shard_map.143 = (f32[1,1,384,2048]{3,2,1,0:T(8,128)}, f32[1,1,384,2048]{3,2,1,0:T(8,128)}, bf16[384,2048]{1,0:T(8,128)(2,1)S(1)}) custom-call(s32[1]{0:T(128)} %copy.20.lead_ref, bf16[256,1024]{1,0:T(8,128)(2,1)S(1)} %fusion.3.refs_0_, bf16[128,1024]{1,0:T(8,128)(2,1)S(1)} %fusion.7.refs_1_, bf16[256,1024]{1,0:T(8,128)(2,1)S(1)} %collective-permute-done.20.refs_2_, ...), custom_call_target="tpu_custom_call" | custom-call | flops 1000 | bytes 1000 | tf_op jit(solution)/shard_map/pallas_call | solution.py:379
  178.7 0.7 fusion.10
  179.4 1.3 convert_add_fusion
  180.7 0.9 slice.128
  182.0 0.7 copy.19
  182.7 3.4 %fusion.1 = bf16[1,1,384,2048]{3,2,1,0:T(8,128)(2,1)} fusion(bf16[1,384,2048]{2,1,0:T(8,128)(2,1)S(1)} %copy-done, bf16[384,2048]{1,0:T(8,128)(2,1)} %collective-permute-done.27, bf16[384,2048]{1,0:T(8,128)(2,1)S(1)} %get-tuple-element.148, pred[]{:T(512)S(6)} %eq.29, pred[]{:T(512)} %bitcast.14), kind=kLoop, calls=%fused_computation.4 | loop fusion | flops 1572864 | bytes 6291458 | tf_op jit(solution)/shard_map/broadcast_in_dim | solution.py:515
  (70 shorter events, 5.3 us)
Async XLA Ops:
  0.6 9.5 %copy-start = (bf16[1,384,2048]{2,1,0:T(8,128)(2,1)S(1)}, bf16[1,384,2048]{2,1,0:T(8,128)(2,1)}, u32[]{:S(2)}) copy-start(bf16[1,384,2048]{2,1,0:T(8,128)(2,1)} %refs_6_.1) | copy-start | bytes 4718596
  5.0 28.6 %collective-permute-start.1 = (bf16[512,1152]{1,0:T(8,128)(2,1)}, bf16[512,1152]{1,0:T(8,128)(2,1)}, u32[]{:S(2)}, u32[]{:S(2)}) collective-permute-start(bf16[512,1152]{1,0:T(8,128)(2,1)} %get-tuple-element.80), channel_id=1, source_target_pairs={{0,1},{1,0},{2,3},{3,2},{4,5},{5,4},{6,7},{7,6},{8,9},{9,8},{10,11... | collective-permute-start | bytes 3538952 | tf_op jit(solution)/shard_map/ppermute | solution.py:38
  7.1 26.8 %collective-permute-start.2 = (bf16[512,1152]{1,0:T(8,128)(2,1)}, bf16[512,1152]{1,0:T(8,128)(2,1)}, u32[]{:S(2)}, u32[]{:S(2)}) collective-permute-start(bf16[512,1152]{1,0:T(8,128)(2,1)} %get-tuple-element.81), channel_id=1, source_target_pairs={{0,2},{1,3},{2,0},{3,1},{4,6},{5,7},{6,4},{7,5},{8,10},{9,11},{10,... | collective-permute-start | bytes 3538952 | tf_op jit(solution)/shard_map/ppermute | solution.py:38
  8.4 25.2 %collective-permute-start = (bf16[128,4224]{1,0:T(8,128)(2,1)}, bf16[128,4224]{1,0:T(8,128)(2,1)S(1)}, u32[]{:S(2)}, u32[]{:S(2)}) collective-permute-start(bf16[128,4224]{1,0:T(8,128)(2,1)} %get-tuple-element.108.refs_0_), channel_id=1, source_target_pairs={{0,4},{1,5},{2,6},{3,7},{4,12},{5,13},{6,14},{7,15},{12,8},{13,9},... | collective-permute-start | bytes 3244040 | tf_op jit(solution)/shard_map/ppermute | solution.py:55
  9.7 48.8 %collective-permute-start.3 = (bf16[512,1152]{1,0:T(8,128)(2,1)}, bf16[512,1152]{1,0:T(8,128)(2,1)}, u32[]{:S(2)}, u32[]{:S(2)}) collective-permute-start(bf16[512,1152]{1,0:T(8,128)(2,1)} %get-tuple-element.81), channel_id=1, source_target_pairs={{0,1},{1,0},{2,3},{3,2},{4,5},{5,4},{6,7},{7,6},{8,9},{9,8},{10,11... | collective-permute-start | bytes 3538952 | tf_op jit(solution)/shard_map/ppermute | solution.py:38
  9.9 49.3 %collective-permute-start.4 = (bf16[512,1152]{1,0:T(8,128)(2,1)}, bf16[512,1152]{1,0:T(8,128)(2,1)}, u32[]{:S(2)}, u32[]{:S(2)}) collective-permute-start(bf16[512,1152]{1,0:T(8,128)(2,1)} %get-tuple-element.80), channel_id=1, source_target_pairs={{0,2},{1,3},{2,0},{3,1},{4,6},{5,7},{6,4},{7,5},{8,10},{9,11},{10,... | collective-permute-start | bytes 3538952 | tf_op jit(solution)/shard_map/ppermute | solution.py:38
  33.6 5.0 %copy-start.3 = (bf16[128,4224]{1,0:T(8,128)(2,1)}, bf16[128,4224]{1,0:T(8,128)(2,1)S(1)}, u32[]{:S(2)}) copy-start(bf16[128,4224]{1,0:T(8,128)(2,1)S(1)} %collective-permute-done.refs_1_.refs_0_) | copy-start | bytes 3244036
  34.0 29.2 %collective-permute-start.5 = (bf16[512,1152]{1,0:T(8,128)(2,1)}, bf16[512,1152]{1,0:T(8,128)(2,1)S(1)}, u32[]{:S(2)}, u32[]{:S(2)}) collective-permute-start(bf16[512,1152]{1,0:T(8,128)(2,1)} %collective-permute-done.1.refs_4_.refs_2_), channel_id=1, source_target_pairs={{16,0},{0,16},{17,1},{1,17},{18,2},{2,18},{19,3},{3,19},{20,4},{4,... | collective-permute-start | bytes 3538952 | tf_op jit(solution)/shard_map/ppermute | solution.py:60
  37.3 25.8 %collective-permute-start.6 = (bf16[512,1152]{1,0:T(8,128)(2,1)}, bf16[512,1152]{1,0:T(8,128)(2,1)S(1)}, u32[]{:S(2)}, u32[]{:S(2)}) collective-permute-start(bf16[512,1152]{1,0:T(8,128)(2,1)} %collective-permute-done.2.refs_9_.refs_7_), channel_id=1, source_target_pairs={{16,0},{0,16},{17,1},{1,17},{18,2},{2,18},{19,3},{3,19},{20,4},{4,... | collective-permute-start | bytes 3538952 | tf_op jit(solution)/shard_map/ppermute | solution.py:60
  37.3 25.8 %collective-permute-start.7 = (bf16[128,4224]{1,0:T(8,128)(2,1)S(1)}, bf16[128,4224]{1,0:T(8,128)(2,1)S(1)}, u32[]{:S(2)}, u32[]{:S(2)}) collective-permute-start(bf16[128,4224]{1,0:T(8,128)(2,1)S(1)} %collective-permute-done.refs_1_.refs_0_), channel_id=1, source_target_pairs={{0,4},{1,5},{2,6},{3,7},{4,12},{5,13},{6,14},{7,15},{12,8},{13,9},... | collective-permute-start | bytes 3244040 | tf_op jit(solution)/shard_map/ppermute | solution.py:55
  63.1 1.5 copy-start.12
  63.1 6.0 %copy-start.9 = (bf16[512,1152]{1,0:T(8,128)(2,1)}, bf16[512,1152]{1,0:T(8,128)(2,1)S(1)}, u32[]{:S(2)}) copy-start(bf16[512,1152]{1,0:T(8,128)(2,1)S(1)} %collective-permute-done.5.refs_6_.refs_4_) | copy-start | bytes 3538948
  63.1 5.9 %copy-start.10 = (bf16[512,1152]{1,0:T(8,128)(2,1)}, bf16[512,1152]{1,0:T(8,128)(2,1)S(1)}, u32[]{:S(2)}) copy-start(bf16[512,1152]{1,0:T(8,128)(2,1)S(1)} %collective-permute-done.6.refs_11_.refs_9_) | copy-start | bytes 3538948
  63.1 4.4 %collective-permute-start.8 = (bf16[512,1152]{1,0:T(8,128)(2,1)}, bf16[512,1152]{1,0:T(8,128)(2,1)S(1)}, u32[]{:S(2)}, u32[]{:S(2)}) collective-permute-start(bf16[512,1152]{1,0:T(8,128)(2,1)} %collective-permute-done.3.refs_5_.refs_3_), channel_id=1, source_target_pairs={{16,0},{0,16},{17,1},{1,17},{18,2},{2,18},{19,3},{3,19},{20,4},{4,... | collective-permute-start | bytes 3538952 | tf_op jit(solution)/shard_map/ppermute | solution.py:60
  64.6 4.5 %collective-permute-start.9 = (bf16[512,1152]{1,0:T(8,128)(2,1)}, bf16[512,1152]{1,0:T(8,128)(2,1)}, u32[]{:S(2)}, u32[]{:S(2)}) collective-permute-start(bf16[512,1152]{1,0:T(8,128)(2,1)} %collective-permute-done.4.refs_8_.refs_6_), channel_id=1, source_target_pairs={{16,0},{0,16},{17,1},{1,17},{18,2},{2,18},{19,3},{3,19},{20,4},{4,... | collective-permute-start | bytes 3538952 | tf_op jit(solution)/shard_map/ppermute | solution.py:60
  65.5 27.9 %collective-permute-start.10 = (bf16[512,1152]{1,0:T(8,128)(2,1)}, bf16[512,1152]{1,0:T(8,128)(2,1)S(1)}, u32[]{:S(2)}, u32[]{:S(2)}) collective-permute-start(bf16[512,1152]{1,0:T(8,128)(2,1)} %collective-permute-done.1.refs_4_.refs_2_), channel_id=1, source_target_pairs={{0,2},{1,3},{2,0},{3,1},{4,6},{5,7},{6,4},{7,5},{8,10},{9,11},{10,... | collective-permute-start | bytes 3538952 | tf_op jit(solution)/shard_map/ppermute | solution.py:38
  66.7 27.5 %collective-permute-start.11 = (bf16[512,1152]{1,0:T(8,128)(2,1)}, bf16[512,1152]{1,0:T(8,128)(2,1)S(1)}, u32[]{:S(2)}, u32[]{:S(2)}) collective-permute-start(bf16[512,1152]{1,0:T(8,128)(2,1)} %collective-permute-done.2.refs_9_.refs_7_), channel_id=1, source_target_pairs={{0,1},{1,0},{2,3},{3,2},{4,5},{5,4},{6,7},{7,6},{8,9},{9,8},{10,11... | collective-permute-start | bytes 3538952 | tf_op jit(solution)/shard_map/ppermute | solution.py:38
  67.0 26.1 %collective-permute-start.12 = (bf16[128,4224]{1,0:T(8,128)(2,1)}, bf16[128,4224]{1,0:T(8,128)(2,1)}, u32[]{:S(2)}, u32[]{:S(2)}) collective-permute-start(bf16[128,4224]{1,0:T(8,128)(2,1)} %copy-done.12), channel_id=1, source_target_pairs={{0,4},{1,5},{2,6},{3,7},{4,12},{5,13},{6,14},{7,15},{12,8},{13,9},... | collective-permute-start | bytes 3244040 | tf_op jit(solution)/shard_map/ppermute | solution.py:55
  67.5 1.6 copy-start.11
  93.4 15.8 %copy-start.5 = (bf16[512,1152]{1,0:T(8,128)(2,1)}, bf16[512,1152]{1,0:T(8,128)(2,1)S(1)}, u32[]{:S(2)}) copy-start(bf16[512,1152]{1,0:T(8,128)(2,1)S(1)} %collective-permute-done.10.refs_2_) | copy-start | bytes 3538948
  94.2 15.0 %copy-start.6 = (bf16[512,1152]{1,0:T(8,128)(2,1)}, bf16[512,1152]{1,0:T(8,128)(2,1)S(1)}, u32[]{:S(2)}) copy-start(bf16[512,1152]{1,0:T(8,128)(2,1)S(1)} %collective-permute-done.11.refs_3_) | copy-start | bytes 3538948
  94.2 15.0 %collective-permute-start.13 = (bf16[512,1152]{1,0:T(8,128)(2,1)S(1)}, bf16[512,1152]{1,0:T(8,128)(2,1)S(1)}, u32[]{:S(2)}, u32[]{:S(2)}) collective-permute-start(bf16[512,1152]{1,0:T(8,128)(2,1)S(1)} %collective-permute-done.10.refs_2_), channel_id=1, source_target_pairs={{16,0},{0,16},{17,1},{1,17},{18,2},{2,18},{19,3},{3,19},{20,4},{4,... | collective-permute-start | bytes 3538952 | tf_op jit(solution)/shard_map/ppermute | solution.py:60
  95.3 14.0 %collective-permute-start.14 = (bf16[512,1152]{1,0:T(8,128)(2,1)S(1)}, bf16[512,1152]{1,0:T(8,128)(2,1)S(1)}, u32[]{:S(2)}, u32[]{:S(2)}) collective-permute-start(bf16[512,1152]{1,0:T(8,128)(2,1)S(1)} %collective-permute-done.11.refs_3_), channel_id=1, source_target_pairs={{16,0},{0,16},{17,1},{1,17},{18,2},{2,18},{19,3},{3,19},{20,4},{4,... | collective-permute-start | bytes 3538952 | tf_op jit(solution)/shard_map/ppermute | solution.py:60
  109.3 1.0 copy-start.7
  109.3 1.4 copy-start.8
  109.3 10.3 %collective-permute-start.15 = (bf16[3,384,1024]{2,1,0:T(8,128)(2,1)}, bf16[3,384,1024]{2,1,0:T(8,128)(2,1)}, u32[]{:S(2)}, u32[]{:S(2)}) collective-permute-start(bf16[3,384,1024]{2,1,0:T(8,128)(2,1)} %bitcast.44), channel_id=1, source_target_pairs={{16,0},{0,16},{17,1},{1,17},{18,2},{2,18},{19,3},{3,19},{20,4},{4,... | collective-permute-start | bytes 7077896 | tf_op jit(solution)/shard_map/ppermute | solution.py:60
  110.7 9.7 %copy-start.4 = (f32[3,384,1024]{2,1,0:T(8,128)S(1)}, f32[3,384,1024]{2,1,0:T(8,128)}, u32[]{:S(2)}) copy-start(f32[3,384,1024]{2,1,0:T(8,128)} %get-tuple-element.134) | copy-start | bytes 14155780
  119.6 18.5 %collective-permute-start.22 = (bf16[128,2176]{1,0:T(8,128)(2,1)}, bf16[128,2176]{1,0:T(8,128)(2,1)S(1)}, u32[]{:S(2)}, u32[]{:S(2)}) collective-permute-start(bf16[128,2176]{1,0:T(8,128)(2,1)} %get-tuple-element.140), channel_id=1, source_target_pairs={{0,4},{1,5},{2,6},{3,7},{4,12},{5,13},{6,14},{7,15},{12,8},{13,9},... | collective-permute-start | bytes 1671176 | tf_op jit(solution)/shard_map/ppermute | solution.py:55
  123.0 13.0 %collective-permute-start.16 = (bf16[256,1024]{1,0:T(8,128)(2,1)}, bf16[256,1024]{1,0:T(8,128)(2,1)S(1)}, u32[]{:S(2)}, u32[]{:S(2)}) collective-permute-start(bf16[256,1024]{1,0:T(8,128)(2,1)} %get-tuple-element.159), channel_id=1, source_target_pairs={{0,1},{1,0},{2,3},{3,2},{4,5},{5,4},{6,7},{7,6},{8,9},{9,8},{10,11... | collective-permute-start | bytes 1572872 | tf_op jit(solution)/shard_map/ppermute | solution.py:38
  123.5 14.7 %copy-start.16 = (bf16[128,2176]{1,0:T(8,128)(2,1)S(1)}, bf16[128,2176]{1,0:T(8,128)(2,1)}, u32[]{:S(2)}) copy-start(bf16[128,2176]{1,0:T(8,128)(2,1)} %get-tuple-element.141) | copy-start | bytes 1671172
  123.5 12.5 %collective-permute-start.17 = (bf16[256,1024]{1,0:T(8,128)(2,1)}, bf16[256,1024]{1,0:T(8,128)(2,1)}, u32[]{:S(2)}, u32[]{:S(2)}) collective-permute-start(bf16[256,1024]{1,0:T(8,128)(2,1)} %get-tuple-element.158), channel_id=1, source_target_pairs={{0,2},{1,3},{2,0},{3,1},{4,6},{5,7},{6,4},{7,5},{8,10},{9,11},{10,... | collective-permute-start | bytes 1572872 | tf_op jit(solution)/shard_map/ppermute | solution.py:38
  136.0 7.6 %copy-start.13 = (f32[1,384,1024]{2,1,0:T(8,128)S(1)}, f32[1,384,1024]{2,1,0:T(8,128)}, u32[]{:S(2)}) copy-start(f32[1,384,1024]{2,1,0:T(8,128)} %get-tuple-element.138) | copy-start | bytes 4718596
  136.0 7.6 %collective-permute-start.18 = (bf16[384,1024]{1,0:T(8,128)(2,1)}, bf16[384,1024]{1,0:T(8,128)(2,1)S(1)}, u32[]{:S(2)}, u32[]{:S(2)}) collective-permute-start(bf16[384,1024]{1,0:T(8,128)(2,1)} %bitcast.45), channel_id=1, source_target_pairs={{16,0},{0,16},{17,1},{1,17},{18,2},{2,18},{19,3},{3,19},{20,4},{4,... | collective-permute-start | bytes 2359304 | tf_op jit(solution)/shard_map/ppermute | solution.py:60
  138.3 15.2 %collective-permute-start.23 = (bf16[128,2176]{1,0:T(8,128)(2,1)S(1)}, bf16[128,2176]{1,0:T(8,128)(2,1)S(1)}, u32[]{:S(2)}, u32[]{:S(2)}) collective-permute-start(bf16[128,2176]{1,0:T(8,128)(2,1)S(1)} %add_convert_fusion.1), channel_id=1, source_target_pairs={{0,4},{1,5},{2,6},{3,7},{4,12},{5,13},{6,14},{7,15},{12,8},{13,9},... | collective-permute-start | bytes 1671176 | tf_op jit(solution)/shard_map/ppermute | solution.py:55
  142.6 10.9 %copy-start.15 = (bf16[128,2176]{1,0:T(8,128)(2,1)S(1)}, bf16[128,2176]{1,0:T(8,128)(2,1)}, u32[]{:S(2)}) copy-start(bf16[128,2176]{1,0:T(8,128)(2,1)} %get-tuple-element.144) | copy-start | bytes 1671172
  142.7 7.7 %collective-permute-start.21 = (bf16[128,1024]{1,0:T(8,128)(2,1)S(1)}, bf16[128,1024]{1,0:T(8,128)(2,1)S(1)}, u32[]{:S(2)}, u32[]{:S(2)}) collective-permute-start(bf16[128,1024]{1,0:T(8,128)(2,1)S(1)} %get-tuple-element.156), channel_id=1, source_target_pairs={{0,1},{1,0},{2,3},{3,2},{4,5},{5,4},{6,7},{7,6},{8,9},{9,8},{10,11... | collective-permute-start | bytes 786440 | tf_op jit(solution)/shard_map/ppermute | solution.py:38
  143.9 23.2 %collective-permute-start.19 = (bf16[384,1024]{1,0:T(8,128)(2,1)S(1)}, bf16[384,1024]{1,0:T(8,128)(2,1)S(1)}, u32[]{:S(2)}, u32[]{:S(2)}) collective-permute-start(bf16[384,1024]{1,0:T(8,128)(2,1)S(1)} %fusion), channel_id=1, source_target_pairs={{0,3},{1,2},{2,1},{3,0},{4,7},{5,6},{6,5},{7,4},{8,11},{9,10},{10,... | collective-permute-start | bytes 2359304 | tf_op jit(solution)/shard_map/ppermute | solution.py:38
  144.5 25.7 %collective-permute-start.24 = (bf16[128,1024]{1,0:T(8,128)(2,1)S(1)}, bf16[128,1024]{1,0:T(8,128)(2,1)S(1)}, u32[]{:S(2)}, u32[]{:S(2)}) collective-permute-start(bf16[128,1024]{1,0:T(8,128)(2,1)S(1)} %get-tuple-element.157), channel_id=1, source_target_pairs={{0,2},{1,3},{2,0},{3,1},{4,6},{5,7},{6,4},{7,5},{8,10},{9,11},{10,... | collective-permute-start | bytes 786440 | tf_op jit(solution)/shard_map/ppermute | solution.py:38
  153.5 19.4 %copy-start.2 = (f32[1,1,384,2048]{3,2,1,0:T(8,128)S(1)}, f32[1,1,384,2048]{3,2,1,0:T(8,128)}, u32[]{:S(2)}) copy-start(f32[1,1,384,2048]{3,2,1,0:T(8,128)} %refs_5_.1) | copy-start | bytes 9437188
  153.6 18.5 %collective-permute-start.26 = (bf16[128,2176]{1,0:T(8,128)(2,1)S(1)}, bf16[128,2176]{1,0:T(8,128)(2,1)S(1)}, u32[]{:S(2)}, u32[]{:S(2)}) collective-permute-start(bf16[128,2176]{1,0:T(8,128)(2,1)S(1)} %add_convert_fusion), channel_id=1, source_target_pairs={{0,4},{1,5},{2,6},{3,7},{4,12},{5,13},{6,14},{7,15},{12,8},{13,9},... | collective-permute-start | bytes 1671176 | tf_op jit(solution)/shard_map/ppermute | solution.py:55
  167.2 5.8 %copy-start.1 = (f32[1,1,384,2048]{3,2,1,0:T(8,128)S(1)}, f32[1,1,384,2048]{3,2,1,0:T(8,128)}, u32[]{:S(2)}) copy-start(f32[1,1,384,2048]{3,2,1,0:T(8,128)} %refs_4_.1) | copy-start | bytes 9437188
  168.9 4.0 %collective-permute-start.20 = (bf16[256,1024]{1,0:T(8,128)(2,1)S(1)}, bf16[256,1024]{1,0:T(8,128)(2,1)S(1)}, u32[]{:S(2)}, u32[]{:S(2)}) collective-permute-start(bf16[256,1024]{1,0:T(8,128)(2,1)S(1)} %fusion.3.refs_0_), channel_id=1, source_target_pairs={{16,0},{0,16},{17,1},{1,17},{18,2},{2,18},{19,3},{3,19},{20,4},{4,... | collective-permute-start | bytes 1572872 | tf_op jit(solution)/shard_map/ppermute | solution.py:60
  171.3 1.6 collective-permute-start.25
  172.1 6.6 %copy-start.17 = (s32[128,8]{0,1:T(8,128)S(1)}, s32[128,8]{0,1:T(8,128)}, u32[]{:S(2)}) copy-start(s32[128,8]{0,1:T(8,128)} %param.12) | copy-start | bytes 12292
  172.1 6.7 %copy-start.18 = (s32[1,2]{1,0:T(1,128)S(1)}, s32[1,2]{1,0:T(1,128)}, u32[]{:S(2)}) copy-start(s32[1,2]{1,0:T(1,128)} %param.18) | copy-start | bytes 28
  172.1 0.8 copy-start.14
  178.2 4.5 %collective-permute-start.27 = (bf16[384,2048]{1,0:T(8,128)(2,1)S(1)}, bf16[384,2048]{1,0:T(8,128)(2,1)}, u32[]{:S(2)}, u32[]{:S(2)}) collective-permute-start(bf16[384,2048]{1,0:T(8,128)(2,1)S(1)} %get-tuple-element.148), channel_id=1, source_target_pairs={{16,0},{0,16},{17,1},{1,17},{18,2},{2,18},{19,3},{3,19},{20,4},{4,... | collective-permute-start | bytes 4718600 | tf_op jit(solution)/shard_map/ppermute | solution.py:60

commit v6 on v5

--- a/solution.py
+++ b/solution.py
@@ -467,35 +467,44 @@
     first = first_pass.call(pick(first_pass), sums=sums)
     first, swapped, keep = lax.optimization_barrier((first, swapped, keep))
     passing = along(first["back0"])
-    cut = half * 2 // 3
-    rows_of = [slice(0, cut), slice(cut, half)]
-
-    def leaving(r, keep, swapped):
-        total = [keep[s][r] + sum(v[s][r].astype(f32) for v in swapped) for s in (1, 2)]
-        return [hop(total[0].astype(bf16), 1), hop(total[1].astype(bf16), 2)]
-
-    sent = leaving(rows_of[0], keep, swapped)
+    cut = half // 2
+    top, low = slice(0, cut), slice(cut, half)
+
+    def summed(s, r, keep, swapped):
+        return keep[s][r] + sum(v[s][r].astype(f32) for v in swapped)
+
+    sent = [
+        hop(summed(1, top, keep, swapped).astype(bf16), 1),
+        hop(summed(2, low, keep, swapped).astype(bf16), 2),
+    ]
     rest_pass = make([3], [0, last_block], [(0, 2)], 2)
     last = rest_pass.call(pick(rest_pass), sums=sums, grads=[(first, (0, 1))])
-    sent, last_keep, last_send, keep, swapped = lax.optimization_barrier(
-        (sent, last["keep"], last["send"], keep, swapped)
+    sent, passing, last_keep, last_send, keep, swapped = lax.optimization_barrier(
+        (sent, passing, last["keep"], last["send"], keep, swapped)
     )
 
     across = last_keep[0]
     for k in range(1, n_dp):
         across = across + turn(last_send[0, k - 1], k).astype(f32)
-    sent_late = leaving(rows_of[1], keep, swapped)
-    sent_across = hop(across.astype(bf16), 3)
+    across = across.astype(bf16)
+    came = [hop(across[top], 1), hop(across[low], 2)]
+    late = None
     for k in range(2, layers):
         term = first["back%d" % (k - 1)] if k < last_block else last["back1"]
         if k == last_block:
-            sent_late[0], passing = lax.optimization_barrier((sent_late[0], passing))
-        passing = along((passing.astype(f32) + term.astype(f32)).astype(bf16))
+            came, passing = lax.optimization_barrier((came, passing))
+            late = [
+                (summed(2, top, keep, swapped) + came[0].astype(f32)).astype(bf16),
+                (summed(1, low, keep, swapped) + came[1].astype(f32)).astype(bf16),
+            ]
+        passing = (passing.astype(f32) + term.astype(f32)).astype(bf16)
+        late, passing = lax.optimization_barrier((late, passing))
+        passing = along(passing)
+    late = [hop(late[0], 2), hop(late[1], 1)]
 
     grads = []
-    for r, came in zip(rows_of, (sent, sent_late)):
-        grad = keep[0][r] + sum(v[0][r].astype(f32) for v in swapped)
-        grad = grad + sum(v.astype(f32) for v in came) + sent_across[r].astype(f32)
+    for r, one_hop, two_hops in zip((top, low), sent, late):
+        grad = summed(0, r, keep, swapped) + one_hop.astype(f32) + two_hops.astype(f32)
         grads.append(grad.astype(bf16))
     halves = [others(grad) for grad in grads]
     halves, passing = lax.optimization_barrier((halves, passing))

time: 186 us -> 184 us (0.989)
    ppermute x11 -> x12, waiting for transfers between devices: 32.6 us -> 21.2 us  [hop(): return lax.ppermute(value, 'expert', [(i, i ^ flip) for i in range(n)])]
    ppermute x6, waiting for transfers between devices: 27.4 us -> 37.6 us  [along(): return lax.ppermute(value, 'expert', pairs)]
    ppermute x11 -> x12, starting transfers between devices: 8.85 us -> 8.32 us  [hop(): return lax.ppermute(value, 'expert', [(i, i ^ flip) for i in range(n)])]
  transfers between devices with their start and end apart: 28 -> 29, of which waited for: 15 -> 17; matrix products, arithmetic and copies ran while one was open for 9% -> 8% of each run, Pallas kernels for 33% -> 33%
where the time goes in v6:
time: 184 us
  Pallas kernels  70.7 us (38%)
  waiting for transfers between devices  61 us (33%)
  starting transfers between devices  28.9 us (16%)
  other arithmetic  16.9 us (9%)
  local copies, waits for them, and re-layouts  4.64 us (3%)
    pallas_call x5, Pallas kernels, call(): pl.pallas_call(functools.partial(self.kernel, len(ins)), out_shape=[jax.S...  61.1 us
    ppermute x6, waiting for transfers between devices, along(): return lax.ppermute(value, 'expert', pairs)  37.6 us
    ppermute x12, waiting for transfers between devices, hop(): return lax.ppermute(value, 'expert', [(i, i ^ flip) for i in range(n)])  21.2 us
    ppermute x11, starting transfers between devices, turn(): return lax.ppermute(value, 'dp', [((r + step) % n, r) for r in range(n)])  12.9 us
    ppermute x12, starting transfers between devices, hop(): return lax.ppermute(value, 'expert', [(i, i ^ flip) for i in range(n)])  8.32 us
    ppermute x6, starting transfers between devices, along(): return lax.ppermute(value, 'expert', pairs)  7.63 us
    pallas_call x1, Pallas kernels, adam_call(): pl.pallas_call(functools.partial(adam_kernel, n_dp, cut), grid=(steps,),...  5.18 us
    concatenate x1, other arithmetic, body(): w_own = jnp.concatenate([w_gu, w_dn.T], 1)  4.92 us
  transfers between devices with their start and end apart: 29, of which 17 were waited for; matrix products, arithmetic and copies ran while one was open for 8% of the time, Pallas kernels for 33%

profile of v6, /device:TPU:1, one launch (start us, length us, event | category | flops | bytes accessed | tf_op | source)
XLA Modules:
  0.0 183.6 jit_solution(10554454491254234888)
XLA Ops:
  0.6 4.4 %shard_map.137 = (bf16[512,1152]{1,0:T(8,128)(2,1)}, bf16[512,1152]{1,0:T(8,128)(2,1)}, bf16[128,4224]{1,0:T(8,128)(2,1)}) custom-call(bf16[128,2048]{1,0:T(8,128)(2,1)} %x_ref.1, bf16[128,2048]{1,0:T(8,128)(2,1)} %y_ref.1, s32[8,128]{1,0:T(8,128)} %bitcast.46, bf16[8,128]{1,0:T(8,128)(2,1)} %bitcast.47, bf16[1,2048,768]{2,1,0:T(8,128)(2,1)} %gu_ref.1, ...), custom_call_target="tpu_custom_call" | custom-call | flops 1000 | bytes 1000 | tf_op jit(solution)/shard_map/pallas_call | solution.py:338
  5.0 2.1 %collective-permute-start.1 = (bf16[512,1152]{1,0:T(8,128)(2,1)}, bf16[512,1152]{1,0:T(8,128)(2,1)}, u32[]{:S(2)}, u32[]{:S(2)}) collective-permute-start(bf16[512,1152]{1,0:T(8,128)(2,1)} %get-tuple-element.85), channel_id=1, source_target_pairs={{0,1},{1,0},{2,3},{3,2},{4,5},{5,4},{6,7},{7,6},{8,9},{9,8},{10,11... | collective-permute-start | bytes 3538952 | tf_op jit(solution)/shard_map/ppermute | solution.py:38
  7.1 1.2 collective-permute-start.2
  8.4 1.3 collective-permute-start
  10.1 1.6 copy.17
  11.7 4.9 %pad_maximum_fusion.refs_2_.refs_3_.refs_1_ = bf16[2048,1152]{1,0:T(8,128)(2,1)} fusion(bf16[2048,384]{1,0:T(8,128)(2,1)} %copy.17, bf16[2048,768]{1,0:T(8,128)(2,1)} %bitcast.45), kind=kLoop, calls=%fused_computation | loop fusion | flops 9437184 | bytes 9437184 | tf_op jit(solution)/shard_map/concatenate | solution.py:417
  16.6 17.0 %collective-permute-done.refs_1_.refs_0_ = bf16[128,4224]{1,0:T(8,128)(2,1)S(1)} collective-permute-done((bf16[128,4224]{1,0:T(8,128)(2,1)}, bf16[128,4224]{1,0:T(8,128)(2,1)S(1)}, u32[]{:S(2)}, u32[]{:S(2)}) %collective-permute-start) | collective-permute-done | bytes 1081376 | tf_op jit(solution)/shard_map/ppermute | solution.py:55
  34.0 3.3 %collective-permute-start.5 = (bf16[512,1152]{1,0:T(8,128)(2,1)}, bf16[512,1152]{1,0:T(8,128)(2,1)S(1)}, u32[]{:S(2)}, u32[]{:S(2)}) collective-permute-start(bf16[512,1152]{1,0:T(8,128)(2,1)} %collective-permute-done.1.refs_4_.refs_2_), channel_id=1, source_target_pairs={{16,0},{0,16},{17,1},{1,17},{18,2},{2,18},{19,3},{3,19},{20,4},{4,... | collective-permute-start | bytes 3538952 | tf_op jit(solution)/shard_map/ppermute | solution.py:60
  37.3 1.3 collective-permute-start.7
  38.6 8.5 %shard_map.138 = (f32[1,384,1024]{2,1,0:T(8,128)}, bf16[1,1,384,1024]{3,2,1,0:T(8,128)(2,1)}, f32[256,2048]{1,0:T(8,128)}, f32[256,128]{1,0:T(8,128)}) custom-call(bf16[128,4224]{1,0:T(8,128)(2,1)} %get-tuple-element.113.refs_0_, bf16[128,4224]{1,0:T(8,128)(2,1)} %copy-done.3, bf16[2048,1152]{1,0:T(8,128)(2,1)} %pad_maximum_fusion.refs_2_.refs_3_.refs_1_), custom_call_target="tpu_custom_call" | custom-call | flops 1000 | bytes 1000 | tf_op jit(solution)/shard_map/pallas_call | solution.py:283
  47.1 11.3 %collective-permute-done.3.refs_5_.refs_3_ = bf16[512,1152]{1,0:T(8,128)(2,1)} collective-permute-done((bf16[512,1152]{1,0:T(8,128)(2,1)}, bf16[512,1152]{1,0:T(8,128)(2,1)}, u32[]{:S(2)}, u32[]{:S(2)}) %collective-permute-start.3) | collective-permute-done | bytes 1179680 | tf_op jit(solution)/shard_map/ppermute | solution.py:38
  58.4 0.8 collective-permute-done.4.refs_8_.refs_6_
  59.2 3.9 %collective-permute-done.7.refs_2_.refs_1_ = bf16[128,4224]{1,0:T(8,128)(2,1)S(1)} collective-permute-done((bf16[128,4224]{1,0:T(8,128)(2,1)S(1)}, bf16[128,4224]{1,0:T(8,128)(2,1)S(1)}, u32[]{:S(2)}, u32[]{:S(2)}) %collective-permute-start.7) | collective-permute-done | bytes 1081376 | tf_op jit(solution)/shard_map/ppermute | solution.py:55
  63.1 1.4 collective-permute-start.8
  64.6 0.9 collective-permute-start.9
  65.5 1.2 collective-permute-start.10
  67.0 0.5 collective-permute-start.12
  67.5 1.6 collective-permute-done.9.refs_10_.refs_8_
  69.1 20.6 %shard_map.139 = (f32[3,384,1024]{2,1,0:T(8,128)}, bf16[3,1,384,1024]{3,2,1,0:T(8,128)(2,1)}, f32[384,2048]{1,0:T(8,128)}, f32[384,128]{1,0:T(8,128)}) custom-call(bf16[128,4224]{1,0:T(8,128)(2,1)} %get-tuple-element.113.refs_0_, bf16[128,4224]{1,0:T(8,128)(2,1)} %copy-done.3, bf16[128,4224]{1,0:T(8,128)(2,1)} %copy-done.12, ...), custom_call_target="tpu_custom_call" | custom-call | flops 1000 | bytes 1000 | tf_op jit(solution)/shard_map/pallas_call | solution.py:283
  89.7 3.3 %collective-permute-done.12.refs_0_.refs_1_ = bf16[128,4224]{1,0:T(8,128)(2,1)} collective-permute-done((bf16[128,4224]{1,0:T(8,128)(2,1)}, bf16[128,4224]{1,0:T(8,128)(2,1)}, u32[]{:S(2)}, u32[]{:S(2)}) %collective-permute-start.12) | collective-permute-done | bytes 1081376 | tf_op jit(solution)/shard_map/ppermute | solution.py:55
  93.4 0.8 collective-permute-done.11.refs_3_
  94.2 1.1 collective-permute-start.13
  95.3 13.9 %shard_map.140 = (f32[3,384,1024]{2,1,0:T(8,128)}, bf16[3,1,384,1024]{3,2,1,0:T(8,128)(2,1)}, f32[128,2048]{1,0:T(8,128)}, f32[128,128]{1,0:T(8,128)}) custom-call(bf16[128,4224]{1,0:T(8,128)(2,1)} %collective-permute-done.12.refs_0_.refs_1_, bf16[2048,1152]{1,0:T(8,128)(2,1)} %pad_maximum_fusion.refs_2_.refs_3_.refs_1_, ...), custom_call_target="tpu_custom_call" | custom-call | flops 1000 | bytes 1000 | tf_op jit(solution)/shard_map/pallas_call | solution.py:283
  109.3 0.6 collective-permute-start.15
  109.9 0.4 copy-done.7
  110.7 8.9 %shard_map.141 = (f32[1,384,1024]{2,1,0:T(8,128)}, bf16[1,1,384,1024]{3,2,1,0:T(8,128)(2,1)}, bf16[128,2176]{1,0:T(8,128)(2,1)}, bf16[128,2176]{1,0:T(8,128)(2,1)}) custom-call(bf16[128,4224]{1,0:T(8,128)(2,1)} %copy-done.3, bf16[128,4224]{1,0:T(8,128)(2,1)} %copy-done.12, bf16[512,1152]{1,0:T(8,128)(2,1)} %copy-done.5, bf16[512,1152]{1,0:T(8,128)(2,1)} %copy-done.6, ...), custom_call_target="tpu_custom_call" | custom-call | flops 1000 | bytes 1000 | tf_op jit(solution)/shard_map/pallas_call | solution.py:283
  119.6 0.8 collective-permute-start.18
  120.5 2.3 %fusion.9 = (bf16[192,1024]{1,0:T(8,128)(2,1)}, bf16[192,1024]{1,0:T(8,128)(2,1)}) fusion(f32[3,384,1024]{2,1,0:T(8,128)S(1)} %copy-done.4, bf16[3,384,1024]{2,1,0:T(8,128)(2,1)} %collective-permute-done.15), kind=kLoop, calls=%fused_computation.24 | loop fusion | flops 1179648 | bytes 3145728 | tf_op jit(solution)/shard_map/convert_element_type | solution.py:478
  122.7 0.5 collective-permute-start.16
  123.5 9.2 %shard_map.142 = (f32[1,384,1024]{2,1,0:T(8,128)}, bf16[1,1,384,1024]{3,2,1,0:T(8,128)(2,1)}, bf16[128,2176]{1,0:T(8,128)(2,1)}, bf16[128,2176]{1,0:T(8,128)(2,1)}) custom-call(bf16[128,4224]{1,0:T(8,128)(2,1)} %get-tuple-element.113.refs_0_, bf16[128,4224]{1,0:T(8,128)(2,1)} %collective-permute-done.12.refs_0_.refs_1_, bf16[512,1152]{1,0:T(8,128)(2,1)} %copy-done.5, ...), custom_call_target="tpu_custom_call" | custom-call | flops 1000 | bytes 1000 | tf_op jit(solution)/shard_map/pallas_call | solution.py:283
  132.9 1.9 %collective-permute-done.18 = bf16[128,2176]{1,0:T(8,128)(2,1)S(1)} collective-permute-done((bf16[128,2176]{1,0:T(8,128)(2,1)}, bf16[128,2176]{1,0:T(8,128)(2,1)S(1)}, u32[]{:S(2)}, u32[]{:S(2)}) %collective-permute-start.18) | collective-permute-done | bytes 557088 | tf_op jit(solution)/shard_map/ppermute | solution.py:55
  134.7 1.4 collective-permute-start.19
  136.2 2.0 %collective-permute-start.22 = (bf16[128,2176]{1,0:T(8,128)(2,1)S(1)}, bf16[128,2176]{1,0:T(8,128)(2,1)S(1)}, u32[]{:S(2)}, u32[]{:S(2)}) collective-permute-start(bf16[128,2176]{1,0:T(8,128)(2,1)S(1)} %add_convert_fusion.1), channel_id=1, source_target_pairs={{0,4},{1,5},{2,6},{3,7},{4,12},{5,13},{6,14},{7,15},{12,8},{13,9},... | collective-permute-start | bytes 1671176 | tf_op jit(solution)/shard_map/ppermute | solution.py:55
  138.6 1.0 collective-permute-start.20
  140.1 11.4 %collective-permute-done.22 = bf16[128,2176]{1,0:T(8,128)(2,1)S(1)} collective-permute-done((bf16[128,2176]{1,0:T(8,128)(2,1)S(1)}, bf16[128,2176]{1,0:T(8,128)(2,1)S(1)}, u32[]{:S(2)}, u32[]{:S(2)}) %collective-permute-start.22) | collective-permute-done | bytes 557088 | tf_op jit(solution)/shard_map/ppermute | solution.py:55
  151.6 1.6 fusion.4
  153.6 0.5 collective-permute-start.25
  154.1 1.7 collective-permute-start.27
  155.8 7.4 %collective-permute-done.23 = bf16[192,1024]{1,0:T(8,128)(2,1)S(1)} collective-permute-done((bf16[192,1024]{1,0:T(8,128)(2,1)S(1)}, bf16[192,1024]{1,0:T(8,128)(2,1)S(1)}, u32[]{:S(2)}, u32[]{:S(2)}) %collective-permute-start.23) | collective-permute-done | bytes 393248 | tf_op jit(solution)/shard_map/ppermute | solution.py:38
  163.2 1.6 fusion.3
  164.9 2.0 %collective-permute-start.24 = (bf16[192,1024]{1,0:T(8,128)(2,1)S(1)}, bf16[192,1024]{1,0:T(8,128)(2,1)S(1)}, u32[]{:S(2)}, u32[]{:S(2)}) collective-permute-start(bf16[192,1024]{1,0:T(8,128)(2,1)S(1)} %get-tuple-element.167.refs_0_), channel_id=1, source_target_pairs={{16,0},{0,16},{17,1},{1,17},{18,2},{2,18},{19,3},{3,19},{20,4},{4,... | collective-permute-start | bytes 1179656 | tf_op jit(solution)/shard_map/ppermute | solution.py:60
  168.8 5.2 %shard_map.143 = (f32[1,1,384,2048]{3,2,1,0:T(8,128)}, f32[1,1,384,2048]{3,2,1,0:T(8,128)}, bf16[384,2048]{1,0:T(8,128)(2,1)S(1)}) custom-call(s32[1]{0:T(128)} %copy.20.lead_ref, bf16[192,1024]{1,0:T(8,128)(2,1)S(1)} %get-tuple-element.167.refs_0_, bf16[192,1024]{1,0:T(8,128)(2,1)S(1)} %get-tuple-element.166.refs_1_, ...), custom_call_target="tpu_custom_call" | custom-call | flops 1000 | bytes 1000 | tf_op jit(solution)/shard_map/pallas_call | solution.py:379
  173.9 2.2 %collective-permute-start.28 = (bf16[384,2048]{1,0:T(8,128)(2,1)S(1)}, bf16[384,2048]{1,0:T(8,128)(2,1)}, u32[]{:S(2)}, u32[]{:S(2)}) collective-permute-start(bf16[384,2048]{1,0:T(8,128)(2,1)S(1)} %get-tuple-element.158), channel_id=1, source_target_pairs={{16,0},{0,16},{17,1},{1,17},{18,2},{2,18},{19,3},{3,19},{20,4},{4,... | collective-permute-start | bytes 4718600 | tf_op jit(solution)/shard_map/ppermute | solution.py:60
  176.2 0.7 fusion.11
  176.9 1.3 convert_add_fusion
  178.2 0.9 slice.122
  179.5 0.7 copy.19
  180.2 3.4 %fusion.1 = bf16[1,1,384,2048]{3,2,1,0:T(8,128)(2,1)} fusion(bf16[1,384,2048]{2,1,0:T(8,128)(2,1)S(1)} %copy-done, bf16[384,2048]{1,0:T(8,128)(2,1)} %collective-permute-done.28, bf16[384,2048]{1,0:T(8,128)(2,1)S(1)} %get-tuple-element.158, pred[]{:T(512)S(6)} %eq.29, pred[]{:T(512)} %bitcast.14), kind=kLoop, calls=%fused_computation.4 | loop fusion | flops 1572864 | bytes 6291458 | tf_op jit(solution)/shard_map/broadcast_in_dim | solution.py:524
  (72 shorter events, 5.4 us)
Async XLA Ops:
  0.6 9.5 %copy-start = (bf16[1,384,2048]{2,1,0:T(8,128)(2,1)S(1)}, bf16[1,384,2048]{2,1,0:T(8,128)(2,1)}, u32[]{:S(2)}) copy-start(bf16[1,384,2048]{2,1,0:T(8,128)(2,1)} %refs_6_.1) | copy-start | bytes 4718596
  5.0 28.6 %collective-permute-start.1 = (bf16[512,1152]{1,0:T(8,128)(2,1)}, bf16[512,1152]{1,0:T(8,128)(2,1)}, u32[]{:S(2)}, u32[]{:S(2)}) collective-permute-start(bf16[512,1152]{1,0:T(8,128)(2,1)} %get-tuple-element.85), channel_id=1, source_target_pairs={{0,1},{1,0},{2,3},{3,2},{4,5},{5,4},{6,7},{7,6},{8,9},{9,8},{10,11... | collective-permute-start | bytes 3538952 | tf_op jit(solution)/shard_map/ppermute | solution.py:38
  7.1 26.8 %collective-permute-start.2 = (bf16[512,1152]{1,0:T(8,128)(2,1)}, bf16[512,1152]{1,0:T(8,128)(2,1)}, u32[]{:S(2)}, u32[]{:S(2)}) collective-permute-start(bf16[512,1152]{1,0:T(8,128)(2,1)} %get-tuple-element.86), channel_id=1, source_target_pairs={{0,2},{1,3},{2,0},{3,1},{4,6},{5,7},{6,4},{7,5},{8,10},{9,11},{10,... | collective-permute-start | bytes 3538952 | tf_op jit(solution)/shard_map/ppermute | solution.py:38
  8.4 25.2 %collective-permute-start = (bf16[128,4224]{1,0:T(8,128)(2,1)}, bf16[128,4224]{1,0:T(8,128)(2,1)S(1)}, u32[]{:S(2)}, u32[]{:S(2)}) collective-permute-start(bf16[128,4224]{1,0:T(8,128)(2,1)} %get-tuple-element.113.refs_0_), channel_id=1, source_target_pairs={{0,4},{1,5},{2,6},{3,7},{4,12},{5,13},{6,14},{7,15},{12,8},{13,9},... | collective-permute-start | bytes 3244040 | tf_op jit(solution)/shard_map/ppermute | solution.py:55
  9.7 48.8 %collective-permute-start.3 = (bf16[512,1152]{1,0:T(8,128)(2,1)}, bf16[512,1152]{1,0:T(8,128)(2,1)}, u32[]{:S(2)}, u32[]{:S(2)}) collective-permute-start(bf16[512,1152]{1,0:T(8,128)(2,1)} %get-tuple-element.86), channel_id=1, source_target_pairs={{0,1},{1,0},{2,3},{3,2},{4,5},{5,4},{6,7},{7,6},{8,9},{9,8},{10,11... | collective-permute-start | bytes 3538952 | tf_op jit(solution)/shard_map/ppermute | solution.py:38
  9.9 49.3 %collective-permute-start.4 = (bf16[512,1152]{1,0:T(8,128)(2,1)}, bf16[512,1152]{1,0:T(8,128)(2,1)}, u32[]{:S(2)}, u32[]{:S(2)}) collective-permute-start(bf16[512,1152]{1,0:T(8,128)(2,1)} %get-tuple-element.85), channel_id=1, source_target_pairs={{0,2},{1,3},{2,0},{3,1},{4,6},{5,7},{6,4},{7,5},{8,10},{9,11},{10,... | collective-permute-start | bytes 3538952 | tf_op jit(solution)/shard_map/ppermute | solution.py:38
  33.6 5.0 %copy-start.3 = (bf16[128,4224]{1,0:T(8,128)(2,1)}, bf16[128,4224]{1,0:T(8,128)(2,1)S(1)}, u32[]{:S(2)}) copy-start(bf16[128,4224]{1,0:T(8,128)(2,1)S(1)} %collective-permute-done.refs_1_.refs_0_) | copy-start | bytes 3244036
  34.0 29.2 %collective-permute-start.5 = (bf16[512,1152]{1,0:T(8,128)(2,1)}, bf16[512,1152]{1,0:T(8,128)(2,1)S(1)}, u32[]{:S(2)}, u32[]{:S(2)}) collective-permute-start(bf16[512,1152]{1,0:T(8,128)(2,1)} %collective-permute-done.1.refs_4_.refs_2_), channel_id=1, source_target_pairs={{16,0},{0,16},{17,1},{1,17},{18,2},{2,18},{19,3},{3,19},{20,4},{4,... | collective-permute-start | bytes 3538952 | tf_op jit(solution)/shard_map/ppermute | solution.py:60
  37.3 25.8 %collective-permute-start.6 = (bf16[512,1152]{1,0:T(8,128)(2,1)}, bf16[512,1152]{1,0:T(8,128)(2,1)S(1)}, u32[]{:S(2)}, u32[]{:S(2)}) collective-permute-start(bf16[512,1152]{1,0:T(8,128)(2,1)} %collective-permute-done.2.refs_9_.refs_7_), channel_id=1, source_target_pairs={{16,0},{0,16},{17,1},{1,17},{18,2},{2,18},{19,3},{3,19},{20,4},{4,... | collective-permute-start | bytes 3538952 | tf_op jit(solution)/shard_map/ppermute | solution.py:60
  37.3 25.8 %collective-permute-start.7 = (bf16[128,4224]{1,0:T(8,128)(2,1)S(1)}, bf16[128,4224]{1,0:T(8,128)(2,1)S(1)}, u32[]{:S(2)}, u32[]{:S(2)}) collective-permute-start(bf16[128,4224]{1,0:T(8,128)(2,1)S(1)} %collective-permute-done.refs_1_.refs_0_), channel_id=1, source_target_pairs={{0,4},{1,5},{2,6},{3,7},{4,12},{5,13},{6,14},{7,15},{12,8},{13,9},... | collective-permute-start | bytes 3244040 | tf_op jit(solution)/shard_map/ppermute | solution.py:55
  63.1 1.5 copy-start.12
  63.1 6.0 %copy-start.9 = (bf16[512,1152]{1,0:T(8,128)(2,1)}, bf16[512,1152]{1,0:T(8,128)(2,1)S(1)}, u32[]{:S(2)}) copy-start(bf16[512,1152]{1,0:T(8,128)(2,1)S(1)} %collective-permute-done.5.refs_6_.refs_4_) | copy-start | bytes 3538948
  63.1 5.9 %copy-start.10 = (bf16[512,1152]{1,0:T(8,128)(2,1)}, bf16[512,1152]{1,0:T(8,128)(2,1)S(1)}, u32[]{:S(2)}) copy-start(bf16[512,1152]{1,0:T(8,128)(2,1)S(1)} %collective-permute-done.6.refs_11_.refs_9_) | copy-start | bytes 3538948
  63.1 4.3 %collective-permute-start.8 = (bf16[512,1152]{1,0:T(8,128)(2,1)}, bf16[512,1152]{1,0:T(8,128)(2,1)S(1)}, u32[]{:S(2)}, u32[]{:S(2)}) collective-permute-start(bf16[512,1152]{1,0:T(8,128)(2,1)} %collective-permute-done.3.refs_5_.refs_3_), channel_id=1, source_target_pairs={{16,0},{0,16},{17,1},{1,17},{18,2},{2,18},{19,3},{3,19},{20,4},{4,... | collective-permute-start | bytes 3538952 | tf_op jit(solution)/shard_map/ppermute | solution.py:60
  64.6 4.5 %collective-permute-start.9 = (bf16[512,1152]{1,0:T(8,128)(2,1)}, bf16[512,1152]{1,0:T(8,128)(2,1)}, u32[]{:S(2)}, u32[]{:S(2)}) collective-permute-start(bf16[512,1152]{1,0:T(8,128)(2,1)} %collective-permute-done.4.refs_8_.refs_6_), channel_id=1, source_target_pairs={{16,0},{0,16},{17,1},{1,17},{18,2},{2,18},{19,3},{3,19},{20,4},{4,... | collective-permute-start | bytes 3538952 | tf_op jit(solution)/shard_map/ppermute | solution.py:60
  65.5 27.9 %collective-permute-start.10 = (bf16[512,1152]{1,0:T(8,128)(2,1)}, bf16[512,1152]{1,0:T(8,128)(2,1)S(1)}, u32[]{:S(2)}, u32[]{:S(2)}) collective-permute-start(bf16[512,1152]{1,0:T(8,128)(2,1)} %collective-permute-done.1.refs_4_.refs_2_), channel_id=1, source_target_pairs={{0,2},{1,3},{2,0},{3,1},{4,6},{5,7},{6,4},{7,5},{8,10},{9,11},{10,... | collective-permute-start | bytes 3538952 | tf_op jit(solution)/shard_map/ppermute | solution.py:38
  66.7 27.5 %collective-permute-start.11 = (bf16[512,1152]{1,0:T(8,128)(2,1)}, bf16[512,1152]{1,0:T(8,128)(2,1)S(1)}, u32[]{:S(2)}, u32[]{:S(2)}) collective-permute-start(bf16[512,1152]{1,0:T(8,128)(2,1)} %collective-permute-done.2.refs_9_.refs_7_), channel_id=1, source_target_pairs={{0,1},{1,0},{2,3},{3,2},{4,5},{5,4},{6,7},{7,6},{8,9},{9,8},{10,11... | collective-permute-start | bytes 3538952 | tf_op jit(solution)/shard_map/ppermute | solution.py:38
  67.0 26.1 %collective-permute-start.12 = (bf16[128,4224]{1,0:T(8,128)(2,1)}, bf16[128,4224]{1,0:T(8,128)(2,1)}, u32[]{:S(2)}, u32[]{:S(2)}) collective-permute-start(bf16[128,4224]{1,0:T(8,128)(2,1)} %copy-done.12), channel_id=1, source_target_pairs={{0,4},{1,5},{2,6},{3,7},{4,12},{5,13},{6,14},{7,15},{12,8},{13,9},... | collective-permute-start | bytes 3244040 | tf_op jit(solution)/shard_map/ppermute | solution.py:55
  67.5 1.6 copy-start.11
  93.4 15.8 %copy-start.5 = (bf16[512,1152]{1,0:T(8,128)(2,1)}, bf16[512,1152]{1,0:T(8,128)(2,1)S(1)}, u32[]{:S(2)}) copy-start(bf16[512,1152]{1,0:T(8,128)(2,1)S(1)} %collective-permute-done.10.refs_2_) | copy-start | bytes 3538948
  94.2 15.0 %copy-start.6 = (bf16[512,1152]{1,0:T(8,128)(2,1)}, bf16[512,1152]{1,0:T(8,128)(2,1)S(1)}, u32[]{:S(2)}) copy-start(bf16[512,1152]{1,0:T(8,128)(2,1)S(1)} %collective-permute-done.11.refs_3_) | copy-start | bytes 3538948
  94.2 15.0 %collective-permute-start.13 = (bf16[512,1152]{1,0:T(8,128)(2,1)S(1)}, bf16[512,1152]{1,0:T(8,128)(2,1)S(1)}, u32[]{:S(2)}, u32[]{:S(2)}) collective-permute-start(bf16[512,1152]{1,0:T(8,128)(2,1)S(1)} %collective-permute-done.10.refs_2_), channel_id=1, source_target_pairs={{16,0},{0,16},{17,1},{1,17},{18,2},{2,18},{19,3},{3,19},{20,4},{4,... | collective-permute-start | bytes 3538952 | tf_op jit(solution)/shard_map/ppermute | solution.py:60
  95.3 14.0 %collective-permute-start.14 = (bf16[512,1152]{1,0:T(8,128)(2,1)S(1)}, bf16[512,1152]{1,0:T(8,128)(2,1)S(1)}, u32[]{:S(2)}, u32[]{:S(2)}) collective-permute-start(bf16[512,1152]{1,0:T(8,128)(2,1)S(1)} %collective-permute-done.11.refs_3_), channel_id=1, source_target_pairs={{16,0},{0,16},{17,1},{1,17},{18,2},{2,18},{19,3},{3,19},{20,4},{4,... | collective-permute-start | bytes 3538952 | tf_op jit(solution)/shard_map/ppermute | solution.py:60
  109.3 1.1 copy-start.7
  109.3 1.5 copy-start.8
  109.3 10.4 %collective-permute-start.15 = (bf16[3,384,1024]{2,1,0:T(8,128)(2,1)}, bf16[3,384,1024]{2,1,0:T(8,128)(2,1)}, u32[]{:S(2)}, u32[]{:S(2)}) collective-permute-start(bf16[3,384,1024]{2,1,0:T(8,128)(2,1)} %bitcast.48), channel_id=1, source_target_pairs={{16,0},{0,16},{17,1},{1,17},{18,2},{2,18},{19,3},{3,19},{20,4},{4,... | collective-permute-start | bytes 7077896 | tf_op jit(solution)/shard_map/ppermute | solution.py:60
  110.7 9.7 %copy-start.4 = (f32[3,384,1024]{2,1,0:T(8,128)S(1)}, f32[3,384,1024]{2,1,0:T(8,128)}, u32[]{:S(2)}) copy-start(f32[3,384,1024]{2,1,0:T(8,128)} %get-tuple-element.140) | copy-start | bytes 14155780
  119.6 15.1 %collective-permute-start.18 = (bf16[128,2176]{1,0:T(8,128)(2,1)}, bf16[128,2176]{1,0:T(8,128)(2,1)S(1)}, u32[]{:S(2)}, u32[]{:S(2)}) collective-permute-start(bf16[128,2176]{1,0:T(8,128)(2,1)} %get-tuple-element.137), channel_id=1, source_target_pairs={{0,4},{1,5},{2,6},{3,7},{4,12},{5,13},{6,14},{7,15},{12,8},{13,9},... | collective-permute-start | bytes 1671176 | tf_op jit(solution)/shard_map/ppermute | solution.py:55
  122.7 10.1 %collective-permute-start.16 = (bf16[192,1024]{1,0:T(8,128)(2,1)}, bf16[192,1024]{1,0:T(8,128)(2,1)S(1)}, u32[]{:S(2)}, u32[]{:S(2)}) collective-permute-start(bf16[192,1024]{1,0:T(8,128)(2,1)} %get-tuple-element.171), channel_id=1, source_target_pairs={{0,1},{1,0},{2,3},{3,2},{4,5},{5,4},{6,7},{7,6},{8,9},{9,8},{10,11... | collective-permute-start | bytes 1179656 | tf_op jit(solution)/shard_map/ppermute | solution.py:38
  123.2 12.9 %copy-start.16 = (bf16[128,2176]{1,0:T(8,128)(2,1)S(1)}, bf16[128,2176]{1,0:T(8,128)(2,1)}, u32[]{:S(2)}) copy-start(bf16[128,2176]{1,0:T(8,128)(2,1)} %get-tuple-element.146) | copy-start | bytes 1671172
  123.3 9.6 %collective-permute-start.17 = (bf16[192,1024]{1,0:T(8,128)(2,1)}, bf16[192,1024]{1,0:T(8,128)(2,1)S(1)}, u32[]{:S(2)}, u32[]{:S(2)}) collective-permute-start(bf16[192,1024]{1,0:T(8,128)(2,1)} %get-tuple-element.170), channel_id=1, source_target_pairs={{0,2},{1,3},{2,0},{3,1},{4,6},{5,7},{6,4},{7,5},{8,10},{9,11},{10,... | collective-permute-start | bytes 1179656 | tf_op jit(solution)/shard_map/ppermute | solution.py:38
  132.7 5.6 %copy-start.13 = (f32[1,384,1024]{2,1,0:T(8,128)S(1)}, f32[1,384,1024]{2,1,0:T(8,128)}, u32[]{:S(2)}) copy-start(f32[1,384,1024]{2,1,0:T(8,128)} %get-tuple-element.143) | copy-start | bytes 4718596
  134.7 3.6 %collective-permute-start.19 = (bf16[384,1024]{1,0:T(8,128)(2,1)}, bf16[384,1024]{1,0:T(8,128)(2,1)S(1)}, u32[]{:S(2)}, u32[]{:S(2)}) collective-permute-start(bf16[384,1024]{1,0:T(8,128)(2,1)} %bitcast.49), channel_id=1, source_target_pairs={{16,0},{0,16},{17,1},{1,17},{18,2},{2,18},{19,3},{3,19},{20,4},{4,... | collective-permute-start | bytes 2359304 | tf_op jit(solution)/shard_map/ppermute | solution.py:60
  136.2 15.2 %collective-permute-start.22 = (bf16[128,2176]{1,0:T(8,128)(2,1)S(1)}, bf16[128,2176]{1,0:T(8,128)(2,1)S(1)}, u32[]{:S(2)}, u32[]{:S(2)}) collective-permute-start(bf16[128,2176]{1,0:T(8,128)(2,1)S(1)} %add_convert_fusion.1), channel_id=1, source_target_pairs={{0,4},{1,5},{2,6},{3,7},{4,12},{5,13},{6,14},{7,15},{12,8},{13,9},... | collective-permute-start | bytes 1671176 | tf_op jit(solution)/shard_map/ppermute | solution.py:55
  138.6 12.9 %copy-start.15 = (bf16[128,2176]{1,0:T(8,128)(2,1)S(1)}, bf16[128,2176]{1,0:T(8,128)(2,1)}, u32[]{:S(2)}) copy-start(bf16[128,2176]{1,0:T(8,128)(2,1)} %get-tuple-element.150) | copy-start | bytes 1671172
  138.6 12.8 %collective-permute-start.20 = (bf16[192,1024]{1,0:T(8,128)(2,1)S(1)}, bf16[192,1024]{1,0:T(8,128)(2,1)S(1)}, u32[]{:S(2)}, u32[]{:S(2)}) collective-permute-start(bf16[192,1024]{1,0:T(8,128)(2,1)S(1)} %get-tuple-element.173), channel_id=1, source_target_pairs={{0,1},{1,0},{2,3},{3,2},{4,5},{5,4},{6,7},{7,6},{8,9},{9,8},{10,11... | collective-permute-start | bytes 1179656 | tf_op jit(solution)/shard_map/ppermute | solution.py:38
  139.7 11.8 %collective-permute-start.21 = (bf16[192,1024]{1,0:T(8,128)(2,1)S(1)}, bf16[192,1024]{1,0:T(8,128)(2,1)S(1)}, u32[]{:S(2)}, u32[]{:S(2)}) collective-permute-start(bf16[192,1024]{1,0:T(8,128)(2,1)S(1)} %get-tuple-element.172), channel_id=1, source_target_pairs={{0,2},{1,3},{2,0},{3,1},{4,6},{5,7},{6,4},{7,5},{8,10},{9,11},{10,... | collective-permute-start | bytes 1179656 | tf_op jit(solution)/shard_map/ppermute | solution.py:38
  151.6 17.1 %copy-start.2 = (f32[1,1,384,2048]{3,2,1,0:T(8,128)S(1)}, f32[1,1,384,2048]{3,2,1,0:T(8,128)}, u32[]{:S(2)}) copy-start(f32[1,1,384,2048]{3,2,1,0:T(8,128)} %refs_5_.1) | copy-start | bytes 9437188
  153.3 15.5 %copy-start.1 = (f32[1,1,384,2048]{3,2,1,0:T(8,128)S(1)}, f32[1,1,384,2048]{3,2,1,0:T(8,128)}, u32[]{:S(2)}) copy-start(f32[1,1,384,2048]{3,2,1,0:T(8,128)} %refs_4_.1) | copy-start | bytes 9437188
  153.3 9.9 %collective-permute-start.23 = (bf16[192,1024]{1,0:T(8,128)(2,1)S(1)}, bf16[192,1024]{1,0:T(8,128)(2,1)S(1)}, u32[]{:S(2)}, u32[]{:S(2)}) collective-permute-start(bf16[192,1024]{1,0:T(8,128)(2,1)S(1)} %get-tuple-element.151), channel_id=1, source_target_pairs={{0,2},{1,3},{2,0},{3,1},{4,6},{5,7},{6,4},{7,5},{8,10},{9,11},{10,... | collective-permute-start | bytes 1179656 | tf_op jit(solution)/shard_map/ppermute | solution.py:38
  153.6 9.6 %collective-permute-start.25 = (bf16[192,1024]{1,0:T(8,128)(2,1)S(1)}, bf16[192,1024]{1,0:T(8,128)(2,1)S(1)}, u32[]{:S(2)}, u32[]{:S(2)}) collective-permute-start(bf16[192,1024]{1,0:T(8,128)(2,1)S(1)} %get-tuple-element.153), channel_id=1, source_target_pairs={{0,1},{1,0},{2,3},{3,2},{4,5},{5,4},{6,7},{7,6},{8,9},{9,8},{10,11... | collective-permute-start | bytes 1179656 | tf_op jit(solution)/shard_map/ppermute | solution.py:38
  154.1 13.7 %collective-permute-start.27 = (bf16[128,2176]{1,0:T(8,128)(2,1)S(1)}, bf16[128,2176]{1,0:T(8,128)(2,1)S(1)}, u32[]{:S(2)}, u32[]{:S(2)}) collective-permute-start(bf16[128,2176]{1,0:T(8,128)(2,1)S(1)} %add_convert_fusion), channel_id=1, source_target_pairs={{0,4},{1,5},{2,6},{3,7},{4,12},{5,13},{6,14},{7,15},{12,8},{13,9},... | collective-permute-start | bytes 1671176 | tf_op jit(solution)/shard_map/ppermute | solution.py:55
  164.9 3.3 %collective-permute-start.24 = (bf16[192,1024]{1,0:T(8,128)(2,1)S(1)}, bf16[192,1024]{1,0:T(8,128)(2,1)S(1)}, u32[]{:S(2)}, u32[]{:S(2)}) collective-permute-start(bf16[192,1024]{1,0:T(8,128)(2,1)S(1)} %get-tuple-element.167.refs_0_), channel_id=1, source_target_pairs={{16,0},{0,16},{17,1},{1,17},{18,2},{2,18},{19,3},{3,19},{20,4},{4,... | collective-permute-start | bytes 1179656 | tf_op jit(solution)/shard_map/ppermute | solution.py:60
  166.9 1.9 %collective-permute-start.26 = (bf16[192,1024]{1,0:T(8,128)(2,1)S(1)}, bf16[192,1024]{1,0:T(8,128)(2,1)S(1)}, u32[]{:S(2)}, u32[]{:S(2)}) collective-permute-start(bf16[192,1024]{1,0:T(8,128)(2,1)S(1)} %get-tuple-element.166.refs_1_), channel_id=1, source_target_pairs={{16,0},{0,16},{17,1},{1,17},{18,2},{2,18},{19,3},{3,19},{20,4},{4,... | collective-permute-start | bytes 1179656 | tf_op jit(solution)/shard_map/ppermute | solution.py:60
  167.6 8.5 %copy-start.17 = (s32[128,8]{0,1:T(8,128)S(1)}, s32[128,8]{0,1:T(8,128)}, u32[]{:S(2)}) copy-start(s32[128,8]{0,1:T(8,128)} %param.12) | copy-start | bytes 12292
  167.6 8.6 %copy-start.18 = (s32[1,2]{1,0:T(1,128)S(1)}, s32[1,2]{1,0:T(1,128)}, u32[]{:S(2)}) copy-start(s32[1,2]{1,0:T(1,128)} %param.18) | copy-start | bytes 28
  167.8 0.8 copy-start.14
  173.9 6.2 %collective-permute-start.28 = (bf16[384,2048]{1,0:T(8,128)(2,1)S(1)}, bf16[384,2048]{1,0:T(8,128)(2,1)}, u32[]{:S(2)}, u32[]{:S(2)}) collective-permute-start(bf16[384,2048]{1,0:T(8,128)(2,1)S(1)} %get-tuple-element.158), channel_id=1, source_target_pairs={{16,0},{0,16},{17,1},{1,17},{18,2},{2,18},{19,3},{3,19},{20,4},{4,... | collective-permute-start | bytes 4718600 | tf_op jit(solution)/shard_map/ppermute | solution.py:60

commit v7 on v6

--- a/solution.py
+++ b/solution.py
@@ -392,7 +392,7 @@
         * n_dp
         + [wide, wide, pl.BlockSpec((1, step, model), lambda i: (0, i, 0))],
         out_specs=[wide, wide, pl.BlockSpec((step, model), lambda i: (i, 0))],
-        compiler_params=pltpu.CompilerParams(vmem_limit_bytes=32 * 2**20),
+        compiler_params=pltpu.CompilerParams(vmem_limit_bytes=12 * 2**20),
         cost_estimate=pl.CostEstimate(
             flops=1000, bytes_accessed=1000, transcendentals=0
         ),

time: 184 us -> 183 us (level)
  no operation moved by 1% of the time
where the time goes in v7:
time: 183 us
  Pallas kernels  70.7 us (39%)
  waiting for transfers between devices  61.4 us (34%)
  starting transfers between devices  28.1 us (15%)
  other arithmetic  16.9 us (9%)
  local copies, waits for them, and re-layouts  4.22 us (2%)
    pallas_call x5, Pallas kernels, call(): pl.pallas_call(functools.partial(self.kernel, len(ins)), out_shape=[jax.S...  61.1 us
    ppermute x6, waiting for transfers between devices, along(): return lax.ppermute(value, 'expert', pairs)  37.6 us
    ppermute x12, waiting for transfers between devices, hop(): return lax.ppermute(value, 'expert', [(i, i ^ flip) for i in range(n)])  21.2 us
    ppermute x11, starting transfers between devices, turn(): return lax.ppermute(value, 'dp', [((r + step) % n, r) for r in range(n)])  12.2 us
    ppermute x12, starting transfers between devices, hop(): return lax.ppermute(value, 'expert', [(i, i ^ flip) for i in range(n)])  8.32 us
    ppermute x6, starting transfers between devices, along(): return lax.ppermute(value, 'expert', pairs)  7.63 us
    pallas_call x1, Pallas kernels, adam_call(): pl.pallas_call(functools.partial(adam_kernel, n_dp, cut), grid=(steps,),...  5.2 us
    concatenate x1, other arithmetic, body(): w_own = jnp.concatenate([w_gu, w_dn.T], 1)  4.92 us
  transfers between devices with their start and end apart: 29, of which 17 were waited for; matrix products, arithmetic and copies ran while one was open for 8% of the time, Pallas kernels for 33%

profile of v7, /device:TPU:1, one launch (start us, length us, event | category | flops | bytes accessed | tf_op | source)
XLA Modules:
  0.0 182.9 jit_solution(12361597047875698181)
XLA Ops:
  0.6 4.4 %shard_map.137 = (bf16[512,1152]{1,0:T(8,128)(2,1)}, bf16[512,1152]{1,0:T(8,128)(2,1)}, bf16[128,4224]{1,0:T(8,128)(2,1)}) custom-call(bf16[128,2048]{1,0:T(8,128)(2,1)} %x_ref.1, bf16[128,2048]{1,0:T(8,128)(2,1)} %y_ref.1, s32[8,128]{1,0:T(8,128)} %bitcast.46, bf16[8,128]{1,0:T(8,128)(2,1)} %bitcast.47, bf16[1,2048,768]{2,1,0:T(8,128)(2,1)} %gu_ref.1, ...), custom_call_target="tpu_custom_call" | custom-call | flops 1000 | bytes 1000 | tf_op jit(solution)/shard_map/pallas_call | solution.py:338
  5.0 2.1 %collective-permute-start.1 = (bf16[512,1152]{1,0:T(8,128)(2,1)}, bf16[512,1152]{1,0:T(8,128)(2,1)}, u32[]{:S(2)}, u32[]{:S(2)}) collective-permute-start(bf16[512,1152]{1,0:T(8,128)(2,1)} %get-tuple-element.85), channel_id=1, source_target_pairs={{0,1},{1,0},{2,3},{3,2},{4,5},{5,4},{6,7},{7,6},{8,9},{9,8},{10,11... | collective-permute-start | bytes 3538952 | tf_op jit(solution)/shard_map/ppermute | solution.py:38
  7.1 1.2 collective-permute-start.2
  8.4 1.3 collective-permute-start
  10.1 1.6 copy.17
  11.7 4.9 %pad_maximum_fusion.refs_2_.refs_3_.refs_1_ = bf16[2048,1152]{1,0:T(8,128)(2,1)} fusion(bf16[2048,384]{1,0:T(8,128)(2,1)} %copy.17, bf16[2048,768]{1,0:T(8,128)(2,1)} %bitcast.45), kind=kLoop, calls=%fused_computation | loop fusion | flops 9437184 | bytes 9437184 | tf_op jit(solution)/shard_map/concatenate | solution.py:417
  16.6 17.0 %collective-permute-done.refs_1_.refs_0_ = bf16[128,4224]{1,0:T(8,128)(2,1)S(1)} collective-permute-done((bf16[128,4224]{1,0:T(8,128)(2,1)}, bf16[128,4224]{1,0:T(8,128)(2,1)S(1)}, u32[]{:S(2)}, u32[]{:S(2)}) %collective-permute-start) | collective-permute-done | bytes 1081376 | tf_op jit(solution)/shard_map/ppermute | solution.py:55
  34.0 3.3 %collective-permute-start.5 = (bf16[512,1152]{1,0:T(8,128)(2,1)}, bf16[512,1152]{1,0:T(8,128)(2,1)S(1)}, u32[]{:S(2)}, u32[]{:S(2)}) collective-permute-start(bf16[512,1152]{1,0:T(8,128)(2,1)} %collective-permute-done.1.refs_4_.refs_2_), channel_id=1, source_target_pairs={{16,0},{0,16},{17,1},{1,17},{18,2},{2,18},{19,3},{3,19},{20,4},{4,... | collective-permute-start | bytes 3538952 | tf_op jit(solution)/shard_map/ppermute | solution.py:60
  37.3 1.3 collective-permute-start.7
  38.6 8.5 %shard_map.138 = (f32[1,384,1024]{2,1,0:T(8,128)}, bf16[1,1,384,1024]{3,2,1,0:T(8,128)(2,1)}, f32[256,2048]{1,0:T(8,128)}, f32[256,128]{1,0:T(8,128)}) custom-call(bf16[128,4224]{1,0:T(8,128)(2,1)} %get-tuple-element.113.refs_0_, bf16[128,4224]{1,0:T(8,128)(2,1)} %copy-done.3, bf16[2048,1152]{1,0:T(8,128)(2,1)} %pad_maximum_fusion.refs_2_.refs_3_.refs_1_), custom_call_target="tpu_custom_call" | custom-call | flops 1000 | bytes 1000 | tf_op jit(solution)/shard_map/pallas_call | solution.py:283
  47.1 11.3 %collective-permute-done.3.refs_5_.refs_3_ = bf16[512,1152]{1,0:T(8,128)(2,1)} collective-permute-done((bf16[512,1152]{1,0:T(8,128)(2,1)}, bf16[512,1152]{1,0:T(8,128)(2,1)}, u32[]{:S(2)}, u32[]{:S(2)}) %collective-permute-start.3) | collective-permute-done | bytes 1179680 | tf_op jit(solution)/shard_map/ppermute | solution.py:38
  58.4 0.8 collective-permute-done.4.refs_8_.refs_6_
  59.2 3.9 %collective-permute-done.7.refs_2_.refs_1_ = bf16[128,4224]{1,0:T(8,128)(2,1)S(1)} collective-permute-done((bf16[128,4224]{1,0:T(8,128)(2,1)S(1)}, bf16[128,4224]{1,0:T(8,128)(2,1)S(1)}, u32[]{:S(2)}, u32[]{:S(2)}) %collective-permute-start.7) | collective-permute-done | bytes 1081376 | tf_op jit(solution)/shard_map/ppermute | solution.py:55
  63.1 1.4 collective-permute-start.8
  64.6 0.9 collective-permute-start.9
  65.5 1.2 collective-permute-start.10
  67.0 0.5 collective-permute-start.12
  67.5 1.6 collective-permute-done.9.refs_10_.refs_8_
  69.1 20.6 %shard_map.139 = (f32[3,384,1024]{2,1,0:T(8,128)}, bf16[3,1,384,1024]{3,2,1,0:T(8,128)(2,1)}, f32[384,2048]{1,0:T(8,128)}, f32[384,128]{1,0:T(8,128)}) custom-call(bf16[128,4224]{1,0:T(8,128)(2,1)} %get-tuple-element.113.refs_0_, bf16[128,4224]{1,0:T(8,128)(2,1)} %copy-done.3, bf16[128,4224]{1,0:T(8,128)(2,1)} %copy-done.12, ...), custom_call_target="tpu_custom_call" | custom-call | flops 1000 | bytes 1000 | tf_op jit(solution)/shard_map/pallas_call | solution.py:283
  89.7 3.3 %collective-permute-done.12.refs_0_.refs_1_ = bf16[128,4224]{1,0:T(8,128)(2,1)} collective-permute-done((bf16[128,4224]{1,0:T(8,128)(2,1)}, bf16[128,4224]{1,0:T(8,128)(2,1)}, u32[]{:S(2)}, u32[]{:S(2)}) %collective-permute-start.12) | collective-permute-done | bytes 1081376 | tf_op jit(solution)/shard_map/ppermute | solution.py:55
  93.4 0.8 collective-permute-done.11.refs_3_
  94.2 1.1 collective-permute-start.13
  95.3 13.9 %shard_map.140 = (f32[3,384,1024]{2,1,0:T(8,128)}, bf16[3,1,384,1024]{3,2,1,0:T(8,128)(2,1)}, f32[128,2048]{1,0:T(8,128)}, f32[128,128]{1,0:T(8,128)}) custom-call(bf16[128,4224]{1,0:T(8,128)(2,1)} %collective-permute-done.12.refs_0_.refs_1_, bf16[2048,1152]{1,0:T(8,128)(2,1)} %pad_maximum_fusion.refs_2_.refs_3_.refs_1_, ...), custom_call_target="tpu_custom_call" | custom-call | flops 1000 | bytes 1000 | tf_op jit(solution)/shard_map/pallas_call | solution.py:283
  109.3 0.6 collective-permute-start.15
  110.7 8.9 %shard_map.141 = (f32[1,384,1024]{2,1,0:T(8,128)}, bf16[1,1,384,1024]{3,2,1,0:T(8,128)(2,1)}, bf16[128,2176]{1,0:T(8,128)(2,1)}, bf16[128,2176]{1,0:T(8,128)(2,1)}) custom-call(bf16[128,4224]{1,0:T(8,128)(2,1)} %copy-done.3, bf16[128,4224]{1,0:T(8,128)(2,1)} %copy-done.12, bf16[512,1152]{1,0:T(8,128)(2,1)} %copy-done.5, bf16[512,1152]{1,0:T(8,128)(2,1)} %copy-done.6, ...), custom_call_target="tpu_custom_call" | custom-call | flops 1000 | bytes 1000 | tf_op jit(solution)/shard_map/pallas_call | solution.py:283
  119.6 0.8 collective-permute-start.18
  120.5 2.3 %fusion.9 = (bf16[192,1024]{1,0:T(8,128)(2,1)}, bf16[192,1024]{1,0:T(8,128)(2,1)}) fusion(f32[3,384,1024]{2,1,0:T(8,128)S(1)} %copy-done.4, bf16[3,384,1024]{2,1,0:T(8,128)(2,1)} %collective-permute-done.15), kind=kLoop, calls=%fused_computation.24 | loop fusion | flops 1179648 | bytes 3145728 | tf_op jit(solution)/shard_map/convert_element_type | solution.py:478
  122.7 0.5 collective-permute-start.16
  123.5 9.2 %shard_map.142 = (f32[1,384,1024]{2,1,0:T(8,128)}, bf16[1,1,384,1024]{3,2,1,0:T(8,128)(2,1)}, bf16[128,2176]{1,0:T(8,128)(2,1)}, bf16[128,2176]{1,0:T(8,128)(2,1)}) custom-call(bf16[128,4224]{1,0:T(8,128)(2,1)} %get-tuple-element.113.refs_0_, bf16[128,4224]{1,0:T(8,128)(2,1)} %collective-permute-done.12.refs_0_.refs_1_, bf16[512,1152]{1,0:T(8,128)(2,1)} %copy-done.5, ...), custom_call_target="tpu_custom_call" | custom-call | flops 1000 | bytes 1000 | tf_op jit(solution)/shard_map/pallas_call | solution.py:283
  132.9 1.9 %collective-permute-done.18 = bf16[128,2176]{1,0:T(8,128)(2,1)S(1)} collective-permute-done((bf16[128,2176]{1,0:T(8,128)(2,1)}, bf16[128,2176]{1,0:T(8,128)(2,1)S(1)}, u32[]{:S(2)}, u32[]{:S(2)}) %collective-permute-start.18) | collective-permute-done | bytes 557088 | tf_op jit(solution)/shard_map/ppermute | solution.py:55
  134.7 1.4 collective-permute-start.19
  136.2 2.0 %collective-permute-start.22 = (bf16[128,2176]{1,0:T(8,128)(2,1)S(1)}, bf16[128,2176]{1,0:T(8,128)(2,1)S(1)}, u32[]{:S(2)}, u32[]{:S(2)}) collective-permute-start(bf16[128,2176]{1,0:T(8,128)(2,1)S(1)} %add_convert_fusion.1), channel_id=1, source_target_pairs={{0,4},{1,5},{2,6},{3,7},{4,12},{5,13},{6,14},{7,15},{12,8},{13,9},... | collective-permute-start | bytes 1671176 | tf_op jit(solution)/shard_map/ppermute | solution.py:55
  138.6 1.0 collective-permute-start.20
  140.1 11.4 %collective-permute-done.22 = bf16[128,2176]{1,0:T(8,128)(2,1)S(1)} collective-permute-done((bf16[128,2176]{1,0:T(8,128)(2,1)S(1)}, bf16[128,2176]{1,0:T(8,128)(2,1)S(1)}, u32[]{:S(2)}, u32[]{:S(2)}) %collective-permute-start.22) | collective-permute-done | bytes 557088 | tf_op jit(solution)/shard_map/ppermute | solution.py:55
  151.6 1.7 fusion.4
  153.6 0.5 collective-permute-start.25
  154.1 1.7 collective-permute-start.27
  155.8 7.4 %collective-permute-done.23 = bf16[192,1024]{1,0:T(8,128)(2,1)S(1)} collective-permute-done((bf16[192,1024]{1,0:T(8,128)(2,1)S(1)}, bf16[192,1024]{1,0:T(8,128)(2,1)S(1)}, u32[]{:S(2)}, u32[]{:S(2)}) %collective-permute-start.23) | collective-permute-done | bytes 393248 | tf_op jit(solution)/shard_map/ppermute | solution.py:38
  163.2 1.6 fusion.3
  164.9 2.0 %collective-permute-start.24 = (bf16[192,1024]{1,0:T(8,128)(2,1)S(1)}, bf16[192,1024]{1,0:T(8,128)(2,1)S(1)}, u32[]{:S(2)}, u32[]{:S(2)}) collective-permute-start(bf16[192,1024]{1,0:T(8,128)(2,1)S(1)} %get-tuple-element.167.refs_0_), channel_id=1, source_target_pairs={{16,0},{0,16},{17,1},{1,17},{18,2},{2,18},{19,3},{3,19},{20,4},{4,... | collective-permute-start | bytes 1179656 | tf_op jit(solution)/shard_map/ppermute | solution.py:60
  168.2 0.6 collective-permute-done.26.refs_3_
  168.8 5.2 %shard_map.143 = (f32[1,1,384,2048]{3,2,1,0:T(8,128)}, f32[1,1,384,2048]{3,2,1,0:T(8,128)}, bf16[384,2048]{1,0:T(8,128)(2,1)S(1)}) custom-call(s32[1]{0:T(128)} %copy.20.lead_ref, bf16[192,1024]{1,0:T(8,128)(2,1)S(1)} %get-tuple-element.167.refs_0_, bf16[192,1024]{1,0:T(8,128)(2,1)S(1)} %get-tuple-element.166.refs_1_, ...), custom_call_target="tpu_custom_call" | custom-call | flops 1000 | bytes 1000 | tf_op jit(solution)/shard_map/pallas_call | solution.py:379
  174.0 1.4 collective-permute-start.28
  175.5 0.7 fusion.11
  176.2 1.3 convert_add_fusion
  177.5 0.9 slice.122
  178.8 0.7 copy.19
  179.5 3.4 %fusion.1 = bf16[1,1,384,2048]{3,2,1,0:T(8,128)(2,1)} fusion(bf16[1,384,2048]{2,1,0:T(8,128)(2,1)S(1)} %copy-done, bf16[384,2048]{1,0:T(8,128)(2,1)} %collective-permute-done.28, bf16[384,2048]{1,0:T(8,128)(2,1)S(1)} %get-tuple-element.158, pred[]{:T(512)S(6)} %eq.29, pred[]{:T(512)} %bitcast.14), kind=kLoop, calls=%fused_computation.4 | loop fusion | flops 1572864 | bytes 6291458 | tf_op jit(solution)/shard_map/broadcast_in_dim | solution.py:524
  (72 shorter events, 5.3 us)
Async XLA Ops:
  0.6 9.5 %copy-start = (bf16[1,384,2048]{2,1,0:T(8,128)(2,1)S(1)}, bf16[1,384,2048]{2,1,0:T(8,128)(2,1)}, u32[]{:S(2)}) copy-start(bf16[1,384,2048]{2,1,0:T(8,128)(2,1)} %refs_6_.1) | copy-start | bytes 4718596
  5.0 28.6 %collective-permute-start.1 = (bf16[512,1152]{1,0:T(8,128)(2,1)}, bf16[512,1152]{1,0:T(8,128)(2,1)}, u32[]{:S(2)}, u32[]{:S(2)}) collective-permute-start(bf16[512,1152]{1,0:T(8,128)(2,1)} %get-tuple-element.85), channel_id=1, source_target_pairs={{0,1},{1,0},{2,3},{3,2},{4,5},{5,4},{6,7},{7,6},{8,9},{9,8},{10,11... | collective-permute-start | bytes 3538952 | tf_op jit(solution)/shard_map/ppermute | solution.py:38
  7.1 26.8 %collective-permute-start.2 = (bf16[512,1152]{1,0:T(8,128)(2,1)}, bf16[512,1152]{1,0:T(8,128)(2,1)}, u32[]{:S(2)}, u32[]{:S(2)}) collective-permute-start(bf16[512,1152]{1,0:T(8,128)(2,1)} %get-tuple-element.86), channel_id=1, source_target_pairs={{0,2},{1,3},{2,0},{3,1},{4,6},{5,7},{6,4},{7,5},{8,10},{9,11},{10,... | collective-permute-start | bytes 3538952 | tf_op jit(solution)/shard_map/ppermute | solution.py:38
  8.4 25.2 %collective-permute-start = (bf16[128,4224]{1,0:T(8,128)(2,1)}, bf16[128,4224]{1,0:T(8,128)(2,1)S(1)}, u32[]{:S(2)}, u32[]{:S(2)}) collective-permute-start(bf16[128,4224]{1,0:T(8,128)(2,1)} %get-tuple-element.113.refs_0_), channel_id=1, source_target_pairs={{0,4},{1,5},{2,6},{3,7},{4,12},{5,13},{6,14},{7,15},{12,8},{13,9},... | collective-permute-start | bytes 3244040 | tf_op jit(solution)/shard_map/ppermute | solution.py:55
  9.7 48.8 %collective-permute-start.3 = (bf16[512,1152]{1,0:T(8,128)(2,1)}, bf16[512,1152]{1,0:T(8,128)(2,1)}, u32[]{:S(2)}, u32[]{:S(2)}) collective-permute-start(bf16[512,1152]{1,0:T(8,128)(2,1)} %get-tuple-element.86), channel_id=1, source_target_pairs={{0,1},{1,0},{2,3},{3,2},{4,5},{5,4},{6,7},{7,6},{8,9},{9,8},{10,11... | collective-permute-start | bytes 3538952 | tf_op jit(solution)/shard_map/ppermute | solution.py:38
  9.9 49.3 %collective-permute-start.4 = (bf16[512,1152]{1,0:T(8,128)(2,1)}, bf16[512,1152]{1,0:T(8,128)(2,1)}, u32[]{:S(2)}, u32[]{:S(2)}) collective-permute-start(bf16[512,1152]{1,0:T(8,128)(2,1)} %get-tuple-element.85), channel_id=1, source_target_pairs={{0,2},{1,3},{2,0},{3,1},{4,6},{5,7},{6,4},{7,5},{8,10},{9,11},{10,... | collective-permute-start | bytes 3538952 | tf_op jit(solution)/shard_map/ppermute | solution.py:38
  33.6 5.0 %copy-start.3 = (bf16[128,4224]{1,0:T(8,128)(2,1)}, bf16[128,4224]{1,0:T(8,128)(2,1)S(1)}, u32[]{:S(2)}) copy-start(bf16[128,4224]{1,0:T(8,128)(2,1)S(1)} %collective-permute-done.refs_1_.refs_0_) | copy-start | bytes 3244036
  34.0 29.2 %collective-permute-start.5 = (bf16[512,1152]{1,0:T(8,128)(2,1)}, bf16[512,1152]{1,0:T(8,128)(2,1)S(1)}, u32[]{:S(2)}, u32[]{:S(2)}) collective-permute-start(bf16[512,1152]{1,0:T(8,128)(2,1)} %collective-permute-done.1.refs_4_.refs_2_), channel_id=1, source_target_pairs={{16,0},{0,16},{17,1},{1,17},{18,2},{2,18},{19,3},{3,19},{20,4},{4,... | collective-permute-start | bytes 3538952 | tf_op jit(solution)/shard_map/ppermute | solution.py:60
  37.3 25.8 %collective-permute-start.6 = (bf16[512,1152]{1,0:T(8,128)(2,1)}, bf16[512,1152]{1,0:T(8,128)(2,1)S(1)}, u32[]{:S(2)}, u32[]{:S(2)}) collective-permute-start(bf16[512,1152]{1,0:T(8,128)(2,1)} %collective-permute-done.2.refs_9_.refs_7_), channel_id=1, source_target_pairs={{16,0},{0,16},{17,1},{1,17},{18,2},{2,18},{19,3},{3,19},{20,4},{4,... | collective-permute-start | bytes 3538952 | tf_op jit(solution)/shard_map/ppermute | solution.py:60
  37.3 25.8 %collective-permute-start.7 = (bf16[128,4224]{1,0:T(8,128)(2,1)S(1)}, bf16[128,4224]{1,0:T(8,128)(2,1)S(1)}, u32[]{:S(2)}, u32[]{:S(2)}) collective-permute-start(bf16[128,4224]{1,0:T(8,128)(2,1)S(1)} %collective-permute-done.refs_1_.refs_0_), channel_id=1, source_target_pairs={{0,4},{1,5},{2,6},{3,7},{4,12},{5,13},{6,14},{7,15},{12,8},{13,9},... | collective-permute-start | bytes 3244040 | tf_op jit(solution)/shard_map/ppermute | solution.py:55
  63.1 1.5 copy-start.12
  63.1 6.0 %copy-start.9 = (bf16[512,1152]{1,0:T(8,128)(2,1)}, bf16[512,1152]{1,0:T(8,128)(2,1)S(1)}, u32[]{:S(2)}) copy-start(bf16[512,1152]{1,0:T(8,128)(2,1)S(1)} %collective-permute-done.5.refs_6_.refs_4_) | copy-start | bytes 3538948
  63.1 5.9 %copy-start.10 = (bf16[512,1152]{1,0:T(8,128)(2,1)}, bf16[512,1152]{1,0:T(8,128)(2,1)S(1)}, u32[]{:S(2)}) copy-start(bf16[512,1152]{1,0:T(8,128)(2,1)S(1)} %collective-permute-done.6.refs_11_.refs_9_) | copy-start | bytes 3538948
  63.1 4.3 %collective-permute-start.8 = (bf16[512,1152]{1,0:T(8,128)(2,1)}, bf16[512,1152]{1,0:T(8,128)(2,1)S(1)}, u32[]{:S(2)}, u32[]{:S(2)}) collective-permute-start(bf16[512,1152]{1,0:T(8,128)(2,1)} %collective-permute-done.3.refs_5_.refs_3_), channel_id=1, source_target_pairs={{16,0},{0,16},{17,1},{1,17},{18,2},{2,18},{19,3},{3,19},{20,4},{4,... | collective-permute-start | bytes 3538952 | tf_op jit(solution)/shard_map/ppermute | solution.py:60
  64.6 4.5 %collective-permute-start.9 = (bf16[512,1152]{1,0:T(8,128)(2,1)}, bf16[512,1152]{1,0:T(8,128)(2,1)}, u32[]{:S(2)}, u32[]{:S(2)}) collective-permute-start(bf16[512,1152]{1,0:T(8,128)(2,1)} %collective-permute-done.4.refs_8_.refs_6_), channel_id=1, source_target_pairs={{16,0},{0,16},{17,1},{1,17},{18,2},{2,18},{19,3},{3,19},{20,4},{4,... | collective-permute-start | bytes 3538952 | tf_op jit(solution)/shard_map/ppermute | solution.py:60
  65.5 27.9 %collective-permute-start.10 = (bf16[512,1152]{1,0:T(8,128)(2,1)}, bf16[512,1152]{1,0:T(8,128)(2,1)S(1)}, u32[]{:S(2)}, u32[]{:S(2)}) collective-permute-start(bf16[512,1152]{1,0:T(8,128)(2,1)} %collective-permute-done.1.refs_4_.refs_2_), channel_id=1, source_target_pairs={{0,2},{1,3},{2,0},{3,1},{4,6},{5,7},{6,4},{7,5},{8,10},{9,11},{10,... | collective-permute-start | bytes 3538952 | tf_op jit(solution)/shard_map/ppermute | solution.py:38
  66.7 27.5 %collective-permute-start.11 = (bf16[512,1152]{1,0:T(8,128)(2,1)}, bf16[512,1152]{1,0:T(8,128)(2,1)S(1)}, u32[]{:S(2)}, u32[]{:S(2)}) collective-permute-start(bf16[512,1152]{1,0:T(8,128)(2,1)} %collective-permute-done.2.refs_9_.refs_7_), channel_id=1, source_target_pairs={{0,1},{1,0},{2,3},{3,2},{4,5},{5,4},{6,7},{7,6},{8,9},{9,8},{10,11... | collective-permute-start | bytes 3538952 | tf_op jit(solution)/shard_map/ppermute | solution.py:38
  67.0 26.1 %collective-permute-start.12 = (bf16[128,4224]{1,0:T(8,128)(2,1)}, bf16[128,4224]{1,0:T(8,128)(2,1)}, u32[]{:S(2)}, u32[]{:S(2)}) collective-permute-start(bf16[128,4224]{1,0:T(8,128)(2,1)} %copy-done.12), channel_id=1, source_target_pairs={{0,4},{1,5},{2,6},{3,7},{4,12},{5,13},{6,14},{7,15},{12,8},{13,9},... | collective-permute-start | bytes 3244040 | tf_op jit(solution)/shard_map/ppermute | solution.py:55
  67.5 1.6 copy-start.11
  93.4 15.8 %copy-start.5 = (bf16[512,1152]{1,0:T(8,128)(2,1)}, bf16[512,1152]{1,0:T(8,128)(2,1)S(1)}, u32[]{:S(2)}) copy-start(bf16[512,1152]{1,0:T(8,128)(2,1)S(1)} %collective-permute-done.10.refs_2_) | copy-start | bytes 3538948
  94.2 15.0 %copy-start.6 = (bf16[512,1152]{1,0:T(8,128)(2,1)}, bf16[512,1152]{1,0:T(8,128)(2,1)S(1)}, u32[]{:S(2)}) copy-start(bf16[512,1152]{1,0:T(8,128)(2,1)S(1)} %collective-permute-done.11.refs_3_) | copy-start | bytes 3538948
  94.2 15.0 %collective-permute-start.13 = (bf16[512,1152]{1,0:T(8,128)(2,1)S(1)}, bf16[512,1152]{1,0:T(8,128)(2,1)S(1)}, u32[]{:S(2)}, u32[]{:S(2)}) collective-permute-start(bf16[512,1152]{1,0:T(8,128)(2,1)S(1)} %collective-permute-done.10.refs_2_), channel_id=1, source_target_pairs={{16,0},{0,16},{17,1},{1,17},{18,2},{2,18},{19,3},{3,19},{20,4},{4,... | collective-permute-start | bytes 3538952 | tf_op jit(solution)/shard_map/ppermute | solution.py:60
  95.3 14.0 %collective-permute-start.14 = (bf16[512,1152]{1,0:T(8,128)(2,1)S(1)}, bf16[512,1152]{1,0:T(8,128)(2,1)S(1)}, u32[]{:S(2)}, u32[]{:S(2)}) collective-permute-start(bf16[512,1152]{1,0:T(8,128)(2,1)S(1)} %collective-permute-done.11.refs_3_), channel_id=1, source_target_pairs={{16,0},{0,16},{17,1},{1,17},{18,2},{2,18},{19,3},{3,19},{20,4},{4,... | collective-permute-start | bytes 3538952 | tf_op jit(solution)/shard_map/ppermute | solution.py:60
  109.3 1.1 copy-start.7
  109.3 1.5 copy-start.8
  109.3 10.4 %collective-permute-start.15 = (bf16[3,384,1024]{2,1,0:T(8,128)(2,1)}, bf16[3,384,1024]{2,1,0:T(8,128)(2,1)}, u32[]{:S(2)}, u32[]{:S(2)}) collective-permute-start(bf16[3,384,1024]{2,1,0:T(8,128)(2,1)} %bitcast.48), channel_id=1, source_target_pairs={{16,0},{0,16},{17,1},{1,17},{18,2},{2,18},{19,3},{3,19},{20,4},{4,... | collective-permute-start | bytes 7077896 | tf_op jit(solution)/shard_map/ppermute | solution.py:60
  110.7 9.7 %copy-start.4 = (f32[3,384,1024]{2,1,0:T(8,128)S(1)}, f32[3,384,1024]{2,1,0:T(8,128)}, u32[]{:S(2)}) copy-start(f32[3,384,1024]{2,1,0:T(8,128)} %get-tuple-element.140) | copy-start | bytes 14155780
  119.6 15.1 %collective-permute-start.18 = (bf16[128,2176]{1,0:T(8,128)(2,1)}, bf16[128,2176]{1,0:T(8,128)(2,1)S(1)}, u32[]{:S(2)}, u32[]{:S(2)}) collective-permute-start(bf16[128,2176]{1,0:T(8,128)(2,1)} %get-tuple-element.137), channel_id=1, source_target_pairs={{0,4},{1,5},{2,6},{3,7},{4,12},{5,13},{6,14},{7,15},{12,8},{13,9},... | collective-permute-start | bytes 1671176 | tf_op jit(solution)/shard_map/ppermute | solution.py:55
  122.7 10.1 %collective-permute-start.16 = (bf16[192,1024]{1,0:T(8,128)(2,1)}, bf16[192,1024]{1,0:T(8,128)(2,1)S(1)}, u32[]{:S(2)}, u32[]{:S(2)}) collective-permute-start(bf16[192,1024]{1,0:T(8,128)(2,1)} %get-tuple-element.171), channel_id=1, source_target_pairs={{0,1},{1,0},{2,3},{3,2},{4,5},{5,4},{6,7},{7,6},{8,9},{9,8},{10,11... | collective-permute-start | bytes 1179656 | tf_op jit(solution)/shard_map/ppermute | solution.py:38
  123.2 12.9 %copy-start.16 = (bf16[128,2176]{1,0:T(8,128)(2,1)S(1)}, bf16[128,2176]{1,0:T(8,128)(2,1)}, u32[]{:S(2)}) copy-start(bf16[128,2176]{1,0:T(8,128)(2,1)} %get-tuple-element.146) | copy-start | bytes 1671172
  123.3 9.6 %collective-permute-start.17 = (bf16[192,1024]{1,0:T(8,128)(2,1)}, bf16[192,1024]{1,0:T(8,128)(2,1)S(1)}, u32[]{:S(2)}, u32[]{:S(2)}) collective-permute-start(bf16[192,1024]{1,0:T(8,128)(2,1)} %get-tuple-element.170), channel_id=1, source_target_pairs={{0,2},{1,3},{2,0},{3,1},{4,6},{5,7},{6,4},{7,5},{8,10},{9,11},{10,... | collective-permute-start | bytes 1179656 | tf_op jit(solution)/shard_map/ppermute | solution.py:38
  132.7 5.6 %copy-start.13 = (f32[1,384,1024]{2,1,0:T(8,128)S(1)}, f32[1,384,1024]{2,1,0:T(8,128)}, u32[]{:S(2)}) copy-start(f32[1,384,1024]{2,1,0:T(8,128)} %get-tuple-element.143) | copy-start | bytes 4718596
  134.7 3.6 %collective-permute-start.19 = (bf16[384,1024]{1,0:T(8,128)(2,1)}, bf16[384,1024]{1,0:T(8,128)(2,1)S(1)}, u32[]{:S(2)}, u32[]{:S(2)}) collective-permute-start(bf16[384,1024]{1,0:T(8,128)(2,1)} %bitcast.49), channel_id=1, source_target_pairs={{16,0},{0,16},{17,1},{1,17},{18,2},{2,18},{19,3},{3,19},{20,4},{4,... | collective-permute-start | bytes 2359304 | tf_op jit(solution)/shard_map/ppermute | solution.py:60
  136.2 15.2 %collective-permute-start.22 = (bf16[128,2176]{1,0:T(8,128)(2,1)S(1)}, bf16[128,2176]{1,0:T(8,128)(2,1)S(1)}, u32[]{:S(2)}, u32[]{:S(2)}) collective-permute-start(bf16[128,2176]{1,0:T(8,128)(2,1)S(1)} %add_convert_fusion.1), channel_id=1, source_target_pairs={{0,4},{1,5},{2,6},{3,7},{4,12},{5,13},{6,14},{7,15},{12,8},{13,9},... | collective-permute-start | bytes 1671176 | tf_op jit(solution)/shard_map/ppermute | solution.py:55
  138.6 12.9 %copy-start.15 = (bf16[128,2176]{1,0:T(8,128)(2,1)S(1)}, bf16[128,2176]{1,0:T(8,128)(2,1)}, u32[]{:S(2)}) copy-start(bf16[128,2176]{1,0:T(8,128)(2,1)} %get-tuple-element.150) | copy-start | bytes 1671172
  138.6 12.8 %collective-permute-start.20 = (bf16[192,1024]{1,0:T(8,128)(2,1)S(1)}, bf16[192,1024]{1,0:T(8,128)(2,1)S(1)}, u32[]{:S(2)}, u32[]{:S(2)}) collective-permute-start(bf16[192,1024]{1,0:T(8,128)(2,1)S(1)} %get-tuple-element.173), channel_id=1, source_target_pairs={{0,1},{1,0},{2,3},{3,2},{4,5},{5,4},{6,7},{7,6},{8,9},{9,8},{10,11... | collective-permute-start | bytes 1179656 | tf_op jit(solution)/shard_map/ppermute | solution.py:38
  139.7 11.8 %collective-permute-start.21 = (bf16[192,1024]{1,0:T(8,128)(2,1)S(1)}, bf16[192,1024]{1,0:T(8,128)(2,1)S(1)}, u32[]{:S(2)}, u32[]{:S(2)}) collective-permute-start(bf16[192,1024]{1,0:T(8,128)(2,1)S(1)} %get-tuple-element.172), channel_id=1, source_target_pairs={{0,2},{1,3},{2,0},{3,1},{4,6},{5,7},{6,4},{7,5},{8,10},{9,11},{10,... | collective-permute-start | bytes 1179656 | tf_op jit(solution)/shard_map/ppermute | solution.py:38
  151.6 17.1 %copy-start.2 = (f32[1,1,384,2048]{3,2,1,0:T(8,128)S(1)}, f32[1,1,384,2048]{3,2,1,0:T(8,128)}, u32[]{:S(2)}) copy-start(f32[1,1,384,2048]{3,2,1,0:T(8,128)} %refs_5_.1) | copy-start | bytes 9437188
  153.3 15.5 %copy-start.1 = (f32[1,1,384,2048]{3,2,1,0:T(8,128)S(1)}, f32[1,1,384,2048]{3,2,1,0:T(8,128)}, u32[]{:S(2)}) copy-start(f32[1,1,384,2048]{3,2,1,0:T(8,128)} %refs_4_.1) | copy-start | bytes 9437188
  153.3 9.9 %collective-permute-start.23 = (bf16[192,1024]{1,0:T(8,128)(2,1)S(1)}, bf16[192,1024]{1,0:T(8,128)(2,1)S(1)}, u32[]{:S(2)}, u32[]{:S(2)}) collective-permute-start(bf16[192,1024]{1,0:T(8,128)(2,1)S(1)} %get-tuple-element.151), channel_id=1, source_target_pairs={{0,2},{1,3},{2,0},{3,1},{4,6},{5,7},{6,4},{7,5},{8,10},{9,11},{10,... | collective-permute-start | bytes 1179656 | tf_op jit(solution)/shard_map/ppermute | solution.py:38
  153.6 9.6 %collective-permute-start.25 = (bf16[192,1024]{1,0:T(8,128)(2,1)S(1)}, bf16[192,1024]{1,0:T(8,128)(2,1)S(1)}, u32[]{:S(2)}, u32[]{:S(2)}) collective-permute-start(bf16[192,1024]{1,0:T(8,128)(2,1)S(1)} %get-tuple-element.153), channel_id=1, source_target_pairs={{0,1},{1,0},{2,3},{3,2},{4,5},{5,4},{6,7},{7,6},{8,9},{9,8},{10,11... | collective-permute-start | bytes 1179656 | tf_op jit(solution)/shard_map/ppermute | solution.py:38
  154.1 13.7 %collective-permute-start.27 = (bf16[128,2176]{1,0:T(8,128)(2,1)S(1)}, bf16[128,2176]{1,0:T(8,128)(2,1)S(1)}, u32[]{:S(2)}, u32[]{:S(2)}) collective-permute-start(bf16[128,2176]{1,0:T(8,128)(2,1)S(1)} %add_convert_fusion), channel_id=1, source_target_pairs={{0,4},{1,5},{2,6},{3,7},{4,12},{5,13},{6,14},{7,15},{12,8},{13,9},... | collective-permute-start | bytes 1671176 | tf_op jit(solution)/shard_map/ppermute | solution.py:55
  164.9 3.3 %collective-permute-start.24 = (bf16[192,1024]{1,0:T(8,128)(2,1)S(1)}, bf16[192,1024]{1,0:T(8,128)(2,1)S(1)}, u32[]{:S(2)}, u32[]{:S(2)}) collective-permute-start(bf16[192,1024]{1,0:T(8,128)(2,1)S(1)} %get-tuple-element.167.refs_0_), channel_id=1, source_target_pairs={{16,0},{0,16},{17,1},{1,17},{18,2},{2,18},{19,3},{3,19},{20,4},{4,... | collective-permute-start | bytes 1179656 | tf_op jit(solution)/shard_map/ppermute | solution.py:60
  166.8 1.9 %collective-permute-start.26 = (bf16[192,1024]{1,0:T(8,128)(2,1)S(1)}, bf16[192,1024]{1,0:T(8,128)(2,1)S(1)}, u32[]{:S(2)}, u32[]{:S(2)}) collective-permute-start(bf16[192,1024]{1,0:T(8,128)(2,1)S(1)} %get-tuple-element.166.refs_1_), channel_id=1, source_target_pairs={{16,0},{0,16},{17,1},{1,17},{18,2},{2,18},{19,3},{3,19},{20,4},{4,... | collective-permute-start | bytes 1179656 | tf_op jit(solution)/shard_map/ppermute | solution.py:60
  167.6 7.8 %copy-start.17 = (s32[128,8]{0,1:T(8,128)S(1)}, s32[128,8]{0,1:T(8,128)}, u32[]{:S(2)}) copy-start(s32[128,8]{0,1:T(8,128)} %param.12) | copy-start | bytes 12292
  167.6 7.9 %copy-start.18 = (s32[1,2]{1,0:T(1,128)S(1)}, s32[1,2]{1,0:T(1,128)}, u32[]{:S(2)}) copy-start(s32[1,2]{1,0:T(1,128)} %param.18) | copy-start | bytes 28
  167.8 6.1 %copy-start.14 = (bf16[128,2176]{1,0:T(8,128)(2,1)}, bf16[128,2176]{1,0:T(8,128)(2,1)S(1)}, u32[]{:S(2)}) copy-start(bf16[128,2176]{1,0:T(8,128)(2,1)S(1)} %collective-permute-done.27) | copy-start | bytes 1671172
  174.0 5.5 %collective-permute-start.28 = (bf16[384,2048]{1,0:T(8,128)(2,1)S(1)}, bf16[384,2048]{1,0:T(8,128)(2,1)}, u32[]{:S(2)}, u32[]{:S(2)}) collective-permute-start(bf16[384,2048]{1,0:T(8,128)(2,1)S(1)} %get-tuple-element.158), channel_id=1, source_target_pairs={{16,0},{0,16},{17,1},{1,17},{18,2},{2,18},{19,3},{3,19},{20,4},{4,... | collective-permute-start | bytes 4718600 | tf_op jit(solution)/shard_map/ppermute | solution.py:60
